TPU v7x, 32 devices: a whole 2x2x4 slice. The times are simulated.
32 devices in a mesh: fsdp: 4 (over y, x), ctx: 8 (over z, core).
Axes of the slice: x: 2, y: 2, z: 4, core: 2. Of those that a mesh axis runs over, the one named last changes fastest.
Arguments:
- tokens: bfloat16 [2, 4, 1024, 1536], P(None, 'fsdp', 'ctx'), may hold values from -6 to 6
- doc_starts: int32 [2, 4, 4], P(None, 'fsdp'), may hold values from 0 to 1023, as said below
- routes: int32 [2, 4, 1024, 4], P(None, 'fsdp', 'ctx'), may hold values from 0 to 7, all different within a row; in each aligned block of 128 rows (0 to 127, 128 to 255, ..., all dimensions but the last counted through in order) at most 80 rows name the same one
- gates: float32 [2, 4, 1024, 4], P(None, 'fsdp', 'ctx'), may hold values from 0.3 to 1.2
- attn_gain: bfloat16 [1536], P('fsdp'), may hold values from 0.25 to 1.75
- w_q: bfloat16 [1536, 1536], P('fsdp'), may hold values from -0.625 to 0.625
- key_value_weight: bfloat16 [1536, 1024], P('fsdp'), may hold values from -0.625 to 0.625
- w_o: bfloat16 [1536, 1536], P('fsdp'), may hold values from -0.15625 to 0.15625
- moe_gain: bfloat16 [1536], P('fsdp'), may hold values from 0.25 to 1.75
- expert_in: bfloat16 [8, 1536, 1024], P('fsdp'), may hold values from -0.15625 to 0.15625
- expert_out: bfloat16 [8, 512, 1536], P('fsdp'), may hold values from -0.25 to 0.25
- cotangent: bfloat16 [2, 4, 1024, 1536], P(None, 'fsdp', 'ctx'), may hold values from -6 to 6
Outputs:
- block_output: bfloat16 [2, 4, 1024, 1536], P(None, 'fsdp', 'ctx')
- input_grad: float32 [2, 4, 1024, 1536], P(None, 'fsdp', 'ctx')
- attn_gain_grad: float32 [1536], P('fsdp')
- w_q_grad: float32 [1536, 1536], P('fsdp')
- w_kv_grad: float32 [1536, 1024], P('fsdp')
- w_o_grad: float32 [1536, 1536], P('fsdp')
- moe_gain_grad: float32 [1536], P('fsdp')
- expert_in_grad: float32 [8, 1536, 1024], P('fsdp')
- expert_out_grad: float32 [8, 512, 1536], P('fsdp')
Inputs may be any that keep to these rules, and one draw needn't show every extreme that they name: `doc_starts`: each sequence's 4 starts rise strictly from 0. `routes`: each row names 4 different experts; among the 128 rows of one device (aligned blocks) no expert is named more than 80 times, and in some block one is named exactly 80 times.
All inputs are finite; a program needn't handle non-finite values.
Results may differ from a plain program's by a relative error of at most 0.019.
Values may be sent and summed in bfloat16 or wider, within the bound.
A program may use at most 320 MiB of HBM per device.

v0:
```python
import jax
import jax.numpy as jnp
from jax import lax
from jax.sharding import PartitionSpec as P

MODEL_WIDTH = 1536
QUERY_HEADS = 24
KEY_VALUE_HEADS = 8
HEAD_SIZE = 64
F = 512
E = 8
TOP = 4
MB = 2


eps = 1e-05
theta = 10000.0


def rms_scale(weight_matrix, gain_vector):
    inverse = lax.rsqrt(jnp.mean(weight_matrix * weight_matrix, axis=-1, keepdims=True) + eps)
    return weight_matrix * inverse * gain_vector


def turn_angles(positions):
    frequency = theta ** (-jnp.arange(0, HEAD_SIZE, 2, dtype=jnp.float32) / HEAD_SIZE)
    angles = positions.astype(jnp.float32)[:, None] * frequency[None, :]
    doubled = jnp.concatenate([angles, angles], axis=1)
    return (jnp.cos(doubled)[:, None, :], jnp.sin(doubled)[:, None, :])


def apply_rotary(value_rows, cosine_table, sine_table):
    half_width = HEAD_SIZE // 2
    turned = jnp.concatenate([-value_rows[..., half_width:], value_rows[..., :half_width]], axis=-1)
    return value_rows * cosine_table + turned * sine_table


def rotate_back(gradient, cosine_table, sine_table):
    half_width = HEAD_SIZE // 2
    scaled = gradient * sine_table
    turned = jnp.concatenate([scaled[..., half_width:], -scaled[..., :half_width]], axis=-1)
    return gradient * cosine_table + turned


def document_index(doc_begin, positions):
    return jnp.sum((doc_begin[None, :] <= positions[:, None]).astype(jnp.int32), axis=1)


def head_rows(value_rows):
    row_count_total = value_rows.shape[0]
    query_group_size = QUERY_HEADS // KEY_VALUE_HEADS
    return (
        value_rows.reshape(row_count_total, KEY_VALUE_HEADS, query_group_size, HEAD_SIZE)
        .transpose(1, 2, 0, 3)
        .reshape(KEY_VALUE_HEADS, query_group_size * row_count_total, HEAD_SIZE)
    )


def token_columns(value_rows, row_count_total):
    query_group_size = QUERY_HEADS // KEY_VALUE_HEADS
    return (
        value_rows.reshape(KEY_VALUE_HEADS, query_group_size, row_count_total, HEAD_SIZE)
        .transpose(2, 0, 1, 3)
        .reshape(row_count_total, QUERY_HEADS * HEAD_SIZE)
    )


def key_blocks(weight_matrix, block_extent):
    overall_rows = weight_matrix.shape[0]
    return weight_matrix.reshape(
        overall_rows // block_extent, block_extent, KEY_VALUE_HEADS, HEAD_SIZE
    ).transpose(0, 2, 1, 3)


def expert_forward(expert_rows, expand, reduce_weight):
    up_gate = jnp.einsum("ecd,edf->ecf", expert_rows, expand, preferred_element_type=jnp.float32)
    active = (jax.nn.silu(up_gate[..., :F]) * up_gate[..., F:]).astype(jnp.bfloat16)
    result = jnp.einsum("ecf,efd->ecd", active, reduce_weight, preferred_element_type=jnp.float32)
    return (up_gate, active, result)


def expert_input_grads(up_gate, result_grad, expand, reduce_weight):
    active_grad = jnp.einsum(
        "ecd,efd->ecf", result_grad, reduce_weight, preferred_element_type=jnp.float32
    )
    gate_part = up_gate[..., :F]
    up_part = up_gate[..., F:]
    sigmoid = jax.nn.sigmoid(gate_part)
    gate_grad = active_grad * up_part * sigmoid * (1.0 + gate_part * (1.0 - sigmoid))
    up_grad = active_grad * gate_part * sigmoid
    both_grad = jnp.concatenate([gate_grad, up_grad], axis=-1).astype(jnp.bfloat16)
    rows_grad = jnp.einsum("ecf,edf->ecd", both_grad, expand, preferred_element_type=jnp.float32)
    return (rows_grad, both_grad)


def expert_weight_grads(expert_rows, both_grad, active, result_grad):
    expand_grad = jnp.einsum(
        "ecd,ecf->edf", expert_rows, both_grad, preferred_element_type=jnp.float32
    )
    reduce_grad = jnp.einsum(
        "ecf,ecd->efd", active, result_grad, preferred_element_type=jnp.float32
    )
    return (expand_grad, reduce_grad)


def expert_share(expand_grad, reduce_grad):
    pieces = (
        lax.psum_scatter(
            expand_grad.astype(jnp.bfloat16), "ctx", scatter_dimension=1, tiled=True
        ).astype(jnp.float32),
        lax.psum_scatter(
            reduce_grad.astype(jnp.bfloat16), "ctx", scatter_dimension=1, tiled=True
        ).astype(jnp.float32),
    )
    summed = (
        lax.all_gather(pieces[0].astype(jnp.bfloat16), "ctx", axis=1, tiled=True).astype(
            jnp.float32
        ),
        lax.all_gather(pieces[1].astype(jnp.bfloat16), "ctx", axis=1, tiled=True).astype(
            jnp.float32
        ),
    )
    return (summed[0], summed[1])


def dense_weight_grads(normed, query_low, pair_low, attn_low, middle_low):
    query_weight_grad = jnp.einsum(
        "td,tq->dq", normed, query_low, preferred_element_type=jnp.float32
    )
    pair_weight_grad = jnp.einsum("td,tk->dk", normed, pair_low, preferred_element_type=jnp.float32)
    output_grad = jnp.einsum("to,td->od", attn_low, middle_low, preferred_element_type=jnp.float32)
    return (query_weight_grad, pair_weight_grad, output_grad)


def dense_share(gain_one_grad, query_weight_grad, pair_weight_grad, output_grad, gain_two_grad):
    pieces = (
        lax.psum_scatter(gain_one_grad, ("fsdp", "ctx"), scatter_dimension=0, tiled=True),
        lax.psum_scatter(query_weight_grad, ("fsdp", "ctx"), scatter_dimension=0, tiled=True),
        lax.psum_scatter(pair_weight_grad, ("fsdp", "ctx"), scatter_dimension=0, tiled=True),
        lax.psum_scatter(output_grad, ("fsdp", "ctx"), scatter_dimension=0, tiled=True),
        lax.psum_scatter(gain_two_grad, ("fsdp", "ctx"), scatter_dimension=0, tiled=True),
    )
    rebuilt = (
        lax.all_gather(pieces[0].astype(jnp.bfloat16), "ctx", axis=0, tiled=True).astype(
            jnp.float32
        ),
        lax.all_gather(pieces[1].astype(jnp.bfloat16), "ctx", axis=0, tiled=True).astype(
            jnp.float32
        ),
        lax.all_gather(pieces[2].astype(jnp.bfloat16), "ctx", axis=0, tiled=True).astype(
            jnp.float32
        ),
        lax.all_gather(pieces[3].astype(jnp.bfloat16), "ctx", axis=0, tiled=True).astype(
            jnp.float32
        ),
        lax.all_gather(pieces[4].astype(jnp.bfloat16), "ctx", axis=0, tiled=True).astype(
            jnp.float32
        ),
    )
    return (rebuilt[0], rebuilt[1], rebuilt[2], rebuilt[3], rebuilt[4])


def add_totals(totals, shares):
    if totals is None:
        return shares
    return jax.tree.map(lambda earlier, current: earlier + current, totals, shares)


def shards(
    tokens,
    doc_starts,
    routes,
    gates,
    attn_gain,
    w_q,
    key_value_weight,
    w_o,
    moe_gain,
    expert_in,
    expert_out,
    cotangent,
):
    device_rows = tokens.shape[2]
    slot_count = device_rows * TOP * 5 // (4 * E)
    context_size = lax.axis_size("ctx")
    length = device_rows * context_size
    block_extent = min(512, length)
    block_count = length // block_extent
    query_group_size = QUERY_HEADS // KEY_VALUE_HEADS
    key_feature_width = KEY_VALUE_HEADS * HEAD_SIZE
    score_scale = 1.0 / HEAD_SIZE
    positions = lax.axis_index("ctx") * device_rows + jnp.arange(device_rows, dtype=jnp.int32)
    everywhere = jnp.arange(length, dtype=jnp.int32)
    cosine_table, sine_table = turn_angles(positions)
    key_place = everywhere.reshape(block_count, block_extent)
    row_place = jnp.tile(positions, query_group_size)
    expert_ids = jnp.arange(E, dtype=jnp.int32)
    row_layout = (KEY_VALUE_HEADS, query_group_size * device_rows)
    zero_rows = jnp.zeros((KEY_VALUE_HEADS, query_group_size * device_rows, HEAD_SIZE), jnp.float32)
    dense_totals = None
    expert_totals = None
    outputs = []
    input_grads = []
    for micro_step in range(MB):
        full_gain_one, full_query, full_pairs, full_output, full_gain_two = (
            lax.all_gather(attn_gain, "fsdp", axis=0, tiled=True),
            lax.all_gather(w_q, "fsdp", axis=0, tiled=True),
            lax.all_gather(key_value_weight, "fsdp", axis=0, tiled=True),
            lax.all_gather(w_o, "fsdp", axis=0, tiled=True),
            lax.all_gather(moe_gain, "fsdp", axis=0, tiled=True),
        )
        residual = tokens[micro_step, 0].astype(jnp.float32)
        gain_one = full_gain_one.astype(jnp.float32)
        normed = rms_scale(residual, gain_one).astype(jnp.bfloat16)
        query_pre = jnp.dot(normed, full_query, preferred_element_type=jnp.float32)
        paired_preactivation = jnp.dot(normed, full_pairs, preferred_element_type=jnp.float32)
        query_rot = apply_rotary(
            query_pre.reshape(device_rows, QUERY_HEADS, HEAD_SIZE), cosine_table, sine_table
        ).astype(jnp.bfloat16)
        key_rot = apply_rotary(
            paired_preactivation[:, :key_feature_width].reshape(
                device_rows, KEY_VALUE_HEADS, HEAD_SIZE
            ),
            cosine_table,
            sine_table,
        ).astype(jnp.bfloat16)
        local_pairs = jnp.concatenate(
            [
                key_rot.reshape(device_rows, key_feature_width),
                paired_preactivation[:, key_feature_width:].astype(jnp.bfloat16),
            ],
            axis=1,
        )
        all_pairs = lax.all_gather(local_pairs, "ctx", axis=0, tiled=True)
        key_all = key_blocks(all_pairs[:, :key_feature_width], block_extent)
        value_all = key_blocks(all_pairs[:, key_feature_width:], block_extent)
        doc_begin = doc_starts[micro_step, 0]
        key_docs = document_index(doc_begin, everywhere).reshape(block_count, block_extent)
        row_docs = jnp.tile(document_index(doc_begin, positions), query_group_size)
        query_rows = head_rows(query_rot)

        def masked_scores(key_part, place_block, docs_block):
            raw_scores = (
                jnp.einsum("hrd,hkd->hrk", query_rows, key_part, preferred_element_type=jnp.float32)
                * score_scale
            )
            visible_mask = (
                (place_block[None, :] <= row_place[:, None])
                & (docs_block[None, :] == row_docs[:, None])
            )[None]
            return (jnp.where(visible_mask, raw_scores, -1e30), visible_mask)

        def stats_step(state_now, element):
            row_max, row_sum = state_now
            key_part, place_block, docs_block = element
            masked, visible_mask = masked_scores(key_part, place_block, docs_block)
            new_max = jnp.maximum(row_max, jnp.max(masked, axis=-1))
            weights = jnp.where(visible_mask, jnp.exp(masked - new_max[..., None]), 0.0)
            return (
                (new_max, row_sum * jnp.exp(row_max - new_max) + jnp.sum(weights, axis=-1)),
                None,
            )

        (row_max, row_sum), _ = lax.scan(
            stats_step,
            (jnp.full(row_layout, -1e30, jnp.float32), jnp.zeros(row_layout, jnp.float32)),
            (key_all, key_place, key_docs),
        )

        def probabilities(key_part, place_block, docs_block):
            masked, visible_mask = masked_scores(key_part, place_block, docs_block)
            return (
                jnp.where(visible_mask, jnp.exp(masked - row_max[..., None]), 0.0)
                / row_sum[..., None]
            )

        def value_step(state_now, element):
            kept_sum, rest_sum = state_now
            key_part, value_part, place_block, docs_block = element
            attn_prob = probabilities(key_part, place_block, docs_block)
            prob_low = attn_prob.astype(jnp.bfloat16)
            prob_rest = (attn_prob - prob_low.astype(jnp.float32)).astype(jnp.bfloat16)
            kept_sum = kept_sum + jnp.einsum(
                "hrk,hkd->hrd", prob_low, value_part, preferred_element_type=jnp.float32
            )
            rest_sum = rest_sum + jnp.einsum(
                "hrk,hkd->hrd", prob_rest, value_part, preferred_element_type=jnp.float32
            )
            return ((kept_sum, rest_sum), None)

        (attn_rows, rest_rows), _ = lax.scan(
            value_step, (zero_rows, zero_rows), (key_all, value_all, key_place, key_docs)
        )
        attn_low = token_columns(attn_rows, device_rows).astype(jnp.bfloat16)
        middle = residual + jnp.dot(attn_low, full_output, preferred_element_type=jnp.float32)
        gain_two = full_gain_two.astype(jnp.float32)
        moe_in = rms_scale(middle, gain_two).astype(jnp.bfloat16)
        route_flat = routes[micro_step, 0].reshape(-1)
        gate_rows = gates[micro_step, 0]
        onehot = (route_flat[:, None] == expert_ids[None, :]).astype(jnp.int32)
        before = jnp.cumsum(onehot, axis=0) - onehot
        target = route_flat * slot_count + jnp.sum(before * onehot, axis=1)
        source = jnp.arange(device_rows * TOP, dtype=jnp.int32) // TOP
        owner_row = jnp.full((E * slot_count,), device_rows, jnp.int32).at[target].set(source)
        slot_gate = jnp.zeros((E * slot_count,), jnp.float32).at[target].set(gate_rows.reshape(-1))
        padded = jnp.concatenate([moe_in, jnp.zeros((1, MODEL_WIDTH), jnp.bfloat16)], axis=0)
        expert_rows = padded[owner_row].reshape(E, slot_count, MODEL_WIDTH)
        owned_rows = lax.all_to_all(expert_rows, "fsdp", split_axis=0, concat_axis=1, tiled=True)
        up_gate, active, owned_result = expert_forward(owned_rows, expert_in, expert_out)
        result = lax.all_to_all(
            owned_result.astype(jnp.bfloat16), "fsdp", split_axis=1, concat_axis=0, tiled=True
        ).astype(owned_result.dtype)
        picked = result.reshape(E * slot_count, MODEL_WIDTH)[target].reshape(
            device_rows, TOP, MODEL_WIDTH
        )
        final_rows = middle + jnp.sum(picked * gate_rows[..., None], axis=1)
        outputs.append(final_rows.astype(jnp.bfloat16))
        out_grad = cotangent[micro_step, 0].astype(jnp.float32)
        grad_pad = jnp.concatenate([out_grad, jnp.zeros((1, MODEL_WIDTH), jnp.float32)], axis=0)
        result_grad = (
            (grad_pad[owner_row] * slot_gate[:, None])
            .astype(jnp.bfloat16)
            .reshape(E, slot_count, MODEL_WIDTH)
        )
        owned_grad = lax.all_to_all(result_grad, "fsdp", split_axis=0, concat_axis=1, tiled=True)
        owned_rows_grad, both_grad = expert_input_grads(up_gate, owned_grad, expert_in, expert_out)
        rows_grad = lax.all_to_all(
            owned_rows_grad.astype(jnp.bfloat16), "fsdp", split_axis=1, concat_axis=0, tiled=True
        ).astype(owned_rows_grad.dtype)
        expert_items = (owned_rows, both_grad, active, owned_grad)
        expand_grad, reduce_grad = expert_weight_grads(
            expert_items[0], expert_items[1], expert_items[2], expert_items[3]
        )
        expert_totals = add_totals(expert_totals, expert_share(expand_grad, reduce_grad))
        moe_in_grad = jnp.sum(
            rows_grad.reshape(E * slot_count, MODEL_WIDTH)[target].reshape(
                device_rows, TOP, MODEL_WIDTH
            ),
            axis=1,
        )
        _, pull_two = jax.vjp(rms_scale, middle, gain_two)
        middle_norm_grad, gain_two_grad = pull_two(moe_in_grad)
        middle_grad = out_grad + middle_norm_grad
        middle_low = middle_grad.astype(jnp.bfloat16)
        attn_grad = jnp.einsum(
            "td,od->to", middle_low, full_output, preferred_element_type=jnp.float32
        )
        grad_rows = head_rows(
            attn_grad.astype(jnp.bfloat16).reshape(device_rows, QUERY_HEADS, HEAD_SIZE)
        )
        row_delta = jnp.sum(grad_rows.astype(jnp.float32) * (attn_rows + rest_rows), axis=-1)

        def grad_step(query_grad, element):
            key_part, value_part, place_block, docs_block = element
            attn_prob = probabilities(key_part, place_block, docs_block)
            prob_grad = jnp.einsum(
                "hrd,hkd->hrk", grad_rows, value_part, preferred_element_type=jnp.float32
            )
            score_grad = (attn_prob * (prob_grad - row_delta[..., None])).astype(jnp.bfloat16)
            query_grad = (
                query_grad
                + jnp.einsum(
                    "hrk,hkd->hrd", score_grad, key_part, preferred_element_type=jnp.float32
                )
                * score_scale
            )
            key_grad = (
                jnp.einsum(
                    "hrk,hrd->hkd", score_grad, query_rows, preferred_element_type=jnp.float32
                )
                * score_scale
            )
            value_grad = jnp.einsum(
                "hrk,hrd->hkd",
                attn_prob.astype(jnp.bfloat16),
                grad_rows,
                preferred_element_type=jnp.float32,
            )
            return (query_grad, (key_grad, value_grad))

        query_grad, (key_grads, value_grads) = lax.scan(
            grad_step, zero_rows, (key_all, value_all, key_place, key_docs)
        )
        pair_grads = jnp.concatenate(
            [
                key_grads.transpose(0, 2, 1, 3).reshape(length, key_feature_width),
                value_grads.transpose(0, 2, 1, 3).reshape(length, key_feature_width),
            ],
            axis=1,
        )
        paired_sum = lax.psum_scatter(
            pair_grads.astype(jnp.bfloat16), "ctx", scatter_dimension=0, tiled=True
        ).astype(jnp.float32)
        key_pre_grad = rotate_back(
            paired_sum[:, :key_feature_width].reshape(device_rows, KEY_VALUE_HEADS, HEAD_SIZE),
            cosine_table,
            sine_table,
        ).reshape(device_rows, key_feature_width)
        pair_low = jnp.concatenate(
            [key_pre_grad, paired_sum[:, key_feature_width:]], axis=1
        ).astype(jnp.bfloat16)
        query_low = (
            rotate_back(
                token_columns(query_grad, device_rows).reshape(device_rows, QUERY_HEADS, HEAD_SIZE),
                cosine_table,
                sine_table,
            )
            .reshape(device_rows, QUERY_HEADS * HEAD_SIZE)
            .astype(jnp.bfloat16)
        )
        normed_grad = jnp.einsum(
            "tq,dq->td", query_low, full_query, preferred_element_type=jnp.float32
        ) + jnp.einsum("tk,dk->td", pair_low, full_pairs, preferred_element_type=jnp.float32)
        _, pull_one = jax.vjp(rms_scale, residual, gain_one)
        residual_grad, gain_one_grad = pull_one(normed_grad)
        input_grads.append(middle_grad + residual_grad)
        query_weight_grad, pair_weight_grad, output_grad = dense_weight_grads(
            normed, query_low, pair_low, attn_low, middle_low
        )
        dense_totals = add_totals(
            dense_totals,
            dense_share(
                gain_one_grad, query_weight_grad, pair_weight_grad, output_grad, gain_two_grad
            ),
        )
    block_output = jnp.stack(outputs)[:, None]
    input_grad = jnp.stack(input_grads)[:, None]
    return (
        block_output,
        input_grad,
        dense_totals[0],
        dense_totals[1],
        dense_totals[2],
        dense_totals[3],
        dense_totals[4],
        expert_totals[0],
        expert_totals[1],
    )


def solution(mesh):
    return jax.shard_map(
        shards,
        mesh=mesh,
        in_specs=(
            P(None, "fsdp", "ctx", None),
            P(None, "fsdp", None),
            P(None, "fsdp", "ctx", None),
            P(None, "fsdp", "ctx", None),
            P("fsdp"),
            P("fsdp", None),
            P("fsdp", None),
            P("fsdp", None),
            P("fsdp"),
            P("fsdp", None, None),
            P("fsdp", None, None),
            P(None, "fsdp", "ctx", None),
        ),
        out_specs=(
            P(None, "fsdp", "ctx", None),
            P(None, "fsdp", "ctx", None),
            P("fsdp"),
            P("fsdp", None),
            P("fsdp", None),
            P("fsdp", None),
            P("fsdp"),
            P("fsdp", None, None),
            P("fsdp", None, None),
        ),
        check_vma=False,
    )
```

profile of v0, /device:TPU:0, one launch (start us, length us, event | category | flops | bytes accessed | tf_op | source)
XLA Modules:
  0.0 1978.0 jit_solution(5220345786003939456)
XLA Ops:
  9.4 9.5 all-gather
  22.0 34.5 %all-gather.16.cloned.1.call-done = bf16[1536,1024]{1,0:T(8,128)(2,1)} async-done(((bf16[384,1024]{1,0:T(8,128)(2,1)}), bf16[1536,1024]{1,0:T(8,128)(2,1)}) %all-gather.16.cloned.1.call-update) | async-done | bytes 3145744 | tf_op jit(solution)/shard_map/all_gather | solution.py:208
  88.0 7.1 gather_fusion.4
  105.1 34.3 %all-gather.1 = bf16[4,1,384]{2,1,0:T(2,128)(2,1)S(1)} all-gather(bf16[1,1,384]{2,1,0:T(2,128)(2,1)S(1)} %reshape.1094), channel_id=1, replica_groups=mesh['fsdp'=4,'ctx'=8] {'fsdp'}, dimensions={0}, use_global_device_ids=true | all-gather | bytes 3840 | tf_op jit(solution)/shard_map/all_gather | solution.py:210
  176.4 24.6 %while.82 = (s32[]{:T(128)}, f32[8,384]{1,0:T(8,128)}, f32[8,384]{1,0:T(8,128)}, s32[2,512]{1,0:T(2,128)S(1)}, s32[2,512]{1,0:T(2,128)}, /*index=5*/bf16[2,8,512...) while((s32[]{:T(128)}, f32[8,384]{1,0:T(8,128)}, ...), condition=%wide.region_6.7_spmd.clone, body=%wide.region_3.6_spmd.clone.sunk | while | flops 214514688 | bytes 15203576 | solution.py:264
  208.3 29.6 %while.83 = (s32[]{:T(128)}, f32[8,384,64]{1,2,0:T(8,128)}, f32[8,384,64]{1,2,0:T(8,128)}, s32[2,512]{1,0:T(2,128)S(1)}, s32[2,512]{1,0:T(2,128)}, /*index=5*/bf...) while((s32[]{:T(128)}, f32[8,384,64]{1,2,0:T(8,128)}, ...), condition=%wide.region_8.9_spmd.clone, body=%wide.region_7.8_spmd.clone.sunk | while | flops 621084672 | bytes 60075288 | solution.py:291
  268.7 7.1 gather_fusion.6
  319.3 23.8 %while.84 = (s32[]{:T(128)}, f32[8,384]{1,0:T(8,128)}, f32[8,384]{1,0:T(8,128)}, s32[2,512]{1,0:T(2,128)S(1)}, s32[2,512]{1,0:T(2,128)}, /*index=5*/bf16[2,8,512...) while((s32[]{:T(128)}, f32[8,384]{1,0:T(8,128)}, ...), condition=%wide.region_21.22_spmd.clone, body=%wide.region_18.21_spmd.clone.sunk | while | flops 214514688 | bytes 15203576 | solution.py:264
  354.9 29.6 %while.85 = (s32[]{:T(128)}, f32[8,384,64]{1,2,0:T(8,128)}, f32[8,384,64]{1,2,0:T(8,128)}, s32[2,512]{1,0:T(2,128)S(1)}, s32[2,512]{1,0:T(2,128)}, /*index=5*/bf...) while((s32[]{:T(128)}, f32[8,384,64]{1,2,0:T(8,128)}, ...), condition=%wide.region_23.24_spmd.clone, body=%wide.region_22.23_spmd.clone.sunk | while | flops 621084672 | bytes 60075288 | solution.py:291
  421.4 7.0 gather_fusion.2
  440.4 16.7 all-to-all-done.2
  495.0 17.4 all-to-all-done.7
  586.8 31.3 %while.86 = (s32[]{:T(128)}, f32[8,384,64]{1,2,0:T(8,128)}, bf16[2,8,512,64]{2,3,1,0:T(8,128)(2,1)}, bf16[2,8,512,64]{2,3,1,0:T(8,128)(2,1)}, s32[2,512]{1,0:T(2...) while((s32[]{:T(128)}, f32[8,384,64]{1,2,0:T(8,128)}, ...), condition=%wide.region_35.36_spmd.clone, body=%wide.region_34.35_spmd.clone.sunk | while | flops 1022230528 | bytes 103308792 | solution.py:381
  630.6 30.8 %while.87 = (s32[]{:T(128)}, f32[8,384,64]{1,2,0:T(8,128)}, bf16[2,8,512,64]{2,3,1,0:T(8,128)(2,1)}, bf16[2,8,512,64]{2,3,1,0:T(8,128)(2,1)}, s32[2,512]{1,0:T(2...) while((s32[]{:T(128)}, f32[8,384,64]{1,2,0:T(8,128)}, ...), condition=%wide.region_43.44_spmd.clone, body=%wide.region_42.43_spmd.clone.sunk | while | flops 1022230528 | bytes 100163000 | solution.py:381
  728.8 117.9 %reduce-scatter.19.cloned.1.call-done = f32[48,1536]{1,0:T(8,128)} async-done(((f32[1536,1536]{1,0:T(8,128)}), f32[48,1536]{1,0:T(8,128)}) %reduce-scatter.19.cloned.1.call-update) | async-done | bytes 294928 | tf_op jit(solution)/shard_map/reduce_scatter | solution.py:138
  848.5 139.7 %reduce-scatter.17.cloned.1.call-done = f32[48,1536]{1,0:T(8,128)} async-done(((f32[1536,1536]{1,0:T(8,128)}), f32[48,1536]{1,0:T(8,128)}) %reduce-scatter.17.cloned.1.call-update) | async-done | bytes 294928 | tf_op jit(solution)/shard_map/reduce_scatter | solution.py:138
  989.9 138.9 %reduce-scatter.27.cloned.1.call-done = f32[48,1536]{1,0:T(8,128)} async-done(((f32[1536,1536]{1,0:T(8,128)}), f32[48,1536]{1,0:T(8,128)}) %reduce-scatter.27.cloned.1.call-update) | async-done | bytes 294928 | tf_op jit(solution)/shard_map/reduce_scatter | solution.py:140
  1130.6 139.8 %reduce-scatter.25.cloned.1.call-done = f32[48,1536]{1,0:T(8,128)} async-done(((f32[1536,1536]{1,0:T(8,128)}), f32[48,1536]{1,0:T(8,128)}) %reduce-scatter.25.cloned.1.call-update) | async-done | bytes 294928 | tf_op jit(solution)/shard_map/reduce_scatter | solution.py:140
  1272.1 69.3 %reduce-scatter.29.cloned.1.call-done = bf16[2,192,1024]{2,1,0:T(8,128)(2,1)} async-done(((bf16[2,1536,1024]{2,1,0:T(8,128)(2,1)}), bf16[2,192,1024]{2,1,0:T(8,128)(2,1)}) %reduce-scatter.29.cloned.1.call-update) | async-done | bytes 786448 | tf_op jit(solution)/shard_map/reduce_scatter | solution.py:108
  1341.5 70.9 %reduce-scatter.31.cloned.1.call-done = bf16[2,192,1024]{2,1,0:T(8,128)(2,1)} async-done(((bf16[2,1536,1024]{2,1,0:T(8,128)(2,1)}), bf16[2,192,1024]{2,1,0:T(8,128)(2,1)}) %reduce-scatter.31.cloned.1.call-update) | async-done | bytes 786448 | tf_op jit(solution)/shard_map/reduce_scatter | solution.py:108
  1428.7 39.2 %all-reduce.12 = (bf16[1536]{0:T(1024)(128)(2,1)S(1)}, bf16[1536]{0:T(1024)(128)(2,1)S(1)}, bf16[1536]{0:T(1024)(128)(2,1)S(1)}, bf16[1536]{0:T(1024)(128)(2,1)S(1)}) all-reduce(f32[1536]{0:T(1024)S(1)} %get-tuple-element.1012, f32[1536]{0:T(1024)S(1)} %get-tuple-element.1015, ...), channel_id=5, replica_groups=mesh['fsdp'=4,'ctx'=8] {'fsdp','ctx'}, use_global_device_ids=true, to_apply=%region_49.50.clone | all-reduce | flops 6144 | bytes 36864
  1469.1 15.9 all-reduce.13
  1496.4 112.4 %reduce-scatter.23.cloned.1.call-done = f32[48,1024]{1,0:T(8,128)} async-done(((f32[1536,1024]{1,0:T(8,128)}), f32[48,1024]{1,0:T(8,128)}) %reduce-scatter.23.cloned.1.call-update) | async-done | bytes 196624 | tf_op jit(solution)/shard_map/reduce_scatter | solution.py:139
  1609.7 119.4 %reduce-scatter.21.cloned.1.call-done = f32[48,1024]{1,0:T(8,128)} async-done(((f32[1536,1024]{1,0:T(8,128)}), f32[48,1024]{1,0:T(8,128)}) %reduce-scatter.21.cloned.1.call-update) | async-done | bytes 196624 | tf_op jit(solution)/shard_map/reduce_scatter | solution.py:139
  1730.1 16.8 all_gather.80
  1746.9 16.4 all_gather.79
  1764.7 14.7 all-gather.26.cloned.1.call-done
  1782.8 20.7 %all-gather.32.cloned.1.call-done = bf16[384,1536]{1,0:T(8,128)(2,1)} async-done(((bf16[48,1536]{1,0:T(8,128)(2,1)}), bf16[384,1536]{1,0:T(8,128)(2,1)}) %all-gather.32.cloned.1.call-update) | async-done | bytes 1179664 | tf_op jit(solution)/shard_map/all_gather | solution.py:153
  1803.5 24.1 %all-gather.30.cloned.1.call-done = bf16[384,1536]{1,0:T(8,128)(2,1)} async-done(((bf16[48,1536]{1,0:T(8,128)(2,1)}), bf16[384,1536]{1,0:T(8,128)(2,1)}) %all-gather.30.cloned.1.call-update) | async-done | bytes 1179664 | tf_op jit(solution)/shard_map/all_gather | solution.py:153
  1831.0 62.6 %all-gather.34.cloned.1.call-done = bf16[2,1536,1024]{2,1,0:T(8,128)(2,1)} async-done(((bf16[2,192,1024]{2,1,0:T(8,128)(2,1)}), bf16[2,1536,1024]{2,1,0:T(8,128)(2,1)}) %all-gather.34.cloned.1.call-update) | async-done | bytes 6291472 | tf_op jit(solution)/shard_map/all_gather | solution.py:116
  1893.6 65.0 %all-gather.36.cloned.1.call-done = bf16[2,1536,1024]{2,1,0:T(8,128)(2,1)} async-done(((bf16[2,192,1024]{2,1,0:T(8,128)(2,1)}), bf16[2,1536,1024]{2,1,0:T(8,128)(2,1)}) %all-gather.36.cloned.1.call-update) | async-done | bytes 6291472 | tf_op jit(solution)/shard_map/all_gather | solution.py:116
  1958.6 12.6 convert_add_fusion
  (804 shorter events, 629.3 us)
Async XLA Ops:
  7.2 49.4 %all-gather.16.cloned.1.call-start = ((), (), s32[]{:S(2)}) async-start(), calls=%async_computation.20 | async-start | bytes 3932160 | tf_op jit(solution)/shard_map/all_gather | solution.py:208
  7.9 138.0 %all-gather.20.cloned.1.call-start = ((), (), s32[]{:S(2)}) async-start(), calls=%async_computation.22 | async-start | bytes 5898240 | tf_op jit(solution)/shard_map/all_gather | solution.py:207
  8.7 157.3 %all-gather.18.cloned.1.call-start = ((), (), s32[]{:S(2)}) async-start(), calls=%async_computation.21 | async-start | bytes 2359296 | tf_op jit(solution)/shard_map/all_gather | solution.py:234
  76.3 167.6 %all-gather.22.cloned.1.call-start = ((), (), s32[]{:S(2)}) async-start(), calls=%async_computation.23 | async-start | bytes 5898240 | tf_op jit(solution)/shard_map/all_gather | solution.py:209
  98.8 157.3 %all-to-all-start.4 = ((bf16[8,80,1536]{2,1,0:T(8,128)(2,1)}), bf16[8,80,1536]{2,1,0:T(8,128)(2,1)}, u32[]{:S(2)}, u32[]{:S(2)}) async-start(bf16[8,80,1536]{2,1,0:T(8,128)(2,1)} %multiply_convert_fusion.1), calls=%async_computation.4 | async-start | bytes 3932160 | tf_op jit(solution)/shard_map/all_to_all | solution.py:325
  103.3 182.3 %all-gather.24.cloned.1.call-start = ((), (), s32[]{:S(2)}) async-start(), calls=%async_computation.24 | async-start | bytes 2359296 | tf_op jit(solution)/shard_map/all_gather | solution.py:234
  256.1 39.9 %all-to-all-start = ((bf16[8,80,1536]{2,1,0:T(8,128)(2,1)}), bf16[8,80,1536]{2,1,0:T(8,128)(2,1)}, u32[]{:S(2)}, u32[]{:S(2)}) async-start(bf16[8,80,1536]{2,1,0:T(8,128)(2,1)} %bitcast.690), calls=%async_computation | async-start | bytes 3932160 | tf_op jit(solution)/shard_map/all_to_all | solution.py:308
  314.9 35.5 %all-to-all-start.5 = ((bf16[2,320,1536]{2,0,1:T(2,128)(2,1)}), bf16[2,320,1536]{2,0,1:T(2,128)(2,1)}, u32[]{:S(2)}, u32[]{:S(2)}) async-start(bf16[2,320,1536]{2,0,1:T(2,128)(2,1)} %copy.306), calls=%async_computation.5 | async-start | bytes 3932160 | tf_op jit(solution)/shard_map/all_to_all | solution.py:327
  350.4 78.0 %all-to-all-start.6 = ((bf16[8,80,1536]{2,1,0:T(8,128)(2,1)}), bf16[8,80,1536]{2,1,0:T(8,128)(2,1)}, u32[]{:S(2)}, u32[]{:S(2)}) async-start(bf16[8,80,1536]{2,1,0:T(8,128)(2,1)} %multiply_convert_fusion), calls=%async_computation.6 | async-start | bytes 3932160 | tf_op jit(solution)/shard_map/all_to_all | solution.py:325
  354.8 362.2 %reduce-scatter.33.cloned.1.call-start = ((), (), s32[]{:S(2)}) async-start(), calls=%async_computation.39 | async-start | bytes 3538944 | tf_op jit(solution)/shard_map/reduce_scatter | solution.py:111
  428.4 28.7 %all-to-all-start.2 = ((bf16[8,80,1536]{2,1,0:T(8,128)(2,1)}), bf16[8,80,1536]{2,1,0:T(8,128)(2,1)}, u32[]{:S(2)}, u32[]{:S(2)}) async-start(bf16[8,80,1536]{2,1,0:T(8,128)(2,1)} %bitcast.691), calls=%async_computation.2 | async-start | bytes 3932160 | tf_op jit(solution)/shard_map/all_to_all | solution.py:308
  457.1 27.8 %all-to-all-start.1 = ((bf16[2,320,1536]{2,0,1:T(2,128)(2,1)}), bf16[2,320,1536]{2,0,1:T(2,128)(2,1)}, u32[]{:S(2)}, u32[]{:S(2)}) async-start(bf16[2,320,1536]{2,0,1:T(2,128)(2,1)} %copy.284), calls=%async_computation.1 | async-start | bytes 3932160 | tf_op jit(solution)/shard_map/all_to_all | solution.py:310
  512.3 43.1 %all-to-all-start.3 = ((bf16[2,320,1536]{2,0,1:T(2,128)(2,1)}), bf16[2,320,1536]{2,0,1:T(2,128)(2,1)}, u32[]{:S(2)}, u32[]{:S(2)}) async-start(bf16[2,320,1536]{2,0,1:T(2,128)(2,1)} %copy.301), calls=%async_computation.3 | async-start | bytes 3932160 | tf_op jit(solution)/shard_map/all_to_all | solution.py:310
  516.8 200.8 %reduce-scatter.35.cloned.1.call-start = ((), (), s32[]{:S(2)}) async-start(), calls=%async_computation.41 | async-start | bytes 3538944 | tf_op jit(solution)/shard_map/reduce_scatter | solution.py:111
  538.3 180.0 %reduce-scatter.37.cloned.1.call-start = ((), (), s32[]{:S(2)}) async-start(), calls=%async_computation.43 | async-start | bytes 2359296
  628.4 91.1 %reduce-scatter.39.cloned.1.call-start = ((), (), s32[]{:S(2)}) async-start(), calls=%async_computation.44 | async-start | bytes 2359296
  671.0 175.8 %reduce-scatter.19.cloned.1.call-start = ((), (), s32[]{:S(2)}) async-start(), calls=%async_computation.27 | async-start | bytes 9732096 | tf_op jit(solution)/shard_map/reduce_scatter | solution.py:138
  682.3 305.9 %reduce-scatter.17.cloned.1.call-start = ((), (), s32[]{:S(2)}) async-start(), calls=%async_computation.25 | async-start | bytes 9732096 | tf_op jit(solution)/shard_map/reduce_scatter | solution.py:138
  687.9 441.0 %reduce-scatter.27.cloned.1.call-start = ((), (), s32[]{:S(2)}) async-start(), calls=%async_computation.33 | async-start | bytes 9732096 | tf_op jit(solution)/shard_map/reduce_scatter | solution.py:140
  694.2 576.2 %reduce-scatter.25.cloned.1.call-start = ((), (), s32[]{:S(2)}) async-start(), calls=%async_computation.31 | async-start | bytes 9732096 | tf_op jit(solution)/shard_map/reduce_scatter | solution.py:140
  700.5 640.9 %reduce-scatter.29.cloned.1.call-start = ((), (), s32[]{:S(2)}) async-start(), calls=%async_computation.35 | async-start | bytes 7077888 | tf_op jit(solution)/shard_map/reduce_scatter | solution.py:108
  708.7 703.6 %reduce-scatter.31.cloned.1.call-start = ((), (), s32[]{:S(2)}) async-start(), calls=%async_computation.37 | async-start | bytes 7077888 | tf_op jit(solution)/shard_map/reduce_scatter | solution.py:108
  717.0 772.1 %all-gather.38.cloned.1.call-start = ((), (), s32[]{:S(2)}) async-start(), calls=%async_computation.40 | async-start | bytes 3538944 | tf_op jit(solution)/shard_map/all_gather | solution.py:119
  717.5 772.3 %all-gather.40.cloned.1.call-start = ((), (), s32[]{:S(2)}) async-start(), calls=%async_computation.42 | async-start | bytes 3538944 | tf_op jit(solution)/shard_map/all_gather | solution.py:119
  718.1 890.7 %reduce-scatter.23.cloned.1.call-start = ((), (), s32[]{:S(2)}) async-start(), calls=%async_computation.30 | async-start | bytes 6488064 | tf_op jit(solution)/shard_map/reduce_scatter | solution.py:139
  724.8 1004.3 %reduce-scatter.21.cloned.1.call-start = ((), (), s32[]{:S(2)}) async-start(), calls=%async_computation.29 | async-start | bytes 6488064 | tf_op jit(solution)/shard_map/reduce_scatter | solution.py:139
  728.8 1035.9 %all-gather.28.cloned.1.call-start = ((), (), s32[]{:S(2)}) async-start(), calls=%async_computation.28 | async-start | bytes 1327104 | tf_op jit(solution)/shard_map/all_gather | solution.py:147
  848.5 930.9 %all-gather.26.cloned.1.call-start = ((), (), s32[]{:S(2)}) async-start(), calls=%async_computation.26 | async-start | bytes 1327104 | tf_op jit(solution)/shard_map/all_gather | solution.py:147
  989.9 813.6 %all-gather.32.cloned.1.call-start = ((), (), s32[]{:S(2)}) async-start(), calls=%async_computation.34 | async-start | bytes 1327104 | tf_op jit(solution)/shard_map/all_gather | solution.py:153
  1130.5 697.1 %all-gather.30.cloned.1.call-start = ((), (), s32[]{:S(2)}) async-start(), calls=%async_computation.32 | async-start | bytes 1327104 | tf_op jit(solution)/shard_map/all_gather | solution.py:153
  1272.1 621.5 %all-gather.34.cloned.1.call-start = ((), (), s32[]{:S(2)}) async-start(), calls=%async_computation.36 | async-start | bytes 7077888 | tf_op jit(solution)/shard_map/all_gather | solution.py:116
  1341.4 617.2 %all-gather.36.cloned.1.call-start = ((), (), s32[]{:S(2)}) async-start(), calls=%async_computation.38 | async-start | bytes 7077888 | tf_op jit(solution)/shard_map/all_gather | solution.py:116
  (191 other events, 4451.6 us)
Sparse Core Ops, SparseCore 0:
  9.9 46.6 all-gather.15
  58.4 76.6 all-gather.19
  137.3 28.6 all-gather.17
  167.7 56.5 all-gather.21
  225.7 29.0 all-gather.23
  397.7 39.8 reduce-scatter.32
  538.4 39.7 reduce-scatter.34
  628.5 35.2 reduce-scatter.36
  671.1 35.1 reduce-scatter.38
  712.6 134.1 reduce-scatter.18
  853.7 134.4 reduce-scatter.16
  994.0 134.8 reduce-scatter.26
  1135.8 134.5 reduce-scatter.24
  1272.6 68.7 reduce-scatter.28
  1344.1 68.1 reduce-scatter.30
  1413.8 37.0 all-gather.37
  1452.3 37.5 all-gather.39
  1495.4 113.3 reduce-scatter.22
  1615.4 113.7 reduce-scatter.20
  1731.2 24.5 all-gather.27
  1758.0 21.3 all-gather.25
  1781.0 22.4 all-gather.31
  1805.1 22.4 all-gather.29
  1829.1 64.4 all-gather.33
  1895.2 63.3 all-gather.35
where the time goes:
time: 1990 us; the launch traced here: 1980 us
  waiting for transfers between devices  1180 us (59%)
  local copies, waits for them, and re-layouts  264 us (13%)
  matrix products  225 us (11%)
  blocking collectives  132 us (7%)
  other arithmetic  124 us (6%)
  starting transfers between devices  37.2 us (2%)
    reduce_scatter x2, waiting for transfers between devices, dense_share(): lax.psum_scatter(output_grad, ('fsdp', 'ctx'), scatter_dimension=0, tiled...  279 us
    reduce_scatter x2, waiting for transfers between devices, dense_share(): lax.psum_scatter(query_weight_grad, ('fsdp', 'ctx'), scatter_dimension=0,...  258 us
    reduce_scatter x2, waiting for transfers between devices, dense_share(): lax.psum_scatter(pair_weight_grad, ('fsdp', 'ctx'), scatter_dimension=0,...  232 us
    reduce_scatter x2, waiting for transfers between devices, expert_share(): lax.psum_scatter(expand_grad.astype(jnp.bfloat16), 'ctx', scatter_dimensi...  140 us
    all_gather x2, waiting for transfers between devices, expert_share(): lax.all_gather(pieces[0].astype(jnp.bfloat16), 'ctx', axis=1, tiled=True)  128 us
    dot_general x12, matrix products, masked_scores(): jnp.einsum('hrd,hkd->hrk', query_rows, key_part, preferred_element_type=j...  55.6 us
    unnamed x2, blocking collectives  55.1 us
    all_gather x2, waiting for transfers between devices, dense_share(): lax.all_gather(pieces[3].astype(jnp.bfloat16), 'ctx', axis=0, tiled=True)  44.8 us
  transfers between devices with their start and end apart: 33, of which 19 were waited for; matrix products, arithmetic and copies ran while one was open for 28% of the time, Pallas kernels for 0%

commit v1 on v0

v1 whole, which is shorter than its diff:
```python
import functools

import jax
import jax.numpy as jnp
from jax import lax
from jax.experimental import pallas as pl
from jax.experimental.pallas import tpu as pltpu
from jax.sharding import PartitionSpec as P

MODEL_WIDTH = 1536
QUERY_HEADS = 24
KEY_VALUE_HEADS = 8
HEAD_SIZE = 64
GROUP = QUERY_HEADS // KEY_VALUE_HEADS
KEY_WIDTH = KEY_VALUE_HEADS * HEAD_SIZE
F = 512
E = 8
TOP = 4
MB = 2
LANES = 128
PAIRS = KEY_WIDTH // LANES
PAIR_QUERY = 2 * GROUP * HEAD_SIZE
F_BLOCK = 256
VMEM_LIMIT = 60 * 1024 * 1024

eps = 1e-05
theta = 10000.0

NT = (((1,), (1,)), ((), ()))
TN = (((0,), (0,)), ((), ()))
bf16 = jnp.bfloat16
f32 = jnp.float32


def dot(left, right, dims=(((1,), (0,)), ((), ()))):
    return lax.dot_general(left, right, dims, preferred_element_type=f32)


def rotation_tables(positions):
    frequency = theta ** (-jnp.arange(0, HEAD_SIZE, 2, dtype=f32) / HEAD_SIZE)
    angles = positions.astype(f32)[:, None] * frequency[None, :]
    cosine, sine = jnp.cos(angles), jnp.sin(angles)
    repeat = LANES // HEAD_SIZE
    cosine = jnp.concatenate([cosine, cosine] * repeat, axis=1)
    sine = jnp.concatenate([-sine, sine] * repeat, axis=1)
    return cosine, sine


def lane_index(shape):
    return lax.broadcasted_iota(jnp.int32, shape, 1)


def rotate(tile, cosine, sine):
    half = HEAD_SIZE // 2
    ahead = pltpu.roll(tile, LANES - half, 1)
    behind = pltpu.roll(tile, half, 1)
    first = lane_index(tile.shape) % HEAD_SIZE < half
    return tile * cosine + jnp.where(first, ahead, behind) * sine


def rotate_pairs_kernel(pair_ref, cosine_ref, sine_ref, out_ref):
    cosine, sine = cosine_ref[...], sine_ref[...]
    for i in range(2 * KEY_WIDTH // LANES):
        cols = slice(i * LANES, (i + 1) * LANES)
        tile = pair_ref[:, cols]
        if i < KEY_WIDTH // LANES:
            tile = rotate(tile, cosine, sine)
        out_ref[:, cols] = tile.astype(bf16)


def rotate_pairs(pair_pre, cosine, sine):
    return pl.pallas_call(
        rotate_pairs_kernel,
        out_shape=jax.ShapeDtypeStruct(pair_pre.shape, bf16),
        compiler_params=pltpu.CompilerParams(vmem_limit_bytes=VMEM_LIMIT),
        name="rotate_pairs",
    )(pair_pre, cosine, sine)


def pair_gradient_kernel(count, cosine_ref, sine_ref, *refs):
    out_ref = refs[-1]
    cosine, sine = cosine_ref[...], sine_ref[...]
    for i in range(2 * KEY_WIDTH // LANES):
        cols = slice(i * LANES, (i + 1) * LANES)
        total = refs[0][:, cols].astype(f32)
        for ref in refs[1:count]:
            total = total + ref[:, cols].astype(f32)
        if i < KEY_WIDTH // LANES:
            total = rotate(total, cosine, -sine)
        out_ref[:, cols] = total.astype(bf16)


def pair_gradient(parts, cosine, sine):
    return pl.pallas_call(
        functools.partial(pair_gradient_kernel, len(parts)),
        out_shape=jax.ShapeDtypeStruct(parts[0].shape, bf16),
        compiler_params=pltpu.CompilerParams(vmem_limit_bytes=VMEM_LIMIT),
        name="pair_gradient",
    )(cosine, sine, *parts)


def grouped(tiles, half):
    mine = lane_index(tiles[0].shape) // HEAD_SIZE == half
    rows = []
    for j in range(GROUP * half, GROUP * half + GROUP):
        tile = tiles[j // 2]
        if j % 2 != half:
            tile = pltpu.roll(tile, HEAD_SIZE, 1)
        rows.append(jnp.where(mine, tile, 0.0))
    return jnp.concatenate(rows, axis=0).astype(bf16)


def ungrouped(per_half, rows):
    heads = []
    for j in range(2 * GROUP):
        half, place = j // GROUP, j % GROUP
        tile = per_half[half][place * rows : (place + 1) * rows]
        if j % 2 != half:
            tile = pltpu.roll(tile, HEAD_SIZE, 1)
        heads.append(tile)
    low = lane_index(heads[0].shape) < HEAD_SIZE
    return [jnp.where(low, heads[2 * i], heads[2 * i + 1]) for i in range(GROUP)]


def query_tiles(query_ref, cosine, sine):
    tiles = []
    for i in range(GROUP):
        tile = rotate(query_ref[:, i * LANES : (i + 1) * LANES], cosine, sine)
        tiles.append(tile.astype(bf16).astype(f32) * (1.0 / HEAD_SIZE))
    return tiles


def attention_forward_kernel(query_ref, cosine_ref, sine_ref, key_ref, value_ref, bias_ref, out_ref):
    rows = query_ref.shape[0]
    tiles = query_tiles(query_ref, cosine_ref[...], sine_ref[...])
    key, value = key_ref[...], value_ref[...]
    bias = bias_ref[...]
    results = []
    for half in range(2):
        scores = dot(grouped(tiles, half), key, NT)
        scores = jnp.concatenate(
            [scores[g * rows : (g + 1) * rows] + bias for g in range(GROUP)], axis=0
        )
        peak = jnp.max(scores, axis=1, keepdims=True)
        weights = jnp.exp(scores - peak)
        total = jnp.sum(weights, axis=1, keepdims=True)
        results.append(dot(weights.astype(bf16), value) / total)
    for i, tile in enumerate(ungrouped(results, rows)):
        out_ref[:, i * LANES : (i + 1) * LANES] = tile.astype(bf16)


def attention_forward(query_pre, cosine, sine, pairs, bias):
    rows, length = bias.shape
    whole = lambda shape: pl.BlockSpec(shape, lambda p: (0, 0))
    return pl.pallas_call(
        attention_forward_kernel,
        grid=(PAIRS,),
        in_specs=[
            pl.BlockSpec((rows, PAIR_QUERY), lambda p: (0, p)),
            whole((rows, LANES)),
            whole((rows, LANES)),
            pl.BlockSpec((length, LANES), lambda p: (0, p)),
            pl.BlockSpec((length, LANES), lambda p: (0, p + PAIRS)),
            whole((rows, length)),
        ],
        out_specs=pl.BlockSpec((rows, PAIR_QUERY), lambda p: (0, p)),
        out_shape=jax.ShapeDtypeStruct((rows, MODEL_WIDTH), bf16),
        compiler_params=pltpu.CompilerParams(vmem_limit_bytes=VMEM_LIMIT),
        cost_estimate=pl.CostEstimate(
            flops=16 * rows * length * MODEL_WIDTH,
            bytes_accessed=4 * length * MODEL_WIDTH,
            transcendentals=rows * length * QUERY_HEADS,
        ),
        name="attention_forward",
    )(query_pre, cosine, sine, pairs, pairs, bias)


def attention_backward_kernel(
    query_ref, cosine_ref, sine_ref, key_ref, value_ref, bias_ref, grad_ref, query_out, pair_out
):
    rows = query_ref.shape[0]
    cosine, sine = cosine_ref[...], sine_ref[...]
    tiles = query_tiles(query_ref, cosine, sine)
    grads = [grad_ref[:, i * LANES : (i + 1) * LANES].astype(f32) for i in range(GROUP)]
    key, value = key_ref[...], value_ref[...]
    key_grad, value_grad = None, None
    query_grads = []
    for half in range(2):
        query = grouped(tiles, half)
        grad = grouped(grads, half)
        scores = dot(key, query, NT) + bias_ref[...]
        weights = jnp.exp(scores - jnp.max(scores, axis=0, keepdims=True))
        prob = weights * (1.0 / jnp.sum(weights, axis=0, keepdims=True))
        prob_grad = dot(value, grad, NT)
        delta = jnp.sum(prob * prob_grad, axis=0, keepdims=True)
        score_grad = (prob * (prob_grad - delta)).astype(bf16)
        value_part = dot(prob.astype(bf16), grad)
        key_part = dot(score_grad, query)
        value_grad = value_part if half == 0 else value_grad + value_part
        key_grad = key_part if half == 0 else key_grad + key_part
        query_grads.append(dot(score_grad, key, TN))
    for i, tile in enumerate(ungrouped(query_grads, rows)):
        tile = rotate(tile * (1.0 / HEAD_SIZE), cosine, -sine)
        query_out[:, i * LANES : (i + 1) * LANES] = tile.astype(bf16)
    first = pl.multiple_of(pl.program_id(0) * LANES, LANES)
    pair_out[:, pl.ds(first, LANES)] = key_grad.astype(bf16)
    pair_out[:, pl.ds(first + KEY_WIDTH, LANES)] = value_grad.astype(bf16)


def attention_backward(query_pre, cosine, sine, pairs, bias, grad):
    rows = query_pre.shape[0]
    length = pairs.shape[0]
    whole = lambda shape: pl.BlockSpec(shape, lambda p: (0, 0))
    return pl.pallas_call(
        attention_backward_kernel,
        grid=(PAIRS,),
        in_specs=[
            pl.BlockSpec((rows, PAIR_QUERY), lambda p: (0, p)),
            whole((rows, LANES)),
            whole((rows, LANES)),
            pl.BlockSpec((length, LANES), lambda p: (0, p)),
            pl.BlockSpec((length, LANES), lambda p: (0, p + PAIRS)),
            whole(bias.shape),
            pl.BlockSpec((rows, PAIR_QUERY), lambda p: (0, p)),
        ],
        out_specs=[
            pl.BlockSpec((rows, PAIR_QUERY), lambda p: (0, p)),
            whole((length, 2 * KEY_WIDTH)),
        ],
        out_shape=[
            jax.ShapeDtypeStruct((rows, MODEL_WIDTH), bf16),
            jax.ShapeDtypeStruct((length, 2 * KEY_WIDTH), bf16),
        ],
        compiler_params=pltpu.CompilerParams(vmem_limit_bytes=VMEM_LIMIT),
        cost_estimate=pl.CostEstimate(
            flops=40 * rows * length * MODEL_WIDTH,
            bytes_accessed=8 * length * MODEL_WIDTH,
            transcendentals=rows * length * QUERY_HEADS,
        ),
        name="attention_backward",
    )(query_pre, cosine, sine, pairs, pairs, bias, grad)


def experts_kernel(parts, rows, steps, combine_ref, gate_ref, up_ref, down_ref, *refs):
    rows_in, grads_in = refs[:parts], refs[parts : 2 * parts]
    refs = refs[2 * parts :]
    results, row_grads = refs[:parts], refs[parts : 2 * parts]
    active_out, gate_out, up_out, rows_all, grads_all, result_sum, grad_sum = refs[2 * parts :]
    step = pl.program_id(0) * pl.num_programs(1) + pl.program_id(1)

    @pl.when(step == 0)
    def _():
        for k in range(parts):
            place = slice(k * rows, (k + 1) * rows)
            rows_all[place] = rows_in[k][...]
            grads_all[place] = grads_in[k][...]
        result_sum[...] = jnp.zeros_like(result_sum)
        grad_sum[...] = jnp.zeros_like(grad_sum)

    inputs, out_grad, combine = rows_all[...], grads_all[...], combine_ref[0]
    gate_weight, up_weight, down_weight = gate_ref[0], up_ref[0], down_ref[0]
    gate = dot(inputs, gate_weight)
    up = dot(inputs, up_weight)
    sigmoid = jax.nn.sigmoid(gate)
    silu = gate * sigmoid
    active = (silu * up * combine).astype(bf16)
    active_grad = dot(out_grad, down_weight, NT) * combine
    gate_grad = (active_grad * up * sigmoid * (1.0 + gate * (1.0 - sigmoid))).astype(bf16)
    up_grad = (active_grad * silu).astype(bf16)
    active_out[...] = active
    gate_out[...] = gate_grad
    up_out[...] = up_grad
    result_sum[...] += dot(active, down_weight)
    grad_sum[...] += dot(gate_grad, gate_weight, NT) + dot(up_grad, up_weight, NT)

    @pl.when(step == steps - 1)
    def _():
        for k in range(parts):
            place = slice(k * rows, (k + 1) * rows)
            results[k][...] = result_sum[place].astype(bf16)
            row_grads[k][...] = grad_sum[place].astype(bf16)


def experts(row_parts, grad_parts, combine, expert_in, expert_out):
    parts = len(row_parts)
    rows = row_parts[0].shape[0]
    held = expert_in.shape[0]
    tokens = parts * rows
    blocks = F // F_BLOCK
    whole = pl.BlockSpec((rows, MODEL_WIDTH), lambda e, b: (0, 0))
    piece = pl.BlockSpec((tokens, F_BLOCK), lambda e, b: (0, e * blocks + b))
    row_shape = jax.ShapeDtypeStruct((rows, MODEL_WIDTH), bf16)
    piece_shape = jax.ShapeDtypeStruct((tokens, held * F), bf16)
    out = pl.pallas_call(
        functools.partial(experts_kernel, parts, rows, held * blocks),
        grid=(held, blocks),
        in_specs=[
            pl.BlockSpec((1, tokens, 1), lambda e, b: (e, 0, 0)),
            pl.BlockSpec((1, MODEL_WIDTH, F_BLOCK), lambda e, b: (e, 0, b)),
            pl.BlockSpec((1, MODEL_WIDTH, F_BLOCK), lambda e, b: (e, 0, b + blocks)),
            pl.BlockSpec((1, F_BLOCK, MODEL_WIDTH), lambda e, b: (e, b, 0)),
        ]
        + [whole] * (2 * parts),
        out_specs=[whole] * (2 * parts) + [piece] * 3,
        out_shape=[row_shape] * (2 * parts) + [piece_shape] * 3,
        scratch_shapes=[
            pltpu.VMEM((tokens, MODEL_WIDTH), bf16),
            pltpu.VMEM((tokens, MODEL_WIDTH), bf16),
            pltpu.VMEM((tokens, MODEL_WIDTH), f32),
            pltpu.VMEM((tokens, MODEL_WIDTH), f32),
        ],
        compiler_params=pltpu.CompilerParams(vmem_limit_bytes=VMEM_LIMIT),
        cost_estimate=pl.CostEstimate(
            flops=12 * tokens * held * MODEL_WIDTH * F,
            bytes_accessed=6 * held * MODEL_WIDTH * F + 20 * tokens * MODEL_WIDTH,
            transcendentals=tokens * held * F,
        ),
        name="experts",
    )(combine, expert_in, expert_in, expert_out, *row_parts, *grad_parts)
    return out[:parts], out[parts : 2 * parts], out[2 * parts :]


def expert_weights_kernel(parts, rows, *refs):
    row_refs, grad_refs = refs[: MB * parts], refs[MB * parts : 2 * MB * parts]
    refs = refs[2 * MB * parts :]
    active_refs, gate_refs, up_refs = refs[:MB], refs[MB : 2 * MB], refs[2 * MB : 3 * MB]
    gate_out, up_out, down_out, turned, grads_all = refs[3 * MB :]
    step = pl.program_id(0) * pl.num_programs(1) + pl.program_id(1)

    @pl.when(step == 0)
    def _():
        for k in range(MB * parts):
            place = slice(k * rows, (k + 1) * rows)
            turned[:, place] = row_refs[k][...].T
            grads_all[place] = grad_refs[k][...]

    join = lambda items: jnp.concatenate([item[...] for item in items], axis=0)
    gate_out[0] = dot(turned[...], join(gate_refs)).astype(bf16)
    up_out[0] = dot(turned[...], join(up_refs)).astype(bf16)
    down_out[0] = dot(join(active_refs), grads_all[...], TN).astype(bf16)


def expert_weights(row_parts, grad_parts, pieces, held):
    rows = row_parts[0].shape[0]
    parts = len(row_parts) // MB
    tokens = parts * rows
    blocks = F // F_BLOCK
    whole = pl.BlockSpec((rows, MODEL_WIDTH), lambda e, b: (0, 0))
    piece = pl.BlockSpec((tokens, F_BLOCK), lambda e, b: (0, e * blocks + b))
    wide = pl.BlockSpec((1, MODEL_WIDTH, F_BLOCK), lambda e, b: (e, 0, b))
    return pl.pallas_call(
        functools.partial(expert_weights_kernel, parts, rows),
        grid=(held, blocks),
        in_specs=[whole] * (2 * MB * parts) + [piece] * (3 * MB),
        out_specs=[wide, wide, pl.BlockSpec((1, F_BLOCK, MODEL_WIDTH), lambda e, b: (e, b, 0))],
        out_shape=[
            jax.ShapeDtypeStruct((held, MODEL_WIDTH, F), bf16),
            jax.ShapeDtypeStruct((held, MODEL_WIDTH, F), bf16),
            jax.ShapeDtypeStruct((held, F, MODEL_WIDTH), bf16),
        ],
        scratch_shapes=[
            pltpu.VMEM((MODEL_WIDTH, MB * tokens), bf16),
            pltpu.VMEM((MB * tokens, MODEL_WIDTH), bf16),
        ],
        compiler_params=pltpu.CompilerParams(vmem_limit_bytes=VMEM_LIMIT),
        cost_estimate=pl.CostEstimate(
            flops=6 * MB * tokens * held * MODEL_WIDTH * F,
            bytes_accessed=6 * held * MODEL_WIDTH * F + 8 * MB * tokens * MODEL_WIDTH,
            transcendentals=0,
        ),
        name="expert_weights",
    )(*row_parts, *grad_parts, *[pieces[m][i] for i in range(3) for m in range(MB)])


class Links:
    def __init__(self):
        self.shards = lax.axis_size("fsdp")
        self.contexts = lax.axis_size("ctx")
        self.chips = self.contexts // 2
        self.shard = lax.axis_index("fsdp")
        self.context = lax.axis_index("ctx")
        self.chip = self.context // 2
        self.core = self.context % 2

    def across(self, array, k):
        return lax.ppermute(array, "fsdp", [(i, i ^ k) for i in range(self.shards)])

    def other_core(self, array):
        return lax.ppermute(array, "ctx", [(i, i ^ 1) for i in range(self.contexts)])

    def shift(self, array, s):
        n = self.contexts
        return lax.ppermute(array, "ctx", [(i, (i + 2 * s) % n) for i in range(n)])

    def step(self, array, first, last, direction):
        pairs = [
            (2 * i + core, 2 * (i + direction) + core) for i in range(first, last + 1) for core in range(2)
        ]
        return lax.ppermute(array, "ctx", pairs)

    def to_relative(self, array):
        width = array.shape[-1] // (2 * self.shards)
        pieces = [[array[..., (2 * b + h) * width : (2 * b + h + 1) * width] for b in range(self.shards)] for h in range(2)]
        return jnp.concatenate(sum(self._swapped(pieces), []), axis=-1)

    def to_absolute(self, array):
        width = array.shape[-1] // (2 * self.shards)
        pieces = [
            [array[..., (h * self.shards + b) * width : (h * self.shards + b + 1) * width] for b in range(self.shards)]
            for h in range(2)
        ]
        pieces = self._swapped(pieces)
        return jnp.concatenate([pieces[h][b] for b in range(self.shards) for h in range(2)], axis=-1)

    def _swapped(self, pieces):
        bit = 1
        while bit < self.shards:
            flag = (self.shard & bit) != 0
            pieces = [[jnp.where(flag, row[b ^ bit], row[b]) for b in range(self.shards)] for row in pieces]
            bit *= 2
        flag = self.core == 1
        return [
            [jnp.where(flag, pieces[1 - h][b], pieces[h][b]) for b in range(self.shards)] for h in range(2)
        ]

    def gather_rows(self, weight):
        half = weight.shape[0] // 2
        mine = lax.dynamic_slice_in_dim(weight, self.core * half, half, 0)
        rest = lax.dynamic_slice_in_dim(weight, (1 - self.core) * half, half, 0)
        arrived = [self.across(mine, k) for k in range(1, self.shards)]
        passed = [self.other_core(part) for part in arrived]
        return jnp.concatenate([mine] + arrived + [rest] + passed, axis=0)

    def scatter_rows(self, grad):
        half = grad.shape[0] // 2
        mine = grad[:half].astype(f32) + self.other_core(grad[half:]).astype(f32)
        mine = mine.astype(bf16)
        size = half // self.shards
        total = mine[:size].astype(f32)
        for k in range(1, self.shards):
            total = total + self.across(mine[k * size : (k + 1) * size], k).astype(f32)
        return total.astype(bf16)

    def core_halves(self, grad):
        half = grad.shape[0] // 2
        mine = lax.dynamic_slice_in_dim(grad, self.core * half, half, 0)
        rest = lax.dynamic_slice_in_dim(grad, (1 - self.core) * half, half, 0)
        return (mine.astype(f32) + self.other_core(rest).astype(f32)).astype(bf16)

    def sum_over_chips(self, half):
        n = self.chips
        size = half.shape[0] // n
        block = lambda j: lax.dynamic_slice_in_dim(half, jnp.clip(j, 0, n - 1) * size, size, 0).astype(f32)
        from_left, from_right = None, None
        for t in range(1, n):
            right, left = block(n - t + self.chip), block(t - n + self.chip)
            if t > 1:
                right = right + from_left.astype(f32)
                left = left + from_right.astype(f32)
            from_left = self.step(right.astype(bf16), 0, t - 1, 1)
            from_right = self.step(left.astype(bf16), n - t, n - 1, -1)
        total = block(self.chip) + from_left.astype(f32) + from_right.astype(f32)
        total = total.astype(bf16)
        going_right, going_left = [total], [total]
        for t in range(1, n):
            going_right.append(self.step(going_right[-1], t - 1, n - 2, 1))
            going_left.append(self.step(going_left[-1], 1, n - t, -1))
        return [total] + [going_right[t] + going_left[n - t] for t in range(1, n)]

    def place_rows(self, blocks, out, column):
        size = blocks[0].shape[0]
        others = [self.other_core(block) for block in blocks]
        for core, items in ((self.core, blocks), (1 - self.core, others)):
            for t, item in enumerate(items):
                row = (core * self.chips + (self.chip - t + self.chips) % self.chips) * size
                out = lax.dynamic_update_slice(out, item.astype(f32), (row, column))
        return out


def shards(
    tokens,
    doc_starts,
    routes,
    gates,
    attn_gain,
    w_q,
    key_value_weight,
    w_o,
    moe_gain,
    expert_in,
    expert_out,
    cotangent,
):
    links = Links()
    rows = tokens.shape[2]
    length = rows * links.contexts
    held = expert_in.shape[0]
    positions = links.context * rows + jnp.arange(rows, dtype=jnp.int32)
    cosine, sine = rotation_tables(positions)
    chips_back = (links.chip - jnp.arange(links.chips, dtype=jnp.int32) + links.chips) % links.chips
    chunk_ids = jnp.concatenate([2 * chips_back + links.core, 2 * chips_back + 1 - links.core])
    key_places = (chunk_ids[:, None] * rows + jnp.arange(rows, dtype=jnp.int32)[None, :]).reshape(length)

    gains = lax.all_gather(jnp.stack([attn_gain, moe_gain]), "fsdp", axis=1, tiled=True).astype(f32)
    gain_one, gain_two = links.to_relative(gains[0]), gains[1]

    pair_weight = links.gather_rows(key_value_weight)
    query_weight = links.gather_rows(w_q)
    output_weight = links.gather_rows(w_o)

    flat_tokens = tokens.reshape(MB * rows, MODEL_WIDTH)
    relative = links.to_relative(flat_tokens).astype(f32)
    scale_one = lax.rsqrt(jnp.mean(relative * relative, axis=-1, keepdims=True) + eps)
    unit_one = relative * scale_one
    normed = (unit_one * gain_one).astype(bf16)
    pairs = rotate_pairs(
        dot(normed, pair_weight), jnp.concatenate([cosine] * MB), jnp.concatenate([sine] * MB)
    )
    query_pre = dot(normed, query_weight)

    expert_ids = jnp.arange(E, dtype=jnp.int32)
    chosen = (routes.reshape(MB, rows, TOP)[..., None] == expert_ids).astype(f32)
    combine = jnp.sum(gates.reshape(MB, rows, TOP)[..., None] * chosen, axis=2)
    combine = jnp.concatenate([combine] + [links.across(combine, k) for k in range(1, links.shards)], axis=1)
    combine = lax.dynamic_slice_in_dim(combine, links.shard * held, held, 2)
    combine = combine.transpose(0, 2, 1)[..., None]

    all_pairs, biases, biases_turned = [], [], []
    for m in range(MB):
        own = pairs[m * rows : (m + 1) * rows]
        near = jnp.concatenate([own] + [links.shift(own, s) for s in range(1, links.chips)], axis=0)
        all_pairs.append(jnp.concatenate([near, links.other_core(near)], axis=0))
        starts = doc_starts[m, 0]
        begin = jnp.max(jnp.where(starts[None, :] <= positions[:, None], starts[None, :], 0), axis=1)
        seen = (key_places[None, :] <= positions[:, None]) & (key_places[None, :] >= begin[:, None])
        biases.append(jnp.where(seen, 0.0, -1e30).astype(f32))
        places, begins = jnp.tile(positions, GROUP), jnp.tile(begin, GROUP)
        seen = (key_places[:, None] <= places[None, :]) & (key_places[:, None] >= begins[None, :])
        biases_turned.append(jnp.where(seen, 0.0, -1e30).astype(f32))

    kept = []
    outputs = []
    for m in range(MB):
        own = slice(m * rows, (m + 1) * rows)
        attn = attention_forward(query_pre[own], cosine, sine, all_pairs[m], biases[m])
        attn = links.to_relative(attn)
        middle = flat_tokens[own].astype(f32) + dot(attn, output_weight)
        scale_two = lax.rsqrt(jnp.mean(middle * middle, axis=-1, keepdims=True) + eps)
        unit_two = middle * scale_two
        moe_in = (unit_two * gain_two).astype(bf16)
        out_grad = cotangent[m, 0]
        row_parts = [moe_in] + [links.across(moe_in, k) for k in range(1, links.shards)]
        grad_parts = [out_grad] + [links.across(out_grad, k) for k in range(1, links.shards)]
        results, row_grads, pieces = experts(row_parts, grad_parts, combine[m], expert_in, expert_out)
        final = middle + results[0].astype(f32)
        for k in range(1, links.shards):
            final = final + links.across(results[k], k).astype(f32)
        outputs.append(final.astype(bf16))
        kept.append((attn, unit_two, scale_two, row_parts, grad_parts, row_grads, pieces))

    expert_grads = expert_weights(
        sum([k[3] for k in kept], []), sum([k[4] for k in kept], []), [k[6] for k in kept], held
    )

    expand_total = jnp.zeros((held * MODEL_WIDTH, 2 * F), f32)
    reduce_total = jnp.zeros((held * F, MODEL_WIDTH), f32)
    gate_grad, up_grad, down_grad = [g.reshape(-1, g.shape[-1]) for g in expert_grads]
    expand_total = links.place_rows(links.sum_over_chips(links.core_halves(gate_grad)), expand_total, 0)
    expand_total = links.place_rows(links.sum_over_chips(links.core_halves(up_grad)), expand_total, F)
    reduce_total = links.place_rows(links.sum_over_chips(links.core_halves(down_grad)), reduce_total, 0)

    input_grads, query_lows, pair_lows, middle_lows = [], [], [], []
    gain_one_grad, gain_two_grad = 0.0, 0.0
    for m in range(MB):
        own = slice(m * rows, (m + 1) * rows)
        attn, unit_two, scale_two, _, _, row_grads, _ = kept[m]
        moe_in_grad = row_grads[0].astype(f32)
        for k in range(1, links.shards):
            moe_in_grad = moe_in_grad + links.across(row_grads[k], k).astype(f32)
        gain_two_grad = gain_two_grad + jnp.sum(moe_in_grad * unit_two, axis=0)
        weighted = moe_in_grad * gain_two
        inner = jnp.mean(weighted * unit_two, axis=-1, keepdims=True)
        middle_grad = cotangent[m, 0].astype(f32) + (weighted - unit_two * inner) * scale_two
        middle_low = middle_grad.astype(bf16)
        attn_grad = links.to_absolute(dot(middle_low, output_weight, NT).astype(bf16))
        query_low, pair_grad = attention_backward(
            query_pre[own], cosine, sine, all_pairs[m], biases_turned[m], attn_grad
        )
        near = links.chips * rows
        part = pair_grad[:near].astype(f32) + links.other_core(pair_grad[near:]).astype(f32)
        part = part.astype(bf16)
        parts = [part[:rows]]
        for s in range(1, links.chips):
            parts.append(links.shift(part[s * rows : (s + 1) * rows], -s))
        pair_low = pair_gradient(parts, cosine, sine)
        normed_grad = dot(query_low, query_weight, NT) + dot(pair_low, pair_weight, NT)
        gain_one_grad = gain_one_grad + jnp.sum(normed_grad * unit_one[own], axis=0)
        weighted = normed_grad * gain_one
        inner = jnp.mean(weighted * unit_one[own], axis=-1, keepdims=True)
        residual_grad = (weighted - unit_one[own] * inner) * scale_one[own]
        input_grads.append(middle_grad + links.to_absolute(residual_grad))
        query_lows.append(query_low)
        pair_lows.append(pair_low)
        middle_lows.append(middle_low)

    join = lambda items: jnp.concatenate(items, axis=0)
    width = w_q.shape[0]

    def dense_total(grad):
        blocks = links.sum_over_chips(links.scatter_rows(grad))
        return links.place_rows(blocks, jnp.zeros((width, grad.shape[1]), f32), 0)

    output_grad = dot(join([k[0] for k in kept]), join(middle_lows), TN).astype(bf16)
    output_total = dense_total(output_grad)
    query_total = dense_total(dot(normed, join(query_lows), TN).astype(bf16))
    pair_weight_grad = dot(normed, join(pair_lows), TN).astype(bf16)
    gain_grads = jnp.stack([gain_one_grad, links.to_relative(gain_two_grad)], axis=1)
    gain_grads = jnp.pad(gain_grads, ((0, 0), (0, LANES - 2))).astype(bf16)
    pair_total = dense_total(jnp.concatenate([pair_weight_grad, gain_grads], axis=1))

    return (
        jnp.stack(outputs)[:, None],
        jnp.stack(input_grads)[:, None],
        pair_total[:, 2 * KEY_WIDTH],
        query_total,
        pair_total[:, : 2 * KEY_WIDTH],
        output_total,
        pair_total[:, 2 * KEY_WIDTH + 1],
        expand_total.reshape(held, MODEL_WIDTH, 2 * F),
        reduce_total.reshape(held, F, MODEL_WIDTH),
    )


def solution(mesh):
    return jax.shard_map(
        shards,
        mesh=mesh,
        in_specs=(
            P(None, "fsdp", "ctx", None),
            P(None, "fsdp", None),
            P(None, "fsdp", "ctx", None),
            P(None, "fsdp", "ctx", None),
            P("fsdp"),
            P("fsdp", None),
            P("fsdp", None),
            P("fsdp", None),
            P("fsdp"),
            P("fsdp", None, None),
            P("fsdp", None, None),
            P(None, "fsdp", "ctx", None),
        ),
        out_specs=(
            P(None, "fsdp", "ctx", None),
            P(None, "fsdp", "ctx", None),
            P("fsdp"),
            P("fsdp", None),
            P("fsdp", None),
            P("fsdp", None),
            P("fsdp"),
            P("fsdp", None, None),
            P("fsdp", None, None),
        ),
        check_vma=False,
    )
```

time: 1990 us -> 908 us (0.46)
  waiting for transfers between devices: 1180 us -> 313 us
  starting transfers between devices: 37.2 us -> 261 us
  matrix products: 225 us -> 35 us
  local copies, waits for them, and re-layouts: 264 us -> 83.8 us
  Pallas kernels: 0 us -> 113 us
  blocking collectives: 132 us -> 19.1 us
  other arithmetic: 124 us -> 68.8 us
    reduce_scatter x10 -> x0, waiting for transfers between devices: 908 us -> none  [the longest x2 279 us: dense_share(): lax.psum_scatter(output_grad, ('fsdp', 'ctx'), scatter_dimension=0, tiled...]
    ppermute x0 -> x172, waiting for transfers between devices: none -> 313 us  [the longest x72 151 us: step(): return lax.ppermute(array, 'ctx', pairs)]
    ppermute x0 -> x172, starting transfers between devices: none -> 261 us  [the longest x72 148 us: step(): return lax.ppermute(array, 'ctx', pairs)]
    all_gather x13 -> x0, waiting for transfers between devices: 227 us -> none  [the longest x2 128 us: expert_share(): lax.all_gather(pieces[0].astype(jnp.bfloat16), 'ctx', axis=1, tiled=True)]
    dot_general x66 -> x13, matrix products: 225 us -> 35 us  [dot(): return lax.dot_general(left, right, dims, preferred_element_type=f32)]
    pallas_call x0 -> x10, Pallas kernels: none -> 113 us  [the longest x2 35.5 us: attention_backward(): pl.pallas_call(attention_backward_kernel, grid=(PAIRS,), in_specs=[pl.Blo...]
    all_gather x4 -> x1, blocking collectives: 77 us -> 19.1 us  [shards(): lax.all_gather(jnp.stack([attn_gain, moe_gain]), 'fsdp', axis=1, tiled=True)]
    unnamed x2 -> x0, blocking collectives: 55.1 us -> none
  transfers between devices with their start and end apart: 33 -> 172, of which waited for: 19 -> 63; matrix products, arithmetic and copies ran while one was open for 28% -> 19% of each run, Pallas kernels for 0% -> 9%
where the time goes in v1:
time: 908 us; the launch traced here: 897 us
  waiting for transfers between devices  313 us (34%)
  starting transfers between devices  261 us (29%)
  Pallas kernels  113 us (12%)
  local copies, waits for them, and re-layouts  83.8 us (9%)
  other arithmetic  68.8 us (8%)
  matrix products  35 us (4%)
  blocking collectives  19.1 us (2%)
    ppermute x72, waiting for transfers between devices, step(): return lax.ppermute(array, 'ctx', pairs)  151 us
    ppermute x72, starting transfers between devices, step(): return lax.ppermute(array, 'ctx', pairs)  148 us
    ppermute x45, waiting for transfers between devices, across(): return lax.ppermute(array, 'fsdp', [(i, i ^ k) for i in range(self.shards)])  127 us
    ppermute x45, starting transfers between devices, across(): return lax.ppermute(array, 'fsdp', [(i, i ^ k) for i in range(self.shards)])  52.6 us
    ppermute x12, starting transfers between devices, shift(): return lax.ppermute(array, 'ctx', [(i, (i + 2 * s) % n) for i in range(n)])  52.5 us
    unnamed x259, local copies, waits for them, and re-layouts  38.2 us
    pallas_call x2, Pallas kernels, attention_backward(): pl.pallas_call(attention_backward_kernel, grid=(PAIRS,), in_specs=[pl.Blo...  35.5 us
    dot_general x13, matrix products, dot(): return lax.dot_general(left, right, dims, preferred_element_type=f32)  35 us
  transfers between devices with their start and end apart: 172, of which 63 were waited for; matrix products, arithmetic and copies ran while one was open for 19% of the time, Pallas kernels for 9%

profile of v1, /device:TPU:0, one launch (start us, length us, event | category | flops | bytes accessed | tf_op | source)
XLA Modules:
  0.0 897.1 jit_solution(8708932878301729172)
XLA Ops:
  16.2 19.1 %all_gather.3 = bf16[2,1536]{1,0:T(2,128)(2,1)S(1)} all-gather(bf16[2,384]{1,0:T(2,128)(2,1)S(1)} %pad_maximum_fusion.5), channel_id=1, replica_groups=mesh['fsdp'=4,'ctx'=8] {'fsdp'}, dimensions={1}, use_global_device_ids=true | all-gather | bytes 7680 | tf_op jit(solution)/shard_map/all_gather | solution.py:504
  59.6 32.4 %collective-permute-done.7 = bf16[192,1024]{1,0:T(8,128)(2,1)} collective-permute-done((bf16[192,1024]{1,0:T(8,128)(2,1)}, bf16[192,1024]{1,0:T(8,128)(2,1)}, u32[]{:S(2)}, u32[]{:S(2)}) %collective-permute-start.7) | collective-permute-done | bytes 393248 | tf_op jit(solution)/shard_map/ppermute | solution.py:386
  109.4 9.8 %collective-permute-done.17 = bf16[192,1536]{1,0:T(8,128)(2,1)S(1)} collective-permute-done((bf16[192,1536]{1,0:T(8,128)(2,1)}, bf16[192,1536]{1,0:T(8,128)(2,1)S(1)}, u32[]{:S(2)}, u32[]{:S(2)}) %collective-permute-start.17) | collective-permute-done | bytes 589856 | tf_op jit(solution)/shard_map/ppermute | solution.py:386
  140.2 9.6 %collective-permute-start.12 = (bf16[128,1024]{1,0:T(8,128)(2,1)S(1)}, bf16[128,1024]{1,0:T(8,128)(2,1)S(1)}, u32[]{:S(2)}, u32[]{:S(2)}) collective-permute-start(bf16[128,1024]{1,0:T(8,128)(2,1)S(1)} %get-tuple-element.375), channel_id=1, source_target_pairs={{0,2},{1,3},{2,4},{3,5},{4,6},{5,7},{6,0},{7,1},{8,10},{9,11},{10,... | collective-permute-start | bytes 786440 | tf_op jit(solution)/shard_map/ppermute | solution.py:393
  151.5 10.0 %collective-permute-start.13 = (bf16[128,1024]{1,0:T(8,128)(2,1)S(1)}, bf16[128,1024]{1,0:T(8,128)(2,1)S(1)}, u32[]{:S(2)}, u32[]{:S(2)}) collective-permute-start(bf16[128,1024]{1,0:T(8,128)(2,1)S(1)} %get-tuple-element.375), channel_id=1, source_target_pairs={{0,4},{1,5},{2,6},{3,7},{4,0},{5,1},{6,2},{7,3},{8,12},{9,13},{10,... | collective-permute-start | bytes 786440 | tf_op jit(solution)/shard_map/ppermute | solution.py:393
  166.0 8.2 collective-permute-done.13
  186.0 9.8 %attention_forward.2 = bf16[128,1536]{1,0:T(8,128)(2,1)} custom-call(f32[128,1536]{1,0:T(8,128)} %get-tuple-element.324.query_ref, f32[128,128]{1,0:T(8,128)} %pad_maximum_fusion.2.cosine_ref, f32[128,128]{1,0:T(8,128)} %pad_maximum_fusion.3.sine_ref, bf16[1024,1024]{1,0:T(8,128)(2,1)} %copy-done.83, bf16[1024,1024]{1,0:T(8,128)(2,1)} %copy-done.83, ...), custom_call_target="tpu_custom_call" | custom-call | flops 3221225472 | bytes 6291456 | tf_op jit(solution)/shard_map/attention_forward/pallas_call | solution.py:155
  207.1 9.6 %attention_forward.3 = bf16[128,1536]{1,0:T(8,128)(2,1)} custom-call(f32[128,1536]{1,0:T(8,128)} %get-tuple-element.325.query_ref, f32[128,128]{1,0:T(8,128)} %pad_maximum_fusion.2.cosine_ref, f32[128,128]{1,0:T(8,128)} %pad_maximum_fusion.3.sine_ref, bf16[1024,1024]{1,0:T(8,128)(2,1)} %copy-done.86, bf16[1024,1024]{1,0:T(8,128)(2,1)} %copy-done.86, ...), custom_call_target="tpu_custom_call" | custom-call | flops 3221225472 | bytes 6291456 | tf_op jit(solution)/shard_map/attention_forward/pallas_call | solution.py:155
  221.7 17.0 %experts.2 = (bf16[128,1536]{1,0:T(8,128)(2,1)}, bf16[128,1536]{1,0:T(8,128)(2,1)}, bf16[128,1536]{1,0:T(8,128)(2,1)}, bf16[128,1536]{1,0:T(8,128)(2,1)}, bf16[1...) custom-call(f32[2,512,1]{2,1,0:T(8,128)} %copy.114.combine_ref, ...), custom_call_target="tpu_custom_call" | custom-call | flops 9663676416 | bytes 25165824 | tf_op jit(solution)/shard_map/experts/pallas_call | solution.py:294
  294.3 8.1 collective-permute-done.38.refs_1_.refs_5_
  308.8 17.5 %experts.3 = (bf16[128,1536]{1,0:T(8,128)(2,1)}, bf16[128,1536]{1,0:T(8,128)(2,1)}, bf16[128,1536]{1,0:T(8,128)(2,1)}, bf16[128,1536]{1,0:T(8,128)(2,1)}, bf16[1...) custom-call(f32[2,512,1]{2,1,0:T(8,128)} %copy.115.combine_ref, ...), custom_call_target="tpu_custom_call" | custom-call | flops 9663676416 | bytes 25165824 | tf_op jit(solution)/shard_map/experts/pallas_call | solution.py:294
  332.6 16.2 %expert_weights.1 = (bf16[2,1536,512]{2,1,0:T(8,128)(2,1)}, bf16[2,1536,512]{2,1,0:T(8,128)(2,1)}, bf16[2,512,1536]{2,1,0:T(8,128)(2,1)}) custom-call(bf16[128,1536]{1,0:T(8,128)(2,1)} %copy-done.69, bf16[128,1536]{1,0:T(8,128)(2,1)} %copy-done.106, bf16[128,1536]{1,0:T(8,128)(2,1)} %collective-permute-done.26.refs_2_, ...), custom_call_target="tpu_custom_call" | custom-call | flops 9663676416 | bytes 22020096 | tf_op jit(solution)/shard_map/expert_weights/pallas_call | solution.py:351
  373.0 17.7 %attention_backward.3 = (bf16[128,1536]{1,0:T(8,128)(2,1)}, bf16[1024,1024]{1,0:T(8,128)(2,1)}) custom-call(f32[128,1536]{1,0:T(8,128)} %get-tuple-element.325.query_ref, f32[128,128]{1,0:T(8,128)} %pad_maximum_fusion.2.cosine_ref, f32[128,128]{1,0:T(8,128)} %pad_maximum_fusion.3.sine_ref, bf16[1024,1024]{1,0:T(8,128)(2,1)} %copy-done.86, ...), custom_call_target="tpu_custom_call" | custom-call | flops 8053063680 | bytes 12582912 | tf_op jit(solution)/shard_map/attention_backward/pallas_call | solution.py:214
  398.2 17.8 %attention_backward.2 = (bf16[128,1536]{1,0:T(8,128)(2,1)}, bf16[1024,1024]{1,0:T(8,128)(2,1)}) custom-call(f32[128,1536]{1,0:T(8,128)} %get-tuple-element.324.query_ref, f32[128,128]{1,0:T(8,128)} %pad_maximum_fusion.2.cosine_ref, f32[128,128]{1,0:T(8,128)} %pad_maximum_fusion.3.sine_ref, bf16[1024,1024]{1,0:T(8,128)(2,1)} %copy-done.83, ...), custom_call_target="tpu_custom_call" | custom-call | flops 8053063680 | bytes 12582912 | tf_op jit(solution)/shard_map/attention_backward/pallas_call | solution.py:214
  433.7 8.3 collective-permute-start.58
  455.1 10.5 %collective-permute-done.59.refs_2_ = bf16[128,1024]{1,0:T(8,128)(2,1)S(1)} collective-permute-done((bf16[128,1024]{1,0:T(8,128)(2,1)S(1)}, bf16[128,1024]{1,0:T(8,128)(2,1)S(1)}, u32[]{:S(2)}, u32[]{:S(2)}) %collective-permute-start.59) | collective-permute-done | bytes 262176 | tf_op jit(solution)/shard_map/ppermute | solution.py:393
  465.6 11.8 %collective-permute-start.53 = (bf16[128,1024]{1,0:T(8,128)(2,1)}, bf16[128,1024]{1,0:T(8,128)(2,1)}, u32[]{:S(2)}, u32[]{:S(2)}) collective-permute-start(bf16[128,1024]{1,0:T(8,128)(2,1)} %get-tuple-element.326), channel_id=1, source_target_pairs={{0,2},{1,3},{2,4},{3,5},{4,6},{5,7},{6,0},{7,1},{8,10},{9,11},{10,... | collective-permute-start | bytes 786440 | tf_op jit(solution)/shard_map/ppermute | solution.py:393
  578.4 13.0 %collective-permute-done.161 = bf16[128,1536]{1,0:T(8,128)(2,1)S(1)} collective-permute-done((bf16[128,1536]{1,0:T(8,128)(2,1)S(1)}, bf16[128,1536]{1,0:T(8,128)(2,1)S(1)}, u32[]{:S(2)}, u32[]{:S(2)}) %collective-permute-start.161) | collective-permute-done | bytes 393248 | tf_op jit(solution)/shard_map/ppermute | solution.py:399
  594.4 6.6 collective-permute-done.127
  613.5 11.9 %collective-permute-done.104 = bf16[192,1536]{1,0:T(8,128)(2,1)S(1)} collective-permute-done((bf16[192,1536]{1,0:T(8,128)(2,1)S(1)}, bf16[192,1536]{1,0:T(8,128)(2,1)S(1)}, u32[]{:S(2)}, u32[]{:S(2)}) %collective-permute-start.104) | collective-permute-done | bytes 589856 | tf_op jit(solution)/shard_map/ppermute | solution.py:386
  670.1 11.8 %collective-permute-start.65 = (bf16[48,1152]{1,0:T(8,128)(2,1)S(1)}, bf16[48,1152]{1,0:T(8,128)(2,1)S(1)}, u32[]{:S(2)}, u32[]{:S(2)}) collective-permute-start(bf16[48,1152]{1,0:T(8,128)(2,1)S(1)} %get-tuple-element.387), channel_id=1, source_target_pairs={{0,2},{1,3},{8,10},{9,11},{16,18},{17,19},{24,26},{25,27}} | collective-permute-start | bytes 331784 | tf_op jit(solution)/shard_map/ppermute | solution.py:399
  709.9 8.9 collective-permute-done.164
  730.3 7.3 collective-permute-done.130
  741.1 11.2 %collective-permute-done.131 = bf16[384,512]{1,0:T(8,128)(2,1)S(1)} collective-permute-done((bf16[384,512]{1,0:T(8,128)(2,1)S(1)}, bf16[384,512]{1,0:T(8,128)(2,1)S(1)}, u32[]{:S(2)}, u32[]{:S(2)}) %collective-permute-start.131) | collective-permute-done | bytes 393248 | tf_op jit(solution)/shard_map/ppermute | solution.py:399
  765.0 6.9 collective-permute-start.91
  774.7 7.7 collective-permute-done.113
  794.6 11.2 %collective-permute-start.71 = (bf16[48,1152]{1,0:T(8,128)(2,1)S(1)}, bf16[48,1152]{1,0:T(8,128)(2,1)S(1)}, u32[]{:S(2)}, u32[]{:S(2)}) collective-permute-start(bf16[48,1152]{1,0:T(8,128)(2,1)S(1)} %get-tuple-element.200), channel_id=1, source_target_pairs={{0,2},{1,3},{2,4},{3,5},{4,6},{5,7},{8,10},{9,11},{10,12},{11,13},... | collective-permute-start | bytes 331784 | tf_op jit(solution)/shard_map/ppermute | solution.py:399
  813.0 11.0 %collective-permute-done.72 = bf16[48,1152]{1,0:T(8,128)(2,1)S(1)} collective-permute-done((bf16[48,1152]{1,0:T(8,128)(2,1)S(1)}, bf16[48,1152]{1,0:T(8,128)(2,1)S(1)}, u32[]{:S(2)}, u32[]{:S(2)}) %collective-permute-start.72) | collective-permute-done | bytes 110624 | tf_op jit(solution)/shard_map/ppermute | solution.py:399
  826.6 6.9 collective-permute-done.73
  849.7 14.7 %collective-permute-done.146 = bf16[384,512]{1,0:T(8,128)(2,1)S(1)} collective-permute-done((bf16[384,512]{1,0:T(8,128)(2,1)S(1)}, bf16[384,512]{1,0:T(8,128)(2,1)S(1)}, u32[]{:S(2)}, u32[]{:S(2)}) %collective-permute-start.146) | collective-permute-done | bytes 393248 | tf_op jit(solution)/shard_map/ppermute | solution.py:399
  866.4 10.9 %collective-permute-done.147 = bf16[384,512]{1,0:T(8,128)(2,1)S(1)} collective-permute-done((bf16[384,512]{1,0:T(8,128)(2,1)S(1)}, bf16[384,512]{1,0:T(8,128)(2,1)S(1)}, u32[]{:S(2)}, u32[]{:S(2)}) %collective-permute-start.147) | collective-permute-done | bytes 393248 | tf_op jit(solution)/shard_map/ppermute | solution.py:399
  881.6 7.4 collective-permute-done.148
  (799 shorter events, 511.7 us)
Async XLA Ops:
  2.1 47.6 %collective-permute-start.24 = (f32[2,128,8]{1,2,0:T(8,128)}, f32[2,128,8]{1,2,0:T(8,128)}, u32[]{:S(2)}, u32[]{:S(2)}) collective-permute-start(f32[2,128,8]{1,2,0:T(8,128)} %select_reduce_fusion), channel_id=1, source_target_pairs={{0,24},{8,16},{16,8},{24,0},{1,25},{9,17},{17,9},{25,1},{2,26},{10... | collective-permute-start | bytes 24584 | tf_op jit(solution)/shard_map/ppermute | solution.py:386
  6.0 45.3 %collective-permute-start.23 = (f32[2,128,8]{1,2,0:T(8,128)}, f32[2,128,8]{1,2,0:T(8,128)}, u32[]{:S(2)}, u32[]{:S(2)}) collective-permute-start(f32[2,128,8]{1,2,0:T(8,128)} %select_reduce_fusion), channel_id=1, source_target_pairs={{0,16},{8,24},{16,0},{24,8},{1,17},{9,25},{17,1},{25,9},{2,18},{10... | collective-permute-start | bytes 24584 | tf_op jit(solution)/shard_map/ppermute | solution.py:386
  6.5 45.3 %collective-permute-start.22 = (f32[2,128,8]{1,2,0:T(8,128)}, f32[2,128,8]{1,2,0:T(8,128)}, u32[]{:S(2)}, u32[]{:S(2)}) collective-permute-start(f32[2,128,8]{1,2,0:T(8,128)} %select_reduce_fusion), channel_id=1, source_target_pairs={{0,8},{8,0},{16,24},{24,16},{1,9},{9,1},{17,25},{25,17},{2,10},{10... | collective-permute-start | bytes 24584 | tf_op jit(solution)/shard_map/ppermute | solution.py:386
  8.7 90.2 %collective-permute-start = (bf16[192,1536]{1,0:T(8,128)(2,1)}, bf16[192,1536]{1,0:T(8,128)(2,1)}, u32[]{:S(2)}, u32[]{:S(2)}) collective-permute-start(bf16[192,1536]{1,0:T(8,128)(2,1)} %get-tuple-element.300), channel_id=1, source_target_pairs={{0,8},{8,0},{16,24},{24,16},{1,9},{9,1},{17,25},{25,17},{2,10},{10... | collective-permute-start | bytes 1769480 | tf_op jit(solution)/shard_map/ppermute | solution.py:386
  12.6 43.7 %collective-permute-start.6 = (bf16[192,1024]{1,0:T(8,128)(2,1)}, bf16[192,1024]{1,0:T(8,128)(2,1)}, u32[]{:S(2)}, u32[]{:S(2)}) collective-permute-start(bf16[192,1024]{1,0:T(8,128)(2,1)} %get-tuple-element.278), channel_id=1, source_target_pairs={{0,8},{8,0},{16,24},{24,16},{1,9},{9,1},{17,25},{25,17},{2,10},{10... | collective-permute-start | bytes 1179656 | tf_op jit(solution)/shard_map/ppermute | solution.py:386
  49.7 52.1 %collective-permute-start.1 = (bf16[192,1536]{1,0:T(8,128)(2,1)}, bf16[192,1536]{1,0:T(8,128)(2,1)}, u32[]{:S(2)}, u32[]{:S(2)}) collective-permute-start(bf16[192,1536]{1,0:T(8,128)(2,1)} %get-tuple-element.300), channel_id=1, source_target_pairs={{0,16},{8,24},{16,0},{24,8},{1,17},{9,25},{17,1},{25,9},{2,18},{10... | collective-permute-start | bytes 1769480 | tf_op jit(solution)/shard_map/ppermute | solution.py:386
  51.3 40.7 %collective-permute-start.7 = (bf16[192,1024]{1,0:T(8,128)(2,1)}, bf16[192,1024]{1,0:T(8,128)(2,1)}, u32[]{:S(2)}, u32[]{:S(2)}) collective-permute-start(bf16[192,1024]{1,0:T(8,128)(2,1)} %get-tuple-element.278), channel_id=1, source_target_pairs={{0,16},{8,24},{16,0},{24,8},{1,17},{9,25},{17,1},{25,9},{2,18},{10... | collective-permute-start | bytes 1179656 | tf_op jit(solution)/shard_map/ppermute | solution.py:386
  51.8 43.4 %collective-permute-start.8 = (bf16[192,1024]{1,0:T(8,128)(2,1)}, bf16[192,1024]{1,0:T(8,128)(2,1)}, u32[]{:S(2)}, u32[]{:S(2)}) collective-permute-start(bf16[192,1024]{1,0:T(8,128)(2,1)} %get-tuple-element.278), channel_id=1, source_target_pairs={{0,24},{8,16},{16,8},{24,0},{1,25},{9,17},{17,9},{25,1},{2,26},{10... | collective-permute-start | bytes 1179656 | tf_op jit(solution)/shard_map/ppermute | solution.py:386
  56.3 48.8 %collective-permute-start.2 = (bf16[192,1536]{1,0:T(8,128)(2,1)}, bf16[192,1536]{1,0:T(8,128)(2,1)S(1)}, u32[]{:S(2)}, u32[]{:S(2)}) collective-permute-start(bf16[192,1536]{1,0:T(8,128)(2,1)} %get-tuple-element.300), channel_id=1, source_target_pairs={{0,24},{8,16},{16,8},{24,0},{1,25},{9,17},{17,9},{25,1},{2,26},{10... | collective-permute-start | bytes 1769480 | tf_op jit(solution)/shard_map/ppermute | solution.py:386
  101.8 104.4 %collective-permute-start.28 = (bf16[128,1536]{1,0:T(8,128)(2,1)}, bf16[128,1536]{1,0:T(8,128)(2,1)}, u32[]{:S(2)}, u32[]{:S(2)}) collective-permute-start(bf16[128,1536]{1,0:T(8,128)(2,1)} %get-tuple-element.348.refs_4_.refs_8_), channel_id=1, source_target_pairs={{0,8},{8,0},{16,24},{24,16},{1,9},{9,1},{17,25},{25,17},{2,10},{10... | collective-permute-start | bytes 1179656 | tf_op jit(solution)/shard_map/ppermute | solution.py:386
  120.0 97.9 %collective-permute-start.29 = (bf16[128,1536]{1,0:T(8,128)(2,1)}, bf16[128,1536]{1,0:T(8,128)(2,1)}, u32[]{:S(2)}, u32[]{:S(2)}) collective-permute-start(bf16[128,1536]{1,0:T(8,128)(2,1)} %get-tuple-element.348.refs_4_.refs_8_), channel_id=1, source_target_pairs={{0,16},{8,24},{16,0},{24,8},{1,17},{9,25},{17,1},{25,9},{2,18},{10... | collective-permute-start | bytes 1179656 | tf_op jit(solution)/shard_map/ppermute | solution.py:386
  177.9 40.1 %collective-permute-start.30 = (bf16[128,1536]{1,0:T(8,128)(2,1)}, bf16[128,1536]{1,0:T(8,128)(2,1)}, u32[]{:S(2)}, u32[]{:S(2)}) collective-permute-start(bf16[128,1536]{1,0:T(8,128)(2,1)} %get-tuple-element.348.refs_4_.refs_8_), channel_id=1, source_target_pairs={{0,24},{8,16},{16,8},{24,0},{1,25},{9,17},{17,9},{25,1},{2,26},{10... | collective-permute-start | bytes 1179656 | tf_op jit(solution)/shard_map/ppermute | solution.py:386
  355.1 78.6 %collective-permute-start.121 = (bf16[1536,512]{1,0:T(8,128)(2,1)}, bf16[1536,512]{1,0:T(8,128)(2,1)}, u32[]{:S(2)}, u32[]{:S(2)}) collective-permute-start(bf16[1536,512]{1,0:T(8,128)(2,1)} %constant_dynamic-slice_fusion.8), channel_id=1, source_target_pairs={{0,1},{1,0},{2,3},{3,2},{4,5},{5,4},{6,7},{7,6},{8,9},{9,8},{10,11... | collective-permute-start | bytes 4718600 | tf_op jit(solution)/shard_map/ppermute | solution.py:389
  355.2 89.8 %collective-permute-start.138 = (bf16[1536,512]{1,0:T(8,128)(2,1)}, bf16[1536,512]{1,0:T(8,128)(2,1)}, u32[]{:S(2)}, u32[]{:S(2)}) collective-permute-start(bf16[1536,512]{1,0:T(8,128)(2,1)} %constant_dynamic-slice_fusion.5), channel_id=1, source_target_pairs={{0,1},{1,0},{2,3},{3,2},{4,5},{5,4},{6,7},{7,6},{8,9},{9,8},{10,11... | collective-permute-start | bytes 4718600 | tf_op jit(solution)/shard_map/ppermute | solution.py:389
  355.7 91.3 %collective-permute-start.155 = (bf16[512,1536]{1,0:T(8,128)(2,1)}, bf16[512,1536]{1,0:T(8,128)(2,1)}, u32[]{:S(2)}, u32[]{:S(2)}) collective-permute-start(bf16[512,1536]{1,0:T(8,128)(2,1)} %constant_dynamic-slice_fusion.2), channel_id=1, source_target_pairs={{0,1},{1,0},{2,3},{3,2},{4,5},{5,4},{6,7},{7,6},{8,9},{9,8},{10,11... | collective-permute-start | bytes 4718600 | tf_op jit(solution)/shard_map/ppermute | solution.py:389
  393.0 36.2 %collective-permute-start.57 = (bf16[512,1024]{1,0:T(8,128)(2,1)}, bf16[512,1024]{1,0:T(8,128)(2,1)S(1)}, u32[]{:S(2)}, u32[]{:S(2)}) collective-permute-start(bf16[512,1024]{1,0:T(8,128)(2,1)} %slice.475), channel_id=1, source_target_pairs={{0,1},{1,0},{2,3},{3,2},{4,5},{5,4},{6,7},{7,6},{8,9},{9,8},{10,11... | collective-permute-start | bytes 3145736 | tf_op jit(solution)/shard_map/ppermute | solution.py:389
  429.2 131.9 %collective-permute-start.81 = (bf16[768,1536]{1,0:T(8,128)(2,1)}, bf16[768,1536]{1,0:T(8,128)(2,1)}, u32[]{:S(2)}, u32[]{:S(2)}) collective-permute-start(bf16[768,1536]{1,0:T(8,128)(2,1)} %slice.616), channel_id=1, source_target_pairs={{0,1},{1,0},{2,3},{3,2},{4,5},{5,4},{6,7},{7,6},{8,9},{9,8},{10,11... | collective-permute-start | bytes 7077896 | tf_op jit(solution)/shard_map/ppermute | solution.py:389
  429.7 134.4 %collective-permute-start.101 = (bf16[768,1536]{1,0:T(8,128)(2,1)}, bf16[768,1536]{1,0:T(8,128)(2,1)}, u32[]{:S(2)}, u32[]{:S(2)}) collective-permute-start(bf16[768,1536]{1,0:T(8,128)(2,1)} %slice.623), channel_id=1, source_target_pairs={{0,1},{1,0},{2,3},{3,2},{4,5},{5,4},{6,7},{7,6},{8,9},{9,8},{10,11... | collective-permute-start | bytes 7077896 | tf_op jit(solution)/shard_map/ppermute | solution.py:389
  482.9 41.0 %collective-permute-start.122 = (bf16[384,512]{1,0:T(8,128)(2,1)}, bf16[384,512]{1,0:T(8,128)(2,1)}, u32[]{:S(2)}, u32[]{:S(2)}) collective-permute-start(bf16[384,512]{1,0:T(8,128)(2,1)} %get-tuple-element.322), channel_id=1, source_target_pairs={{0,2},{1,3},{8,10},{9,11},{16,18},{17,19},{24,26},{25,27}} | collective-permute-start | bytes 1179656 | tf_op jit(solution)/shard_map/ppermute | solution.py:399
  488.0 40.3 %collective-permute-start.125 = (bf16[384,512]{1,0:T(8,128)(2,1)}, bf16[384,512]{1,0:T(8,128)(2,1)}, u32[]{:S(2)}, u32[]{:S(2)}) collective-permute-start(bf16[384,512]{1,0:T(8,128)(2,1)} %get-tuple-element.323), channel_id=1, source_target_pairs={{6,4},{7,5},{14,12},{15,13},{22,20},{23,21},{30,28},{31,29}} | collective-permute-start | bytes 1179656 | tf_op jit(solution)/shard_map/ppermute | solution.py:399
  489.5 36.9 %collective-permute-start.139 = (bf16[384,512]{1,0:T(8,128)(2,1)}, bf16[384,512]{1,0:T(8,128)(2,1)}, u32[]{:S(2)}, u32[]{:S(2)}) collective-permute-start(bf16[384,512]{1,0:T(8,128)(2,1)} %get-tuple-element.318), channel_id=1, source_target_pairs={{0,2},{1,3},{8,10},{9,11},{16,18},{17,19},{24,26},{25,27}} | collective-permute-start | bytes 1179656 | tf_op jit(solution)/shard_map/ppermute | solution.py:399
  553.2 41.1 %collective-permute-start.124 = (bf16[384,512]{1,0:T(8,128)(2,1)S(1)}, bf16[384,512]{1,0:T(8,128)(2,1)S(1)}, u32[]{:S(2)}, u32[]{:S(2)}) collective-permute-start(bf16[384,512]{1,0:T(8,128)(2,1)S(1)} %get-tuple-element.320), channel_id=1, source_target_pairs={{0,2},{1,3},{2,4},{3,5},{4,6},{5,7},{8,10},{9,11},{10,12},{11,13},... | collective-permute-start | bytes 1179656 | tf_op jit(solution)/shard_map/ppermute | solution.py:399
  572.2 36.0 %collective-permute-start.84 = (bf16[192,1536]{1,0:T(8,128)(2,1)S(1)}, bf16[192,1536]{1,0:T(8,128)(2,1)}, u32[]{:S(2)}, u32[]{:S(2)}) collective-permute-start(bf16[192,1536]{1,0:T(8,128)(2,1)S(1)} %get-tuple-element.305), channel_id=1, source_target_pairs={{0,24},{8,16},{16,8},{24,0},{1,25},{9,17},{17,9},{25,1},{2,26},{10... | collective-permute-start | bytes 1769480 | tf_op jit(solution)/shard_map/ppermute | solution.py:386
  573.9 35.9 %collective-permute-start.83 = (bf16[192,1536]{1,0:T(8,128)(2,1)S(1)}, bf16[192,1536]{1,0:T(8,128)(2,1)}, u32[]{:S(2)}, u32[]{:S(2)}) collective-permute-start(bf16[192,1536]{1,0:T(8,128)(2,1)S(1)} %get-tuple-element.306), channel_id=1, source_target_pairs={{0,16},{8,24},{16,0},{24,8},{1,17},{9,25},{17,1},{25,9},{2,18},{10... | collective-permute-start | bytes 1769480 | tf_op jit(solution)/shard_map/ppermute | solution.py:386
  594.4 41.1 %collective-permute-start.61 = (bf16[768,1152]{1,0:T(8,128)(2,1)}, bf16[768,1152]{1,0:T(8,128)(2,1)}, u32[]{:S(2)}, u32[]{:S(2)}) collective-permute-start(bf16[768,1152]{1,0:T(8,128)(2,1)} %slice.609), channel_id=1, source_target_pairs={{0,1},{1,0},{2,3},{3,2},{4,5},{5,4},{6,7},{7,6},{8,9},{9,8},{10,11... | collective-permute-start | bytes 5308424 | tf_op jit(solution)/shard_map/ppermute | solution.py:389
  601.8 242.5 %collective-permute-start.141 = (bf16[384,512]{1,0:T(8,128)(2,1)}, bf16[384,512]{1,0:T(8,128)(2,1)}, u32[]{:S(2)}, u32[]{:S(2)}) collective-permute-start(bf16[384,512]{1,0:T(8,128)(2,1)} %get-tuple-element.316), channel_id=1, source_target_pairs={{0,2},{1,3},{2,4},{3,5},{4,6},{5,7},{8,10},{9,11},{10,12},{11,13},... | collective-permute-start | bytes 1179656 | tf_op jit(solution)/shard_map/ppermute | solution.py:399
  625.5 83.2 %collective-permute-start.162 = (bf16[128,1536]{1,0:T(8,128)(2,1)S(1)}, bf16[128,1536]{1,0:T(8,128)(2,1)S(1)}, u32[]{:S(2)}, u32[]{:S(2)}) collective-permute-start(bf16[128,1536]{1,0:T(8,128)(2,1)S(1)} %copy-done.71), channel_id=1, source_target_pairs={{0,2},{1,3},{2,4},{3,5},{4,6},{5,7},{8,10},{9,11},{10,12},{11,13},... | collective-permute-start | bytes 1179656 | tf_op jit(solution)/shard_map/ppermute | solution.py:399
  659.3 40.6 %collective-permute-start.163 = (bf16[128,1536]{1,0:T(8,128)(2,1)S(1)}, bf16[128,1536]{1,0:T(8,128)(2,1)S(1)}, u32[]{:S(2)}, u32[]{:S(2)}) collective-permute-start(bf16[128,1536]{1,0:T(8,128)(2,1)S(1)} %copy-done.71), channel_id=1, source_target_pairs={{2,0},{3,1},{4,2},{5,3},{6,4},{7,5},{10,8},{11,9},{12,10},{13,11},... | collective-permute-start | bytes 1179656 | tf_op jit(solution)/shard_map/ppermute | solution.py:399
  724.1 38.2 %collective-permute-start.134 = (bf16[384,512]{1,0:T(8,128)(2,1)S(1)}, bf16[384,512]{1,0:T(8,128)(2,1)S(1)}, u32[]{:S(2)}, u32[]{:S(2)}) collective-permute-start(bf16[384,512]{1,0:T(8,128)(2,1)S(1)} %get-tuple-element.176), channel_id=1, source_target_pairs={{0,1},{1,0},{2,3},{3,2},{4,5},{5,4},{6,7},{7,6},{8,9},{9,8},{10,11... | collective-permute-start | bytes 1179656 | tf_op jit(solution)/shard_map/ppermute | solution.py:389
  763.7 81.0 %collective-permute-start.144 = (bf16[384,512]{1,0:T(8,128)(2,1)S(1)}, bf16[384,512]{1,0:T(8,128)(2,1)S(1)}, u32[]{:S(2)}, u32[]{:S(2)}) collective-permute-start(bf16[384,512]{1,0:T(8,128)(2,1)S(1)} %copy-done.66), channel_id=1, source_target_pairs={{2,0},{3,1},{4,2},{5,3},{6,4},{7,5},{10,8},{11,9},{12,10},{13,11},... | collective-permute-start | bytes 1179656 | tf_op jit(solution)/shard_map/ppermute | solution.py:399
  846.0 32.6 %collective-permute-start.80 = (bf16[48,1152]{1,0:T(8,128)(2,1)S(1)}, bf16[48,1152]{1,0:T(8,128)(2,1)S(1)}, u32[]{:S(2)}, u32[]{:S(2)}) collective-permute-start(bf16[48,1152]{1,0:T(8,128)(2,1)S(1)} %get-tuple-element.194), channel_id=1, source_target_pairs={{0,1},{1,0},{2,3},{3,2},{4,5},{5,4},{6,7},{7,6},{8,9},{9,8},{10,11... | collective-permute-start | bytes 331784 | tf_op jit(solution)/shard_map/ppermute | solution.py:389
  849.6 40.6 %collective-permute-start.151 = (bf16[384,512]{1,0:T(8,128)(2,1)S(1)}, bf16[384,512]{1,0:T(8,128)(2,1)S(1)}, u32[]{:S(2)}, u32[]{:S(2)}) collective-permute-start(bf16[384,512]{1,0:T(8,128)(2,1)S(1)} %get-tuple-element.168), channel_id=1, source_target_pairs={{0,1},{1,0},{2,3},{3,2},{4,5},{5,4},{6,7},{7,6},{8,9},{9,8},{10,11... | collective-permute-start | bytes 1179656 | tf_op jit(solution)/shard_map/ppermute | solution.py:389
  (256 other events, 3108.0 us)

commit v2 on v1

--- a/solution.py
+++ b/solution.py
@@ -477,6 +477,274 @@
         return out
 
 
+MESH = pl.DeviceIdType.MESH
+LINE = 4
+PIECES = 4
+DENSE_PIECES = 2
+ADD_ROWS = 64
+
+
+def add_into(out, *parts):
+    rows = out.shape[0]
+    size = max(d for d in range(16, ADD_ROWS + 1, 16) if rows % d == 0)
+
+    def body(i, carry):
+        place = pl.ds(pl.multiple_of(i * size, size), size)
+        total = parts[0][place].astype(f32)
+        for part in parts[1:]:
+            total = total + part[place].astype(f32)
+        out[place] = total.astype(out.dtype)
+        return carry
+
+    lax.fori_loop(0, rows // size, body, 0)
+
+
+class Piece:
+    def __init__(self, own, near, far, out, out_rows):
+        self.own, self.near, self.far, self.out, self.out_rows = own, near, far, out, out_rows
+
+
+def reduce_kernel(experts_n, dense_n, shards_n, *refs):
+    count = experts_n + dense_n
+    sources, outs = refs[:count], refs[count : 2 * count]
+    refs = list(refs[2 * count :])
+    take = lambda n: [refs.pop(0) for _ in range(n)]
+    own, other = take(count), take(count)
+    across = take(dense_n)
+    near, far = take(count), take(count)
+    load_sem, core_sem, across_sem, near_sem, far_sem, back_sem, pass_sem, store_sem = refs
+
+    shard, context = lax.axis_index("fsdp"), lax.axis_index("ctx")
+    core, chip = context % 2, context // 2
+    partner = {"ctx": 2 * chip + 1 - core}
+    inner = (chip == 1) | (chip == 2)
+    outer_device = {"ctx": 2 * (3 * (chip // 2)) + core}
+    inner_device = {"ctx": 2 * (1 + chip // 2) + core}
+    facing_device = {"ctx": 2 * (3 - chip) + core}
+
+    def peer(k):
+        x, y = (shard % 2 + k % 2) % 2, (shard // 2 + k // 2) % 2
+        return {"fsdp": 2 * y + x}
+
+    def send(source, target, sems, index, device):
+        return pltpu.make_async_remote_copy(
+            src_ref=source,
+            dst_ref=target,
+            send_sem=sems.at[0, index],
+            recv_sem=sems.at[1, index],
+            device_id=device,
+            device_id_type=MESH,
+        )
+
+    barrier = pltpu.get_barrier_semaphore()
+    greet = lambda device: pl.semaphore_signal(barrier, inc=1, device_id=device, device_id_type=MESH)
+    greet(partner)
+    for k in range(1, shards_n):
+        greet(peer(k))
+
+    @pl.when(inner)
+    def _():
+        greet(outer_device)
+        greet(facing_device)
+
+    @pl.when(jnp.logical_not(inner))
+    def _():
+        greet(inner_device)
+
+    pl.semaphore_wait(barrier, shards_n + jnp.where(inner, 2, 1))
+
+    loads, trades = [], []
+    pieces = []
+    for a in range(count):
+        rows = own[a].shape[0]
+        if a < experts_n:
+            mine = pl.multiple_of(core * rows, rows)
+            rest = pl.multiple_of((1 - core) * rows, rows)
+            parts = PIECES
+        else:
+            mine, rest = 0, rows
+            parts = 1
+        size = rows // parts
+        for j in range(parts):
+            i = len(loads)
+            place = slice(j * size, (j + 1) * size)
+            loads.append(
+                pltpu.make_async_copy(
+                    sources[a].at[pl.ds(mine + j * size, size)], own[a].at[place], load_sem.at[i]
+                )
+            )
+            trades.append(
+                send(
+                    sources[a].at[pl.ds(rest + j * size, size)], other[a].at[place], core_sem, i, partner
+                )
+            )
+        total = near[a].shape[0]
+        parts = PIECES if a < experts_n else DENSE_PIECES
+        size = total // parts
+        for j in range(parts):
+            place = slice(j * size, (j + 1) * size)
+            at = pl.multiple_of(core * total, total) + j * size
+            pieces.append(
+                Piece(own[a].at[place], near[a].at[place], far[a].at[place], outs[a], pl.ds(at, size))
+            )
+    expert_pieces = experts_n * PIECES
+    order = list(range(2)) + list(range(expert_pieces, expert_pieces + dense_n)) + list(range(2, expert_pieces))
+    for i in order:
+        loads[i].start()
+        trades[i].start()
+
+    crossings = []
+
+    def meet_expert(i):
+        a, j = i // PIECES, i % PIECES
+        size = own[a].shape[0] // PIECES
+        place = slice(j * size, (j + 1) * size)
+        loads[i].wait()
+        trades[i].wait_recv()
+        add_into(own[a].at[place], own[a].at[place], other[a].at[place])
+
+    def meet_dense(d):
+        a, i = experts_n + d, expert_pieces + d
+        loads[i].wait()
+        trades[i].wait_recv()
+        add_into(own[a], own[a], other[a])
+        size = own[a].shape[0] // shards_n
+        for k in range(1, shards_n):
+            copy = send(
+                own[a].at[k * size : (k + 1) * size],
+                across[d].at[k - 1],
+                across_sem,
+                d * (shards_n - 1) + k - 1,
+                peer(k),
+            )
+            copy.start()
+            crossings.append(copy)
+
+    def gather_dense(d):
+        a = experts_n + d
+        size = own[a].shape[0] // shards_n
+        for k in range(1, shards_n):
+            crossings[d * (shards_n - 1) + k - 1].wait_recv()
+        add_into(own[a].at[0:size], own[a].at[0:size], *[across[d].at[k - 1] for k in range(1, shards_n)])
+
+    number = len(pieces)
+    inward = [send(p.own, p.near, near_sem, i, inner_device) for i, p in enumerate(pieces)]
+    facing = [send(p.own, p.far, far_sem, i, facing_device) for i, p in enumerate(pieces)]
+    outward = [send(p.near, p.out.at[p.out_rows], back_sem, i, outer_device) for i, p in enumerate(pieces)]
+    passed_inner = [send(p.near, p.out.at[p.out_rows], pass_sem, i, partner) for i, p in enumerate(pieces)]
+    passed_outer = [
+        send(p.out.at[p.out_rows], p.out.at[p.out_rows], pass_sem, i, partner) for i, p in enumerate(pieces)
+    ]
+    stores = [
+        pltpu.make_async_copy(p.near, p.out.at[p.out_rows], store_sem.at[i]) for i, p in enumerate(pieces)
+    ]
+
+    def ready(i):
+        if i < expert_pieces:
+            meet_expert(i)
+            if 1 <= i <= dense_n:
+                meet_dense(i - 1)
+        elif (i - expert_pieces) % DENSE_PIECES == 0:
+            gather_dense((i - expert_pieces) // DENSE_PIECES)
+
+        @pl.when(jnp.logical_not(inner))
+        def _():
+            inward[i].start()
+
+    def halfway(i):
+        inward[i].wait_recv()
+        add_into(pieces[i].own, pieces[i].own, pieces[i].near)
+        facing[i].start()
+
+    def finish(i):
+        facing[i].wait_recv()
+        add_into(pieces[i].near, pieces[i].own, pieces[i].far)
+        outward[i].start()
+        passed_inner[i].start()
+        stores[i].start()
+
+    def forward(i):
+        outward[i].wait_recv()
+        passed_outer[i].start()
+
+    lag = 6
+    for i in range(number + lag):
+        if i < number:
+            ready(i)
+
+        @pl.when(inner)
+        def _():
+            if i < number:
+                halfway(i)
+            if 1 <= i <= number:
+                finish(i - 1)
+
+        @pl.when(jnp.logical_not(inner))
+        def _():
+            if i >= lag:
+                forward(i - lag)
+
+    for trade in trades:
+        trade.wait_send()
+    for crossing in crossings:
+        crossing.wait_send()
+
+    @pl.when(inner)
+    def _():
+        for i in range(number):
+            facing[i].wait_send()
+            outward[i].wait_send()
+            stores[i].wait()
+            passed_inner[i].wait_send()
+
+    @pl.when(jnp.logical_not(inner))
+    def _():
+        for i in range(number):
+            inward[i].wait_send()
+            passed_outer[i].wait_send()
+
+    for i in range(number):
+        passed_outer[i].wait_recv()
+
+
+def reduce_weights(expert_grads, dense_grads, shards_n):
+    arrays = list(expert_grads) + list(dense_grads)
+    experts_n, dense_n = len(expert_grads), len(dense_grads)
+    out_rows = [g.shape[0] for g in expert_grads] + [g.shape[0] // shards_n for g in dense_grads]
+    half = lambda g: pltpu.VMEM((g.shape[0] // 2, g.shape[1]), bf16)
+    line = [pltpu.VMEM((r // 2, g.shape[1]), bf16) for r, g in zip(out_rows, arrays)]
+    across = [pltpu.VMEM((shards_n - 1, g.shape[0] // (2 * shards_n), g.shape[1]), bf16) for g in dense_grads]
+    first = experts_n * PIECES + dense_n
+    number = experts_n * PIECES + dense_n * DENSE_PIECES
+    dma = pltpu.SemaphoreType.DMA
+    anywhere = pl.BlockSpec(memory_space=pl.ANY)
+    return pl.pallas_call(
+        functools.partial(reduce_kernel, experts_n, dense_n, shards_n),
+        in_specs=[anywhere] * len(arrays),
+        out_specs=[anywhere] * len(arrays),
+        out_shape=[jax.ShapeDtypeStruct((r, g.shape[1]), bf16) for r, g in zip(out_rows, arrays)],
+        scratch_shapes=[half(g) for g in arrays]
+        + [half(g) for g in arrays]
+        + across
+        + line
+        + line
+        + [
+            dma((first,)),
+            dma((2, first)),
+            dma((2, dense_n * (shards_n - 1))),
+            dma((2, number)),
+            dma((2, number)),
+            dma((2, number)),
+            dma((2, number)),
+            dma((number,)),
+        ],
+        compiler_params=pltpu.CompilerParams(
+            collective_id=0, has_side_effects=True, vmem_limit_bytes=VMEM_LIMIT
+        ),
+        name="reduce_weights",
+    )(*arrays)
+
+
 def shards(
     tokens,
     doc_starts,
@@ -562,12 +830,7 @@
         sum([k[3] for k in kept], []), sum([k[4] for k in kept], []), [k[6] for k in kept], held
     )
 
-    expand_total = jnp.zeros((held * MODEL_WIDTH, 2 * F), f32)
-    reduce_total = jnp.zeros((held * F, MODEL_WIDTH), f32)
-    gate_grad, up_grad, down_grad = [g.reshape(-1, g.shape[-1]) for g in expert_grads]
-    expand_total = links.place_rows(links.sum_over_chips(links.core_halves(gate_grad)), expand_total, 0)
-    expand_total = links.place_rows(links.sum_over_chips(links.core_halves(up_grad)), expand_total, F)
-    reduce_total = links.place_rows(links.sum_over_chips(links.core_halves(down_grad)), reduce_total, 0)
+    expert_grads = [g.reshape(-1, g.shape[-1]) for g in expert_grads]
 
     input_grads, query_lows, pair_lows, middle_lows = [], [], [], []
     gain_one_grad, gain_two_grad = 0.0, 0.0
@@ -606,17 +869,29 @@
     join = lambda items: jnp.concatenate(items, axis=0)
     width = w_q.shape[0]
 
-    def dense_total(grad):
-        blocks = links.sum_over_chips(links.scatter_rows(grad))
-        return links.place_rows(blocks, jnp.zeros((width, grad.shape[1]), f32), 0)
-
     output_grad = dot(join([k[0] for k in kept]), join(middle_lows), TN).astype(bf16)
-    output_total = dense_total(output_grad)
-    query_total = dense_total(dot(normed, join(query_lows), TN).astype(bf16))
+    query_grad = dot(normed, join(query_lows), TN).astype(bf16)
     pair_weight_grad = dot(normed, join(pair_lows), TN).astype(bf16)
     gain_grads = jnp.stack([gain_one_grad, links.to_relative(gain_two_grad)], axis=1)
     gain_grads = jnp.pad(gain_grads, ((0, 0), (0, LANES - 2))).astype(bf16)
-    pair_total = dense_total(jnp.concatenate([pair_weight_grad, gain_grads], axis=1))
+    dense_grads = [output_grad, query_grad, jnp.concatenate([pair_weight_grad, gain_grads], axis=1)]
+    if links.chips == LINE and links.shards == 4 and held == 2:
+        totals = reduce_weights(expert_grads, dense_grads, links.shards)
+        gate_total, up_total, down_total, output_total, query_total, pair_total = [t.astype(f32) for t in totals]
+        expand_total = jnp.concatenate([gate_total, up_total], axis=1)
+    else:
+        expand_total = jnp.zeros((held * MODEL_WIDTH, 2 * F), f32)
+        down_total = jnp.zeros((held * F, MODEL_WIDTH), f32)
+        sums = [links.sum_over_chips(links.core_halves(g)) for g in expert_grads]
+        expand_total = links.place_rows(sums[0], expand_total, 0)
+        expand_total = links.place_rows(sums[1], expand_total, F)
+        down_total = links.place_rows(sums[2], down_total, 0)
+        output_total, query_total, pair_total = [
+            links.place_rows(
+                links.sum_over_chips(links.scatter_rows(g)), jnp.zeros((width, g.shape[1]), f32), 0
+            )
+            for g in dense_grads
+        ]
 
     return (
         jnp.stack(outputs)[:, None],
@@ -627,7 +902,7 @@
         output_total,
         pair_total[:, 2 * KEY_WIDTH + 1],
         expand_total.reshape(held, MODEL_WIDTH, 2 * F),
-        reduce_total.reshape(held, F, MODEL_WIDTH),
+        down_total.reshape(held, F, MODEL_WIDTH),
     )
 
 

time: 908 us -> 675 us (0.74)
  waiting for transfers between devices: 313 us -> 134 us
  starting transfers between devices: 261 us -> 89.5 us
  Pallas kernels: 113 us -> 280 us
  local copies, waits for them, and re-layouts: 83.8 us -> 54.4 us
  blocking collectives: 19.1 us -> 7.08 us
    pallas_call x0 -> x1, Pallas kernels: none -> 167 us  [reduce_weights(): pl.pallas_call(functools.partial(reduce_kernel, experts_n, dense_n, shard...]
    ppermute x72 -> x0, waiting for transfers between devices: 151 us -> none  [step(): return lax.ppermute(array, 'ctx', pairs)]
    ppermute x72 -> x0, starting transfers between devices: 148 us -> none  [step(): return lax.ppermute(array, 'ctx', pairs)]
    ppermute x45 -> x36, waiting for transfers between devices: 127 us -> 87.5 us  [across(): return lax.ppermute(array, 'fsdp', [(i, i ^ k) for i in range(self.shards)])]
    ppermute x12, waiting for transfers between devices: 23.1 us -> 44.6 us  [shift(): return lax.ppermute(array, 'ctx', [(i, (i + 2 * s) % n) for i in range(n)])]
    convert_element_type x27 -> x3, other arithmetic: 20.8 us -> 6.1 us  [shards(): t.astype(f32)]
    all_gather x1, blocking collectives: 19.1 us -> 7.08 us  [shards(): lax.all_gather(jnp.stack([attn_gain, moe_gain]), 'fsdp', axis=1, tiled=True)]
    ppermute x12, starting transfers between devices: 52.5 us -> 42.2 us  [shift(): return lax.ppermute(array, 'ctx', [(i, (i + 2 * s) % n) for i in range(n)])]
  transfers between devices with their start and end apart: 172 -> 61, of which waited for: 63 -> 26; matrix products, arithmetic and copies ran while one was open for 19% -> 13% of each run, Pallas kernels for 9% -> 9%
where the time goes in v2:
time: 675 us; the launch traced here: 667 us
  Pallas kernels  280 us (41%)
  waiting for transfers between devices  134 us (20%)
  starting transfers between devices  89.5 us (13%)
  other arithmetic  60.6 us (9%)
  local copies, waits for them, and re-layouts  54.4 us (8%)
  matrix products  40 us (6%)
  blocking collectives  7.08 us (1%)
    pallas_call x1, Pallas kernels, reduce_weights(): pl.pallas_call(functools.partial(reduce_kernel, experts_n, dense_n, shard...  167 us
    ppermute x36, waiting for transfers between devices, across(): return lax.ppermute(array, 'fsdp', [(i, i ^ k) for i in range(self.shards)])  87.5 us
    ppermute x36, starting transfers between devices, across(): return lax.ppermute(array, 'fsdp', [(i, i ^ k) for i in range(self.shards)])  44.6 us
    ppermute x12, waiting for transfers between devices, shift(): return lax.ppermute(array, 'ctx', [(i, (i + 2 * s) % n) for i in range(n)])  44.6 us
    ppermute x12, starting transfers between devices, shift(): return lax.ppermute(array, 'ctx', [(i, (i + 2 * s) % n) for i in range(n)])  42.2 us
    dot_general x13, matrix products, dot(): return lax.dot_general(left, right, dims, preferred_element_type=f32)  40 us
    pallas_call x2, Pallas kernels, attention_backward(): pl.pallas_call(attention_backward_kernel, grid=(PAIRS,), in_specs=[pl.Blo...  35.4 us
    pallas_call x2, Pallas kernels, experts(): pl.pallas_call(functools.partial(experts_kernel, parts, rows, held * bloc...  34.5 us
  transfers between devices with their start and end apart: 61, of which 26 were waited for; matrix products, arithmetic and copies ran while one was open for 13% of the time, Pallas kernels for 9%

profile of v2, /device:TPU:0, one launch (start us, length us, event | category | flops | bytes accessed | tf_op | source)
XLA Modules:
  0.0 667.3 jit_solution(4026597081405424767)
XLA Ops:
  18.0 7.1 %all_gather.3 = bf16[2,1536]{1,0:T(2,128)(2,1)S(1)} all-gather(bf16[2,384]{1,0:T(2,128)(2,1)S(1)} %pad_maximum_fusion.6), channel_id=1, replica_groups=mesh['fsdp'=4,'ctx'=8] {'fsdp'}, dimensions={1}, use_global_device_ids=true | all-gather | bytes 7680 | tf_op jit(solution)/shard_map/all_gather | solution.py:772
  52.9 8.6 %collective-permute-done = bf16[192,1536]{1,0:T(8,128)(2,1)} collective-permute-done((bf16[192,1536]{1,0:T(8,128)(2,1)}, bf16[192,1536]{1,0:T(8,128)(2,1)}, u32[]{:S(2)}, u32[]{:S(2)}) %collective-permute-start) | collective-permute-done | bytes 589856 | tf_op jit(solution)/shard_map/ppermute | solution.py:386
  69.1 5.0 collective-permute-done.2
  75.9 10.9 %collective-permute-done.16 = bf16[192,1536]{1,0:T(8,128)(2,1)S(1)} collective-permute-done((bf16[192,1536]{1,0:T(8,128)(2,1)}, bf16[192,1536]{1,0:T(8,128)(2,1)S(1)}, u32[]{:S(2)}, u32[]{:S(2)}) %collective-permute-start.16) | collective-permute-done | bytes 589856 | tf_op jit(solution)/shard_map/ppermute | solution.py:386
  108.3 9.5 %collective-permute-start.34 = (bf16[128,1024]{1,0:T(8,128)(2,1)S(1)}, bf16[128,1024]{1,0:T(8,128)(2,1)S(1)}, u32[]{:S(2)}, u32[]{:S(2)}) collective-permute-start(bf16[128,1024]{1,0:T(8,128)(2,1)S(1)} %get-tuple-element.295), channel_id=1, source_target_pairs={{0,2},{1,3},{2,4},{3,5},{4,6},{5,7},{6,0},{7,1},{8,10},{9,11},{10,... | collective-permute-start | bytes 786440 | tf_op jit(solution)/shard_map/ppermute | solution.py:393
  119.6 10.1 %collective-permute-start.35 = (bf16[128,1024]{1,0:T(8,128)(2,1)S(1)}, bf16[128,1024]{1,0:T(8,128)(2,1)S(1)}, u32[]{:S(2)}, u32[]{:S(2)}) collective-permute-start(bf16[128,1024]{1,0:T(8,128)(2,1)S(1)} %get-tuple-element.295), channel_id=1, source_target_pairs={{0,4},{1,5},{2,6},{3,7},{4,0},{5,1},{6,2},{7,3},{8,12},{9,13},{10,... | collective-permute-start | bytes 786440 | tf_op jit(solution)/shard_map/ppermute | solution.py:393
  133.3 9.2 %collective-permute-done.35 = bf16[128,1024]{1,0:T(8,128)(2,1)S(1)} collective-permute-done((bf16[128,1024]{1,0:T(8,128)(2,1)S(1)}, bf16[128,1024]{1,0:T(8,128)(2,1)S(1)}, u32[]{:S(2)}, u32[]{:S(2)}) %collective-permute-start.35) | collective-permute-done | bytes 262176 | tf_op jit(solution)/shard_map/ppermute | solution.py:393
  154.9 9.8 %attention_forward.2 = bf16[128,1536]{1,0:T(8,128)(2,1)} custom-call(f32[128,1536]{1,0:T(8,128)} %get-tuple-element.249.query_ref, f32[128,128]{1,0:T(8,128)} %pad_maximum_fusion.3.cosine_ref, f32[128,128]{1,0:T(8,128)} %pad_maximum_fusion.4.sine_ref, bf16[1024,1024]{1,0:T(8,128)(2,1)} %copy-done.70, bf16[1024,1024]{1,0:T(8,128)(2,1)} %copy-done.70, ...), custom_call_target="tpu_custom_call" | custom-call | flops 3221225472 | bytes 6291456 | tf_op jit(solution)/shard_map/attention_forward/pallas_call | solution.py:155
  176.1 9.6 %attention_forward.3 = bf16[128,1536]{1,0:T(8,128)(2,1)} custom-call(f32[128,1536]{1,0:T(8,128)} %get-tuple-element.250.query_ref, f32[128,128]{1,0:T(8,128)} %pad_maximum_fusion.3.cosine_ref, f32[128,128]{1,0:T(8,128)} %pad_maximum_fusion.4.sine_ref, bf16[1024,1024]{1,0:T(8,128)(2,1)} %copy-done.69, bf16[1024,1024]{1,0:T(8,128)(2,1)} %copy-done.69, ...), custom_call_target="tpu_custom_call" | custom-call | flops 3221225472 | bytes 6291456 | tf_op jit(solution)/shard_map/attention_forward/pallas_call | solution.py:155
  190.3 17.0 %experts.2 = (bf16[128,1536]{1,0:T(8,128)(2,1)}, bf16[128,1536]{1,0:T(8,128)(2,1)}, bf16[128,1536]{1,0:T(8,128)(2,1)}, bf16[128,1536]{1,0:T(8,128)(2,1)}, bf16[1...) custom-call(f32[2,512,1]{2,1,0:T(8,128)} %copy.59.combine_ref, ...), custom_call_target="tpu_custom_call" | custom-call | flops 9663676416 | bytes 25165824 | tf_op jit(solution)/shard_map/experts/pallas_call | solution.py:294
  214.0 5.6 collective-permute-done.31
  225.2 4.1 collective-permute-done.32
  231.4 5.1 collective-permute-done.47
  238.0 8.1 %collective-permute-done.48 = bf16[128,1536]{1,0:T(8,128)(2,1)S(1)} collective-permute-done((bf16[128,1536]{1,0:T(8,128)(2,1)}, bf16[128,1536]{1,0:T(8,128)(2,1)S(1)}, u32[]{:S(2)}, u32[]{:S(2)}) %collective-permute-start.48) | collective-permute-done | bytes 393248 | tf_op jit(solution)/shard_map/ppermute | solution.py:386
  258.3 4.7 collective-permute-done.42.refs_6_.refs_14_
  263.0 7.4 %collective-permute-done.38.refs_1_.refs_5_ = bf16[128,1536]{1,0:T(8,128)(2,1)} collective-permute-done((bf16[128,1536]{1,0:T(8,128)(2,1)S(1)}, bf16[128,1536]{1,0:T(8,128)(2,1)}, u32[]{:S(2)}, u32[]{:S(2)}) %collective-permute-start.38) | collective-permute-done | bytes 393248 | tf_op jit(solution)/shard_map/ppermute | solution.py:386
  270.4 7.1 %collective-permute-done.39.refs_2_.refs_6_ = bf16[128,1536]{1,0:T(8,128)(2,1)} collective-permute-done((bf16[128,1536]{1,0:T(8,128)(2,1)S(1)}, bf16[128,1536]{1,0:T(8,128)(2,1)}, u32[]{:S(2)}, u32[]{:S(2)}) %collective-permute-start.39) | collective-permute-done | bytes 393248 | tf_op jit(solution)/shard_map/ppermute | solution.py:386
  277.5 17.5 %experts.3 = (bf16[128,1536]{1,0:T(8,128)(2,1)}, bf16[128,1536]{1,0:T(8,128)(2,1)}, bf16[128,1536]{1,0:T(8,128)(2,1)}, bf16[128,1536]{1,0:T(8,128)(2,1)}, bf16[1...) custom-call(f32[2,512,1]{2,1,0:T(8,128)} %copy.60.combine_ref, ...), custom_call_target="tpu_custom_call" | custom-call | flops 9663676416 | bytes 25165824 | tf_op jit(solution)/shard_map/experts/pallas_call | solution.py:294
  301.1 6.2 collective-permute-done.44
  308.8 16.3 %expert_weights.1 = (bf16[2,1536,512]{2,1,0:T(8,128)(2,1)}, bf16[2,1536,512]{2,1,0:T(8,128)(2,1)}, bf16[2,512,1536]{2,1,0:T(8,128)(2,1)}) custom-call(bf16[128,1536]{1,0:T(8,128)(2,1)} %copy-done.54, bf16[128,1536]{1,0:T(8,128)(2,1)} %copy-done.96, bf16[128,1536]{1,0:T(8,128)(2,1)} %collective-permute-done.26.refs_2_, ...), custom_call_target="tpu_custom_call" | custom-call | flops 9663676416 | bytes 22020096 | tf_op jit(solution)/shard_map/expert_weights/pallas_call | solution.py:351
  325.2 5.5 collective-permute-done.55
  337.5 4.1 convolution_convert_fusion.4
  342.7 17.8 %attention_backward.2 = (bf16[128,1536]{1,0:T(8,128)(2,1)}, bf16[1024,1024]{1,0:T(8,128)(2,1)}) custom-call(f32[128,1536]{1,0:T(8,128)} %get-tuple-element.249.query_ref, f32[128,128]{1,0:T(8,128)} %pad_maximum_fusion.3.cosine_ref, f32[128,128]{1,0:T(8,128)} %pad_maximum_fusion.4.sine_ref, bf16[1024,1024]{1,0:T(8,128)(2,1)} %copy-done.70, ...), custom_call_target="tpu_custom_call" | custom-call | flops 8053063680 | bytes 12582912 | tf_op jit(solution)/shard_map/attention_backward/pallas_call | solution.py:214
  362.8 4.0 convolution_convert_fusion.3
  368.0 17.6 %attention_backward.3 = (bf16[128,1536]{1,0:T(8,128)(2,1)}, bf16[1024,1024]{1,0:T(8,128)(2,1)}) custom-call(f32[128,1536]{1,0:T(8,128)} %get-tuple-element.250.query_ref, f32[128,128]{1,0:T(8,128)} %pad_maximum_fusion.3.cosine_ref, f32[128,128]{1,0:T(8,128)} %pad_maximum_fusion.4.sine_ref, bf16[1024,1024]{1,0:T(8,128)(2,1)} %copy-done.69, ...), custom_call_target="tpu_custom_call" | custom-call | flops 8053063680 | bytes 12582912 | tf_op jit(solution)/shard_map/attention_backward/pallas_call | solution.py:214
  400.2 8.3 %collective-permute-start.51 = (bf16[128,1024]{1,0:T(8,128)(2,1)S(1)}, bf16[128,1024]{1,0:T(8,128)(2,1)S(1)}, u32[]{:S(2)}, u32[]{:S(2)}) collective-permute-start(bf16[128,1024]{1,0:T(8,128)(2,1)S(1)} %get-tuple-element.253), channel_id=1, source_target_pairs={{0,6},{1,7},{2,0},{3,1},{4,2},{5,3},{6,4},{7,5},{8,14},{9,15},{10,... | collective-permute-start | bytes 786440 | tf_op jit(solution)/shard_map/ppermute | solution.py:393
  416.4 15.0 %collective-permute-done.52.refs_2_ = bf16[128,1024]{1,0:T(8,128)(2,1)S(1)} collective-permute-done((bf16[128,1024]{1,0:T(8,128)(2,1)S(1)}, bf16[128,1024]{1,0:T(8,128)(2,1)S(1)}, u32[]{:S(2)}, u32[]{:S(2)}) %collective-permute-start.52) | collective-permute-done | bytes 262176 | tf_op jit(solution)/shard_map/ppermute | solution.py:393
  437.6 15.2 %collective-permute-done.59.refs_2_ = bf16[128,1024]{1,0:T(8,128)(2,1)S(1)} collective-permute-done((bf16[128,1024]{1,0:T(8,128)(2,1)}, bf16[128,1024]{1,0:T(8,128)(2,1)S(1)}, u32[]{:S(2)}, u32[]{:S(2)}) %collective-permute-start.59) | collective-permute-done | bytes 262176 | tf_op jit(solution)/shard_map/ppermute | solution.py:393
  455.9 3.9 convolution_convert_fusion.2
  467.5 4.0 fusion.1.refs_5_
  471.5 167.1 %reduce_weights.1 = (bf16[3072,512]{1,0:T(8,128)(2,1)}, bf16[3072,512]{1,0:T(8,128)(2,1)}, bf16[1024,1536]{1,0:T(8,128)(2,1)}, bf16[384,1536]{1,0:T(8,128)(2,1)}...) custom-call(bf16[3072,512]{1,0:T(8,128)(2,1)} %bitcast.93, bf16[3072,512]{1,0:T(8,128)(2,1)} %bitcast.94, ...), custom_call_target="tpu_custom_call" | custom-call | tf_op jit(solution)/shard_map/reduce_weights/pallas_call | solution.py:721
  645.5 6.4 convert.48
  (459 shorter events, 217.0 us)
Async XLA Ops:
  2.7 38.8 %collective-permute-start.6 = (bf16[192,1024]{1,0:T(8,128)(2,1)}, bf16[192,1024]{1,0:T(8,128)(2,1)}, u32[]{:S(2)}, u32[]{:S(2)}) collective-permute-start(bf16[192,1024]{1,0:T(8,128)(2,1)} %get-tuple-element.224), channel_id=1, source_target_pairs={{0,8},{8,0},{16,24},{24,16},{1,9},{9,1},{17,25},{25,17},{2,10},{10... | collective-permute-start | bytes 1179656 | tf_op jit(solution)/shard_map/ppermute | solution.py:386
  5.6 39.1 %collective-permute-start.7 = (bf16[192,1024]{1,0:T(8,128)(2,1)}, bf16[192,1024]{1,0:T(8,128)(2,1)}, u32[]{:S(2)}, u32[]{:S(2)}) collective-permute-start(bf16[192,1024]{1,0:T(8,128)(2,1)} %get-tuple-element.224), channel_id=1, source_target_pairs={{0,16},{8,24},{16,0},{24,8},{1,17},{9,25},{17,1},{25,9},{2,18},{10... | collective-permute-start | bytes 1179656 | tf_op jit(solution)/shard_map/ppermute | solution.py:386
  8.4 27.1 %collective-permute-start.22 = (f32[2,128,8]{1,2,0:T(8,128)}, f32[2,128,8]{1,2,0:T(8,128)}, u32[]{:S(2)}, u32[]{:S(2)}) collective-permute-start(f32[2,128,8]{1,2,0:T(8,128)} %select_reduce_fusion), channel_id=1, source_target_pairs={{0,8},{8,0},{16,24},{24,16},{1,9},{9,1},{17,25},{25,17},{2,10},{10... | collective-permute-start | bytes 24584 | tf_op jit(solution)/shard_map/ppermute | solution.py:386
  9.0 28.1 %collective-permute-start.23 = (f32[2,128,8]{1,2,0:T(8,128)}, f32[2,128,8]{1,2,0:T(8,128)}, u32[]{:S(2)}, u32[]{:S(2)}) collective-permute-start(f32[2,128,8]{1,2,0:T(8,128)} %select_reduce_fusion), channel_id=1, source_target_pairs={{0,16},{8,24},{16,0},{24,8},{1,17},{9,25},{17,1},{25,9},{2,18},{10... | collective-permute-start | bytes 24584 | tf_op jit(solution)/shard_map/ppermute | solution.py:386
  9.0 29.6 %collective-permute-start.24 = (f32[2,128,8]{1,2,0:T(8,128)}, f32[2,128,8]{1,2,0:T(8,128)}, u32[]{:S(2)}, u32[]{:S(2)}) collective-permute-start(f32[2,128,8]{1,2,0:T(8,128)} %select_reduce_fusion), channel_id=1, source_target_pairs={{0,24},{8,16},{16,8},{24,0},{1,25},{9,17},{17,9},{25,1},{2,26},{10... | collective-permute-start | bytes 24584 | tf_op jit(solution)/shard_map/ppermute | solution.py:386
  37.1 24.5 %collective-permute-start = (bf16[192,1536]{1,0:T(8,128)(2,1)}, bf16[192,1536]{1,0:T(8,128)(2,1)}, u32[]{:S(2)}, u32[]{:S(2)}) collective-permute-start(bf16[192,1536]{1,0:T(8,128)(2,1)} %get-tuple-element.246), channel_id=1, source_target_pairs={{0,8},{8,0},{16,24},{24,16},{1,9},{9,1},{17,25},{25,17},{2,10},{10... | collective-permute-start | bytes 1769480 | tf_op jit(solution)/shard_map/ppermute | solution.py:386
  38.6 29.1 %collective-permute-start.1 = (bf16[192,1536]{1,0:T(8,128)(2,1)}, bf16[192,1536]{1,0:T(8,128)(2,1)S(1)}, u32[]{:S(2)}, u32[]{:S(2)}) collective-permute-start(bf16[192,1536]{1,0:T(8,128)(2,1)} %get-tuple-element.246), channel_id=1, source_target_pairs={{0,16},{8,24},{16,0},{24,8},{1,17},{9,25},{17,1},{25,9},{2,18},{10... | collective-permute-start | bytes 1769480 | tf_op jit(solution)/shard_map/ppermute | solution.py:386
  41.5 32.6 %collective-permute-start.2 = (bf16[192,1536]{1,0:T(8,128)(2,1)}, bf16[192,1536]{1,0:T(8,128)(2,1)S(1)}, u32[]{:S(2)}, u32[]{:S(2)}) collective-permute-start(bf16[192,1536]{1,0:T(8,128)(2,1)} %get-tuple-element.246), channel_id=1, source_target_pairs={{0,24},{8,16},{16,8},{24,0},{1,25},{9,17},{17,9},{25,1},{2,26},{10... | collective-permute-start | bytes 1769480 | tf_op jit(solution)/shard_map/ppermute | solution.py:386
  44.7 42.0 %collective-permute-start.16 = (bf16[192,1536]{1,0:T(8,128)(2,1)}, bf16[192,1536]{1,0:T(8,128)(2,1)S(1)}, u32[]{:S(2)}, u32[]{:S(2)}) collective-permute-start(bf16[192,1536]{1,0:T(8,128)(2,1)} %get-tuple-element.212), channel_id=1, source_target_pairs={{0,8},{8,0},{16,24},{24,16},{1,9},{9,1},{17,25},{25,17},{2,10},{10... | collective-permute-start | bytes 1769480 | tf_op jit(solution)/shard_map/ppermute | solution.py:386
  48.9 38.8 %collective-permute-start.17 = (bf16[192,1536]{1,0:T(8,128)(2,1)}, bf16[192,1536]{1,0:T(8,128)(2,1)S(1)}, u32[]{:S(2)}, u32[]{:S(2)}) collective-permute-start(bf16[192,1536]{1,0:T(8,128)(2,1)} %get-tuple-element.212), channel_id=1, source_target_pairs={{0,16},{8,24},{16,0},{24,8},{1,17},{9,25},{17,1},{25,9},{2,18},{10... | collective-permute-start | bytes 1769480 | tf_op jit(solution)/shard_map/ppermute | solution.py:386
  61.6 37.6 %collective-permute-start.18 = (bf16[192,1536]{1,0:T(8,128)(2,1)}, bf16[192,1536]{1,0:T(8,128)(2,1)S(1)}, u32[]{:S(2)}, u32[]{:S(2)}) collective-permute-start(bf16[192,1536]{1,0:T(8,128)(2,1)} %get-tuple-element.212), channel_id=1, source_target_pairs={{0,24},{8,16},{16,8},{24,0},{1,25},{9,17},{17,9},{25,1},{2,26},{10... | collective-permute-start | bytes 1769480 | tf_op jit(solution)/shard_map/ppermute | solution.py:386
  67.7 107.0 %collective-permute-start.28 = (bf16[128,1536]{1,0:T(8,128)(2,1)}, bf16[128,1536]{1,0:T(8,128)(2,1)}, u32[]{:S(2)}, u32[]{:S(2)}) collective-permute-start(bf16[128,1536]{1,0:T(8,128)(2,1)} %get-tuple-element.273.refs_4_.refs_8_), channel_id=1, source_target_pairs={{0,8},{8,0},{16,24},{24,16},{1,9},{9,1},{17,25},{25,17},{2,10},{10... | collective-permute-start | bytes 1179656 | tf_op jit(solution)/shard_map/ppermute | solution.py:386
  89.0 98.0 %collective-permute-start.29 = (bf16[128,1536]{1,0:T(8,128)(2,1)}, bf16[128,1536]{1,0:T(8,128)(2,1)}, u32[]{:S(2)}, u32[]{:S(2)}) collective-permute-start(bf16[128,1536]{1,0:T(8,128)(2,1)} %get-tuple-element.273.refs_4_.refs_8_), channel_id=1, source_target_pairs={{0,16},{8,24},{16,0},{24,8},{1,17},{9,25},{17,1},{25,9},{2,18},{10... | collective-permute-start | bytes 1179656 | tf_op jit(solution)/shard_map/ppermute | solution.py:386
  119.6 24.6 %collective-permute-start.3 = (bf16[192,1536]{1,0:T(8,128)(2,1)}, bf16[192,1536]{1,0:T(8,128)(2,1)S(1)}, u32[]{:S(2)}, u32[]{:S(2)}) collective-permute-start(bf16[192,1536]{1,0:T(8,128)(2,1)} %collective-permute-done), channel_id=1, source_target_pairs={{0,1},{1,0},{2,3},{3,2},{4,5},{5,4},{6,7},{7,6},{8,9},{9,8},{10,11... | collective-permute-start | bytes 1769480 | tf_op jit(solution)/shard_map/ppermute | solution.py:389
  146.3 40.7 %collective-permute-start.30 = (bf16[128,1536]{1,0:T(8,128)(2,1)}, bf16[128,1536]{1,0:T(8,128)(2,1)}, u32[]{:S(2)}, u32[]{:S(2)}) collective-permute-start(bf16[128,1536]{1,0:T(8,128)(2,1)} %get-tuple-element.273.refs_4_.refs_8_), channel_id=1, source_target_pairs={{0,24},{8,16},{16,8},{24,0},{1,25},{9,17},{17,9},{25,1},{2,26},{10... | collective-permute-start | bytes 1179656 | tf_op jit(solution)/shard_map/ppermute | solution.py:386
  212.0 24.6 %collective-permute-start.47 = (bf16[128,1536]{1,0:T(8,128)(2,1)}, bf16[128,1536]{1,0:T(8,128)(2,1)S(1)}, u32[]{:S(2)}, u32[]{:S(2)}) collective-permute-start(bf16[128,1536]{1,0:T(8,128)(2,1)} %get-tuple-element.53), channel_id=1, source_target_pairs={{0,8},{8,0},{16,24},{24,16},{1,9},{9,1},{17,25},{25,17},{2,10},{10... | collective-permute-start | bytes 1179656 | tf_op jit(solution)/shard_map/ppermute | solution.py:386
  213.0 33.0 %collective-permute-start.48 = (bf16[128,1536]{1,0:T(8,128)(2,1)}, bf16[128,1536]{1,0:T(8,128)(2,1)S(1)}, u32[]{:S(2)}, u32[]{:S(2)}) collective-permute-start(bf16[128,1536]{1,0:T(8,128)(2,1)} %get-tuple-element.54), channel_id=1, source_target_pairs={{0,16},{8,24},{16,0},{24,8},{1,17},{9,25},{17,1},{25,9},{2,18},{10... | collective-permute-start | bytes 1179656 | tf_op jit(solution)/shard_map/ppermute | solution.py:386
  220.4 25.7 %collective-permute-start.49 = (bf16[128,1536]{1,0:T(8,128)(2,1)}, bf16[128,1536]{1,0:T(8,128)(2,1)S(1)}, u32[]{:S(2)}, u32[]{:S(2)}) collective-permute-start(bf16[128,1536]{1,0:T(8,128)(2,1)} %get-tuple-element.55), channel_id=1, source_target_pairs={{0,24},{8,16},{16,8},{24,0},{1,25},{9,17},{17,9},{25,1},{2,26},{10... | collective-permute-start | bytes 1179656 | tf_op jit(solution)/shard_map/ppermute | solution.py:386
  229.3 24.1 %collective-permute-start.41 = (bf16[128,1536]{1,0:T(8,128)(2,1)}, bf16[128,1536]{1,0:T(8,128)(2,1)S(1)}, u32[]{:S(2)}, u32[]{:S(2)}) collective-permute-start(bf16[128,1536]{1,0:T(8,128)(2,1)} %get-tuple-element.274.refs_4_.refs_12_), channel_id=1, source_target_pairs={{0,8},{8,0},{16,24},{24,16},{1,9},{9,1},{17,25},{25,17},{2,10},{10... | collective-permute-start | bytes 1179656 | tf_op jit(solution)/shard_map/ppermute | solution.py:386
  230.3 32.7 %collective-permute-start.42 = (bf16[128,1536]{1,0:T(8,128)(2,1)}, bf16[128,1536]{1,0:T(8,128)(2,1)}, u32[]{:S(2)}, u32[]{:S(2)}) collective-permute-start(bf16[128,1536]{1,0:T(8,128)(2,1)} %get-tuple-element.274.refs_4_.refs_12_), channel_id=1, source_target_pairs={{0,16},{8,24},{16,0},{24,8},{1,17},{9,25},{17,1},{25,9},{2,18},{10... | collective-permute-start | bytes 1179656 | tf_op jit(solution)/shard_map/ppermute | solution.py:386
  236.5 26.5 %collective-permute-start.43 = (bf16[128,1536]{1,0:T(8,128)(2,1)}, bf16[128,1536]{1,0:T(8,128)(2,1)}, u32[]{:S(2)}, u32[]{:S(2)}) collective-permute-start(bf16[128,1536]{1,0:T(8,128)(2,1)} %get-tuple-element.274.refs_4_.refs_12_), channel_id=1, source_target_pairs={{0,24},{8,16},{16,8},{24,0},{1,25},{9,17},{17,9},{25,1},{2,26},{10... | collective-permute-start | bytes 1179656 | tf_op jit(solution)/shard_map/ppermute | solution.py:386
  250.3 27.1 %collective-permute-start.39 = (bf16[128,1536]{1,0:T(8,128)(2,1)S(1)}, bf16[128,1536]{1,0:T(8,128)(2,1)}, u32[]{:S(2)}, u32[]{:S(2)}) collective-permute-start(bf16[128,1536]{1,0:T(8,128)(2,1)S(1)} %get-tuple-element.351.refs_0_.refs_4_), channel_id=1, source_target_pairs={{0,16},{8,24},{16,0},{24,8},{1,17},{9,25},{17,1},{25,9},{2,18},{10... | collective-permute-start | bytes 1179656 | tf_op jit(solution)/shard_map/ppermute | solution.py:386
  253.4 24.1 %collective-permute-start.40 = (bf16[128,1536]{1,0:T(8,128)(2,1)S(1)}, bf16[128,1536]{1,0:T(8,128)(2,1)}, u32[]{:S(2)}, u32[]{:S(2)}) collective-permute-start(bf16[128,1536]{1,0:T(8,128)(2,1)S(1)} %get-tuple-element.351.refs_0_.refs_4_), channel_id=1, source_target_pairs={{0,24},{8,16},{16,8},{24,0},{1,25},{9,17},{17,9},{25,1},{2,26},{10... | collective-permute-start | bytes 1179656 | tf_op jit(solution)/shard_map/ppermute | solution.py:386
  296.5 28.6 %collective-permute-start.45 = (bf16[128,1536]{1,0:T(8,128)(2,1)}, bf16[128,1536]{1,0:T(8,128)(2,1)}, u32[]{:S(2)}, u32[]{:S(2)}) collective-permute-start(bf16[128,1536]{1,0:T(8,128)(2,1)} %get-tuple-element.50), channel_id=1, source_target_pairs={{0,16},{8,24},{16,0},{24,8},{1,17},{9,25},{17,1},{25,9},{2,18},{10... | collective-permute-start | bytes 1179656 | tf_op jit(solution)/shard_map/ppermute | solution.py:386
  297.6 27.5 %collective-permute-start.46 = (bf16[128,1536]{1,0:T(8,128)(2,1)}, bf16[128,1536]{1,0:T(8,128)(2,1)}, u32[]{:S(2)}, u32[]{:S(2)}) collective-permute-start(bf16[128,1536]{1,0:T(8,128)(2,1)} %get-tuple-element.51), channel_id=1, source_target_pairs={{0,24},{8,16},{16,8},{24,0},{1,25},{9,17},{17,9},{25,1},{2,26},{10... | collective-permute-start | bytes 1179656 | tf_op jit(solution)/shard_map/ppermute | solution.py:386
  299.1 26.1 %collective-permute-start.54 = (bf16[128,1536]{1,0:T(8,128)(2,1)}, bf16[128,1536]{1,0:T(8,128)(2,1)}, u32[]{:S(2)}, u32[]{:S(2)}) collective-permute-start(bf16[128,1536]{1,0:T(8,128)(2,1)} %get-tuple-element.59), channel_id=1, source_target_pairs={{0,8},{8,0},{16,24},{24,16},{1,9},{9,1},{17,25},{25,17},{2,10},{10... | collective-permute-start | bytes 1179656 | tf_op jit(solution)/shard_map/ppermute | solution.py:386
  300.0 30.7 %collective-permute-start.55 = (bf16[128,1536]{1,0:T(8,128)(2,1)}, bf16[128,1536]{1,0:T(8,128)(2,1)}, u32[]{:S(2)}, u32[]{:S(2)}) collective-permute-start(bf16[128,1536]{1,0:T(8,128)(2,1)} %get-tuple-element.60), channel_id=1, source_target_pairs={{0,16},{8,24},{16,0},{24,8},{1,17},{9,25},{17,1},{25,9},{2,18},{10... | collective-permute-start | bytes 1179656 | tf_op jit(solution)/shard_map/ppermute | solution.py:386
  307.3 23.3 %collective-permute-start.56 = (bf16[128,1536]{1,0:T(8,128)(2,1)}, bf16[128,1536]{1,0:T(8,128)(2,1)}, u32[]{:S(2)}, u32[]{:S(2)}) collective-permute-start(bf16[128,1536]{1,0:T(8,128)(2,1)} %get-tuple-element.61), channel_id=1, source_target_pairs={{0,24},{8,16},{16,8},{24,0},{1,25},{9,17},{17,9},{25,1},{2,26},{10... | collective-permute-start | bytes 1179656 | tf_op jit(solution)/shard_map/ppermute | solution.py:386
  362.8 34.8 %collective-permute-start.50 = (bf16[512,1024]{1,0:T(8,128)(2,1)}, bf16[512,1024]{1,0:T(8,128)(2,1)}, u32[]{:S(2)}, u32[]{:S(2)}) collective-permute-start(bf16[512,1024]{1,0:T(8,128)(2,1)} %slice.397), channel_id=1, source_target_pairs={{0,1},{1,0},{2,3},{3,2},{4,5},{5,4},{6,7},{7,6},{8,9},{9,8},{10,11... | collective-permute-start | bytes 3145736 | tf_op jit(solution)/shard_map/ppermute | solution.py:389
  411.9 25.7 %collective-permute-start.58 = (bf16[128,1024]{1,0:T(8,128)(2,1)}, bf16[128,1024]{1,0:T(8,128)(2,1)S(1)}, u32[]{:S(2)}, u32[]{:S(2)}) collective-permute-start(bf16[128,1024]{1,0:T(8,128)(2,1)} %get-tuple-element.257), channel_id=1, source_target_pairs={{0,6},{1,7},{2,0},{3,1},{4,2},{5,3},{6,4},{7,5},{8,14},{9,15},{10,... | collective-permute-start | bytes 786440 | tf_op jit(solution)/shard_map/ppermute | solution.py:393
  415.2 37.7 %collective-permute-start.59 = (bf16[128,1024]{1,0:T(8,128)(2,1)}, bf16[128,1024]{1,0:T(8,128)(2,1)S(1)}, u32[]{:S(2)}, u32[]{:S(2)}) collective-permute-start(bf16[128,1024]{1,0:T(8,128)(2,1)} %get-tuple-element.256), channel_id=1, source_target_pairs={{0,4},{1,5},{2,6},{3,7},{4,0},{5,1},{6,2},{7,3},{8,12},{9,13},{10,... | collective-permute-start | bytes 786440 | tf_op jit(solution)/shard_map/ppermute | solution.py:393
  416.3 36.5 %collective-permute-start.60 = (bf16[128,1024]{1,0:T(8,128)(2,1)}, bf16[128,1024]{1,0:T(8,128)(2,1)S(1)}, u32[]{:S(2)}, u32[]{:S(2)}) collective-permute-start(bf16[128,1024]{1,0:T(8,128)(2,1)} %get-tuple-element.255), channel_id=1, source_target_pairs={{0,2},{1,3},{2,4},{3,5},{4,6},{5,7},{6,0},{7,1},{8,10},{9,11},{10,... | collective-permute-start | bytes 786440 | tf_op jit(solution)/shard_map/ppermute | solution.py:393
  (131 other events, 1654.0 us)

commit v3 on v2

--- a/solution.py
+++ b/solution.py
@@ -58,23 +58,23 @@
     return tile * cosine + jnp.where(first, ahead, behind) * sine
 
 
-def rotate_pairs_kernel(pair_ref, cosine_ref, sine_ref, out_ref):
+def rotate_columns_kernel(rotated, values_ref, cosine_ref, sine_ref, out_ref):
     cosine, sine = cosine_ref[...], sine_ref[...]
-    for i in range(2 * KEY_WIDTH // LANES):
+    for i in range(values_ref.shape[1] // LANES):
         cols = slice(i * LANES, (i + 1) * LANES)
-        tile = pair_ref[:, cols]
-        if i < KEY_WIDTH // LANES:
+        tile = values_ref[:, cols]
+        if i < rotated // LANES:
             tile = rotate(tile, cosine, sine)
         out_ref[:, cols] = tile.astype(bf16)
 
 
-def rotate_pairs(pair_pre, cosine, sine):
+def rotate_columns(values, cosine, sine, rotated):
     return pl.pallas_call(
-        rotate_pairs_kernel,
-        out_shape=jax.ShapeDtypeStruct(pair_pre.shape, bf16),
+        functools.partial(rotate_columns_kernel, rotated),
+        out_shape=jax.ShapeDtypeStruct(values.shape, bf16),
         compiler_params=pltpu.CompilerParams(vmem_limit_bytes=VMEM_LIMIT),
-        name="rotate_pairs",
-    )(pair_pre, cosine, sine)
+        name="rotate_columns",
+    )(values, cosine, sine)
 
 
 def pair_gradient_kernel(count, cosine_ref, sine_ref, *refs):
@@ -122,17 +122,14 @@
     return [jnp.where(low, heads[2 * i], heads[2 * i + 1]) for i in range(GROUP)]
 
 
-def query_tiles(query_ref, cosine, sine):
-    tiles = []
-    for i in range(GROUP):
-        tile = rotate(query_ref[:, i * LANES : (i + 1) * LANES], cosine, sine)
-        tiles.append(tile.astype(bf16).astype(f32) * (1.0 / HEAD_SIZE))
-    return tiles
-
-
-def attention_forward_kernel(query_ref, cosine_ref, sine_ref, key_ref, value_ref, bias_ref, out_ref):
+def query_tiles(query_ref):
+    scale = 1.0 / HEAD_SIZE
+    return [query_ref[:, i * LANES : (i + 1) * LANES].astype(f32) * scale for i in range(GROUP)]
+
+
+def attention_forward_kernel(query_ref, key_ref, value_ref, bias_ref, out_ref):
     rows = query_ref.shape[0]
-    tiles = query_tiles(query_ref, cosine_ref[...], sine_ref[...])
+    tiles = query_tiles(query_ref)
     key, value = key_ref[...], value_ref[...]
     bias = bias_ref[...]
     results = []
@@ -149,19 +146,16 @@
         out_ref[:, i * LANES : (i + 1) * LANES] = tile.astype(bf16)
 
 
-def attention_forward(query_pre, cosine, sine, pairs, bias):
+def attention_forward(m, query, pairs, bias):
     rows, length = bias.shape
-    whole = lambda shape: pl.BlockSpec(shape, lambda p: (0, 0))
     return pl.pallas_call(
         attention_forward_kernel,
         grid=(PAIRS,),
         in_specs=[
-            pl.BlockSpec((rows, PAIR_QUERY), lambda p: (0, p)),
-            whole((rows, LANES)),
-            whole((rows, LANES)),
-            pl.BlockSpec((length, LANES), lambda p: (0, p)),
-            pl.BlockSpec((length, LANES), lambda p: (0, p + PAIRS)),
-            whole((rows, length)),
+            pl.BlockSpec((rows, PAIR_QUERY), lambda p: (m, p)),
+            pl.BlockSpec((None, length, LANES), lambda p: (m, 0, p)),
+            pl.BlockSpec((None, length, LANES), lambda p: (m, 0, p + PAIRS)),
+            pl.BlockSpec((rows, length), lambda p: (0, 0)),
         ],
         out_specs=pl.BlockSpec((rows, PAIR_QUERY), lambda p: (0, p)),
         out_shape=jax.ShapeDtypeStruct((rows, MODEL_WIDTH), bf16),
@@ -172,7 +166,7 @@
             transcendentals=rows * length * QUERY_HEADS,
         ),
         name="attention_forward",
-    )(query_pre, cosine, sine, pairs, pairs, bias)
+    )(query, pairs, pairs, bias)
 
 
 def attention_backward_kernel(
@@ -180,7 +174,7 @@
 ):
     rows = query_ref.shape[0]
     cosine, sine = cosine_ref[...], sine_ref[...]
-    tiles = query_tiles(query_ref, cosine, sine)
+    tiles = query_tiles(query_ref)
     grads = [grad_ref[:, i * LANES : (i + 1) * LANES].astype(f32) for i in range(GROUP)]
     key, value = key_ref[...], value_ref[...]
     key_grad, value_grad = None, None
@@ -207,19 +201,19 @@
     pair_out[:, pl.ds(first + KEY_WIDTH, LANES)] = value_grad.astype(bf16)
 
 
-def attention_backward(query_pre, cosine, sine, pairs, bias, grad):
-    rows = query_pre.shape[0]
-    length = pairs.shape[0]
+def attention_backward(m, query, cosine, sine, pairs, bias, grad):
+    rows = cosine.shape[0]
+    length = pairs.shape[1]
     whole = lambda shape: pl.BlockSpec(shape, lambda p: (0, 0))
     return pl.pallas_call(
         attention_backward_kernel,
         grid=(PAIRS,),
         in_specs=[
-            pl.BlockSpec((rows, PAIR_QUERY), lambda p: (0, p)),
+            pl.BlockSpec((rows, PAIR_QUERY), lambda p: (m, p)),
             whole((rows, LANES)),
             whole((rows, LANES)),
-            pl.BlockSpec((length, LANES), lambda p: (0, p)),
-            pl.BlockSpec((length, LANES), lambda p: (0, p + PAIRS)),
+            pl.BlockSpec((None, length, LANES), lambda p: (m, 0, p)),
+            pl.BlockSpec((None, length, LANES), lambda p: (m, 0, p + PAIRS)),
             whole(bias.shape),
             pl.BlockSpec((rows, PAIR_QUERY), lambda p: (0, p)),
         ],
@@ -238,7 +232,7 @@
             transcendentals=rows * length * QUERY_HEADS,
         ),
         name="attention_backward",
-    )(query_pre, cosine, sine, pairs, pairs, bias, grad)
+    )(query, cosine, sine, pairs, pairs, bias, grad)
 
 
 def experts_kernel(parts, rows, steps, combine_ref, gate_ref, up_ref, down_ref, *refs):
@@ -392,93 +386,324 @@
         n = self.contexts
         return lax.ppermute(array, "ctx", [(i, (i + 2 * s) % n) for i in range(n)])
 
-    def step(self, array, first, last, direction):
-        pairs = [
-            (2 * i + core, 2 * (i + direction) + core) for i in range(first, last + 1) for core in range(2)
-        ]
-        return lax.ppermute(array, "ctx", pairs)
-
-    def to_relative(self, array):
-        width = array.shape[-1] // (2 * self.shards)
-        pieces = [[array[..., (2 * b + h) * width : (2 * b + h + 1) * width] for b in range(self.shards)] for h in range(2)]
-        return jnp.concatenate(sum(self._swapped(pieces), []), axis=-1)
-
-    def to_absolute(self, array):
-        width = array.shape[-1] // (2 * self.shards)
-        pieces = [
-            [array[..., (h * self.shards + b) * width : (h * self.shards + b + 1) * width] for b in range(self.shards)]
-            for h in range(2)
-        ]
-        pieces = self._swapped(pieces)
-        return jnp.concatenate([pieces[h][b] for b in range(self.shards) for h in range(2)], axis=-1)
-
-    def _swapped(self, pieces):
-        bit = 1
-        while bit < self.shards:
-            flag = (self.shard & bit) != 0
-            pieces = [[jnp.where(flag, row[b ^ bit], row[b]) for b in range(self.shards)] for row in pieces]
-            bit *= 2
-        flag = self.core == 1
-        return [
-            [jnp.where(flag, pieces[1 - h][b], pieces[h][b]) for b in range(self.shards)] for h in range(2)
-        ]
-
-    def gather_rows(self, weight):
-        half = weight.shape[0] // 2
-        mine = lax.dynamic_slice_in_dim(weight, self.core * half, half, 0)
-        rest = lax.dynamic_slice_in_dim(weight, (1 - self.core) * half, half, 0)
-        arrived = [self.across(mine, k) for k in range(1, self.shards)]
-        passed = [self.other_core(part) for part in arrived]
-        return jnp.concatenate([mine] + arrived + [rest] + passed, axis=0)
-
-    def scatter_rows(self, grad):
-        half = grad.shape[0] // 2
-        mine = grad[:half].astype(f32) + self.other_core(grad[half:]).astype(f32)
-        mine = mine.astype(bf16)
-        size = half // self.shards
-        total = mine[:size].astype(f32)
-        for k in range(1, self.shards):
-            total = total + self.across(mine[k * size : (k + 1) * size], k).astype(f32)
-        return total.astype(bf16)
-
-    def core_halves(self, grad):
-        half = grad.shape[0] // 2
-        mine = lax.dynamic_slice_in_dim(grad, self.core * half, half, 0)
-        rest = lax.dynamic_slice_in_dim(grad, (1 - self.core) * half, half, 0)
-        return (mine.astype(f32) + self.other_core(rest).astype(f32)).astype(bf16)
-
-    def sum_over_chips(self, half):
-        n = self.chips
-        size = half.shape[0] // n
-        block = lambda j: lax.dynamic_slice_in_dim(half, jnp.clip(j, 0, n - 1) * size, size, 0).astype(f32)
-        from_left, from_right = None, None
-        for t in range(1, n):
-            right, left = block(n - t + self.chip), block(t - n + self.chip)
-            if t > 1:
-                right = right + from_left.astype(f32)
-                left = left + from_right.astype(f32)
-            from_left = self.step(right.astype(bf16), 0, t - 1, 1)
-            from_right = self.step(left.astype(bf16), n - t, n - 1, -1)
-        total = block(self.chip) + from_left.astype(f32) + from_right.astype(f32)
-        total = total.astype(bf16)
-        going_right, going_left = [total], [total]
-        for t in range(1, n):
-            going_right.append(self.step(going_right[-1], t - 1, n - 2, 1))
-            going_left.append(self.step(going_left[-1], 1, n - t, -1))
-        return [total] + [going_right[t] + going_left[n - t] for t in range(1, n)]
-
-    def place_rows(self, blocks, out, column):
-        size = blocks[0].shape[0]
-        others = [self.other_core(block) for block in blocks]
-        for core, items in ((self.core, blocks), (1 - self.core, others)):
-            for t, item in enumerate(items):
-                row = (core * self.chips + (self.chip - t + self.chips) % self.chips) * size
-                out = lax.dynamic_update_slice(out, item.astype(f32), (row, column))
-        return out
-
 
 MESH = pl.DeviceIdType.MESH
 LINE = 4
+
+
+class Place:
+    def __init__(self):
+        self.shard, self.context = lax.axis_index("fsdp"), lax.axis_index("ctx")
+        self.core, self.chip = self.context % 2, self.context // 2
+        self.partner = {"ctx": 2 * self.chip + 1 - self.core}
+
+    def peer_index(self, k):
+        x, y = (self.shard % 2 + k % 2) % 2, (self.shard // 2 + k // 2) % 2
+        return 2 * y + x
+
+    def peer(self, k):
+        return {"fsdp": self.peer_index(k)}
+
+    def chip_device(self, chip):
+        return {"ctx": 2 * chip + self.core}
+
+
+def remote(source, target, sems, index, device):
+    return pltpu.make_async_remote_copy(
+        src_ref=source,
+        dst_ref=target,
+        send_sem=sems.at[0, index],
+        recv_sem=sems.at[1, index],
+        device_id=device,
+        device_id_type=MESH,
+    )
+
+
+def greet(device):
+    pl.semaphore_signal(pltpu.get_barrier_semaphore(), inc=1, device_id=device, device_id_type=MESH)
+
+
+SHARDS = 4
+GAIN_ROWS = 16
+
+
+def project_kernel(
+    tokens_ref, cosine_ref, sine_ref, gain_ref, pair_src, query_src, output_src, *refs
+):
+    outs, refs = refs[:6], refs[6:]
+    normed_out, query_out, gains, pair_out, query_weight_out, output_weight_out = outs[0], outs[1], outs[2], *outs[3:6]
+    pairs_out = refs[0]
+    weights, own_pairs = refs[1:4], refs[4]
+    load_sem, store_sem, gain_sem, direct_sem, relay_sem, pass_sem, right_sem, left_sem, core_sem, own_sem = refs[5:]
+    sources = (pair_src, query_src, output_src)
+    weight_outs = (pair_out, query_weight_out, output_weight_out)
+    place = Place()
+    core, chip, shard = place.core, place.chip, place.shard
+    rows = cosine_ref.shape[0]
+    held = pair_src.shape[0]
+    half, quarter = held // 2, held // 4
+
+    has_left, has_right = chip > 0, chip < LINE - 1
+    greet(place.partner)
+    for k in range(1, SHARDS):
+        greet(place.peer(k))
+
+    @pl.when(has_left)
+    def _():
+        greet(place.chip_device(chip - 1))
+
+    @pl.when(has_right)
+    def _():
+        greet(place.chip_device(chip + 1))
+
+    neighbours = jnp.where(has_left, 1, 0) + jnp.where(has_right, 1, 0)
+    pl.semaphore_wait(pltpu.get_barrier_semaphore(), SHARDS + neighbours)
+
+    def rows_of(owner, piece, size):
+        return pl.ds(pl.multiple_of(owner * held + core * half, half) + piece, size)
+
+    gains[pl.ds(pl.multiple_of(shard * GAIN_ROWS, GAIN_ROWS), GAIN_ROWS)] = gain_ref[...]
+    gain_copies = []
+    for k in range(1, SHARDS):
+        target = gains.at[pl.ds(pl.multiple_of(shard * GAIN_ROWS, GAIN_ROWS), GAIN_ROWS)]
+        gain_copies.append(remote(gain_ref, target, gain_sem, k - 1, place.peer(k)))
+
+    loads, directs, relays, passes = [], [], [], []
+    for w in range(3):
+        weight = weights[w]
+        own_rows = pl.ds(pl.multiple_of(shard * held, held), held)
+        loads.append(pltpu.make_async_copy(sources[w], weight.at[own_rows], load_sem.at[w]))
+        mine = sources[w].at[pl.ds(pl.multiple_of(core * half, half), half)]
+        spot = weight.at[rows_of(shard, 0, half)]
+        directs.append([remote(mine, spot, direct_sem, 2 * w + k - 1, place.peer(k)) for k in (1, 2)])
+        relay, onward = [], []
+        for k in (1, 2):
+            spot = weight.at[rows_of(place.peer_index(k), (k - 1) * quarter, quarter)]
+            relay.append(remote(spot, spot, relay_sem, 2 * w + k - 1, place.peer(3 - k)))
+            spot = weight.at[rows_of(place.peer_index(k), 0, half)]
+            onward.append(remote(spot, spot, pass_sem, 4 * w + k - 1, place.partner))
+        for k in (1, 2):
+            spot = weight.at[rows_of(place.peer_index(3), (k - 1) * quarter, quarter)]
+            onward.append(remote(spot, spot, pass_sem, 4 * w + k + 1, place.partner))
+        relays.append(relay)
+        passes.append(onward)
+
+    def send_weight(w):
+        for copy in directs[w]:
+            copy.start()
+
+    def relay_weight(w):
+        for k in (1, 2):
+            directs[w][k - 1].wait_recv()
+            relays[w][k - 1].start()
+        for k in (1, 2):
+            passes[w][k - 1].start()
+
+    def pass_weight(w):
+        for k in (1, 2):
+            relays[w][k - 1].wait_recv()
+            passes[w][k + 1].start()
+
+    def store(w):
+        return pltpu.make_async_copy(weights[w], weight_outs[w], store_sem.at[w])
+
+    def settle_weight(w):
+        loads[w].wait()
+        for copy in passes[w]:
+            copy.wait_recv()
+        store(w).start()
+
+    for copy in gain_copies:
+        copy.start()
+    send_weight(0)
+    for load in loads:
+        load.start()
+
+    values = tokens_ref[...].astype(f32)
+    scale = lax.rsqrt(jnp.mean(values * values, axis=-1, keepdims=True) + eps)
+    for copy in gain_copies:
+        copy.wait_recv()
+    for b in range(SHARDS):
+        columns = slice(b * held, (b + 1) * held)
+        gain = gains[b * GAIN_ROWS : b * GAIN_ROWS + 1].astype(f32)
+        normed_out[:, columns] = (values[:, columns] * scale * gain).astype(bf16)
+
+    relay_weight(0)
+    send_weight(1)
+    pass_weight(0)
+    settle_weight(0)
+    cosine, sine = cosine_ref[...], sine_ref[...]
+
+    def project(weight, column, rotated):
+        result = dot(normed_out[...], weight[:, pl.ds(column, 2 * LANES)])
+        tiles = []
+        for m in range(MB):
+            for i in range(2):
+                tile = result[m * rows : (m + 1) * rows, i * LANES : (i + 1) * LANES]
+                tiles.append((m, i, rotate(tile, cosine, sine) if rotated else tile))
+        return tiles
+
+    def pair_block(b, rotated):
+        column = pl.multiple_of(b * 2 * LANES, 2 * LANES)
+        for m, i, tile in project(weights[0], column, rotated):
+            own_pairs[m, :, pl.ds(column + i * LANES, LANES)] = tile.astype(bf16)
+
+    blocks = KEY_WIDTH // (2 * LANES)
+    for b in range(blocks):
+        pair_block(b, True)
+    for b in range(blocks, 2 * blocks):
+        pair_block(b, False)
+
+    def chunk(m, owner):
+        return pairs_out.at[m, pl.ds(pl.multiple_of((2 * owner + core) * rows, rows), rows)]
+
+    def moves(m, t, direction):
+        owner = chip - direction * (t - 1)
+        source = own_pairs.at[m] if t == 1 else chunk(m, jnp.clip(owner, 0, LANES_CHIP))
+        sems = right_sem if direction > 0 else left_sem
+        target = chunk(m, jnp.clip(owner, 0, LANES_CHIP))
+        device = place.chip_device(jnp.clip(chip + direction, 0, LANES_CHIP))
+        return remote(source, target, sems, m * (LINE - 1) + t - 1, device)
+
+    def sends(t, direction):
+        owner = chip - direction * (t - 1)
+        if direction > 0:
+            return (chip < LINE - 1) & (owner >= 0)
+        return (chip > 0) & (owner <= LINE - 1)
+
+    def gets(t, direction):
+        owner = chip - direction * t
+        return owner >= 0 if direction > 0 else owner <= LINE - 1
+
+    def from_far(m, t, direction):
+        owner = jnp.clip(chip - direction * t, 0, LANES_CHIP)
+        sems = right_sem if direction > 0 else left_sem
+        return remote(chunk(m, owner), chunk(m, owner), sems, m * (LINE - 1) + t - 1, place.partner)
+
+    def pass_chunk(m, t, direction):
+        owner = jnp.clip(chip - direction * t, 0, LANES_CHIP)
+        index = (m * LINE + t) * 2 + (1 if direction > 0 else 0)
+        return remote(chunk(m, owner), chunk(m, owner), core_sem, index, place.partner)
+
+    def send_step(m, t):
+        for direction in (1, -1):
+
+            @pl.when(sends(t, direction))
+            def _():
+                moves(m, t, direction).start()
+
+    def take_step(m, t):
+        for direction in (1, -1):
+
+            @pl.when(gets(t, direction))
+            def _():
+                from_far(m, t, direction).wait_recv()
+                if t < LINE - 1:
+
+                    @pl.when(sends(t + 1, direction))
+                    def _():
+                        moves(m, t + 1, direction).start()
+
+                pass_chunk(m, t, direction).start()
+
+    own_copies = []
+    for m in range(MB):
+        send_step(m, 1)
+        own_copies.append(
+            (
+                pltpu.make_async_copy(own_pairs.at[m], chunk(m, chip), own_sem.at[m]),
+                remote(own_pairs.at[m], chunk(m, chip), core_sem, m * LINE * 2, place.partner),
+            )
+        )
+        own_copies[-1][0].start()
+        own_copies[-1][1].start()
+
+    relay_weight(1)
+    send_weight(2)
+    take_step(0, 1)
+    take_step(1, 1)
+    pass_weight(1)
+    take_step(0, 2)
+    settle_weight(1)
+
+    def query_block(b, carry):
+        column = pl.multiple_of(b * 2 * LANES, 2 * LANES)
+        for m, i, tile in project(weights[1], column, True):
+            query_out[m * rows : (m + 1) * rows, pl.ds(column + i * LANES, LANES)] = tile.astype(bf16)
+        return carry
+
+    lax.fori_loop(0, MODEL_WIDTH // (2 * LANES), query_block, 0)
+    take_step(1, 2)
+    relay_weight(2)
+    take_step(0, 3)
+    take_step(1, 3)
+    pass_weight(2)
+    settle_weight(2)
+
+    for copy in gain_copies:
+        copy.wait_send()
+    for w in range(3):
+        for copy in directs[w] + relays[w] + passes[w]:
+            copy.wait_send()
+        store(w).wait()
+    for m in range(MB):
+        own_copies[m][0].wait()
+        own_copies[m][1].wait()
+        for t in range(1, LINE):
+            for direction in (1, -1):
+
+                @pl.when(sends(t, direction))
+                def _():
+                    moves(m, t, direction).wait_send()
+
+                @pl.when(gets(t, direction))
+                def _():
+                    pass_chunk(m, t, direction).wait()
+
+
+LANES_CHIP = LINE - 1
+
+
+def project_all(tokens, cosine, sine, gains, pair_weight, query_weight, output_weight, length):
+    held = pair_weight.shape[0]
+    rows = cosine.shape[0]
+    dma = pltpu.SemaphoreType.DMA
+    anywhere = pl.BlockSpec(memory_space=pl.ANY)
+    vmem = pl.BlockSpec(memory_space=pltpu.VMEM)
+    sources = (pair_weight, query_weight, output_weight)
+    full = [jax.ShapeDtypeStruct((SHARDS * held, w.shape[1]), bf16) for w in sources]
+    return pl.pallas_call(
+        project_kernel,
+        in_specs=[vmem] * 4 + [anywhere] * 3,
+        out_specs=[vmem] * 3 + [anywhere] * 4,
+        out_shape=[
+            jax.ShapeDtypeStruct(tokens.shape, bf16),
+            jax.ShapeDtypeStruct((tokens.shape[0], query_weight.shape[1]), bf16),
+            jax.ShapeDtypeStruct((SHARDS * GAIN_ROWS, held), bf16),
+        ]
+        + full
+        + [jax.ShapeDtypeStruct((MB, length, 2 * KEY_WIDTH), bf16)],
+        scratch_shapes=[pltpu.VMEM(f.shape, bf16) for f in full]
+        + [
+            pltpu.VMEM((MB, rows, 2 * KEY_WIDTH), bf16),
+            dma((3,)),
+            dma((3,)),
+            dma((2, SHARDS - 1)),
+            dma((2, 6)),
+            dma((2, 6)),
+            dma((2, 12)),
+            dma((2, MB * (LINE - 1))),
+            dma((2, MB * (LINE - 1))),
+            dma((2, 2 * MB * LINE)),
+            dma((MB,)),
+        ],
+        compiler_params=pltpu.CompilerParams(
+            collective_id=1, has_side_effects=True, vmem_limit_bytes=VMEM_LIMIT
+        ),
+        name="project",
+    )(tokens, cosine, sine, gains, *sources)
+
+
 PIECES = 4
 DENSE_PIECES = 2
 ADD_ROWS = 64
@@ -510,37 +735,22 @@
     refs = list(refs[2 * count :])
     take = lambda n: [refs.pop(0) for _ in range(n)]
     own, other = take(count), take(count)
-    across = take(dense_n)
+    across, crossed = take(dense_n), take(dense_n)
     near, far = take(count), take(count)
     load_sem, core_sem, across_sem, near_sem, far_sem, back_sem, pass_sem, store_sem = refs
 
-    shard, context = lax.axis_index("fsdp"), lax.axis_index("ctx")
-    core, chip = context % 2, context // 2
-    partner = {"ctx": 2 * chip + 1 - core}
+    place = Place()
+    core, chip, shard = place.core, place.chip, place.shard
+    partner = place.partner
     inner = (chip == 1) | (chip == 2)
-    outer_device = {"ctx": 2 * (3 * (chip // 2)) + core}
-    inner_device = {"ctx": 2 * (1 + chip // 2) + core}
-    facing_device = {"ctx": 2 * (3 - chip) + core}
-
-    def peer(k):
-        x, y = (shard % 2 + k % 2) % 2, (shard // 2 + k // 2) % 2
-        return {"fsdp": 2 * y + x}
-
-    def send(source, target, sems, index, device):
-        return pltpu.make_async_remote_copy(
-            src_ref=source,
-            dst_ref=target,
-            send_sem=sems.at[0, index],
-            recv_sem=sems.at[1, index],
-            device_id=device,
-            device_id_type=MESH,
-        )
-
-    barrier = pltpu.get_barrier_semaphore()
-    greet = lambda device: pl.semaphore_signal(barrier, inc=1, device_id=device, device_id_type=MESH)
+    outer_device = place.chip_device(3 * (chip // 2))
+    inner_device = place.chip_device(1 + chip // 2)
+    facing_device = place.chip_device(3 - chip)
+    send = remote
+
     greet(partner)
     for k in range(1, shards_n):
-        greet(peer(k))
+        greet(place.peer(k))
 
     @pl.when(inner)
     def _():
@@ -551,42 +761,36 @@
     def _():
         greet(inner_device)
 
-    pl.semaphore_wait(barrier, shards_n + jnp.where(inner, 2, 1))
+    pl.semaphore_wait(pltpu.get_barrier_semaphore(), shards_n + jnp.where(inner, 2, 1))
 
     loads, trades = [], []
     pieces = []
     for a in range(count):
-        rows = own[a].shape[0]
         if a < experts_n:
-            mine = pl.multiple_of(core * rows, rows)
-            rest = pl.multiple_of((1 - core) * rows, rows)
-            parts = PIECES
+            rows = own[a].shape[0]
+            size = rows // PIECES
+            views = [
+                (
+                    sources[a].at[pl.ds(pl.multiple_of(core * rows, rows) + j * size, size)],
+                    sources[a].at[pl.ds(pl.multiple_of((1 - core) * rows, rows) + j * size, size)],
+                    slice(j * size, (j + 1) * size),
+                )
+                for j in range(PIECES)
+            ]
         else:
-            mine, rest = 0, rows
-            parts = 1
-        size = rows // parts
-        for j in range(parts):
+            views = [(sources[a].at[:, core], sources[a].at[:, 1 - core], slice(0, shards_n))]
+        for mine, rest, spot in views:
             i = len(loads)
-            place = slice(j * size, (j + 1) * size)
-            loads.append(
-                pltpu.make_async_copy(
-                    sources[a].at[pl.ds(mine + j * size, size)], own[a].at[place], load_sem.at[i]
-                )
-            )
-            trades.append(
-                send(
-                    sources[a].at[pl.ds(rest + j * size, size)], other[a].at[place], core_sem, i, partner
-                )
-            )
+            loads.append(pltpu.make_async_copy(mine, own[a].at[spot], load_sem.at[i]))
+            trades.append(send(rest, other[a].at[spot], core_sem, i, partner))
         total = near[a].shape[0]
         parts = PIECES if a < experts_n else DENSE_PIECES
         size = total // parts
         for j in range(parts):
-            place = slice(j * size, (j + 1) * size)
+            spot = slice(j * size, (j + 1) * size)
             at = pl.multiple_of(core * total, total) + j * size
-            pieces.append(
-                Piece(own[a].at[place], near[a].at[place], far[a].at[place], outs[a], pl.ds(at, size))
-            )
+            start = own[a] if a < experts_n else crossed[a - experts_n]
+            pieces.append(Piece(start.at[spot], near[a].at[spot], far[a].at[spot], outs[a], pl.ds(at, size)))
     expert_pieces = experts_n * PIECES
     order = list(range(2)) + list(range(expert_pieces, expert_pieces + dense_n)) + list(range(2, expert_pieces))
     for i in order:
@@ -598,34 +802,28 @@
     def meet_expert(i):
         a, j = i // PIECES, i % PIECES
         size = own[a].shape[0] // PIECES
-        place = slice(j * size, (j + 1) * size)
+        spot = slice(j * size, (j + 1) * size)
         loads[i].wait()
         trades[i].wait_recv()
-        add_into(own[a].at[place], own[a].at[place], other[a].at[place])
+        add_into(own[a].at[spot], own[a].at[spot], other[a].at[spot])
 
     def meet_dense(d):
         a, i = experts_n + d, expert_pieces + d
         loads[i].wait()
         trades[i].wait_recv()
-        add_into(own[a], own[a], other[a])
-        size = own[a].shape[0] // shards_n
+        for b in range(shards_n):
+            add_into(own[a].at[b], own[a].at[b], other[a].at[b])
         for k in range(1, shards_n):
-            copy = send(
-                own[a].at[k * size : (k + 1) * size],
-                across[d].at[k - 1],
-                across_sem,
-                d * (shards_n - 1) + k - 1,
-                peer(k),
-            )
+            index = d * (shards_n - 1) + k - 1
+            copy = send(own[a].at[place.peer_index(k)], across[d].at[k - 1], across_sem, index, place.peer(k))
             copy.start()
             crossings.append(copy)
 
     def gather_dense(d):
-        a = experts_n + d
-        size = own[a].shape[0] // shards_n
         for k in range(1, shards_n):
             crossings[d * (shards_n - 1) + k - 1].wait_recv()
-        add_into(own[a].at[0:size], own[a].at[0:size], *[across[d].at[k - 1] for k in range(1, shards_n)])
+        arrived = [across[d].at[k - 1] for k in range(1, shards_n)]
+        add_into(crossed[d], own[experts_n + d].at[shard], *arrived)
 
     number = len(pieces)
     inward = [send(p.own, p.near, near_sem, i, inner_device) for i, p in enumerate(pieces)]
@@ -708,12 +906,15 @@
 
 
 def reduce_weights(expert_grads, dense_grads, shards_n):
-    arrays = list(expert_grads) + list(dense_grads)
     experts_n, dense_n = len(expert_grads), len(dense_grads)
+    columns = [g.shape[1] for g in (*expert_grads, *dense_grads)]
     out_rows = [g.shape[0] for g in expert_grads] + [g.shape[0] // shards_n for g in dense_grads]
-    half = lambda g: pltpu.VMEM((g.shape[0] // 2, g.shape[1]), bf16)
-    line = [pltpu.VMEM((r // 2, g.shape[1]), bf16) for r, g in zip(out_rows, arrays)]
-    across = [pltpu.VMEM((shards_n - 1, g.shape[0] // (2 * shards_n), g.shape[1]), bf16) for g in dense_grads]
+    halves = [pltpu.VMEM((g.shape[0] // 2, g.shape[1]), bf16) for g in expert_grads]
+    dense_grads = [g.reshape(shards_n, 2, g.shape[0] // (2 * shards_n), g.shape[1]) for g in dense_grads]
+    arrays = list(expert_grads) + dense_grads
+    halves += [pltpu.VMEM((g.shape[0],) + g.shape[2:], bf16) for g in dense_grads]
+    line = [pltpu.VMEM((r // 2, c), bf16) for r, c in zip(out_rows, columns)]
+    across = [pltpu.VMEM((shards_n - 1,) + g.shape[2:], bf16) for g in dense_grads]
     first = experts_n * PIECES + dense_n
     number = experts_n * PIECES + dense_n * DENSE_PIECES
     dma = pltpu.SemaphoreType.DMA
@@ -722,12 +923,8 @@
         functools.partial(reduce_kernel, experts_n, dense_n, shards_n),
         in_specs=[anywhere] * len(arrays),
         out_specs=[anywhere] * len(arrays),
-        out_shape=[jax.ShapeDtypeStruct((r, g.shape[1]), bf16) for r, g in zip(out_rows, arrays)],
-        scratch_shapes=[half(g) for g in arrays]
-        + [half(g) for g in arrays]
-        + across
-        + line
-        + line
+        out_shape=[jax.ShapeDtypeStruct((r, c), bf16) for r, c in zip(out_rows, columns)],
+        scratch_shapes=halves + halves + across + line[experts_n:] + line + line
         + [
             dma((first,)),
             dma((2, first)),
@@ -763,28 +960,33 @@
     rows = tokens.shape[2]
     length = rows * links.contexts
     held = expert_in.shape[0]
+    chained = links.chips == LINE and links.shards == SHARDS and held == 2
     positions = links.context * rows + jnp.arange(rows, dtype=jnp.int32)
     cosine, sine = rotation_tables(positions)
-    chips_back = (links.chip - jnp.arange(links.chips, dtype=jnp.int32) + links.chips) % links.chips
-    chunk_ids = jnp.concatenate([2 * chips_back + links.core, 2 * chips_back + 1 - links.core])
-    key_places = (chunk_ids[:, None] * rows + jnp.arange(rows, dtype=jnp.int32)[None, :]).reshape(length)
-
-    gains = lax.all_gather(jnp.stack([attn_gain, moe_gain]), "fsdp", axis=1, tiled=True).astype(f32)
-    gain_one, gain_two = links.to_relative(gains[0]), gains[1]
-
-    pair_weight = links.gather_rows(key_value_weight)
-    query_weight = links.gather_rows(w_q)
-    output_weight = links.gather_rows(w_o)
-
+    key_places = jnp.arange(length, dtype=jnp.int32)
+    width = w_q.shape[0]
     flat_tokens = tokens.reshape(MB * rows, MODEL_WIDTH)
-    relative = links.to_relative(flat_tokens).astype(f32)
-    scale_one = lax.rsqrt(jnp.mean(relative * relative, axis=-1, keepdims=True) + eps)
-    unit_one = relative * scale_one
-    normed = (unit_one * gain_one).astype(bf16)
-    pairs = rotate_pairs(
-        dot(normed, pair_weight), jnp.concatenate([cosine] * MB), jnp.concatenate([sine] * MB)
-    )
-    query_pre = dot(normed, query_weight)
+    flat_values = flat_tokens.astype(f32)
+    scale_one = lax.rsqrt(jnp.mean(flat_values * flat_values, axis=-1, keepdims=True) + eps)
+    unit_one = flat_values * scale_one
+
+    if chained:
+        packed = jnp.pad(jnp.stack([attn_gain, moe_gain]), ((0, GAIN_ROWS - 2), (0, 0)))
+        normed, query, gains, pair_weight, query_weight, output_weight, pairs = project_all(
+            flat_tokens, cosine, sine, packed, key_value_weight, w_q, w_o, length
+        )
+        gains = gains.reshape(SHARDS, GAIN_ROWS, width).astype(f32)
+        gain_one, gain_two = gains[:, 0].reshape(MODEL_WIDTH), gains[:, 1].reshape(MODEL_WIDTH)
+    else:
+        gather = lambda w: lax.all_gather(w, "fsdp", axis=0, tiled=True)
+        pair_weight, query_weight, output_weight = gather(key_value_weight), gather(w_q), gather(w_o)
+        gain_one, gain_two = gather(attn_gain).astype(f32), gather(moe_gain).astype(f32)
+        normed = (unit_one * gain_one).astype(bf16)
+        both = lambda table: jnp.concatenate([table] * MB)
+        own_pairs = rotate_columns(dot(normed, pair_weight), both(cosine), both(sine), KEY_WIDTH)
+        query = rotate_columns(dot(normed, query_weight), both(cosine), both(sine), MODEL_WIDTH)
+        own_pairs = own_pairs.reshape(MB, rows, 2 * KEY_WIDTH)
+        pairs = lax.all_gather(own_pairs, "ctx", axis=1, tiled=True)
 
     expert_ids = jnp.arange(E, dtype=jnp.int32)
     chosen = (routes.reshape(MB, rows, TOP)[..., None] == expert_ids).astype(f32)
@@ -793,11 +995,8 @@
     combine = lax.dynamic_slice_in_dim(combine, links.shard * held, held, 2)
     combine = combine.transpose(0, 2, 1)[..., None]
 
-    all_pairs, biases, biases_turned = [], [], []
+    biases, biases_turned = [], []
     for m in range(MB):
-        own = pairs[m * rows : (m + 1) * rows]
-        near = jnp.concatenate([own] + [links.shift(own, s) for s in range(1, links.chips)], axis=0)
-        all_pairs.append(jnp.concatenate([near, links.other_core(near)], axis=0))
         starts = doc_starts[m, 0]
         begin = jnp.max(jnp.where(starts[None, :] <= positions[:, None], starts[None, :], 0), axis=1)
         seen = (key_places[None, :] <= positions[:, None]) & (key_places[None, :] >= begin[:, None])
@@ -810,8 +1009,7 @@
     outputs = []
     for m in range(MB):
         own = slice(m * rows, (m + 1) * rows)
-        attn = attention_forward(query_pre[own], cosine, sine, all_pairs[m], biases[m])
-        attn = links.to_relative(attn)
+        attn = attention_forward(m, query, pairs, biases[m])
         middle = flat_tokens[own].astype(f32) + dot(attn, output_weight)
         scale_two = lax.rsqrt(jnp.mean(middle * middle, axis=-1, keepdims=True) + eps)
         unit_two = middle * scale_two
@@ -845,53 +1043,51 @@
         inner = jnp.mean(weighted * unit_two, axis=-1, keepdims=True)
         middle_grad = cotangent[m, 0].astype(f32) + (weighted - unit_two * inner) * scale_two
         middle_low = middle_grad.astype(bf16)
-        attn_grad = links.to_absolute(dot(middle_low, output_weight, NT).astype(bf16))
+        attn_grad = dot(middle_low, output_weight, NT).astype(bf16)
         query_low, pair_grad = attention_backward(
-            query_pre[own], cosine, sine, all_pairs[m], biases_turned[m], attn_grad
+            m, query, cosine, sine, pairs, biases_turned[m], attn_grad
         )
-        near = links.chips * rows
-        part = pair_grad[:near].astype(f32) + links.other_core(pair_grad[near:]).astype(f32)
-        part = part.astype(bf16)
-        parts = [part[:rows]]
-        for s in range(1, links.chips):
-            parts.append(links.shift(part[s * rows : (s + 1) * rows], -s))
+        if chained:
+            pair_grad = pair_grad.reshape(links.chips, 2, rows, 2 * KEY_WIDTH)
+            core_part = lambda core: lax.dynamic_index_in_dim(pair_grad, core, 1, keepdims=False)
+            part = core_part(links.core).astype(f32)
+            part = (part + links.other_core(core_part(1 - links.core)).astype(f32)).astype(bf16)
+            chip_part = lambda s: lax.dynamic_index_in_dim(
+                part, (links.chip - s + links.chips) % links.chips, 0, keepdims=False
+            )
+            parts = [chip_part(0)]
+            for s in range(1, links.chips):
+                parts.append(links.shift(chip_part(s), -s))
+        else:
+            parts = [lax.psum_scatter(pair_grad, "ctx", scatter_dimension=0, tiled=True)]
         pair_low = pair_gradient(parts, cosine, sine)
         normed_grad = dot(query_low, query_weight, NT) + dot(pair_low, pair_weight, NT)
         gain_one_grad = gain_one_grad + jnp.sum(normed_grad * unit_one[own], axis=0)
         weighted = normed_grad * gain_one
         inner = jnp.mean(weighted * unit_one[own], axis=-1, keepdims=True)
         residual_grad = (weighted - unit_one[own] * inner) * scale_one[own]
-        input_grads.append(middle_grad + links.to_absolute(residual_grad))
+        input_grads.append(middle_grad + residual_grad)
         query_lows.append(query_low)
         pair_lows.append(pair_low)
         middle_lows.append(middle_low)
 
     join = lambda items: jnp.concatenate(items, axis=0)
-    width = w_q.shape[0]
 
     output_grad = dot(join([k[0] for k in kept]), join(middle_lows), TN).astype(bf16)
     query_grad = dot(normed, join(query_lows), TN).astype(bf16)
     pair_weight_grad = dot(normed, join(pair_lows), TN).astype(bf16)
-    gain_grads = jnp.stack([gain_one_grad, links.to_relative(gain_two_grad)], axis=1)
+    gain_grads = jnp.stack([gain_one_grad, gain_two_grad], axis=1)
     gain_grads = jnp.pad(gain_grads, ((0, 0), (0, LANES - 2))).astype(bf16)
     dense_grads = [output_grad, query_grad, jnp.concatenate([pair_weight_grad, gain_grads], axis=1)]
-    if links.chips == LINE and links.shards == 4 and held == 2:
+    if chained:
         totals = reduce_weights(expert_grads, dense_grads, links.shards)
-        gate_total, up_total, down_total, output_total, query_total, pair_total = [t.astype(f32) for t in totals]
-        expand_total = jnp.concatenate([gate_total, up_total], axis=1)
     else:
-        expand_total = jnp.zeros((held * MODEL_WIDTH, 2 * F), f32)
-        down_total = jnp.zeros((held * F, MODEL_WIDTH), f32)
-        sums = [links.sum_over_chips(links.core_halves(g)) for g in expert_grads]
-        expand_total = links.place_rows(sums[0], expand_total, 0)
-        expand_total = links.place_rows(sums[1], expand_total, F)
-        down_total = links.place_rows(sums[2], down_total, 0)
-        output_total, query_total, pair_total = [
-            links.place_rows(
-                links.sum_over_chips(links.scatter_rows(g)), jnp.zeros((width, g.shape[1]), f32), 0
-            )
-            for g in dense_grads
-        ]
+        totals = [lax.psum(g, "ctx") for g in expert_grads]
+        for g in dense_grads:
+            part = lax.psum_scatter(g, "fsdp", scatter_dimension=0, tiled=True)
+            totals.append(lax.psum(part, "ctx"))
+    gate_total, up_total, down_total, output_total, query_total, pair_total = [t.astype(f32) for t in totals]
+    expand_total = jnp.concatenate([gate_total, up_total], axis=1)
 
     return (
         jnp.stack(outputs)[:, None],

time: 675 us -> 597 us (0.88)
  Pallas kernels: 280 us -> 340 us
  starting transfers between devices: 89.5 us -> 45.6 us
  local copies, waits for them, and re-layouts: 54.4 us -> 22.6 us
  waiting for transfers between devices: 134 us -> 105 us
  other arithmetic: 60.6 us -> 40.8 us
  matrix products: 40 us -> 32 us
  blocking collectives: 7.08 us -> 0 us
    pallas_call x1, Pallas kernels: 2.55 us -> 66.5 us  [project_all(): pl.pallas_call(project_kernel, in_specs=[vmem] * 4 + [anywhere] * 3, out_...]
    ppermute x12 -> x6, starting transfers between devices: 42.2 us -> 13 us  [shift(): return lax.ppermute(array, 'ctx', [(i, (i + 2 * s) % n) for i in range(n)])]
    unnamed x231 -> x136, local copies, waits for them, and re-layouts: 28.9 us -> 2.54 us
    ppermute x36 -> x27, waiting for transfers between devices: 87.5 us -> 70.7 us  [across(): return lax.ppermute(array, 'fsdp', [(i, i ^ k) for i in range(self.shards)])]
    ppermute x36 -> x27, starting transfers between devices: 44.6 us -> 32 us  [across(): return lax.ppermute(array, 'fsdp', [(i, i ^ k) for i in range(self.shards)])]
    ppermute x12 -> x6, waiting for transfers between devices: 44.6 us -> 33.8 us  [shift(): return lax.ppermute(array, 'ctx', [(i, (i + 2 * s) % n) for i in range(n)])]
    select_n x22 -> x0, other arithmetic: 9.27 us -> none  [_swapped(): jnp.where(flag, pieces[1 - h][b], pieces[h][b])]
    slice x8 -> x1, local copies, waits for them, and re-layouts: 9.42 us -> 0.62 us  [shards(): gains[:, 0].reshape(MODEL_WIDTH)]
  transfers between devices with their start and end apart: 61 -> 35, of which waited for: 26 -> 17; matrix products, arithmetic and copies ran while one was open for 13% -> 7% of each run, Pallas kernels for 9% -> 8%
where the time goes in v3:
time: 597 us; the launch traced here: 588 us
  Pallas kernels  340 us (57%)
  waiting for transfers between devices  105 us (18%)
  starting transfers between devices  45.6 us (8%)
  other arithmetic  40.8 us (7%)
  matrix products  32 us (5%)
  local copies, waits for them, and re-layouts  22.6 us (4%)
    pallas_call x1, Pallas kernels, reduce_weights(): pl.pallas_call(functools.partial(reduce_kernel, experts_n, dense_n, shard...  165 us
    ppermute x27, waiting for transfers between devices, across(): return lax.ppermute(array, 'fsdp', [(i, i ^ k) for i in range(self.shards)])  70.7 us
    pallas_call x1, Pallas kernels, project_all(): pl.pallas_call(project_kernel, in_specs=[vmem] * 4 + [anywhere] * 3, out_...  66.5 us
    pallas_call x2, Pallas kernels, attention_backward(): pl.pallas_call(attention_backward_kernel, grid=(PAIRS,), in_specs=[pl.Blo...  34.7 us
    pallas_call x2, Pallas kernels, experts(): pl.pallas_call(functools.partial(experts_kernel, parts, rows, held * bloc...  34.4 us
    ppermute x6, waiting for transfers between devices, shift(): return lax.ppermute(array, 'ctx', [(i, (i + 2 * s) % n) for i in range(n)])  33.8 us
    dot_general x11, matrix products, dot(): return lax.dot_general(left, right, dims, preferred_element_type=f32)  32 us
    ppermute x27, starting transfers between devices, across(): return lax.ppermute(array, 'fsdp', [(i, i ^ k) for i in range(self.shards)])  32 us
  transfers between devices with their start and end apart: 35, of which 17 were waited for; matrix products, arithmetic and copies ran while one was open for 7% of the time, Pallas kernels for 8%

profile of v3, /device:TPU:0, one launch (start us, length us, event | category | flops | bytes accessed | tf_op | source)
XLA Modules:
  0.0 587.7 jit_solution(7553772648149865535)
XLA Ops:
  7.0 66.5 %project.1 = (bf16[256,1536]{1,0:T(8,128)(2,1)}, bf16[256,1536]{1,0:T(8,128)(2,1)}, bf16[64,384]{1,0:T(8,128)(2,1)}, bf16[1536,1024]{1,0:T(8,128)(2,1)}, bf16[15...) custom-call(bf16[256,1536]{1,0:T(8,128)(2,1)} %bitcast.128, ...), custom_call_target="tpu_custom_call" | custom-call | tf_op jit(solution)/shard_map/project/pallas_call | solution.py:675
  73.4 9.3 %attention_forward.2 = bf16[128,1536]{1,0:T(8,128)(2,1)} custom-call(bf16[256,1536]{1,0:T(8,128)(2,1)} %get-tuple-element.51.query_ref, bf16[2,1024,1024]{2,1,0:T(8,128)(2,1)} %get-tuple-element.52.key_ref.value_ref, bf16[2,1024,1024]{2,1,0:T(8,128)(2,1)} %get-tuple-element.52.key_ref.value_ref, f32[128,1024]{1,0:T(8,128)} %get-tuple-element.188.bias_ref), custom_call_target="tpu_custom_call" | custom-call | flops 3221225472 | bytes 6291456 | tf_op jit(solution)/shard_map/attention_forward/pallas_call | solution.py:151
  82.8 3.4 multiply_reduce_fusion.10
  103.8 9.2 %attention_forward.3 = bf16[128,1536]{1,0:T(8,128)(2,1)} custom-call(bf16[256,1536]{1,0:T(8,128)(2,1)} %get-tuple-element.51.query_ref, bf16[2,1024,1024]{2,1,0:T(8,128)(2,1)} %get-tuple-element.52.key_ref.value_ref, bf16[2,1024,1024]{2,1,0:T(8,128)(2,1)} %get-tuple-element.52.key_ref.value_ref, f32[128,1024]{1,0:T(8,128)} %get-tuple-element.189.bias_ref), custom_call_target="tpu_custom_call" | custom-call | flops 3221225472 | bytes 6291456 | tf_op jit(solution)/shard_map/attention_forward/pallas_call | solution.py:151
  114.7 4.1 collective-permute-done.6.refs_5_.refs_9_
  119.5 6.3 %collective-permute-done.8.refs_7_.refs_11_ = bf16[128,1536]{1,0:T(8,128)(2,1)} collective-permute-done((bf16[128,1536]{1,0:T(8,128)(2,1)S(1)}, bf16[128,1536]{1,0:T(8,128)(2,1)}, u32[]{:S(2)}, u32[]{:S(2)}) %collective-permute-start.8) | collective-permute-done | bytes 393248 | tf_op jit(solution)/shard_map/ppermute | solution.py:380
  125.8 17.4 %experts.2 = (bf16[128,1536]{1,0:T(8,128)(2,1)}, bf16[128,1536]{1,0:T(8,128)(2,1)}, bf16[128,1536]{1,0:T(8,128)(2,1)}, bf16[128,1536]{1,0:T(8,128)(2,1)}, bf16[1...) custom-call(f32[2,512,1]{2,1,0:T(8,128)} %copy.54.combine_ref, ...), custom_call_target="tpu_custom_call" | custom-call | flops 9663676416 | bytes 25165824 | tf_op jit(solution)/shard_map/experts/pallas_call | solution.py:288
  144.2 3.2 multiply_reduce_fusion.9
  153.1 12.6 %collective-permute-done.10 = bf16[128,1536]{1,0:T(8,128)(2,1)S(1)} collective-permute-done((bf16[128,1536]{1,0:T(8,128)(2,1)}, bf16[128,1536]{1,0:T(8,128)(2,1)S(1)}, u32[]{:S(2)}, u32[]{:S(2)}) %collective-permute-start.10) | collective-permute-done | bytes 393248 | tf_op jit(solution)/shard_map/ppermute | solution.py:380
  169.4 11.6 %collective-permute-done.22 = bf16[128,1536]{1,0:T(8,128)(2,1)S(1)} collective-permute-done((bf16[128,1536]{1,0:T(8,128)(2,1)S(1)}, bf16[128,1536]{1,0:T(8,128)(2,1)S(1)}, u32[]{:S(2)}, u32[]{:S(2)}) %collective-permute-start.22) | collective-permute-done | bytes 393248 | tf_op jit(solution)/shard_map/ppermute | solution.py:380
  189.9 4.2 collective-permute-done.15.refs_5_.refs_13_
  202.8 8.2 %collective-permute-done.12.refs_1_.refs_5_ = bf16[128,1536]{1,0:T(8,128)(2,1)} collective-permute-done((bf16[128,1536]{1,0:T(8,128)(2,1)}, bf16[128,1536]{1,0:T(8,128)(2,1)}, u32[]{:S(2)}, u32[]{:S(2)}) %collective-permute-start.12) | collective-permute-done | bytes 393248 | tf_op jit(solution)/shard_map/ppermute | solution.py:380
  211.0 5.5 collective-permute-done.14.refs_3_.refs_7_
  216.5 17.0 %experts.3 = (bf16[128,1536]{1,0:T(8,128)(2,1)}, bf16[128,1536]{1,0:T(8,128)(2,1)}, bf16[128,1536]{1,0:T(8,128)(2,1)}, bf16[128,1536]{1,0:T(8,128)(2,1)}, bf16[1...) custom-call(f32[2,512,1]{2,1,0:T(8,128)} %copy.55.combine_ref, ...), custom_call_target="tpu_custom_call" | custom-call | flops 9663676416 | bytes 25165824 | tf_op jit(solution)/shard_map/experts/pallas_call | solution.py:288
  239.9 6.0 %collective-permute-done.18 = bf16[128,1536]{1,0:T(8,128)(2,1)S(1)} collective-permute-done((bf16[128,1536]{1,0:T(8,128)(2,1)}, bf16[128,1536]{1,0:T(8,128)(2,1)S(1)}, u32[]{:S(2)}, u32[]{:S(2)}) %collective-permute-start.18) | collective-permute-done | bytes 393248 | tf_op jit(solution)/shard_map/ppermute | solution.py:380
  247.5 16.4 %expert_weights.1 = (bf16[2,1536,512]{2,1,0:T(8,128)(2,1)}, bf16[2,1536,512]{2,1,0:T(8,128)(2,1)}, bf16[2,512,1536]{2,1,0:T(8,128)(2,1)}) custom-call(bf16[128,1536]{1,0:T(8,128)(2,1)} %copy-done.36, bf16[128,1536]{1,0:T(8,128)(2,1)} %copy-done.58, bf16[128,1536]{1,0:T(8,128)(2,1)} %collective-permute-done.4.refs_2_, ...), custom_call_target="tpu_custom_call" | custom-call | flops 9663676416 | bytes 22020096 | tf_op jit(solution)/shard_map/expert_weights/pallas_call | solution.py:345
  264.0 4.6 collective-permute-done.29
  268.6 3.8 multiply_reduce_fusion.1
  272.4 3.1 fusion.40
  277.9 17.3 %attention_backward.2 = (bf16[128,1536]{1,0:T(8,128)(2,1)}, bf16[1024,1024]{1,0:T(8,128)(2,1)}) custom-call(bf16[256,1536]{1,0:T(8,128)(2,1)} %get-tuple-element.51.query_ref, f32[128,128]{1,0:T(8,128)} %pad_maximum_fusion.2.cosine_ref, f32[128,128]{1,0:T(8,128)} %pad_maximum_fusion.3.sine_ref, bf16[2,1024,1024]{2,1,0:T(8,128)(2,1)} %get-tuple-element.52.key_ref.value_ref, ...), custom_call_target="tpu_custom_call" | custom-call | flops 8053063680 | bytes 12582912 | tf_op jit(solution)/shard_map/attention_backward/pallas_call | solution.py:208
  296.6 4.7 convolution_convert_fusion.3.grad_ref
  301.3 17.5 %attention_backward.3 = (bf16[128,1536]{1,0:T(8,128)(2,1)}, bf16[1024,1024]{1,0:T(8,128)(2,1)}) custom-call(bf16[256,1536]{1,0:T(8,128)(2,1)} %get-tuple-element.51.query_ref, f32[128,128]{1,0:T(8,128)} %pad_maximum_fusion.2.cosine_ref, f32[128,128]{1,0:T(8,128)} %pad_maximum_fusion.3.sine_ref, bf16[2,1024,1024]{2,1,0:T(8,128)(2,1)} %get-tuple-element.52.key_ref.value_ref, ...), custom_call_target="tpu_custom_call" | custom-call | flops 8053063680 | bytes 12582912 | tf_op jit(solution)/shard_map/attention_backward/pallas_call | solution.py:208
  320.6 4.0 fusion.42
  324.6 3.6 convolution_convert_fusion
  328.3 3.6 convolution_convert_fusion.1
  336.2 4.9 collective-permute-start.25
  351.9 15.2 %collective-permute-done.26.refs_2_ = bf16[128,1024]{1,0:T(8,128)(2,1)S(1)} collective-permute-done((bf16[128,1024]{1,0:T(8,128)(2,1)S(1)}, bf16[128,1024]{1,0:T(8,128)(2,1)S(1)}, u32[]{:S(2)}, u32[]{:S(2)}) %collective-permute-start.26) | collective-permute-done | bytes 262176 | tf_op jit(solution)/shard_map/ppermute | solution.py:387
  370.3 18.0 %collective-permute-done.33.refs_2_ = bf16[128,1024]{1,0:T(8,128)(2,1)} collective-permute-done((bf16[128,1024]{1,0:T(8,128)(2,1)S(1)}, bf16[128,1024]{1,0:T(8,128)(2,1)}, u32[]{:S(2)}, u32[]{:S(2)}) %collective-permute-start.33) | collective-permute-done | bytes 262176 | tf_op jit(solution)/shard_map/ppermute | solution.py:387
  396.6 3.8 copy.58
  400.4 165.2 %reduce_weights.1 = (bf16[3072,512]{1,0:T(8,128)(2,1)}, bf16[3072,512]{1,0:T(8,128)(2,1)}, bf16[1024,1536]{1,0:T(8,128)(2,1)}, bf16[384,1536]{1,0:T(8,128)(2,1)}...) custom-call(bf16[3072,512]{1,0:T(8,128)(2,1)} %bitcast.131, bf16[3072,512]{1,0:T(8,128)(2,1)} %bitcast.132, ...), custom_call_target="tpu_custom_call" | custom-call | tf_op jit(solution)/shard_map/reduce_weights/pallas_call | solution.py:922
  571.2 6.4 %convert.25 = f32[2,1536,1024]{2,1,0:T(8,128)} convert(bf16[2,1536,1024]{2,1,0:T(8,128)(2,1)S(1)} %bitcast.124) | non-fusion elementwise | flops 3145728 | bytes 18874368 | tf_op jit(solution)/shard_map/reshape | solution.py:1100
  577.6 3.6 convert.26
  (261 shorter events, 105.7 us)
Async XLA Ops:
  87.0 14.6 %collective-permute-start.3 = (bf16[128,1536]{1,0:T(8,128)(2,1)S(1)}, bf16[128,1536]{1,0:T(8,128)(2,1)S(1)}, u32[]{:S(2)}, u32[]{:S(2)}) collective-permute-start(bf16[128,1536]{1,0:T(8,128)(2,1)S(1)} %multiply_convert_fusion.1.refs_0_), channel_id=1, source_target_pairs={{0,8},{8,0},{16,24},{24,16},{1,9},{9,1},{17,25},{25,17},{2,10},{10... | collective-permute-start | bytes 1179656 | tf_op jit(solution)/shard_map/ppermute | solution.py:380
  87.7 27.0 %collective-permute-start.4 = (bf16[128,1536]{1,0:T(8,128)(2,1)S(1)}, bf16[128,1536]{1,0:T(8,128)(2,1)}, u32[]{:S(2)}, u32[]{:S(2)}) collective-permute-start(bf16[128,1536]{1,0:T(8,128)(2,1)S(1)} %multiply_convert_fusion.1.refs_0_), channel_id=1, source_target_pairs={{0,16},{8,24},{16,0},{24,8},{1,17},{9,25},{17,1},{25,9},{2,18},{10... | collective-permute-start | bytes 1179656 | tf_op jit(solution)/shard_map/ppermute | solution.py:380
  98.1 16.7 %collective-permute-start.5 = (bf16[128,1536]{1,0:T(8,128)(2,1)S(1)}, bf16[128,1536]{1,0:T(8,128)(2,1)}, u32[]{:S(2)}, u32[]{:S(2)}) collective-permute-start(bf16[128,1536]{1,0:T(8,128)(2,1)S(1)} %multiply_convert_fusion.1.refs_0_), channel_id=1, source_target_pairs={{0,24},{8,16},{16,8},{24,0},{1,25},{9,17},{17,9},{25,1},{2,26},{10... | collective-permute-start | bytes 1179656 | tf_op jit(solution)/shard_map/ppermute | solution.py:380
  99.6 19.2 %collective-permute-start.6 = (bf16[128,1536]{1,0:T(8,128)(2,1)S(1)}, bf16[128,1536]{1,0:T(8,128)(2,1)}, u32[]{:S(2)}, u32[]{:S(2)}) collective-permute-start(bf16[128,1536]{1,0:T(8,128)(2,1)S(1)} %get-tuple-element.172.refs_4_.refs_8_), channel_id=1, source_target_pairs={{0,8},{8,0},{16,24},{24,16},{1,9},{9,1},{17,25},{25,17},{2,10},{10... | collective-permute-start | bytes 1179656 | tf_op jit(solution)/shard_map/ppermute | solution.py:380
  100.2 19.3 %collective-permute-start.7 = (bf16[128,1536]{1,0:T(8,128)(2,1)S(1)}, bf16[128,1536]{1,0:T(8,128)(2,1)}, u32[]{:S(2)}, u32[]{:S(2)}) collective-permute-start(bf16[128,1536]{1,0:T(8,128)(2,1)S(1)} %get-tuple-element.172.refs_4_.refs_8_), channel_id=1, source_target_pairs={{0,16},{8,24},{16,0},{24,8},{1,17},{9,25},{17,1},{25,9},{2,18},{10... | collective-permute-start | bytes 1179656 | tf_op jit(solution)/shard_map/ppermute | solution.py:380
  102.3 23.5 %collective-permute-start.8 = (bf16[128,1536]{1,0:T(8,128)(2,1)S(1)}, bf16[128,1536]{1,0:T(8,128)(2,1)}, u32[]{:S(2)}, u32[]{:S(2)}) collective-permute-start(bf16[128,1536]{1,0:T(8,128)(2,1)S(1)} %get-tuple-element.172.refs_4_.refs_8_), channel_id=1, source_target_pairs={{0,24},{8,16},{16,8},{24,0},{1,25},{9,17},{17,9},{25,1},{2,26},{10... | collective-permute-start | bytes 1179656 | tf_op jit(solution)/shard_map/ppermute | solution.py:380
  143.4 22.3 %collective-permute-start.10 = (bf16[128,1536]{1,0:T(8,128)(2,1)}, bf16[128,1536]{1,0:T(8,128)(2,1)S(1)}, u32[]{:S(2)}, u32[]{:S(2)}) collective-permute-start(bf16[128,1536]{1,0:T(8,128)(2,1)} %get-tuple-element.57), channel_id=1, source_target_pairs={{0,16},{8,24},{16,0},{24,8},{1,17},{9,25},{17,1},{25,9},{2,18},{10... | collective-permute-start | bytes 1179656 | tf_op jit(solution)/shard_map/ppermute | solution.py:380
  147.4 19.3 %collective-permute-start.11 = (bf16[128,1536]{1,0:T(8,128)(2,1)S(1)}, bf16[128,1536]{1,0:T(8,128)(2,1)S(1)}, u32[]{:S(2)}, u32[]{:S(2)}) collective-permute-start(bf16[128,1536]{1,0:T(8,128)(2,1)S(1)} %copy-done.63), channel_id=1, source_target_pairs={{0,24},{8,16},{16,8},{24,0},{1,25},{9,17},{17,9},{25,1},{2,26},{10... | collective-permute-start | bytes 1179656 | tf_op jit(solution)/shard_map/ppermute | solution.py:380
  149.6 19.1 %collective-permute-start.21 = (bf16[128,1536]{1,0:T(8,128)(2,1)S(1)}, bf16[128,1536]{1,0:T(8,128)(2,1)S(1)}, u32[]{:S(2)}, u32[]{:S(2)}) collective-permute-start(bf16[128,1536]{1,0:T(8,128)(2,1)S(1)} %copy-done.62), channel_id=1, source_target_pairs={{0,8},{8,0},{16,24},{24,16},{1,9},{9,1},{17,25},{25,17},{2,10},{10... | collective-permute-start | bytes 1179656 | tf_op jit(solution)/shard_map/ppermute | solution.py:380
  150.8 30.2 %collective-permute-start.22 = (bf16[128,1536]{1,0:T(8,128)(2,1)S(1)}, bf16[128,1536]{1,0:T(8,128)(2,1)S(1)}, u32[]{:S(2)}, u32[]{:S(2)}) collective-permute-start(bf16[128,1536]{1,0:T(8,128)(2,1)S(1)} %copy-done.61), channel_id=1, source_target_pairs={{0,16},{8,24},{16,0},{24,8},{1,17},{9,25},{17,1},{25,9},{2,18},{10... | collective-permute-start | bytes 1179656 | tf_op jit(solution)/shard_map/ppermute | solution.py:380
  151.6 31.0 %collective-permute-start.23 = (bf16[128,1536]{1,0:T(8,128)(2,1)S(1)}, bf16[128,1536]{1,0:T(8,128)(2,1)S(1)}, u32[]{:S(2)}, u32[]{:S(2)}) collective-permute-start(bf16[128,1536]{1,0:T(8,128)(2,1)S(1)} %copy-done.60), channel_id=1, source_target_pairs={{0,24},{8,16},{16,8},{24,0},{1,25},{9,17},{17,9},{25,1},{2,26},{10... | collective-permute-start | bytes 1179656 | tf_op jit(solution)/shard_map/ppermute | solution.py:380
  165.7 19.9 %collective-permute-start.9 = (bf16[128,1536]{1,0:T(8,128)(2,1)S(1)}, bf16[128,1536]{1,0:T(8,128)(2,1)S(1)}, u32[]{:S(2)}, u32[]{:S(2)}) collective-permute-start(bf16[128,1536]{1,0:T(8,128)(2,1)S(1)} %copy-done.59), channel_id=1, source_target_pairs={{0,8},{8,0},{16,24},{24,16},{1,9},{9,1},{17,25},{25,17},{2,10},{10... | collective-permute-start | bytes 1179656 | tf_op jit(solution)/shard_map/ppermute | solution.py:380
  166.7 27.4 %collective-permute-start.15 = (bf16[128,1536]{1,0:T(8,128)(2,1)}, bf16[128,1536]{1,0:T(8,128)(2,1)}, u32[]{:S(2)}, u32[]{:S(2)}) collective-permute-start(bf16[128,1536]{1,0:T(8,128)(2,1)} %get-tuple-element.173.refs_4_.refs_12_), channel_id=1, source_target_pairs={{0,8},{8,0},{16,24},{24,16},{1,9},{9,1},{17,25},{25,17},{2,10},{10... | collective-permute-start | bytes 1179656 | tf_op jit(solution)/shard_map/ppermute | solution.py:380
  168.7 33.1 %collective-permute-start.16 = (bf16[128,1536]{1,0:T(8,128)(2,1)}, bf16[128,1536]{1,0:T(8,128)(2,1)}, u32[]{:S(2)}, u32[]{:S(2)}) collective-permute-start(bf16[128,1536]{1,0:T(8,128)(2,1)} %get-tuple-element.173.refs_4_.refs_12_), channel_id=1, source_target_pairs={{0,16},{8,24},{16,0},{24,8},{1,17},{9,25},{17,1},{25,9},{2,18},{10... | collective-permute-start | bytes 1179656 | tf_op jit(solution)/shard_map/ppermute | solution.py:380
  181.0 21.8 %collective-permute-start.17 = (bf16[128,1536]{1,0:T(8,128)(2,1)}, bf16[128,1536]{1,0:T(8,128)(2,1)}, u32[]{:S(2)}, u32[]{:S(2)}) collective-permute-start(bf16[128,1536]{1,0:T(8,128)(2,1)} %get-tuple-element.173.refs_4_.refs_12_), channel_id=1, source_target_pairs={{0,24},{8,16},{16,8},{24,0},{1,25},{9,17},{17,9},{25,1},{2,26},{10... | collective-permute-start | bytes 1179656 | tf_op jit(solution)/shard_map/ppermute | solution.py:380
  187.8 23.2 %collective-permute-start.12 = (bf16[128,1536]{1,0:T(8,128)(2,1)}, bf16[128,1536]{1,0:T(8,128)(2,1)}, u32[]{:S(2)}, u32[]{:S(2)}) collective-permute-start(bf16[128,1536]{1,0:T(8,128)(2,1)} %get-tuple-element.174.refs_0_.refs_4_), channel_id=1, source_target_pairs={{0,8},{8,0},{16,24},{24,16},{1,9},{9,1},{17,25},{25,17},{2,10},{10... | collective-permute-start | bytes 1179656 | tf_op jit(solution)/shard_map/ppermute | solution.py:380
  188.6 22.4 %collective-permute-start.13 = (bf16[128,1536]{1,0:T(8,128)(2,1)}, bf16[128,1536]{1,0:T(8,128)(2,1)}, u32[]{:S(2)}, u32[]{:S(2)}) collective-permute-start(bf16[128,1536]{1,0:T(8,128)(2,1)} %get-tuple-element.174.refs_0_.refs_4_), channel_id=1, source_target_pairs={{0,16},{8,24},{16,0},{24,8},{1,17},{9,25},{17,1},{25,9},{2,18},{10... | collective-permute-start | bytes 1179656 | tf_op jit(solution)/shard_map/ppermute | solution.py:380
  194.1 22.4 %collective-permute-start.14 = (bf16[128,1536]{1,0:T(8,128)(2,1)}, bf16[128,1536]{1,0:T(8,128)(2,1)}, u32[]{:S(2)}, u32[]{:S(2)}) collective-permute-start(bf16[128,1536]{1,0:T(8,128)(2,1)} %get-tuple-element.174.refs_0_.refs_4_), channel_id=1, source_target_pairs={{0,24},{8,16},{16,8},{24,0},{1,25},{9,17},{17,9},{25,1},{2,26},{10... | collective-permute-start | bytes 1179656 | tf_op jit(solution)/shard_map/ppermute | solution.py:380
  233.5 12.3 %collective-permute-start.18 = (bf16[128,1536]{1,0:T(8,128)(2,1)}, bf16[128,1536]{1,0:T(8,128)(2,1)S(1)}, u32[]{:S(2)}, u32[]{:S(2)}) collective-permute-start(bf16[128,1536]{1,0:T(8,128)(2,1)} %get-tuple-element.60), channel_id=1, source_target_pairs={{0,8},{8,0},{16,24},{24,16},{1,9},{9,1},{17,25},{25,17},{2,10},{10... | collective-permute-start | bytes 1179656 | tf_op jit(solution)/shard_map/ppermute | solution.py:380
  235.4 28.5 %collective-permute-start.19 = (bf16[128,1536]{1,0:T(8,128)(2,1)}, bf16[128,1536]{1,0:T(8,128)(2,1)}, u32[]{:S(2)}, u32[]{:S(2)}) collective-permute-start(bf16[128,1536]{1,0:T(8,128)(2,1)} %get-tuple-element.61), channel_id=1, source_target_pairs={{0,16},{8,24},{16,0},{24,8},{1,17},{9,25},{17,1},{25,9},{2,18},{10... | collective-permute-start | bytes 1179656 | tf_op jit(solution)/shard_map/ppermute | solution.py:380
  236.4 27.6 %collective-permute-start.20 = (bf16[128,1536]{1,0:T(8,128)(2,1)}, bf16[128,1536]{1,0:T(8,128)(2,1)}, u32[]{:S(2)}, u32[]{:S(2)}) collective-permute-start(bf16[128,1536]{1,0:T(8,128)(2,1)} %get-tuple-element.62), channel_id=1, source_target_pairs={{0,24},{8,16},{16,8},{24,0},{1,25},{9,17},{17,9},{25,1},{2,26},{10... | collective-permute-start | bytes 1179656 | tf_op jit(solution)/shard_map/ppermute | solution.py:380
  237.7 26.3 %collective-permute-start.28 = (bf16[128,1536]{1,0:T(8,128)(2,1)}, bf16[128,1536]{1,0:T(8,128)(2,1)}, u32[]{:S(2)}, u32[]{:S(2)}) collective-permute-start(bf16[128,1536]{1,0:T(8,128)(2,1)} %get-tuple-element.72), channel_id=1, source_target_pairs={{0,8},{8,0},{16,24},{24,16},{1,9},{9,1},{17,25},{25,17},{2,10},{10... | collective-permute-start | bytes 1179656 | tf_op jit(solution)/shard_map/ppermute | solution.py:380
  238.9 29.7 %collective-permute-start.29 = (bf16[128,1536]{1,0:T(8,128)(2,1)}, bf16[128,1536]{1,0:T(8,128)(2,1)}, u32[]{:S(2)}, u32[]{:S(2)}) collective-permute-start(bf16[128,1536]{1,0:T(8,128)(2,1)} %get-tuple-element.73), channel_id=1, source_target_pairs={{0,16},{8,24},{16,0},{24,8},{1,17},{9,25},{17,1},{25,9},{2,18},{10... | collective-permute-start | bytes 1179656 | tf_op jit(solution)/shard_map/ppermute | solution.py:380
  245.8 22.7 %collective-permute-start.30 = (bf16[128,1536]{1,0:T(8,128)(2,1)}, bf16[128,1536]{1,0:T(8,128)(2,1)}, u32[]{:S(2)}, u32[]{:S(2)}) collective-permute-start(bf16[128,1536]{1,0:T(8,128)(2,1)} %get-tuple-element.74), channel_id=1, source_target_pairs={{0,24},{8,16},{16,8},{24,0},{1,25},{9,17},{17,9},{25,1},{2,26},{10... | collective-permute-start | bytes 1179656 | tf_op jit(solution)/shard_map/ppermute | solution.py:380
  296.5 37.1 %collective-permute-start.24 = (bf16[4,128,1024]{2,1,0:T(8,128)(2,1)S(1)}, bf16[4,128,1024]{2,1,0:T(8,128)(2,1)}, u32[]{:S(2)}, u32[]{:S(2)}) collective-permute-start(bf16[4,128,1024]{2,1,0:T(8,128)(2,1)S(1)} %dynamic-slice_bitcast_fusion.1), channel_id=1, source_target_pairs={{0,1},{1,0},{2,3},{3,2},{4,5},{5,4},{6,7},{7,6},{8,9},{9,8},{10,11... | collective-permute-start | bytes 3145736 | tf_op jit(solution)/shard_map/ppermute | solution.py:383
  320.1 24.0 %collective-permute-start.31 = (bf16[4,128,1024]{2,1,0:T(8,128)(2,1)S(1)}, bf16[4,128,1024]{2,1,0:T(8,128)(2,1)S(1)}, u32[]{:S(2)}, u32[]{:S(2)}) collective-permute-start(bf16[4,128,1024]{2,1,0:T(8,128)(2,1)S(1)} %dynamic-slice_bitcast_fusion), channel_id=1, source_target_pairs={{0,1},{1,0},{2,3},{3,2},{4,5},{5,4},{6,7},{7,6},{8,9},{9,8},{10,11... | collective-permute-start | bytes 3145736 | tf_op jit(solution)/shard_map/ppermute | solution.py:383
  336.2 12.0 %collective-permute-start.25 = (bf16[128,1024]{1,0:T(8,128)(2,1)S(1)}, bf16[128,1024]{1,0:T(8,128)(2,1)S(1)}, u32[]{:S(2)}, u32[]{:S(2)}) collective-permute-start(bf16[128,1024]{1,0:T(8,128)(2,1)S(1)} %get-tuple-element.162), channel_id=1, source_target_pairs={{0,6},{1,7},{2,0},{3,1},{4,2},{5,3},{6,4},{7,5},{8,14},{9,15},{10,... | collective-permute-start | bytes 786440 | tf_op jit(solution)/shard_map/ppermute | solution.py:387
  341.1 26.1 %collective-permute-start.26 = (bf16[128,1024]{1,0:T(8,128)(2,1)S(1)}, bf16[128,1024]{1,0:T(8,128)(2,1)S(1)}, u32[]{:S(2)}, u32[]{:S(2)}) collective-permute-start(bf16[128,1024]{1,0:T(8,128)(2,1)S(1)} %get-tuple-element.161), channel_id=1, source_target_pairs={{0,4},{1,5},{2,6},{3,7},{4,0},{5,1},{6,2},{7,3},{8,12},{9,13},{10,... | collective-permute-start | bytes 786440 | tf_op jit(solution)/shard_map/ppermute | solution.py:387
  342.5 24.7 %collective-permute-start.27 = (bf16[128,1024]{1,0:T(8,128)(2,1)S(1)}, bf16[128,1024]{1,0:T(8,128)(2,1)S(1)}, u32[]{:S(2)}, u32[]{:S(2)}) collective-permute-start(bf16[128,1024]{1,0:T(8,128)(2,1)S(1)} %get-tuple-element.160), channel_id=1, source_target_pairs={{0,2},{1,3},{2,4},{3,5},{4,6},{5,7},{6,0},{7,1},{8,10},{9,11},{10,... | collective-permute-start | bytes 786440 | tf_op jit(solution)/shard_map/ppermute | solution.py:387
  345.3 25.0 %collective-permute-start.32 = (bf16[128,1024]{1,0:T(8,128)(2,1)S(1)}, bf16[128,1024]{1,0:T(8,128)(2,1)}, u32[]{:S(2)}, u32[]{:S(2)}) collective-permute-start(bf16[128,1024]{1,0:T(8,128)(2,1)S(1)} %get-tuple-element.166), channel_id=1, source_target_pairs={{0,6},{1,7},{2,0},{3,1},{4,2},{5,3},{6,4},{7,5},{8,14},{9,15},{10,... | collective-permute-start | bytes 786440 | tf_op jit(solution)/shard_map/ppermute | solution.py:387
  347.6 40.7 %collective-permute-start.33 = (bf16[128,1024]{1,0:T(8,128)(2,1)S(1)}, bf16[128,1024]{1,0:T(8,128)(2,1)}, u32[]{:S(2)}, u32[]{:S(2)}) collective-permute-start(bf16[128,1024]{1,0:T(8,128)(2,1)S(1)} %get-tuple-element.165), channel_id=1, source_target_pairs={{0,4},{1,5},{2,6},{3,7},{4,0},{5,1},{6,2},{7,3},{8,12},{9,13},{10,... | collective-permute-start | bytes 786440 | tf_op jit(solution)/shard_map/ppermute | solution.py:387
  348.2 40.1 %collective-permute-start.34 = (bf16[128,1024]{1,0:T(8,128)(2,1)S(1)}, bf16[128,1024]{1,0:T(8,128)(2,1)}, u32[]{:S(2)}, u32[]{:S(2)}) collective-permute-start(bf16[128,1024]{1,0:T(8,128)(2,1)S(1)} %get-tuple-element.164), channel_id=1, source_target_pairs={{0,2},{1,3},{2,4},{3,5},{4,6},{5,7},{6,0},{7,1},{8,10},{9,11},{10,... | collective-permute-start | bytes 786440 | tf_op jit(solution)/shard_map/ppermute | solution.py:387
  (71 other events, 777.9 us)

commit v4 on v3

--- a/solution.py
+++ b/solution.py
@@ -127,11 +127,8 @@
     return [query_ref[:, i * LANES : (i + 1) * LANES].astype(f32) * scale for i in range(GROUP)]
 
 
-def attention_forward_kernel(query_ref, key_ref, value_ref, bias_ref, out_ref):
-    rows = query_ref.shape[0]
-    tiles = query_tiles(query_ref)
-    key, value = key_ref[...], value_ref[...]
-    bias = bias_ref[...]
+def attention_pair(tiles, key, value, bias):
+    rows = bias.shape[0]
     results = []
     for half in range(2):
         scores = dot(grouped(tiles, half), key, NT)
@@ -142,7 +139,12 @@
         weights = jnp.exp(scores - peak)
         total = jnp.sum(weights, axis=1, keepdims=True)
         results.append(dot(weights.astype(bf16), value) / total)
-    for i, tile in enumerate(ungrouped(results, rows)):
+    return ungrouped(results, rows)
+
+
+def attention_forward_kernel(query_ref, key_ref, value_ref, bias_ref, out_ref):
+    tiles = attention_pair(query_tiles(query_ref), key_ref[...], value_ref[...], bias_ref[...])
+    for i, tile in enumerate(tiles):
         out_ref[:, i * LANES : (i + 1) * LANES] = tile.astype(bf16)
 
 
@@ -235,6 +237,20 @@
     )(query, cosine, sine, pairs, pairs, bias, grad)
 
 
+def expert_block(inputs, out_grad, combine, gate_weight, up_weight, down_weight):
+    gate = dot(inputs, gate_weight)
+    up = dot(inputs, up_weight)
+    sigmoid = jax.nn.sigmoid(gate)
+    silu = gate * sigmoid
+    active = (silu * up * combine).astype(bf16)
+    active_grad = dot(out_grad, down_weight, NT) * combine
+    gate_grad = (active_grad * up * sigmoid * (1.0 + gate * (1.0 - sigmoid))).astype(bf16)
+    up_grad = (active_grad * silu).astype(bf16)
+    result = dot(active, down_weight)
+    row_grad = dot(gate_grad, gate_weight, NT) + dot(up_grad, up_weight, NT)
+    return active, gate_grad, up_grad, result, row_grad
+
+
 def experts_kernel(parts, rows, steps, combine_ref, gate_ref, up_ref, down_ref, *refs):
     rows_in, grads_in = refs[:parts], refs[parts : 2 * parts]
     refs = refs[2 * parts :]
@@ -252,20 +268,14 @@
         grad_sum[...] = jnp.zeros_like(grad_sum)
 
     inputs, out_grad, combine = rows_all[...], grads_all[...], combine_ref[0]
-    gate_weight, up_weight, down_weight = gate_ref[0], up_ref[0], down_ref[0]
-    gate = dot(inputs, gate_weight)
-    up = dot(inputs, up_weight)
-    sigmoid = jax.nn.sigmoid(gate)
-    silu = gate * sigmoid
-    active = (silu * up * combine).astype(bf16)
-    active_grad = dot(out_grad, down_weight, NT) * combine
-    gate_grad = (active_grad * up * sigmoid * (1.0 + gate * (1.0 - sigmoid))).astype(bf16)
-    up_grad = (active_grad * silu).astype(bf16)
+    active, gate_grad, up_grad, result, row_grad = expert_block(
+        inputs, out_grad, combine, gate_ref[0], up_ref[0], down_ref[0]
+    )
     active_out[...] = active
     gate_out[...] = gate_grad
     up_out[...] = up_grad
-    result_sum[...] += dot(active, down_weight)
-    grad_sum[...] += dot(gate_grad, gate_weight, NT) + dot(up_grad, up_weight, NT)
+    result_sum[...] += result
+    grad_sum[...] += row_grad
 
     @pl.when(step == steps - 1)
     def _():
@@ -314,56 +324,43 @@
     return out[:parts], out[parts : 2 * parts], out[2 * parts :]
 
 
-def expert_weights_kernel(parts, rows, *refs):
-    row_refs, grad_refs = refs[: MB * parts], refs[MB * parts : 2 * MB * parts]
-    refs = refs[2 * MB * parts :]
-    active_refs, gate_refs, up_refs = refs[:MB], refs[MB : 2 * MB], refs[2 * MB : 3 * MB]
-    gate_out, up_out, down_out, turned, grads_all = refs[3 * MB :]
+def expert_weights_kernel(rows_ref, grads_ref, active_ref, gate_ref, up_ref, gate_out, up_out, down_out, turned):
     step = pl.program_id(0) * pl.num_programs(1) + pl.program_id(1)
 
     @pl.when(step == 0)
     def _():
-        for k in range(MB * parts):
-            place = slice(k * rows, (k + 1) * rows)
-            turned[:, place] = row_refs[k][...].T
-            grads_all[place] = grad_refs[k][...]
-
-    join = lambda items: jnp.concatenate([item[...] for item in items], axis=0)
-    gate_out[0] = dot(turned[...], join(gate_refs)).astype(bf16)
-    up_out[0] = dot(turned[...], join(up_refs)).astype(bf16)
-    down_out[0] = dot(join(active_refs), grads_all[...], TN).astype(bf16)
-
-
-def expert_weights(row_parts, grad_parts, pieces, held):
-    rows = row_parts[0].shape[0]
-    parts = len(row_parts) // MB
-    tokens = parts * rows
+        turned[...] = rows_ref[...].T
+
+    gate_out[0] = dot(turned[...], gate_ref[...]).astype(bf16)
+    up_out[0] = dot(turned[...], up_ref[...]).astype(bf16)
+    down_out[0] = dot(active_ref[...], grads_ref[...], TN).astype(bf16)
+
+
+def expert_weights(rows, grads, active, gate, up, held):
+    tokens = rows.shape[0]
     blocks = F // F_BLOCK
-    whole = pl.BlockSpec((rows, MODEL_WIDTH), lambda e, b: (0, 0))
+    whole = pl.BlockSpec((tokens, MODEL_WIDTH), lambda e, b: (0, 0))
     piece = pl.BlockSpec((tokens, F_BLOCK), lambda e, b: (0, e * blocks + b))
     wide = pl.BlockSpec((1, MODEL_WIDTH, F_BLOCK), lambda e, b: (e, 0, b))
     return pl.pallas_call(
-        functools.partial(expert_weights_kernel, parts, rows),
+        expert_weights_kernel,
         grid=(held, blocks),
-        in_specs=[whole] * (2 * MB * parts) + [piece] * (3 * MB),
+        in_specs=[whole] * 2 + [piece] * 3,
         out_specs=[wide, wide, pl.BlockSpec((1, F_BLOCK, MODEL_WIDTH), lambda e, b: (e, b, 0))],
         out_shape=[
             jax.ShapeDtypeStruct((held, MODEL_WIDTH, F), bf16),
             jax.ShapeDtypeStruct((held, MODEL_WIDTH, F), bf16),
             jax.ShapeDtypeStruct((held, F, MODEL_WIDTH), bf16),
         ],
-        scratch_shapes=[
-            pltpu.VMEM((MODEL_WIDTH, MB * tokens), bf16),
-            pltpu.VMEM((MB * tokens, MODEL_WIDTH), bf16),
-        ],
+        scratch_shapes=[pltpu.VMEM((MODEL_WIDTH, tokens), bf16)],
         compiler_params=pltpu.CompilerParams(vmem_limit_bytes=VMEM_LIMIT),
         cost_estimate=pl.CostEstimate(
-            flops=6 * MB * tokens * held * MODEL_WIDTH * F,
-            bytes_accessed=6 * held * MODEL_WIDTH * F + 8 * MB * tokens * MODEL_WIDTH,
+            flops=6 * tokens * held * MODEL_WIDTH * F,
+            bytes_accessed=6 * held * MODEL_WIDTH * F + 8 * tokens * MODEL_WIDTH,
             transcendentals=0,
         ),
         name="expert_weights",
-    )(*row_parts, *grad_parts, *[pieces[m][i] for i in range(3) for m in range(MB)])
+    )(rows, grads, active, gate, up)
 
 
 class Links:
@@ -427,14 +424,55 @@
 GAIN_ROWS = 16
 
 
+class Square:
+    def __init__(self, place, blocks, direct_sem, relay_sem, base=0):
+        half = blocks.shape[1] // 2
+        own = blocks.at[place.shard]
+        self.directs = [remote(own, own, direct_sem, base + k - 1, place.peer(k)) for k in (1, 2)]
+        self.relays = []
+        for k in (1, 2):
+            spot = blocks.at[place.peer_index(k), (k - 1) * half : k * half]
+            self.relays.append(remote(spot, spot, relay_sem, base + k - 1, place.peer(3 - k)))
+
+    def start(self):
+        for copy in self.directs:
+            copy.start()
+
+    def pass_on(self):
+        for direct, relay in zip(self.directs, self.relays):
+            direct.wait_recv()
+            relay.start()
+
+    def finish(self):
+        for copy in self.relays:
+            copy.wait_recv()
+
+    def drain(self):
+        for copy in self.directs + self.relays:
+            copy.wait_send()
+
+
 def project_kernel(
-    tokens_ref, cosine_ref, sine_ref, gain_ref, pair_src, query_src, output_src, *refs
+    tokens_ref, cosine_ref, sine_ref, gain_ref, combine_ref, grad_ref, pair_src, query_src, output_src, *refs
 ):
-    outs, refs = refs[:6], refs[6:]
-    normed_out, query_out, gains, pair_out, query_weight_out, output_weight_out = outs[0], outs[1], outs[2], *outs[3:6]
-    pairs_out = refs[0]
-    weights, own_pairs = refs[1:4], refs[4]
-    load_sem, store_sem, gain_sem, direct_sem, relay_sem, pass_sem, right_sem, left_sem, core_sem, own_sem = refs[5:]
+    normed_out, query_out, gains, combine_out, grads_out = refs[:5]
+    pair_out, query_weight_out, output_weight_out, pairs_out = refs[5:9]
+    weights, own_pairs = refs[9:12], refs[12]
+    (
+        load_sem,
+        store_sem,
+        gain_sem,
+        combine_sem,
+        direct_sem,
+        relay_sem,
+        pass_sem,
+        right_sem,
+        left_sem,
+        core_sem,
+        own_sem,
+        square_direct_sem,
+        square_relay_sem,
+    ) = refs[13:]
     sources = (pair_src, query_src, output_src)
     weight_outs = (pair_out, query_weight_out, output_weight_out)
     place = Place()
@@ -467,6 +505,12 @@
     for k in range(1, SHARDS):
         target = gains.at[pl.ds(pl.multiple_of(shard * GAIN_ROWS, GAIN_ROWS), GAIN_ROWS)]
         gain_copies.append(remote(gain_ref, target, gain_sem, k - 1, place.peer(k)))
+    combine_out[shard] = combine_ref[...]
+    combine_copies = [
+        remote(combine_ref, combine_out.at[shard], combine_sem, k - 1, place.peer(k)) for k in range(1, SHARDS)
+    ]
+    grads_out[shard] = grad_ref[...]
+    square = Square(place, grads_out, square_direct_sem, square_relay_sem)
 
     loads, directs, relays, passes = [], [], [], []
     for w in range(3):
@@ -635,11 +679,19 @@
     lax.fori_loop(0, MODEL_WIDTH // (2 * LANES), query_block, 0)
     take_step(1, 2)
     relay_weight(2)
+    square.start()
+    for copy in combine_copies:
+        copy.start()
     take_step(0, 3)
+    pass_weight(2)
+    square.pass_on()
     take_step(1, 3)
-    pass_weight(2)
     settle_weight(2)
-
+    square.finish()
+
+    square.drain()
+    for copy in combine_copies:
+        copy.wait()
     for copy in gain_copies:
         copy.wait_send()
     for w in range(3):
@@ -664,7 +716,7 @@
 LANES_CHIP = LINE - 1
 
 
-def project_all(tokens, cosine, sine, gains, pair_weight, query_weight, output_weight, length):
+def project_all(tokens, cosine, sine, gains, combine, grads, pair_weight, query_weight, output_weight, length):
     held = pair_weight.shape[0]
     rows = cosine.shape[0]
     dma = pltpu.SemaphoreType.DMA
@@ -674,12 +726,14 @@
     full = [jax.ShapeDtypeStruct((SHARDS * held, w.shape[1]), bf16) for w in sources]
     return pl.pallas_call(
         project_kernel,
-        in_specs=[vmem] * 4 + [anywhere] * 3,
-        out_specs=[vmem] * 3 + [anywhere] * 4,
+        in_specs=[vmem] * 6 + [anywhere] * 3,
+        out_specs=[vmem] * 5 + [anywhere] * 4,
         out_shape=[
             jax.ShapeDtypeStruct(tokens.shape, bf16),
             jax.ShapeDtypeStruct((tokens.shape[0], query_weight.shape[1]), bf16),
             jax.ShapeDtypeStruct((SHARDS * GAIN_ROWS, held), bf16),
+            jax.ShapeDtypeStruct((SHARDS,) + combine.shape, f32),
+            jax.ShapeDtypeStruct((SHARDS,) + grads.shape, bf16),
         ]
         + full
         + [jax.ShapeDtypeStruct((MB, length, 2 * KEY_WIDTH), bf16)],
@@ -689,6 +743,7 @@
             dma((3,)),
             dma((3,)),
             dma((2, SHARDS - 1)),
+            dma((2, SHARDS - 1)),
             dma((2, 6)),
             dma((2, 6)),
             dma((2, 12)),
@@ -696,12 +751,228 @@
             dma((2, MB * (LINE - 1))),
             dma((2, 2 * MB * LINE)),
             dma((MB,)),
+            dma((2, 2)),
+            dma((2, 2)),
         ],
         compiler_params=pltpu.CompilerParams(
             collective_id=1, has_side_effects=True, vmem_limit_bytes=VMEM_LIMIT
         ),
         name="project",
-    )(tokens, cosine, sine, gains, *sources)
+    )(tokens, cosine, sine, gains, combine, grads, *sources)
+
+
+def layer_kernel(
+    query_ref,
+    pairs_ref,
+    bias_ref,
+    tokens_ref,
+    gain_ref,
+    grads_ref,
+    own_grad_ref,
+    combine_ref,
+    output_src,
+    expand_src,
+    shrink_src,
+    attn_out,
+    middle_out,
+    rows_out,
+    grads_out,
+    results_out,
+    row_grads_out,
+    active_out,
+    gate_out,
+    up_out,
+    output_weight,
+    expand,
+    shrink,
+    rows_all,
+    grads_all,
+    result_sum,
+    grad_sum,
+    results,
+    row_grads,
+    active,
+    gate,
+    up,
+    load_sem,
+    direct_sem,
+    relay_sem,
+    emit_sem,
+):
+    place = Place()
+    shard = place.shard
+    rows = bias_ref.shape[1]
+    held = expand.shape[0]
+    tokens = SHARDS * rows
+    loads = [
+        pltpu.make_async_copy(source, target, load_sem.at[i])
+        for i, (source, target) in enumerate(
+            ((output_src, output_weight), (expand_src, expand), (shrink_src, shrink))
+        )
+    ]
+    for load in loads:
+        load.start()
+    for k in (1, 2):
+        greet(place.peer(k))
+    pl.semaphore_wait(pltpu.get_barrier_semaphore(), 2)
+
+    grads_all[shard] = own_grad_ref[...]
+    grad_square = Square(place, grads_all, direct_sem, relay_sem)
+    row_squares = [Square(place, rows_all.at[m], direct_sem, relay_sem, 2 + 2 * m) for m in range(MB)]
+    grad_square.start()
+
+    def attend(m):
+        own = slice(m * rows, (m + 1) * rows)
+
+        def pair(p, carry):
+            column = pl.multiple_of(p * PAIR_QUERY, PAIR_QUERY)
+            lane = pl.multiple_of(p * LANES, LANES)
+            scale = 1.0 / HEAD_SIZE
+            tiles = [
+                query_ref[own, pl.ds(column + i * LANES, LANES)].astype(f32) * scale for i in range(GROUP)
+            ]
+            key = pairs_ref[m, :, pl.ds(lane, LANES)]
+            value = pairs_ref[m, :, pl.ds(lane + KEY_WIDTH, LANES)]
+            for i, tile in enumerate(attention_pair(tiles, key, value, bias_ref[m])):
+                attn_out[own, pl.ds(column + i * LANES, LANES)] = tile.astype(bf16)
+            return carry
+
+        lax.fori_loop(0, PAIRS, pair, 0)
+
+    def project(m):
+        own = slice(m * rows, (m + 1) * rows)
+        middle = tokens_ref[own].astype(f32) + dot(attn_out[own], output_weight[...])
+        middle_out[own] = middle
+        scale = lax.rsqrt(jnp.mean(middle * middle, axis=-1, keepdims=True) + eps)
+        rows_all[m, shard] = (middle * scale * gain_ref[...]).astype(bf16)
+
+    def emits(m):
+        pairs = (
+            (rows_all.at[m], rows_out.at[m]),
+            (results, results_out.at[m]),
+            (row_grads, row_grads_out.at[m]),
+            (active, active_out.at[m]),
+            (gate, gate_out.at[m]),
+            (up, up_out.at[m]),
+        )
+        return [pltpu.make_async_copy(a, b, emit_sem.at[m * len(pairs) + i]) for i, (a, b) in enumerate(pairs)]
+
+    def expert_steps(m, between):
+        inputs = rows_all.at[m]
+        out_grads = grads_ref if m == 0 else grads_all
+        steps = [(e, b) for e in range(held) for b in range(F // F_BLOCK)]
+        for i, (e, b) in enumerate(steps):
+            weights = combine_ref[:, m * rows : (m + 1) * rows, :].reshape(tokens, LANES)
+            combine = jnp.sum(
+                jnp.where(lane_index(weights.shape) == shard * held + e, weights, 0.0), axis=1, keepdims=True
+            )
+            columns = slice(b * F_BLOCK, (b + 1) * F_BLOCK)
+            up_columns = slice(F + b * F_BLOCK, F + (b + 1) * F_BLOCK)
+            a, g, u, result, row_grad = expert_block(
+                inputs[...].reshape(tokens, MODEL_WIDTH),
+                out_grads[...].reshape(tokens, MODEL_WIDTH),
+                combine,
+                expand[e, :, columns],
+                expand[e, :, up_columns],
+                shrink[e, columns, :],
+            )
+            spot = slice(e * F + b * F_BLOCK, e * F + (b + 1) * F_BLOCK)
+            active[:, spot], gate[:, spot], up[:, spot] = a, g, u
+            if i == 0:
+                result_sum[...] = result
+                grad_sum[...] = row_grad
+            elif i < len(steps) - 1:
+                result_sum[...] += result
+                grad_sum[...] += row_grad
+            else:
+                shape = (SHARDS, rows, MODEL_WIDTH)
+                results[...] = (result_sum[...] + result).astype(bf16).reshape(shape)
+                row_grads[...] = (grad_sum[...] + row_grad).astype(bf16).reshape(shape)
+            if i in between:
+                between[i]()
+
+    attend(0)
+    grad_square.pass_on()
+    loads[0].wait()
+    project(0)
+    row_squares[0].start()
+    attend(1)
+    row_squares[0].pass_on()
+    project(1)
+    row_squares[1].start()
+    loads[1].wait()
+    loads[2].wait()
+    row_squares[0].finish()
+    expert_steps(0, {1: row_squares[1].pass_on})
+    for emit in emits(0):
+        emit.start()
+    row_squares[1].finish()
+    grad_square.finish()
+    grads_emit = pltpu.make_async_copy(grads_all, grads_out, load_sem.at[3])
+    grads_emit.start()
+    for emit in emits(0):
+        emit.wait()
+    expert_steps(1, {})
+    for emit in emits(1):
+        emit.start()
+    grads_emit.wait()
+    grad_square.drain()
+    for square in row_squares:
+        square.drain()
+    for emit in emits(1):
+        emit.wait()
+
+
+def layer(query, pairs, bias, tokens, gain, grads, own_grad, combine, output_weight, expert_in, expert_out):
+    held = expert_in.shape[0]
+    rows = own_grad.shape[0]
+    wide = SHARDS * rows
+    dma = pltpu.SemaphoreType.DMA
+    anywhere = pl.BlockSpec(memory_space=pl.ANY)
+    vmem = pl.BlockSpec(memory_space=pltpu.VMEM)
+    blocks = jax.ShapeDtypeStruct((MB, SHARDS, rows, MODEL_WIDTH), bf16)
+    pieces = jax.ShapeDtypeStruct((MB, wide, held * F), bf16)
+    block = pltpu.VMEM((SHARDS, rows, MODEL_WIDTH), bf16)
+    total = pltpu.VMEM((wide, MODEL_WIDTH), f32)
+    piece = pltpu.VMEM((wide, held * F), bf16)
+    return pl.pallas_call(
+        layer_kernel,
+        in_specs=[vmem] * 8 + [anywhere] * 3,
+        out_specs=[vmem] * 2 + [anywhere] * 7,
+        out_shape=[
+            jax.ShapeDtypeStruct(tokens.shape, bf16),
+            jax.ShapeDtypeStruct(tokens.shape, f32),
+            blocks,
+            jax.ShapeDtypeStruct(blocks.shape[1:], bf16),
+            blocks,
+            blocks,
+            pieces,
+            pieces,
+            pieces,
+        ],
+        scratch_shapes=[
+            pltpu.VMEM(output_weight.shape, bf16),
+            pltpu.VMEM(expert_in.shape, bf16),
+            pltpu.VMEM(expert_out.shape, bf16),
+            pltpu.VMEM((MB, SHARDS, rows, MODEL_WIDTH), bf16),
+            block,
+            total,
+            total,
+            block,
+            block,
+            piece,
+            piece,
+            piece,
+            dma((4,)),
+            dma((2, 2 + 2 * MB)),
+            dma((2, 2 + 2 * MB)),
+            dma((6 * MB,)),
+        ],
+        compiler_params=pltpu.CompilerParams(
+            collective_id=2, has_side_effects=True, vmem_limit_bytes=VMEM_LIMIT
+        ),
+        name="layer",
+    )(query, pairs, bias, tokens, gain, grads, own_grad, combine, output_weight, expert_in, expert_out)
 
 
 PIECES = 4
@@ -970,11 +1241,26 @@
     scale_one = lax.rsqrt(jnp.mean(flat_values * flat_values, axis=-1, keepdims=True) + eps)
     unit_one = flat_values * scale_one
 
+    expert_ids = jnp.arange(E, dtype=jnp.int32)
+    chosen = (routes.reshape(MB, rows, TOP)[..., None] == expert_ids).astype(f32)
+    combine = jnp.sum(gates.reshape(MB, rows, TOP)[..., None] * chosen, axis=2)
+
     if chained:
         packed = jnp.pad(jnp.stack([attn_gain, moe_gain]), ((0, GAIN_ROWS - 2), (0, 0)))
-        normed, query, gains, pair_weight, query_weight, output_weight, pairs = project_all(
-            flat_tokens, cosine, sine, packed, key_value_weight, w_q, w_o, length
+        spread = jnp.pad(combine.reshape(MB * rows, E), ((0, 0), (0, LANES - E)))
+        projected = project_all(
+            flat_tokens,
+            cosine,
+            sine,
+            packed,
+            spread,
+            cotangent[0, 0],
+            key_value_weight,
+            w_q,
+            w_o,
+            length,
         )
+        normed, query, gains, combine, grads, pair_weight, query_weight, output_weight, pairs = projected
         gains = gains.reshape(SHARDS, GAIN_ROWS, width).astype(f32)
         gain_one, gain_two = gains[:, 0].reshape(MODEL_WIDTH), gains[:, 1].reshape(MODEL_WIDTH)
     else:
@@ -988,12 +1274,9 @@
         own_pairs = own_pairs.reshape(MB, rows, 2 * KEY_WIDTH)
         pairs = lax.all_gather(own_pairs, "ctx", axis=1, tiled=True)
 
-    expert_ids = jnp.arange(E, dtype=jnp.int32)
-    chosen = (routes.reshape(MB, rows, TOP)[..., None] == expert_ids).astype(f32)
-    combine = jnp.sum(gates.reshape(MB, rows, TOP)[..., None] * chosen, axis=2)
-    combine = jnp.concatenate([combine] + [links.across(combine, k) for k in range(1, links.shards)], axis=1)
-    combine = lax.dynamic_slice_in_dim(combine, links.shard * held, held, 2)
-    combine = combine.transpose(0, 2, 1)[..., None]
+        combine = jnp.concatenate([combine] + [links.across(combine, k) for k in range(1, links.shards)], axis=1)
+        combine = lax.dynamic_slice_in_dim(combine, links.shard * held, held, 2)
+        combine = combine.transpose(0, 2, 1)[..., None]
 
     biases, biases_turned = [], []
     for m in range(MB):
@@ -1005,39 +1288,86 @@
         seen = (key_places[:, None] <= places[None, :]) & (key_places[:, None] >= begins[None, :])
         biases_turned.append(jnp.where(seen, 0.0, -1e30).astype(f32))
 
-    kept = []
-    outputs = []
-    for m in range(MB):
-        own = slice(m * rows, (m + 1) * rows)
-        attn = attention_forward(m, query, pairs, biases[m])
-        middle = flat_tokens[own].astype(f32) + dot(attn, output_weight)
-        scale_two = lax.rsqrt(jnp.mean(middle * middle, axis=-1, keepdims=True) + eps)
-        unit_two = middle * scale_two
-        moe_in = (unit_two * gain_two).astype(bf16)
-        out_grad = cotangent[m, 0]
-        row_parts = [moe_in] + [links.across(moe_in, k) for k in range(1, links.shards)]
-        grad_parts = [out_grad] + [links.across(out_grad, k) for k in range(1, links.shards)]
-        results, row_grads, pieces = experts(row_parts, grad_parts, combine[m], expert_in, expert_out)
-        final = middle + results[0].astype(f32)
-        for k in range(1, links.shards):
-            final = final + links.across(results[k], k).astype(f32)
-        outputs.append(final.astype(bf16))
-        kept.append((attn, unit_two, scale_two, row_parts, grad_parts, row_grads, pieces))
-
-    expert_grads = expert_weights(
-        sum([k[3] for k in kept], []), sum([k[4] for k in kept], []), [k[6] for k in kept], held
-    )
-
+    middles, attns, results, row_grads = [], [], [], []
+    if chained:
+        (
+            attn_all,
+            middle_all,
+            row_blocks,
+            grad_blocks,
+            result_blocks,
+            row_grad_blocks,
+            active,
+            gate,
+            up,
+        ) = layer(
+            query,
+            pairs,
+            jnp.stack(biases),
+            flat_tokens,
+            gain_two[None],
+            grads,
+            cotangent[1, 0],
+            combine,
+            output_weight,
+            expert_in,
+            expert_out,
+        )
+        flat = lambda a: a.reshape(-1, a.shape[-1])
+        expert_grads = expert_weights(
+            flat(row_blocks),
+            jnp.concatenate([flat(grads), flat(grad_blocks)], axis=0),
+            flat(active),
+            flat(gate),
+            flat(up),
+            held,
+        )
+        for m in range(MB):
+            own = slice(m * rows, (m + 1) * rows)
+            middles.append(middle_all[own])
+            attns.append(attn_all[own])
+            pick = lambda blocks, k: lax.dynamic_index_in_dim(blocks[m], links.shard ^ k, 0, keepdims=False)
+            for blocks, sums in ((result_blocks, results), (row_grad_blocks, row_grads)):
+                total = pick(blocks, 0).astype(f32)
+                for k in range(1, links.shards):
+                    total = total + links.across(pick(blocks, k), k).astype(f32)
+                sums.append(total)
+    else:
+        rows_kept, grads_kept, pieces_kept = [], [], []
+        for m in range(MB):
+            own = slice(m * rows, (m + 1) * rows)
+            attn = attention_forward(m, query, pairs, biases[m])
+            middle = flat_tokens[own].astype(f32) + dot(attn, output_weight)
+            scale_two = lax.rsqrt(jnp.mean(middle * middle, axis=-1, keepdims=True) + eps)
+            moe_in = (middle * scale_two * gain_two).astype(bf16)
+            out_grad = cotangent[m, 0]
+            row_parts = [moe_in] + [links.across(moe_in, k) for k in range(1, links.shards)]
+            grad_parts = [out_grad] + [links.across(out_grad, k) for k in range(1, links.shards)]
+            result, row_grad, pieces = experts(row_parts, grad_parts, combine[m], expert_in, expert_out)
+            for parts, sums in ((result, results), (row_grad, row_grads)):
+                total = parts[0].astype(f32)
+                for k in range(1, links.shards):
+                    total = total + links.across(parts[k], k).astype(f32)
+                sums.append(total)
+            middles.append(middle)
+            attns.append(attn)
+            rows_kept += row_parts
+            grads_kept += grad_parts
+            pieces_kept.append(pieces)
+        merge = lambda items: jnp.concatenate(items, axis=0)
+        expert_grads = expert_weights(
+            merge(rows_kept), merge(grads_kept), *[merge([p[i] for p in pieces_kept]) for i in range(3)], held
+        )
     expert_grads = [g.reshape(-1, g.shape[-1]) for g in expert_grads]
+    outputs = [(middles[m] + results[m]).astype(bf16) for m in range(MB)]
 
     input_grads, query_lows, pair_lows, middle_lows = [], [], [], []
     gain_one_grad, gain_two_grad = 0.0, 0.0
     for m in range(MB):
         own = slice(m * rows, (m + 1) * rows)
-        attn, unit_two, scale_two, _, _, row_grads, _ = kept[m]
-        moe_in_grad = row_grads[0].astype(f32)
-        for k in range(1, links.shards):
-            moe_in_grad = moe_in_grad + links.across(row_grads[k], k).astype(f32)
+        scale_two = lax.rsqrt(jnp.mean(middles[m] * middles[m], axis=-1, keepdims=True) + eps)
+        unit_two = middles[m] * scale_two
+        moe_in_grad = row_grads[m]
         gain_two_grad = gain_two_grad + jnp.sum(moe_in_grad * unit_two, axis=0)
         weighted = moe_in_grad * gain_two
         inner = jnp.mean(weighted * unit_two, axis=-1, keepdims=True)
@@ -1073,7 +1403,7 @@
 
     join = lambda items: jnp.concatenate(items, axis=0)
 
-    output_grad = dot(join([k[0] for k in kept]), join(middle_lows), TN).astype(bf16)
+    output_grad = dot(join(attns), join(middle_lows), TN).astype(bf16)
     query_grad = dot(normed, join(query_lows), TN).astype(bf16)
     pair_weight_grad = dot(normed, join(pair_lows), TN).astype(bf16)
     gain_grads = jnp.stack([gain_one_grad, gain_two_grad], axis=1)

time: 597 us -> 533 us (0.89)
  waiting for transfers between devices: 105 us -> 29.3 us
  Pallas kernels: 340 us -> 363 us
  starting transfers between devices: 45.6 us -> 25.5 us
  local copies, waits for them, and re-layouts: 22.6 us -> 36 us
    ppermute x27 -> x12, waiting for transfers between devices: 70.7 us -> 3.02 us  [across(): return lax.ppermute(array, 'fsdp', [(i, i ^ k) for i in range(self.shards)])]
    pallas_call x6 -> x3, Pallas kernels: 136 us -> 157 us  [the longest x1 80.6 us: project_all(): pl.pallas_call(project_kernel, in_specs=[vmem] * 6 + [anywhere] * 3, out_...]
    ppermute x27 -> x12, starting transfers between devices: 32 us -> 15.3 us  [across(): return lax.ppermute(array, 'fsdp', [(i, i ^ k) for i in range(self.shards)])]
    ppermute x6, waiting for transfers between devices: 33.8 us -> 26.2 us  [shift(): return lax.ppermute(array, 'ctx', [(i, (i + 2 * s) % n) for i in range(n)])]
    dot_general x11 -> x9, matrix products: 32 us -> 27.4 us  [dot(): return lax.dot_general(left, right, dims, preferred_element_type=f32)]
  transfers between devices with their start and end apart: 35 -> 20, of which waited for: 17 -> 4; matrix products, arithmetic and copies ran while one was open for 7% -> 14% of each run, Pallas kernels for 8% -> 39%
where the time goes in v4:
time: 533 us; the launch traced here: 526 us
  Pallas kernels  363 us (68%)
  other arithmetic  43 us (8%)
  local copies, waits for them, and re-layouts  36 us (7%)
  waiting for transfers between devices  29.3 us (5%)
  matrix products  27.4 us (5%)
  starting transfers between devices  25.5 us (5%)
    pallas_call x1, Pallas kernels, reduce_weights(): pl.pallas_call(functools.partial(reduce_kernel, experts_n, dense_n, shard...  167 us
    pallas_call x1, Pallas kernels, project_all(): pl.pallas_call(project_kernel, in_specs=[vmem] * 6 + [anywhere] * 3, out_...  80.6 us
    pallas_call x1, Pallas kernels, layer(): pl.pallas_call(layer_kernel, in_specs=[vmem] * 8 + [anywhere] * 3, out_sp...  60.6 us
    pallas_call x2, Pallas kernels, attention_backward(): pl.pallas_call(attention_backward_kernel, grid=(PAIRS,), in_specs=[pl.Blo...  34.6 us
    dot_general x9, matrix products, dot(): return lax.dot_general(left, right, dims, preferred_element_type=f32)  27.4 us
    ppermute x6, waiting for transfers between devices, shift(): return lax.ppermute(array, 'ctx', [(i, (i + 2 * s) % n) for i in range(n)])  26.2 us
    pallas_call x1, Pallas kernels, expert_weights(): pl.pallas_call(expert_weights_kernel, grid=(held, blocks), in_specs=[whol...  16.1 us
    ppermute x12, starting transfers between devices, across(): return lax.ppermute(array, 'fsdp', [(i, i ^ k) for i in range(self.shards)])  15.3 us
  transfers between devices with their start and end apart: 20, of which 4 were waited for; matrix products, arithmetic and copies ran while one was open for 14% of the time, Pallas kernels for 39%

profile of v4, /device:TPU:0, one launch (start us, length us, event | category | flops | bytes accessed | tf_op | source)
XLA Modules:
  0.0 526.2 jit_solution(15995706626884611101)
XLA Ops:
  7.4 80.6 %project.1 = (bf16[256,1536]{1,0:T(8,128)(2,1)}, bf16[256,1536]{1,0:T(8,128)(2,1)}, bf16[64,384]{1,0:T(8,128)(2,1)}, f32[4,256,128]{2,1,0:T(8,128)}, bf16[4,128,...) custom-call(bf16[256,1536]{1,0:T(8,128)(2,1)} %bitcast.168, ...), custom_call_target="tpu_custom_call" | custom-call | tf_op jit(solution)/shard_map/project/pallas_call | solution.py:727
  91.5 60.6 %layer.1 = (bf16[256,1536]{1,0:T(8,128)(2,1)}, f32[256,1536]{1,0:T(8,128)}, bf16[2,4,128,1536]{3,2,1,0:T(8,128)(2,1)}, bf16[4,128,1536]{2,1,0:T(8,128)(2,1)}, bf...) custom-call(bf16[256,1536]{1,0:T(8,128)(2,1)} %get-tuple-element.40., ...), custom_call_target="tpu_custom_call" | custom-call | tf_op jit(solution)/shard_map/layer/pallas_call | solution.py:938
  152.1 2.1 fusion.49
  156.3 2.6 collective-permute-start.6
  173.4 16.1 %expert_weights.1 = (bf16[2,1536,512]{2,1,0:T(8,128)(2,1)}, bf16[2,1536,512]{2,1,0:T(8,128)(2,1)}, bf16[2,512,1536]{2,1,0:T(8,128)(2,1)}) custom-call(bf16[1024,1536]{1,0:T(8,128)(2,1)} %bitcast.184, bf16[1024,1536]{1,0:T(8,128)(2,1)} %pad_maximum_fusion.2.grads_ref, bf16[1024,1024]{1,0:T(8,128)(2,1)} %bitcast.185, bf16[1024,1024]{1,0:T(8,128)(2,1)} %bitcast.186, ...), custom_call_target="tpu_custom_call" | custom-call | flops 9663676416 | bytes 22020096 | tf_op jit(solution)/shard_map/expert_weights/pallas_call | solution.py:345
  190.0 2.3 dynamic-slice_bitcast_fusion.10
  195.1 3.2 fusion.4
  198.4 3.0 collective-permute-done.15
  201.3 2.5 multiply_reduce_fusion.2
  205.0 2.4 convolution_convert_fusion.4.grad_ref
  207.4 17.2 %attention_backward.2 = (bf16[128,1536]{1,0:T(8,128)(2,1)}, bf16[1024,1024]{1,0:T(8,128)(2,1)}) custom-call(bf16[256,1536]{1,0:T(8,128)(2,1)} %get-tuple-element.40.query_ref, f32[128,128]{1,0:T(8,128)} %pad_maximum_fusion.4.cosine_ref, f32[128,128]{1,0:T(8,128)} %pad_maximum_fusion.5.sine_ref, ...), custom_call_target="tpu_custom_call" | custom-call | flops 8053063680 | bytes 12582912 | tf_op jit(solution)/shard_map/attention_backward/pallas_call | solution.py:210
  224.6 2.3 dynamic-slice_bitcast_fusion.1
  226.9 4.7 convolution_convert_fusion.3.grad_ref
  231.6 17.4 %attention_backward.3 = (bf16[128,1536]{1,0:T(8,128)(2,1)}, bf16[1024,1024]{1,0:T(8,128)(2,1)}) custom-call(bf16[256,1536]{1,0:T(8,128)(2,1)} %get-tuple-element.40.query_ref, f32[128,128]{1,0:T(8,128)} %pad_maximum_fusion.4.cosine_ref, f32[128,128]{1,0:T(8,128)} %pad_maximum_fusion.5.sine_ref, ...), custom_call_target="tpu_custom_call" | custom-call | flops 8053063680 | bytes 12582912 | tf_op jit(solution)/shard_map/attention_backward/pallas_call | solution.py:210
  251.0 5.0 fusion.51
  256.0 3.6 convolution_convert_fusion
  259.6 2.5 fusion.52
  264.7 3.9 collective-permute-start.10
  270.8 3.1 collective-permute-start.17
  276.9 3.6 convolution_convert_fusion.1
  280.5 11.9 %collective-permute-done.11.refs_2_ = bf16[128,1024]{1,0:T(8,128)(2,1)S(1)} collective-permute-done((bf16[128,1024]{1,0:T(8,128)(2,1)S(1)}, bf16[128,1024]{1,0:T(8,128)(2,1)S(1)}, u32[]{:S(2)}, u32[]{:S(2)}) %collective-permute-start.11) | collective-permute-done | bytes 262176 | tf_op jit(solution)/shard_map/ppermute | solution.py:384
  295.9 2.2 pair_gradient.2
  299.5 13.9 %collective-permute-done.18.refs_2_ = bf16[128,1024]{1,0:T(8,128)(2,1)} collective-permute-done((bf16[128,1024]{1,0:T(8,128)(2,1)}, bf16[128,1024]{1,0:T(8,128)(2,1)}, u32[]{:S(2)}, u32[]{:S(2)}) %collective-permute-start.18) | collective-permute-done | bytes 262176 | tf_op jit(solution)/shard_map/ppermute | solution.py:384
  315.5 2.2 pair_gradient.3
  317.7 2.2 convolution_convert_fusion.2
  321.2 2.2 multiply_reduce_fusion.4
  325.5 5.8 %copy.49 = bf16[1536,1152]{1,0:T(8,128)(2,1)} copy(bf16[1536,1152]{0,1:T(8,128)(2,1)} %pad_maximum_fusion.1) | data formatting | bytes 7077888 | tf_op jit(solution)/shard_map/concatenate | solution.py:1411
  331.2 166.9 %reduce_weights.1 = (bf16[3072,512]{1,0:T(8,128)(2,1)}, bf16[3072,512]{1,0:T(8,128)(2,1)}, bf16[1024,1536]{1,0:T(8,128)(2,1)}, bf16[384,1536]{1,0:T(8,128)(2,1)}...) custom-call(bf16[3072,512]{1,0:T(8,128)(2,1)} %bitcast.172, bf16[3072,512]{1,0:T(8,128)(2,1)} %bitcast.173, ...), custom_call_target="tpu_custom_call" | custom-call | tf_op jit(solution)/shard_map/reduce_weights/pallas_call | solution.py:1193
  499.7 2.3 add_bitcast_fusion
  502.1 3.8 pad_maximum_fusion
  507.3 6.4 %convert.29 = f32[2,1536,1024]{2,1,0:T(8,128)} convert(bf16[2,1536,1024]{2,1,0:T(8,128)(2,1)S(1)} %bitcast.164) | non-fusion elementwise | flops 3145728 | bytes 18874368 | tf_op jit(solution)/shard_map/reshape | solution.py:1430
  513.7 3.6 convert.30
  (199 shorter events, 62.3 us)
Async XLA Ops:
  155.3 9.9 %copy-start.1 = (bf16[2,1,128,1536]{3,2,1,0:T(8,128)(2,1)S(1)}, bf16[2,1,128,1536]{3,2,1,0:T(8,128)(2,1)}, u32[]{:S(2)}) copy-start(bf16[2,1,128,1536]{3,2,1,0:T(8,128)(2,1)} %param.12) | copy-start | bytes 2359300
  156.3 9.1 %copy-start = (f32[256,1536]{1,0:T(8,128)S(1)}, f32[256,1536]{1,0:T(8,128)}, u32[]{:S(2)}) copy-start(f32[256,1536]{1,0:T(8,128)} %get-tuple-element.46) | copy-start | bytes 4718596
  156.3 36.0 %collective-permute-start.6 = (bf16[128,1536]{1,0:T(8,128)(2,1)S(1)}, bf16[128,1536]{1,0:T(8,128)(2,1)S(1)}, u32[]{:S(2)}, u32[]{:S(2)}) collective-permute-start(bf16[128,1536]{1,0:T(8,128)(2,1)S(1)} %get-tuple-element.137), channel_id=1, source_target_pairs={{0,8},{8,0},{16,24},{24,16},{1,9},{9,1},{17,25},{25,17},{2,10},{10... | collective-permute-start | bytes 1179656 | tf_op jit(solution)/shard_map/ppermute | solution.py:377
  158.9 39.4 %collective-permute-start.7 = (bf16[128,1536]{1,0:T(8,128)(2,1)}, bf16[128,1536]{1,0:T(8,128)(2,1)}, u32[]{:S(2)}, u32[]{:S(2)}) collective-permute-start(bf16[128,1536]{1,0:T(8,128)(2,1)} %get-tuple-element.139), channel_id=1, source_target_pairs={{0,16},{8,24},{16,0},{24,8},{1,17},{9,25},{17,1},{25,9},{2,18},{10... | collective-permute-start | bytes 1179656 | tf_op jit(solution)/shard_map/ppermute | solution.py:377
  158.9 39.4 %collective-permute-start.8 = (bf16[128,1536]{1,0:T(8,128)(2,1)}, bf16[128,1536]{1,0:T(8,128)(2,1)}, u32[]{:S(2)}, u32[]{:S(2)}) collective-permute-start(bf16[128,1536]{1,0:T(8,128)(2,1)} %get-tuple-element.138), channel_id=1, source_target_pairs={{0,24},{8,16},{16,8},{24,0},{1,25},{9,17},{17,9},{25,1},{2,26},{10... | collective-permute-start | bytes 1179656 | tf_op jit(solution)/shard_map/ppermute | solution.py:377
  161.4 36.9 %collective-permute-start.13 = (bf16[128,1536]{1,0:T(8,128)(2,1)}, bf16[128,1536]{1,0:T(8,128)(2,1)}, u32[]{:S(2)}, u32[]{:S(2)}) collective-permute-start(bf16[128,1536]{1,0:T(8,128)(2,1)} %get-tuple-element.140), channel_id=1, source_target_pairs={{0,8},{8,0},{16,24},{24,16},{1,9},{9,1},{17,25},{25,17},{2,10},{10... | collective-permute-start | bytes 1179656 | tf_op jit(solution)/shard_map/ppermute | solution.py:377
  163.4 34.9 %collective-permute-start.14 = (bf16[128,1536]{1,0:T(8,128)(2,1)}, bf16[128,1536]{1,0:T(8,128)(2,1)}, u32[]{:S(2)}, u32[]{:S(2)}) collective-permute-start(bf16[128,1536]{1,0:T(8,128)(2,1)} %get-tuple-element.142), channel_id=1, source_target_pairs={{0,16},{8,24},{16,0},{24,8},{1,17},{9,25},{17,1},{25,9},{2,18},{10... | collective-permute-start | bytes 1179656 | tf_op jit(solution)/shard_map/ppermute | solution.py:377
  192.4 9.0 %collective-permute-start.15 = (bf16[128,1536]{1,0:T(8,128)(2,1)}, bf16[128,1536]{1,0:T(8,128)(2,1)}, u32[]{:S(2)}, u32[]{:S(2)}) collective-permute-start(bf16[128,1536]{1,0:T(8,128)(2,1)} %get-tuple-element.141), channel_id=1, source_target_pairs={{0,24},{8,16},{16,8},{24,0},{1,25},{9,17},{17,9},{25,1},{2,26},{10... | collective-permute-start | bytes 1179656 | tf_op jit(solution)/shard_map/ppermute | solution.py:377
  195.1 9.9 %slice-start = ((s8[4718592]{0:T(1024)(128)(4,1)}), s8[4194304]{0:T(1024)(128)(4,1)S(1)}, s32[]{:S(2)}) async-start(s8[4718592]{0:T(1024)(128)(4,1)} %bitcast.160), calls=%async_computation | async-start | bytes 8388608
  205.0 21.9 %copy-start.18 = (bf16[128,1536]{1,0:T(8,128)(2,1)}, bf16[128,1536]{1,0:T(8,128)(2,1)S(1)}, u32[]{:S(2)}) copy-start(bf16[128,1536]{1,0:T(8,128)(2,1)S(1)} %get-tuple-element.132) | copy-start | bytes 1179652
  226.9 35.3 %collective-permute-start.9 = (bf16[4,128,1024]{2,1,0:T(8,128)(2,1)}, bf16[4,128,1024]{2,1,0:T(8,128)(2,1)}, u32[]{:S(2)}, u32[]{:S(2)}) collective-permute-start(bf16[4,128,1024]{2,1,0:T(8,128)(2,1)} %dynamic-slice_bitcast_fusion.1), channel_id=1, source_target_pairs={{0,1},{1,0},{2,3},{3,2},{4,5},{5,4},{6,7},{7,6},{8,9},{9,8},{10,11... | collective-permute-start | bytes 3145736 | tf_op jit(solution)/shard_map/ppermute | solution.py:380
  250.4 19.0 %collective-permute-start.16 = (bf16[4,128,1024]{2,1,0:T(8,128)(2,1)S(1)}, bf16[4,128,1024]{2,1,0:T(8,128)(2,1)S(1)}, u32[]{:S(2)}, u32[]{:S(2)}) collective-permute-start(bf16[4,128,1024]{2,1,0:T(8,128)(2,1)S(1)} %dynamic-slice_bitcast_fusion), channel_id=1, source_target_pairs={{0,1},{1,0},{2,3},{3,2},{4,5},{5,4},{6,7},{7,6},{8,9},{9,8},{10,11... | collective-permute-start | bytes 3145736 | tf_op jit(solution)/shard_map/ppermute | solution.py:380
  251.0 8.6 %slice-start.2 = ((s8[4718592]{0:T(1024)(128)(4,1)}), s8[4194304]{0:T(1024)(128)(4,1)S(1)}, s32[]{:S(2)}) async-start(s8[4718592]{0:T(1024)(128)(4,1)} %bitcast.165), calls=%async_computation.2 | async-start | bytes 8388608
  262.1 7.2 %copy-start.27 = (bf16[1024,1024]{1,0:T(8,128)(2,1)S(1)}, bf16[1024,1024]{1,0:T(8,128)(2,1)}, u32[]{:S(2)}) copy-start(bf16[1024,1024]{1,0:T(8,128)(2,1)} %get-tuple-element.54) | copy-start | bytes 6291460
  264.7 10.6 %collective-permute-start.10 = (bf16[128,1024]{1,0:T(8,128)(2,1)S(1)}, bf16[128,1024]{1,0:T(8,128)(2,1)S(1)}, u32[]{:S(2)}, u32[]{:S(2)}) collective-permute-start(bf16[128,1024]{1,0:T(8,128)(2,1)S(1)} %get-tuple-element.151), channel_id=1, source_target_pairs={{0,6},{1,7},{2,0},{3,1},{4,2},{5,3},{6,4},{7,5},{8,14},{9,15},{10,... | collective-permute-start | bytes 786440 | tf_op jit(solution)/shard_map/ppermute | solution.py:384
  268.6 23.8 %collective-permute-start.11 = (bf16[128,1024]{1,0:T(8,128)(2,1)S(1)}, bf16[128,1024]{1,0:T(8,128)(2,1)S(1)}, u32[]{:S(2)}, u32[]{:S(2)}) collective-permute-start(bf16[128,1024]{1,0:T(8,128)(2,1)S(1)} %get-tuple-element.150), channel_id=1, source_target_pairs={{0,4},{1,5},{2,6},{3,7},{4,0},{5,1},{6,2},{7,3},{8,12},{9,13},{10,... | collective-permute-start | bytes 786440 | tf_op jit(solution)/shard_map/ppermute | solution.py:384
  268.6 8.3 %copy-start.17 = (bf16[128,1536]{1,0:T(8,128)(2,1)S(1)}, bf16[128,1536]{1,0:T(8,128)(2,1)}, u32[]{:S(2)}) copy-start(bf16[128,1536]{1,0:T(8,128)(2,1)} %copy-done.16) | copy-start | bytes 1179652
  268.6 8.3 %copy-start.19 = (bf16[128,1536]{1,0:T(8,128)(2,1)S(1)}, bf16[128,1536]{1,0:T(8,128)(2,1)}, u32[]{:S(2)}) copy-start(bf16[128,1536]{1,0:T(8,128)(2,1)} %copy-done.18) | copy-start | bytes 1179652
  268.6 8.3 %copy-start.32 = (bf16[256,1536]{1,0:T(8,128)(2,1)S(1)}, bf16[256,1536]{1,0:T(8,128)(2,1)}, u32[]{:S(2)}) copy-start(bf16[256,1536]{1,0:T(8,128)(2,1)} %get-tuple-element.63) | copy-start | bytes 2359300
  268.6 25.8 %collective-permute-start.12 = (bf16[128,1024]{1,0:T(8,128)(2,1)S(1)}, bf16[128,1024]{1,0:T(8,128)(2,1)S(1)}, u32[]{:S(2)}, u32[]{:S(2)}) collective-permute-start(bf16[128,1024]{1,0:T(8,128)(2,1)S(1)} %get-tuple-element.149), channel_id=1, source_target_pairs={{0,2},{1,3},{2,4},{3,5},{4,6},{5,7},{6,0},{7,1},{8,10},{9,11},{10,... | collective-permute-start | bytes 786440 | tf_op jit(solution)/shard_map/ppermute | solution.py:384
  270.8 27.3 %collective-permute-start.17 = (bf16[128,1024]{1,0:T(8,128)(2,1)}, bf16[128,1024]{1,0:T(8,128)(2,1)}, u32[]{:S(2)}, u32[]{:S(2)}) collective-permute-start(bf16[128,1024]{1,0:T(8,128)(2,1)} %get-tuple-element.155), channel_id=1, source_target_pairs={{0,6},{1,7},{2,0},{3,1},{4,2},{5,3},{6,4},{7,5},{8,14},{9,15},{10,... | collective-permute-start | bytes 786440 | tf_op jit(solution)/shard_map/ppermute | solution.py:384
  273.9 39.5 %collective-permute-start.18 = (bf16[128,1024]{1,0:T(8,128)(2,1)}, bf16[128,1024]{1,0:T(8,128)(2,1)}, u32[]{:S(2)}, u32[]{:S(2)}) collective-permute-start(bf16[128,1024]{1,0:T(8,128)(2,1)} %get-tuple-element.154), channel_id=1, source_target_pairs={{0,4},{1,5},{2,6},{3,7},{4,0},{5,1},{6,2},{7,3},{8,12},{9,13},{10,... | collective-permute-start | bytes 786440 | tf_op jit(solution)/shard_map/ppermute | solution.py:384
  276.1 39.4 %collective-permute-start.19 = (bf16[128,1024]{1,0:T(8,128)(2,1)}, bf16[128,1024]{1,0:T(8,128)(2,1)}, u32[]{:S(2)}, u32[]{:S(2)}) collective-permute-start(bf16[128,1024]{1,0:T(8,128)(2,1)} %get-tuple-element.153), channel_id=1, source_target_pairs={{0,2},{1,3},{2,4},{3,5},{4,6},{5,7},{6,0},{7,1},{8,10},{9,11},{10,... | collective-permute-start | bytes 786440 | tf_op jit(solution)/shard_map/ppermute | solution.py:384
  292.4 205.7 %collective-permute-start = (bf16[128,1536]{1,0:T(8,128)(2,1)}, bf16[128,1536]{1,0:T(8,128)(2,1)}, u32[]{:S(2)}, u32[]{:S(2)}) collective-permute-start(bf16[128,1536]{1,0:T(8,128)(2,1)} %get-tuple-element.143), channel_id=1, source_target_pairs={{0,8},{8,0},{16,24},{24,16},{1,9},{9,1},{17,25},{25,17},{2,10},{10... | collective-permute-start | bytes 1179656 | tf_op jit(solution)/shard_map/ppermute | solution.py:377
  295.1 204.6 %collective-permute-start.1 = (bf16[128,1536]{1,0:T(8,128)(2,1)}, bf16[128,1536]{1,0:T(8,128)(2,1)}, u32[]{:S(2)}, u32[]{:S(2)}) collective-permute-start(bf16[128,1536]{1,0:T(8,128)(2,1)} %get-tuple-element.145), channel_id=1, source_target_pairs={{0,16},{8,24},{16,0},{24,8},{1,17},{9,25},{17,1},{25,9},{2,18},{10... | collective-permute-start | bytes 1179656 | tf_op jit(solution)/shard_map/ppermute | solution.py:377
  298.1 201.6 %collective-permute-start.2 = (bf16[128,1536]{1,0:T(8,128)(2,1)}, bf16[128,1536]{1,0:T(8,128)(2,1)}, u32[]{:S(2)}, u32[]{:S(2)}) collective-permute-start(bf16[128,1536]{1,0:T(8,128)(2,1)} %get-tuple-element.144), channel_id=1, source_target_pairs={{0,24},{8,16},{16,8},{24,0},{1,25},{9,17},{17,9},{25,1},{2,26},{10... | collective-permute-start | bytes 1179656 | tf_op jit(solution)/shard_map/ppermute | solution.py:377
  313.4 208.1 %collective-permute-start.3 = (bf16[128,1536]{1,0:T(8,128)(2,1)}, bf16[128,1536]{1,0:T(8,128)(2,1)}, u32[]{:S(2)}, u32[]{:S(2)}) collective-permute-start(bf16[128,1536]{1,0:T(8,128)(2,1)} %get-tuple-element.146), channel_id=1, source_target_pairs={{0,8},{8,0},{16,24},{24,16},{1,9},{9,1},{17,25},{25,17},{2,10},{10... | collective-permute-start | bytes 1179656 | tf_op jit(solution)/shard_map/ppermute | solution.py:377
  315.4 206.1 %collective-permute-start.4 = (bf16[128,1536]{1,0:T(8,128)(2,1)}, bf16[128,1536]{1,0:T(8,128)(2,1)}, u32[]{:S(2)}, u32[]{:S(2)}) collective-permute-start(bf16[128,1536]{1,0:T(8,128)(2,1)} %get-tuple-element.148), channel_id=1, source_target_pairs={{0,16},{8,24},{16,0},{24,8},{1,17},{9,25},{17,1},{25,9},{2,18},{10... | collective-permute-start | bytes 1179656 | tf_op jit(solution)/shard_map/ppermute | solution.py:377
  331.2 168.5 %copy-start.6 = (f32[128,1536]{1,0:T(8,128)S(1)}, f32[128,1536]{1,0:T(8,128)}, u32[]{:S(2)}) copy-start(f32[128,1536]{1,0:T(8,128)} %copy-done.5) | copy-start | bytes 2359300
  331.2 168.5 %copy-start.42 = (f32[128]{0:T(128)S(1)}, f32[128]{0:T(128)}, u32[]{:S(2)}) copy-start(f32[128]{0:T(128)} %add_rsqrt_fusion.1) | copy-start | bytes 1540
  331.2 168.5 %copy-start.44 = (f32[128]{0:T(128)S(1)}, f32[128]{0:T(128)}, u32[]{:S(2)}) copy-start(f32[128]{0:T(128)} %get-tuple-element.164) | copy-start | bytes 1540
  498.2 23.4 %collective-permute-start.5 = (bf16[128,1536]{1,0:T(8,128)(2,1)}, bf16[128,1536]{1,0:T(8,128)(2,1)S(1)}, u32[]{:S(2)}, u32[]{:S(2)}) collective-permute-start(bf16[128,1536]{1,0:T(8,128)(2,1)} %get-tuple-element.147), channel_id=1, source_target_pairs={{0,24},{8,16},{16,8},{24,0},{1,25},{9,17},{17,9},{25,1},{2,26},{10... | collective-permute-start | bytes 1179656 | tf_op jit(solution)/shard_map/ppermute | solution.py:377
  (39 other events, 121.9 us)

commit v5 on v1

v5 whole, which is shorter than its diff:
```python
import functools
import types

import jax
import jax.numpy as jnp
import numpy as np
from jax import lax
from jax.experimental import pallas as pl
from jax.experimental.pallas import tpu as pltpu
from jax.sharding import PartitionSpec as P

MODEL_WIDTH = 1536
QUERY_HEADS = 24
KEY_VALUE_HEADS = 8
HEAD_SIZE = 64
GROUP = QUERY_HEADS // KEY_VALUE_HEADS
KEY_WIDTH = KEY_VALUE_HEADS * HEAD_SIZE
F = 512
E = 8
TOP = 4
MB = 2
LANES = 128
PAIRS = KEY_WIDTH // LANES
PAIR_QUERY = 2 * GROUP * HEAD_SIZE
F_BLOCK = 256
VMEM_LIMIT = 60 * 1024 * 1024

eps = 1e-05
theta = 10000.0

NT = (((1,), (1,)), ((), ()))
TN = (((0,), (0,)), ((), ()))
bf16 = jnp.bfloat16
f32 = jnp.float32


def dot(left, right, dims=(((1,), (0,)), ((), ()))):
    return lax.dot_general(left, right, dims, preferred_element_type=f32)


def rotation_tables(positions):
    frequency = theta ** (-jnp.arange(0, HEAD_SIZE, 2, dtype=f32) / HEAD_SIZE)
    angles = positions.astype(f32)[:, None] * frequency[None, :]
    cosine, sine = jnp.cos(angles), jnp.sin(angles)
    repeat = LANES // HEAD_SIZE
    cosine = jnp.concatenate([cosine, cosine] * repeat, axis=1)
    sine = jnp.concatenate([-sine, sine] * repeat, axis=1)
    return cosine, sine


def rotation_constants(length):
    frequency = theta ** (-np.arange(0, HEAD_SIZE, 2, dtype=np.float64) / HEAD_SIZE)
    angles = np.arange(length, dtype=np.float64)[:, None] * frequency[None, :]
    cosine, sine = np.cos(angles), np.sin(angles)
    repeat = LANES // HEAD_SIZE
    cosine = np.concatenate([cosine, cosine] * repeat, axis=1)
    sine = np.concatenate([-sine, sine] * repeat, axis=1)
    return jnp.asarray(np.stack([cosine, sine]).astype(np.float32))


def visible_bias(starts, m, context, shape, query_axis):
    rows = shape[query_axis]
    narrow = (rows, 1) if query_axis == 0 else (1, rows)
    query = context * rows + lax.broadcasted_iota(jnp.int32, narrow, query_axis)
    begin = jnp.zeros(narrow, jnp.int32)
    for i in range(starts.shape[1]):
        begin = jnp.maximum(begin, jnp.where(query >= starts[m, i], starts[m, i], 0))
    key = lax.broadcasted_iota(jnp.int32, shape, 1 - query_axis)
    return jnp.where((key <= query) & (key >= begin), 0.0, -1e30).astype(f32)


def lane_index(shape):
    return lax.broadcasted_iota(jnp.int32, shape, 1)


def rotate(tile, cosine, sine):
    half = HEAD_SIZE // 2
    ahead = pltpu.roll(tile, LANES - half, 1)
    behind = pltpu.roll(tile, half, 1)
    first = lane_index(tile.shape) % HEAD_SIZE < half
    return tile * cosine + jnp.where(first, ahead, behind) * sine


def rotate_columns_kernel(rotated, values_ref, cosine_ref, sine_ref, out_ref):
    cosine, sine = cosine_ref[...], sine_ref[...]
    for i in range(values_ref.shape[1] // LANES):
        cols = slice(i * LANES, (i + 1) * LANES)
        tile = values_ref[:, cols]
        if i < rotated // LANES:
            tile = rotate(tile, cosine, sine)
        out_ref[:, cols] = tile.astype(bf16)


def rotate_columns(values, cosine, sine, rotated):
    return pl.pallas_call(
        functools.partial(rotate_columns_kernel, rotated),
        out_shape=jax.ShapeDtypeStruct(values.shape, bf16),
        compiler_params=pltpu.CompilerParams(vmem_limit_bytes=VMEM_LIMIT),
        name="rotate_columns",
    )(values, cosine, sine)


def pair_gradient_kernel(count, cosine_ref, sine_ref, *refs):
    out_ref = refs[-1]
    cosine, sine = cosine_ref[...], sine_ref[...]
    for i in range(2 * KEY_WIDTH // LANES):
        cols = slice(i * LANES, (i + 1) * LANES)
        total = refs[0][:, cols].astype(f32)
        for ref in refs[1:count]:
            total = total + ref[:, cols].astype(f32)
        if i < KEY_WIDTH // LANES:
            total = rotate(total, cosine, -sine)
        out_ref[:, cols] = total.astype(bf16)


def pair_gradient(parts, cosine, sine):
    return pl.pallas_call(
        functools.partial(pair_gradient_kernel, len(parts)),
        out_shape=jax.ShapeDtypeStruct(parts[0].shape, bf16),
        compiler_params=pltpu.CompilerParams(vmem_limit_bytes=VMEM_LIMIT),
        name="pair_gradient",
    )(cosine, sine, *parts)


def grouped(tiles, half):
    mine = lane_index(tiles[0].shape) // HEAD_SIZE == half
    rows = []
    for j in range(GROUP * half, GROUP * half + GROUP):
        tile = tiles[j // 2]
        if j % 2 != half:
            tile = pltpu.roll(tile, HEAD_SIZE, 1)
        rows.append(jnp.where(mine, tile, 0.0))
    return jnp.concatenate(rows, axis=0).astype(bf16)


def ungrouped(per_half, rows):
    heads = []
    for j in range(2 * GROUP):
        half, place = j // GROUP, j % GROUP
        tile = per_half[half][place * rows : (place + 1) * rows]
        if j % 2 != half:
            tile = pltpu.roll(tile, HEAD_SIZE, 1)
        heads.append(tile)
    low = lane_index(heads[0].shape) < HEAD_SIZE
    return [jnp.where(low, heads[2 * i], heads[2 * i + 1]) for i in range(GROUP)]


def query_tiles(query_ref):
    scale = 1.0 / HEAD_SIZE
    return [query_ref[:, i * LANES : (i + 1) * LANES].astype(f32) * scale for i in range(GROUP)]


def attention_pair(tiles, key, value, bias):
    rows = bias.shape[0]
    results = []
    for half in range(2):
        scores = dot(grouped(tiles, half), key, NT)
        scores = jnp.concatenate(
            [scores[g * rows : (g + 1) * rows] + bias for g in range(GROUP)], axis=0
        )
        peak = jnp.max(scores, axis=1, keepdims=True)
        weights = jnp.exp(scores - peak)
        total = jnp.sum(weights, axis=1, keepdims=True)
        results.append(dot(weights.astype(bf16), value) / total)
    return ungrouped(results, rows)


def attention_forward_kernel(query_ref, key_ref, value_ref, bias_ref, out_ref):
    tiles = attention_pair(query_tiles(query_ref), key_ref[...], value_ref[...], bias_ref[...])
    for i, tile in enumerate(tiles):
        out_ref[:, i * LANES : (i + 1) * LANES] = tile.astype(bf16)


def attention_forward(m, query, pairs, bias):
    rows, length = bias.shape
    return pl.pallas_call(
        attention_forward_kernel,
        grid=(PAIRS,),
        in_specs=[
            pl.BlockSpec((rows, PAIR_QUERY), lambda p: (m, p)),
            pl.BlockSpec((None, length, LANES), lambda p: (m, 0, p)),
            pl.BlockSpec((None, length, LANES), lambda p: (m, 0, p + PAIRS)),
            pl.BlockSpec((rows, length), lambda p: (0, 0)),
        ],
        out_specs=pl.BlockSpec((rows, PAIR_QUERY), lambda p: (0, p)),
        out_shape=jax.ShapeDtypeStruct((rows, MODEL_WIDTH), bf16),
        compiler_params=pltpu.CompilerParams(vmem_limit_bytes=VMEM_LIMIT),
        cost_estimate=pl.CostEstimate(
            flops=16 * rows * length * MODEL_WIDTH,
            bytes_accessed=4 * length * MODEL_WIDTH,
            transcendentals=rows * length * QUERY_HEADS,
        ),
        name="attention_forward",
    )(query, pairs, pairs, bias)


def attention_pair_gradient(tiles, grads, key, value, bias):
    rows = tiles[0].shape[0]
    key_grad, value_grad = None, None
    query_grads = []
    for half in range(2):
        query = grouped(tiles, half)
        grad = grouped(grads, half)
        scores = dot(key, query, NT) + bias
        weights = jnp.exp(scores - jnp.max(scores, axis=0, keepdims=True))
        prob = weights * (1.0 / jnp.sum(weights, axis=0, keepdims=True))
        prob_grad = dot(value, grad, NT)
        delta = jnp.sum(prob * prob_grad, axis=0, keepdims=True)
        score_grad = (prob * (prob_grad - delta)).astype(bf16)
        value_part = dot(prob.astype(bf16), grad)
        key_part = dot(score_grad, query)
        value_grad = value_part if half == 0 else value_grad + value_part
        key_grad = key_part if half == 0 else key_grad + key_part
        query_grads.append(dot(score_grad, key, TN))
    return ungrouped(query_grads, rows), key_grad, value_grad


def attention_backward_kernel(
    query_ref, cosine_ref, sine_ref, key_ref, value_ref, bias_ref, grad_ref, query_out, pair_out
):
    cosine, sine = cosine_ref[...], sine_ref[...]
    grads = [grad_ref[:, i * LANES : (i + 1) * LANES].astype(f32) for i in range(GROUP)]
    query_grads, key_grad, value_grad = attention_pair_gradient(
        query_tiles(query_ref), grads, key_ref[...], value_ref[...], bias_ref[...]
    )
    for i, tile in enumerate(query_grads):
        tile = rotate(tile * (1.0 / HEAD_SIZE), cosine, -sine)
        query_out[:, i * LANES : (i + 1) * LANES] = tile.astype(bf16)
    first = pl.multiple_of(pl.program_id(0) * LANES, LANES)
    pair_out[:, pl.ds(first, LANES)] = key_grad.astype(bf16)
    pair_out[:, pl.ds(first + KEY_WIDTH, LANES)] = value_grad.astype(bf16)


def attention_backward(m, query, cosine, sine, pairs, bias, grad):
    rows = cosine.shape[0]
    length = pairs.shape[1]
    whole = lambda shape: pl.BlockSpec(shape, lambda p: (0, 0))
    return pl.pallas_call(
        attention_backward_kernel,
        grid=(PAIRS,),
        in_specs=[
            pl.BlockSpec((rows, PAIR_QUERY), lambda p: (m, p)),
            whole((rows, LANES)),
            whole((rows, LANES)),
            pl.BlockSpec((None, length, LANES), lambda p: (m, 0, p)),
            pl.BlockSpec((None, length, LANES), lambda p: (m, 0, p + PAIRS)),
            whole(bias.shape),
            pl.BlockSpec((rows, PAIR_QUERY), lambda p: (0, p)),
        ],
        out_specs=[
            pl.BlockSpec((rows, PAIR_QUERY), lambda p: (0, p)),
            whole((length, 2 * KEY_WIDTH)),
        ],
        out_shape=[
            jax.ShapeDtypeStruct((rows, MODEL_WIDTH), bf16),
            jax.ShapeDtypeStruct((length, 2 * KEY_WIDTH), bf16),
        ],
        compiler_params=pltpu.CompilerParams(vmem_limit_bytes=VMEM_LIMIT),
        cost_estimate=pl.CostEstimate(
            flops=40 * rows * length * MODEL_WIDTH,
            bytes_accessed=8 * length * MODEL_WIDTH,
            transcendentals=rows * length * QUERY_HEADS,
        ),
        name="attention_backward",
    )(query, cosine, sine, pairs, pairs, bias, grad)


def expert_block(inputs, out_grad, combine, gate_weight, up_weight, down_weight):
    gate = dot(inputs, gate_weight)
    up = dot(inputs, up_weight)
    sigmoid = jax.nn.sigmoid(gate)
    silu = gate * sigmoid
    active = (silu * up * combine).astype(bf16)
    active_grad = dot(out_grad, down_weight, NT) * combine
    gate_grad = (active_grad * up * sigmoid * (1.0 + gate * (1.0 - sigmoid))).astype(bf16)
    up_grad = (active_grad * silu).astype(bf16)
    result = dot(active, down_weight)
    row_grad = dot(gate_grad, gate_weight, NT) + dot(up_grad, up_weight, NT)
    return active, gate_grad, up_grad, result, row_grad


def experts_kernel(parts, rows, steps, combine_ref, gate_ref, up_ref, down_ref, *refs):
    rows_in, grads_in = refs[:parts], refs[parts : 2 * parts]
    refs = refs[2 * parts :]
    results, row_grads = refs[:parts], refs[parts : 2 * parts]
    active_out, gate_out, up_out, rows_all, grads_all, result_sum, grad_sum = refs[2 * parts :]
    step = pl.program_id(0) * pl.num_programs(1) + pl.program_id(1)

    @pl.when(step == 0)
    def _():
        for k in range(parts):
            place = slice(k * rows, (k + 1) * rows)
            rows_all[place] = rows_in[k][...]
            grads_all[place] = grads_in[k][...]
        result_sum[...] = jnp.zeros_like(result_sum)
        grad_sum[...] = jnp.zeros_like(grad_sum)

    inputs, out_grad, combine = rows_all[...], grads_all[...], combine_ref[0]
    active, gate_grad, up_grad, result, row_grad = expert_block(
        inputs, out_grad, combine, gate_ref[0], up_ref[0], down_ref[0]
    )
    active_out[...] = active
    gate_out[...] = gate_grad
    up_out[...] = up_grad
    result_sum[...] += result
    grad_sum[...] += row_grad

    @pl.when(step == steps - 1)
    def _():
        for k in range(parts):
            place = slice(k * rows, (k + 1) * rows)
            results[k][...] = result_sum[place].astype(bf16)
            row_grads[k][...] = grad_sum[place].astype(bf16)


def experts(row_parts, grad_parts, combine, expert_in, expert_out):
    parts = len(row_parts)
    rows = row_parts[0].shape[0]
    held = expert_in.shape[0]
    tokens = parts * rows
    blocks = F // F_BLOCK
    whole = pl.BlockSpec((rows, MODEL_WIDTH), lambda e, b: (0, 0))
    piece = pl.BlockSpec((tokens, F_BLOCK), lambda e, b: (0, e * blocks + b))
    row_shape = jax.ShapeDtypeStruct((rows, MODEL_WIDTH), bf16)
    piece_shape = jax.ShapeDtypeStruct((tokens, held * F), bf16)
    out = pl.pallas_call(
        functools.partial(experts_kernel, parts, rows, held * blocks),
        grid=(held, blocks),
        in_specs=[
            pl.BlockSpec((1, tokens, 1), lambda e, b: (e, 0, 0)),
            pl.BlockSpec((1, MODEL_WIDTH, F_BLOCK), lambda e, b: (e, 0, b)),
            pl.BlockSpec((1, MODEL_WIDTH, F_BLOCK), lambda e, b: (e, 0, b + blocks)),
            pl.BlockSpec((1, F_BLOCK, MODEL_WIDTH), lambda e, b: (e, b, 0)),
        ]
        + [whole] * (2 * parts),
        out_specs=[whole] * (2 * parts) + [piece] * 3,
        out_shape=[row_shape] * (2 * parts) + [piece_shape] * 3,
        scratch_shapes=[
            pltpu.VMEM((tokens, MODEL_WIDTH), bf16),
            pltpu.VMEM((tokens, MODEL_WIDTH), bf16),
            pltpu.VMEM((tokens, MODEL_WIDTH), f32),
            pltpu.VMEM((tokens, MODEL_WIDTH), f32),
        ],
        compiler_params=pltpu.CompilerParams(vmem_limit_bytes=VMEM_LIMIT),
        cost_estimate=pl.CostEstimate(
            flops=12 * tokens * held * MODEL_WIDTH * F,
            bytes_accessed=6 * held * MODEL_WIDTH * F + 20 * tokens * MODEL_WIDTH,
            transcendentals=tokens * held * F,
        ),
        name="experts",
    )(combine, expert_in, expert_in, expert_out, *row_parts, *grad_parts)
    return out[:parts], out[parts : 2 * parts], out[2 * parts :]


def expert_weights_kernel(rows_ref, grads_ref, active_ref, gate_ref, up_ref, gate_out, up_out, down_out, turned):
    step = pl.program_id(0) * pl.num_programs(1) + pl.program_id(1)

    @pl.when(step == 0)
    def _():
        turned[...] = rows_ref[...].T

    gate_out[0] = dot(turned[...], gate_ref[...]).astype(bf16)
    up_out[0] = dot(turned[...], up_ref[...]).astype(bf16)
    down_out[0] = dot(active_ref[...], grads_ref[...], TN).astype(bf16)


def expert_weights(rows, grads, active, gate, up, held):
    tokens = rows.shape[0]
    blocks = F // F_BLOCK
    whole = pl.BlockSpec((tokens, MODEL_WIDTH), lambda e, b: (0, 0))
    piece = pl.BlockSpec((tokens, F_BLOCK), lambda e, b: (0, e * blocks + b))
    wide = pl.BlockSpec((1, MODEL_WIDTH, F_BLOCK), lambda e, b: (e, 0, b))
    return pl.pallas_call(
        expert_weights_kernel,
        grid=(held, blocks),
        in_specs=[whole] * 2 + [piece] * 3,
        out_specs=[wide, wide, pl.BlockSpec((1, F_BLOCK, MODEL_WIDTH), lambda e, b: (e, b, 0))],
        out_shape=[
            jax.ShapeDtypeStruct((held, MODEL_WIDTH, F), bf16),
            jax.ShapeDtypeStruct((held, MODEL_WIDTH, F), bf16),
            jax.ShapeDtypeStruct((held, F, MODEL_WIDTH), bf16),
        ],
        scratch_shapes=[pltpu.VMEM((MODEL_WIDTH, tokens), bf16)],
        compiler_params=pltpu.CompilerParams(vmem_limit_bytes=VMEM_LIMIT),
        cost_estimate=pl.CostEstimate(
            flops=6 * tokens * held * MODEL_WIDTH * F,
            bytes_accessed=6 * held * MODEL_WIDTH * F + 8 * tokens * MODEL_WIDTH,
            transcendentals=0,
        ),
        name="expert_weights",
    )(rows, grads, active, gate, up)


class Links:
    def __init__(self):
        self.shards = lax.axis_size("fsdp")
        self.contexts = lax.axis_size("ctx")
        self.chips = self.contexts // 2
        self.shard = lax.axis_index("fsdp")
        self.context = lax.axis_index("ctx")
        self.chip = self.context // 2
        self.core = self.context % 2

    def across(self, array, k):
        return lax.ppermute(array, "fsdp", [(i, i ^ k) for i in range(self.shards)])

    def other_core(self, array):
        return lax.ppermute(array, "ctx", [(i, i ^ 1) for i in range(self.contexts)])

    def shift(self, array, s):
        n = self.contexts
        return lax.ppermute(array, "ctx", [(i, (i + 2 * s) % n) for i in range(n)])


MESH = pl.DeviceIdType.MESH
LINE = 4


class Place:
    def __init__(self):
        self.shard, self.context = lax.axis_index("fsdp"), lax.axis_index("ctx")
        self.core, self.chip = self.context % 2, self.context // 2
        self.partner = {"ctx": 2 * self.chip + 1 - self.core}

    def peer_index(self, k):
        x, y = (self.shard % 2 + k % 2) % 2, (self.shard // 2 + k // 2) % 2
        return 2 * y + x

    def peer(self, k):
        return {"fsdp": self.peer_index(k)}

    def chip_device(self, chip):
        return {"ctx": 2 * chip + self.core}


def remote(source, target, sems, index, device):
    return pltpu.make_async_remote_copy(
        src_ref=source,
        dst_ref=target,
        send_sem=sems.at[0, index],
        recv_sem=sems.at[1, index],
        device_id=device,
        device_id_type=MESH,
    )


def greet(device):
    pl.semaphore_signal(pltpu.get_barrier_semaphore(), inc=1, device_id=device, device_id_type=MESH)


SHARDS = 4
GAIN_ROWS = 16


class Square:
    def __init__(self, place, blocks, direct_sem, relay_sem, base=0):
        half = blocks.shape[1] // 2
        own = blocks.at[place.shard]
        self.directs = [remote(own, own, direct_sem, base + k - 1, place.peer(k)) for k in (1, 2)]
        self.relays = []
        for k in (1, 2):
            spot = blocks.at[place.peer_index(k), (k - 1) * half : k * half]
            self.relays.append(remote(spot, spot, relay_sem, base + k - 1, place.peer(3 - k)))

    def start(self):
        for copy in self.directs:
            copy.start()

    def pass_on(self):
        for direct, relay in zip(self.directs, self.relays):
            direct.wait_recv()
            relay.start()

    def finish(self):
        for copy in self.relays:
            copy.wait_recv()

    def drain(self):
        for copy in self.directs + self.relays:
            copy.wait_send()


LAST = LINE - 1
WIDE = 4


def forward_kernel(
    tokens,
    routes,
    gates,
    gain_pair,
    cotangent,
    starts,
    tables,
    pair_src,
    query_src,
    output_src,
    expand_src,
    shrink_src,
    turned_normed,
    query,
    turned_attn,
    middle,
    gains,
    cosine,
    sine,
    pair_out,
    query_out,
    output_out,
    pairs,
    rows_out,
    grads_out,
    results_out,
    row_grads_out,
    active_out,
    gate_out,
    up_out,
    pair_weight,
    query_weight,
    output_weight,
    expand,
    shrink,
    own_pairs,
    normed,
    combine_in,
    combine_own,
    attn,
    bias,
    combine,
    rows_all,
    grads_all,
    result_sum,
    grad_sum,
    key_value,
    load_sem,
    table_sem,
    store_sem,
    expert_sem,
    gain_sem,
    combine_sem,
    direct_sem,
    relay_sem,
    pass_sem,
    right_sem,
    left_sem,
    core_sem,
    own_sem,
    square_direct_sem,
    square_relay_sem,
    key_sem,
    emit_sem,
):
    r = types.SimpleNamespace(**locals())
    place = Place()
    core, chip, shard = place.core, place.chip, place.shard
    local = pltpu.make_async_copy
    rows = r.cosine.shape[0]
    wide = SHARDS * rows
    held = r.pair_src.shape[0]
    half, quarter = held // 2, held // 4
    greet_line(place)
    length = r.bias.shape[2]

    def rows_of(owner, piece, size):
        return pl.ds(pl.multiple_of(owner * held + core * half, half) + piece, size)

    sources = (r.pair_src, r.query_src, r.output_src)
    weights = (r.pair_weight, r.query_weight, r.output_weight)
    weight_outs = (r.pair_out, r.query_out, r.output_out)
    loads, directs, relays, passes, stores = [], [], [], [], []
    for w in range(3):
        weight = weights[w]
        own_rows = pl.ds(pl.multiple_of(shard * held, held), held)
        loads.append(local(sources[w], weight.at[own_rows], r.load_sem.at[w]))
        stores.append(local(weight, weight_outs[w], r.store_sem.at[w]))
        mine = sources[w].at[pl.ds(pl.multiple_of(core * half, half), half)]
        spot = weight.at[rows_of(shard, 0, half)]
        directs.append([remote(mine, spot, r.direct_sem, 2 * w + k - 1, place.peer(k)) for k in (1, 2)])
        relay, onward = [], []
        for k in (1, 2):
            spot = weight.at[rows_of(place.peer_index(k), (k - 1) * quarter, quarter)]
            relay.append(remote(spot, spot, r.relay_sem, 2 * w + k - 1, place.peer(3 - k)))
            spot = weight.at[rows_of(place.peer_index(k), 0, half)]
            onward.append(remote(spot, spot, r.pass_sem, 4 * w + k - 1, place.partner))
        for k in (1, 2):
            spot = weight.at[rows_of(place.peer_index(3), (k - 1) * quarter, quarter)]
            onward.append(remote(spot, spot, r.pass_sem, 4 * w + k + 1, place.partner))
        relays.append(relay)
        passes.append(onward)

    def send_weight(w):
        for copy in directs[w]:
            copy.start()

    def relay_weight(w):
        for k in (1, 2):
            directs[w][k - 1].wait_recv()
            relays[w][k - 1].start()
        for k in (1, 2):
            passes[w][k - 1].start()

    def pass_weight(w):
        for k in (1, 2):
            relays[w][k - 1].wait_recv()
            passes[w][k + 1].start()

    def settle_weight(w):
        loads[w].wait()
        for copy in passes[w]:
            copy.wait_recv()
        stores[w].start()

    def sent_weight(w):
        for copy in directs[w] + relays[w] + passes[w]:
            copy.wait_send()
        stores[w].wait()

    send_weight(0)

    gain_rows = r.gains.at[pl.ds(pl.multiple_of(shard * GAIN_ROWS, GAIN_ROWS), GAIN_ROWS)]
    gain_rows[...] = jnp.concatenate([r.gain_pair[...], jnp.zeros((GAIN_ROWS - 2, held), bf16)], axis=0)
    expert_row = lax.broadcasted_iota(jnp.int32, (E, rows), 0)
    for m in range(MB):
        combine = jnp.zeros((E, rows), f32)
        for k in range(TOP):
            combine += jnp.where(expert_row == r.routes[m, k : k + 1], r.gates[m, k : k + 1], 0.0)
        r.combine_own[:, m * rows : (m + 1) * rows] = combine
    r.combine_in[shard] = r.combine_own[...]
    small_copies = []
    for k in range(1, SHARDS):
        small_copies.append(remote(gain_rows, gain_rows, r.gain_sem, k - 1, place.peer(k)))
        small_copies.append(remote(r.combine_own, r.combine_in.at[shard], r.combine_sem, k - 1, place.peer(k)))

    for copy in small_copies:
        copy.start()
    at = pl.ds(pl.multiple_of(place.context * rows, rows), rows)
    table_loads = [
        local(r.tables.at[i, at], table, r.table_sem.at[i]) for i, table in enumerate((r.cosine, r.sine))
    ]
    for load in table_loads + loads:
        load.start()
    expert_loads = [
        local(r.expand_src, r.expand, r.expert_sem.at[0]),
        local(r.shrink_src, r.shrink, r.expert_sem.at[1]),
    ]
    for load in expert_loads:
        load.start()
    for m in range(MB):
        r.grads_all[m, shard] = r.cotangent[m * rows : (m + 1) * rows]
    grad_squares = [Square(place, r.grads_all.at[m], r.square_direct_sem, r.square_relay_sem, 2 * m) for m in range(MB)]
    row_squares = [
        Square(place, r.rows_all.at[m], r.square_direct_sem, r.square_relay_sem, 2 * (MB + m)) for m in range(MB)
    ]

    def gain_times(values, row, write):
        for b in range(SHARDS):
            columns = slice(b * held, (b + 1) * held)
            at = b * GAIN_ROWS + row
            write(columns, (values[:, columns] * r.gains[at : at + 1].astype(f32)).astype(bf16))

    values = r.tokens[...].astype(f32)
    unit = values * lax.rsqrt(jnp.mean(values * values, axis=-1, keepdims=True) + eps)
    for copy in small_copies:
        copy.wait_recv()

    def write_normed(columns, value):
        r.normed[:, columns] = value

    gain_times(unit, 0, write_normed)
    r.turned_normed[...] = r.normed[...].T
    for b in range(SHARDS):
        spread = jnp.concatenate([r.combine_in[b], jnp.zeros((LANES - E, MB * rows), f32)], axis=0)
        r.combine[b] = spread.T
    for m in range(MB):
        r.bias[m] = visible_bias(r.starts, m, place.context, (rows, length), 0)
    for load in table_loads:
        load.wait()

    relay_weight(0)
    send_weight(1)
    pass_weight(0)
    settle_weight(0)
    cosine, sine = r.cosine[...], r.sine[...]

    def project(weight, column, rotated):
        result = dot(r.normed[...], weight[:, pl.ds(column, WIDE * LANES)])
        tiles = []
        for m in range(MB):
            for i in range(WIDE):
                tile = result[m * rows : (m + 1) * rows, i * LANES : (i + 1) * LANES]
                tiles.append((m, i, rotate(tile, cosine, sine) if rotated else tile))
        return tiles

    blocks = KEY_WIDTH // (WIDE * LANES)
    for b in range(2 * blocks):
        column = b * WIDE * LANES
        for m, i, tile in project(r.pair_weight, column, b < blocks):
            r.own_pairs[m, :, pl.ds(column + i * LANES, LANES)] = tile.astype(bf16)

    def chunk(m, owner):
        owner = jnp.clip(owner, 0, LAST)
        return r.pairs.at[m, pl.ds(pl.multiple_of((2 * owner + core) * rows, rows), rows)]

    def move(m, t, direction):
        target = chunk(m, chip - direction * (t - 1))
        source = r.own_pairs.at[m] if t == 1 else target
        sems = r.right_sem if direction > 0 else r.left_sem
        device = place.chip_device(jnp.clip(chip + direction, 0, LAST))
        return remote(source, target, sems, m * LAST + t - 1, device)

    def sends(t, direction):
        owner = chip - direction * (t - 1)
        if direction > 0:
            return (chip < LAST) & (owner >= 0)
        return (chip > 0) & (owner <= LAST)

    def gets(t, direction):
        owner = chip - direction * t
        return owner >= 0 if direction > 0 else owner <= LAST

    def came(m, t, direction):
        spot = chunk(m, chip - direction * t)
        sems = r.right_sem if direction > 0 else r.left_sem
        return remote(spot, spot, sems, m * LAST + t - 1, place.partner)

    def pass_chunk(m, t, direction):
        spot = chunk(m, chip - direction * t)
        index = (m * LINE + t) * 2 + (1 if direction > 0 else 0)
        return remote(spot, spot, r.core_sem, index, place.partner)

    def take_step(m, t):
        for direction in (1, -1):

            @pl.when(gets(t, direction))
            def _():
                came(m, t, direction).wait_recv()
                if t < LAST:

                    @pl.when(sends(t + 1, direction))
                    def _():
                        move(m, t + 1, direction).start()

                pass_chunk(m, t, direction).start()

    own_copies = []
    for m in range(MB):
        for direction in (1, -1):

            @pl.when(sends(1, direction))
            def _():
                move(m, 1, direction).start()

        own_copies.append(
            (
                local(r.own_pairs.at[m], chunk(m, chip), r.own_sem.at[m]),
                remote(r.own_pairs.at[m], chunk(m, chip), r.core_sem, m * LINE * 2, place.partner),
            )
        )
        for copy in own_copies[m]:
            copy.start()

    def settle_pairs(m):
        own_copies[m][0].wait()
        own_copies[m][1].wait()
        for t in range(1, LINE):
            for direction in (1, -1):

                @pl.when(gets(t, direction))
                def _():
                    pass_chunk(m, t, direction).wait()

    def query_block(b, carry):
        column = pl.multiple_of(b * WIDE * LANES, WIDE * LANES)
        for m, i, tile in project(r.query_weight, column, True):
            r.query[m * rows : (m + 1) * rows, pl.ds(column + i * LANES, LANES)] = tile.astype(bf16)
        return carry

    def key_load(m, p, slot, i):
        lane = pl.multiple_of(p * LANES, LANES) + i * KEY_WIDTH
        return local(r.pairs.at[m, :, pl.ds(lane, LANES)], r.key_value.at[slot, i], r.key_sem.at[slot, i])

    def attend(m):
        own = slice(m * rows, (m + 1) * rows)
        for i in range(2):
            key_load(m, 0, 0, i).start()

        def pair(p, carry):
            slot = p % 2
            for i in range(2):
                key_load(m, p, slot, i).wait()

            @pl.when(p + 1 < PAIRS)
            def _():
                for i in range(2):
                    key_load(m, p + 1, 1 - slot, i).start()

            column = pl.multiple_of(p * PAIR_QUERY, PAIR_QUERY)
            columns = [pl.ds(column + i * LANES, LANES) for i in range(GROUP)]
            tiles = [r.query[own, c].astype(f32) * (1.0 / HEAD_SIZE) for c in columns]
            results = attention_pair(tiles, r.key_value[slot, 0], r.key_value[slot, 1], r.bias[m])
            for c, tile in zip(columns, results):
                r.attn[own, c] = tile.astype(bf16)
            return carry

        lax.fori_loop(0, PAIRS, pair, 0)
        r.turned_attn[:, own] = r.attn[own].T

    def finish_attention(m):
        own = slice(m * rows, (m + 1) * rows)
        middle = r.tokens[own].astype(f32) + dot(r.attn[own], r.output_weight[...])
        r.middle[own] = middle
        unit = middle * lax.rsqrt(jnp.mean(middle * middle, axis=-1, keepdims=True) + eps)

        def write(columns, value):
            r.rows_all[m, shard, :, columns] = value

        gain_times(unit, 1, write)

    active, gate, up = [r.pair_weight.at[i * wide : (i + 1) * wide] for i in range(3)]
    results, row_grads = [r.query_weight.at[i * wide : (i + 1) * wide] for i in range(2)]

    def emits(m):
        pairs = (
            (r.rows_all.at[m], r.rows_out.at[m]),
            (r.grads_all.at[m], r.grads_out.at[m]),
            (results, r.results_out.at[m]),
            (row_grads, r.row_grads_out.at[m]),
            (active, r.active_out.at[m]),
            (gate, r.gate_out.at[m]),
            (up, r.up_out.at[m]),
        )
        return [local(a, b, r.emit_sem.at[m * len(pairs) + i]) for i, (a, b) in enumerate(pairs)]

    def expert_steps(m, between):
        steps = [(e, b) for e in range(r.expand.shape[0]) for b in range(F // F_BLOCK)]
        for i, (e, b) in enumerate(steps):
            weight = r.combine[:, m * rows : (m + 1) * rows, :].reshape(wide, LANES)
            expert = shard * r.expand.shape[0] + e
            chosen = jnp.where(lane_index(weight.shape) == expert, weight, 0.0)
            columns = slice(b * F_BLOCK, (b + 1) * F_BLOCK)
            up_columns = slice(F + b * F_BLOCK, F + (b + 1) * F_BLOCK)
            a, g, u, result, row_grad = expert_block(
                r.rows_all[m].reshape(wide, MODEL_WIDTH),
                r.grads_all[m].reshape(wide, MODEL_WIDTH),
                jnp.sum(chosen, axis=1, keepdims=True),
                r.expand[e, :, columns],
                r.expand[e, :, up_columns],
                r.shrink[e, columns, :],
            )
            spot = slice(e * F + b * F_BLOCK, e * F + (b + 1) * F_BLOCK)
            active[:, spot], gate[:, spot], up[:, spot] = a, g, u
            if i == 0:
                r.result_sum[...] = result
                r.grad_sum[...] = row_grad
            elif i < len(steps) - 1:
                r.result_sum[...] += result
                r.grad_sum[...] += row_grad
            else:
                results[...] = (r.result_sum[...] + result).astype(bf16)
                row_grads[...] = (r.grad_sum[...] + row_grad).astype(bf16)
            if i in between:
                between[i]()

    relay_weight(1)
    send_weight(2)
    take_step(0, 1)
    take_step(1, 1)
    pass_weight(1)
    take_step(0, 2)
    settle_weight(1)
    lax.fori_loop(0, MODEL_WIDTH // (WIDE * LANES), query_block, 0)
    relay_weight(2)
    grad_squares[0].start()
    take_step(1, 2)
    take_step(0, 3)
    settle_pairs(0)
    attend(0)
    pass_weight(2)
    grad_squares[0].pass_on()
    take_step(1, 3)
    settle_weight(2)
    finish_attention(0)
    row_squares[0].start()
    settle_pairs(1)
    attend(1)
    row_squares[0].pass_on()
    finish_attention(1)
    row_squares[1].start()
    grad_squares[1].start()
    for load in expert_loads:
        load.wait()
    sent_weight(0)
    sent_weight(1)
    grad_squares[0].finish()
    row_squares[0].finish()
    expert_steps(0, {1: row_squares[1].pass_on})
    for emit in emits(0):
        emit.start()
    grad_squares[1].pass_on()
    row_squares[1].finish()
    for emit in emits(0):
        emit.wait()
    grad_squares[1].finish()
    expert_steps(1, {})
    for emit in emits(1):
        emit.start()

    for copy in small_copies:
        copy.wait_send()
    sent_weight(2)
    for m in range(MB):
        for t in range(1, LINE):
            for direction in (1, -1):

                @pl.when(sends(t, direction))
                def _():
                    move(m, t, direction).wait_send()

    for square in grad_squares + row_squares:
        square.drain()
    for emit in emits(1):
        emit.wait()


def forward(tokens, routes, gates, gain_pair, cotangent, starts, tables, weights, expert_in, expert_out):
    rows = tokens.shape[0] // MB
    length = tables.shape[1]
    wide = SHARDS * rows
    held = weights[0].shape[0]
    dma = pltpu.SemaphoreType.DMA
    anywhere = pl.BlockSpec(memory_space=pl.ANY)
    vmem = pl.BlockSpec(memory_space=pltpu.VMEM)
    shape = jax.ShapeDtypeStruct
    low = lambda *s: pltpu.VMEM(s, bf16)
    full = [(SHARDS * held, w.shape[1]) for w in weights]
    blocks = (MB, SHARDS, rows, MODEL_WIDTH)
    return pl.pallas_call(
        forward_kernel,
        in_specs=[vmem] * 5 + [pl.BlockSpec(memory_space=pltpu.SMEM)] + [anywhere] * 6,
        out_specs=[vmem] * 7 + [anywhere] * 11,
        out_shape=[
            shape(tokens.shape[::-1], bf16),
            shape(tokens.shape, bf16),
            shape(tokens.shape[::-1], bf16),
            shape(tokens.shape, f32),
            shape((SHARDS * GAIN_ROWS, held), bf16),
            shape((rows, LANES), f32),
            shape((rows, LANES), f32),
        ]
        + [shape(f, bf16) for f in full]
        + [
            shape((MB, length, 2 * KEY_WIDTH), bf16),
            shape(blocks, bf16),
            shape(blocks, bf16),
            shape((MB, wide, MODEL_WIDTH), bf16),
            shape((MB, wide, MODEL_WIDTH), bf16),
        ]
        + [shape((MB, wide, 2 * F), bf16)] * 3,
        scratch_shapes=[low(*f) for f in full]
        + [
            low(*expert_in.shape),
            low(*expert_out.shape),
            low(MB, rows, 2 * KEY_WIDTH),
            low(*tokens.shape),
            pltpu.VMEM((SHARDS, E, MB * rows), f32),
            pltpu.VMEM((E, MB * rows), f32),
            low(*tokens.shape),
            pltpu.VMEM((MB, rows, length), f32),
            pltpu.VMEM((SHARDS, MB * rows, LANES), f32),
            low(*blocks),
            low(*blocks),
            pltpu.VMEM((wide, MODEL_WIDTH), f32),
            pltpu.VMEM((wide, MODEL_WIDTH), f32),
            low(2, 2, length, LANES),
            dma((3,)),
            dma((2,)),
            dma((3,)),
            dma((2,)),
            dma((2, SHARDS - 1)),
            dma((2, SHARDS - 1)),
            dma((2, 6)),
            dma((2, 6)),
            dma((2, 12)),
            dma((2, MB * LAST)),
            dma((2, MB * LAST)),
            dma((2, 2 * MB * LINE)),
            dma((MB,)),
            dma((2, 4 * MB)),
            dma((2, 4 * MB)),
            dma((2, 2)),
            dma((7 * MB,)),
        ],
        compiler_params=pltpu.CompilerParams(
            collective_id=1, has_side_effects=True, vmem_limit_bytes=VMEM_LIMIT
        ),
        name="forward",
    )(tokens, routes, gates, gain_pair, cotangent, starts, tables, *weights, expert_in, expert_out)


ADD_ROWS = 64


def add_into(out, *parts):
    rows = out.shape[0]
    size = max(d for d in range(16, ADD_ROWS + 1, 16) if rows % d == 0)

    def body(i, carry):
        spot = pl.ds(pl.multiple_of(i * size, size), size)
        total = parts[0][spot].astype(f32)
        for part in parts[1:]:
            total = total + part[spot].astype(f32)
        out[spot] = total.astype(out.dtype)
        return carry

    lax.fori_loop(0, rows // size, body, 0)


def greet_line(place):
    has_left, has_right = place.chip > 0, place.chip < LINE - 1
    greet(place.partner)
    for k in range(1, SHARDS):
        greet(place.peer(k))

    @pl.when(has_left)
    def _():
        greet(place.chip_device(place.chip - 1))

    @pl.when(has_right)
    def _():
        greet(place.chip_device(place.chip + 1))

    neighbours = jnp.where(has_left, 1, 0) + jnp.where(has_right, 1, 0)
    pl.semaphore_wait(pltpu.get_barrier_semaphore(), SHARDS + neighbours)


class Line:
    def __init__(self, place, pieces, sems):
        near_sem, far_sem, back_sem, pass_sem, store_sem = sems
        chip = place.chip
        self.inner = (chip == 1) | (chip == 2)
        outer = place.chip_device(3 * (chip // 2))
        inner = place.chip_device(1 + chip // 2)
        facing = place.chip_device(3 - chip)
        self.pieces = pieces
        numbered = list(enumerate(pieces))
        self.inward = [remote(p[0], p[1], near_sem, i, inner) for i, p in numbered]
        self.facing = [remote(p[0], p[2], far_sem, i, facing) for i, p in numbered]
        self.outward = [remote(p[1], p[3], back_sem, i, outer) for i, p in numbered]
        self.pass_inner = [remote(p[1], p[3], pass_sem, i, place.partner) for i, p in numbered]
        self.pass_outer = [remote(p[3], p[3], pass_sem, i, place.partner) for i, p in numbered]
        self.stores = [pltpu.make_async_copy(p[1], p[3], store_sem.at[i]) for i, p in numbered]

    def ready(self, *items):
        @pl.when(jnp.logical_not(self.inner))
        def _():
            for i in items:
                self.inward[i].start()

    def serve(self, halfway=(), finish=(), forward=()):
        @pl.when(self.inner)
        def _():
            for i in halfway:
                self.inward[i].wait_recv()
                own, near = self.pieces[i][:2]
                add_into(own, own, near)
                self.facing[i].start()
            for i in finish:
                self.facing[i].wait_recv()
                own, near, far = self.pieces[i][:3]
                add_into(near, own, far)
                self.outward[i].start()
                self.pass_inner[i].start()
                self.stores[i].start()

        @pl.when(jnp.logical_not(self.inner))
        def _():
            for i in forward:
                self.outward[i].wait_recv()
                self.pass_outer[i].start()

    def drain(self):
        @pl.when(self.inner)
        def _():
            for i in range(len(self.pieces)):
                self.facing[i].wait_send()
                self.outward[i].wait_send()
                self.pass_inner[i].wait_send()
                self.stores[i].wait()

        @pl.when(jnp.logical_not(self.inner))
        def _():
            for i in range(len(self.pieces)):
                self.inward[i].wait_send()
                self.pass_outer[i].wait_send()

        for copy in self.pass_outer:
            copy.wait_recv()


def line_sems(number):
    dma = pltpu.SemaphoreType.DMA
    return [dma((2, number))] * 4 + [dma((number,))]


def split_rows(ref, parts):
    size = ref.shape[0] // parts
    return [ref.at[j * size : (j + 1) * size] for j in range(parts)]


def out_halves(place, ref, parts):
    half = ref.shape[0] // 2
    size = half // parts
    first = pl.multiple_of(place.core * half, half)
    return [ref.at[pl.ds(first + j * size, size)] for j in range(parts)]


def line_pieces(place, own, near, far, out, parts):
    return list(
        zip(split_rows(own, parts), split_rows(near, parts), split_rows(far, parts), out_halves(place, out, parts))
    )


class PairSum:
    def __init__(self, place, own, sources, others, lands, core_sem, left_sem):
        self.place, self.own, self.others, self.lands, self.left_sem = place, own, others, lands, left_sem
        self.trades = [remote(sources(j), others.at[j], core_sem, j, place.partner) for j in range(LINE)]
        self.past = LAST - place.chip

    def trade(self):
        for copy in self.trades:
            copy.start()

    def move(self, t):
        owner = jnp.clip(self.place.chip - (LINE - t), 0, LAST)
        device = self.place.chip_device(jnp.clip(self.place.chip - 1, 0, LAST))
        return remote(self.own(owner), self.lands.at[t - 1], self.left_sem, t - 1, device)

    def meet(self):
        for j in range(LINE):
            self.trades[j].wait_recv()
            add_into(self.own(j), self.own(j), self.others.at[j])

        @pl.when(self.past == 0)
        def _():
            for t in range(1, LINE):
                self.move(t).start()

    def take(self, t):
        self.move(t).wait_recv()
        owner = jnp.clip(self.place.chip - (LAST - t), 0, LAST)
        add_into(self.own(owner), self.own(owner), self.lands.at[t - 1])

    def step(self, t):
        @pl.when((self.past >= 1) & (self.past <= min(t - 1, LINE - 2)))
        def _():
            self.take(t - 1)
            self.move(t).start()

    def finish(self, out, cosine, sine):
        @pl.when(self.past >= 1)
        def _():
            self.take(LAST)

        mine = self.own(self.place.chip)
        for i in range(2 * KEY_WIDTH // LANES):
            columns = slice(i * LANES, (i + 1) * LANES)
            tile = mine[:, columns]
            if i < KEY_WIDTH // LANES:
                tile = rotate(tile.astype(f32), cosine[...], -sine[...]).astype(bf16)
            out[:, columns] = tile

    def drain(self):
        for copy in self.trades:
            copy.wait_send()
        for t in range(1, LINE):

            @pl.when((self.past <= t - 1) & (self.past <= LINE - 2))
            def _():
                self.move(t).wait_send()


PARTS = 4


def backward_kernel(
    query,
    starts,
    cosine,
    sine,
    middle,
    cotangent,
    gain,
    pairs,
    rows_src,
    grads_src,
    active_src,
    gate_src,
    up_src,
    results_src,
    row_grads_src,
    output_src,
    query_low,
    pair_low,
    middle_low,
    middle_grad,
    gain_grad,
    block_output,
    gate_total,
    up_total,
    gate_rest,
    up_rest,
    down_rest,
    pair_grad,
    rows,
    turned,
    grads,
    pool,
    send_gate,
    send_up,
    send_down,
    own_gate,
    own_up,
    own_down,
    other_gate,
    other_up,
    other_down,
    near_gate,
    near_up,
    far_gate,
    far_up,
    row_grad_own,
    row_grad_in,
    result_own,
    result_in,
    attn_grad,
    key_value,
    bias,
    pair_other,
    land_left,
    load_sem,
    weight_sem,
    trade_sem,
    rest_sem,
    row_sem,
    result_sem,
    key_sem,
    core_sem,
    left_sem,
    near_sem,
    far_sem,
    back_sem,
    pass_sem,
    store_sem,
):
    r = types.SimpleNamespace(**locals())
    place = Place()
    core, chip, shard = place.core, place.chip, place.shard
    rows = r.cosine.shape[0]
    tokens = MB * SHARDS * rows
    side = MODEL_WIDTH // 2
    local = pltpu.make_async_copy

    wide = SHARDS * rows
    loads = []

    def load(source, target):
        loads.append(local(source, target, r.load_sem.at[len(loads)]))
        loads[-1].start()
        return loads[-1]

    flat = lambda ref, m: [(ref.at[m, k], m * wide + k * rows) for k in range(SHARDS)]
    row_loads, grad_loads, piece_loads = [], [], []
    for m in range(MB):
        for source, at in flat(r.rows_src, m):
            row_loads.append(load(source, r.rows.at[at : at + rows]))
        for source, at in flat(r.grads_src, m):
            grad_loads.append(load(source, r.grads.at[at : at + rows]))
    for i, ref in enumerate((r.active_src, r.gate_src, r.up_src)):
        for m in range(MB):
            at = i * tokens + m * wide
            piece_loads.append(load(ref.at[m], r.pool.at[at : at + wide]))
    own_loads = [load(r.row_grads_src.at[m, shard], r.row_grad_own.at[m]) for m in range(MB)]
    own_loads.append(load(r.results_src.at[0, shard], r.result_own))

    greet_line(place)

    row_copies, result_copies = [], []
    for m in range(MB):
        for k in range(1, SHARDS):
            i = m * (SHARDS - 1) + k - 1
            at = place.peer_index(k)
            row_copies.append(
                remote(r.row_grads_src.at[m, at], r.row_grad_in.at[m, k - 1], r.row_sem, i, place.peer(k))
            )
            if m == 0:
                result_copies.append(
                    remote(r.results_src.at[m, at], r.result_in.at[k - 1], r.result_sem, i, place.peer(k))
                )
    for copy in row_copies:
        copy.start()

    for m in range(MB):
        r.bias[m] = visible_bias(r.starts, m, place.context, r.bias.shape[1:], 1)

    for copy in row_loads:
        copy.wait()
    r.turned[...] = r.rows[...].T
    sends = (r.send_gate, r.send_up, r.send_down)
    owns = (r.own_gate, r.own_up, r.own_down)
    others = (r.other_gate, r.other_up, r.other_down)
    trades = [
        [remote(sends[i], others[i].at[b], r.trade_sem, b * 3 + i, place.partner) for i in range(3)]
        for b in range(2)
    ]

    def weight_block(b, expert, outs):
        column = pl.ds(pl.multiple_of(expert * F + b * F_BLOCK, F_BLOCK), F_BLOCK)
        for i in range(2):
            outs[i][...] = dot(r.turned[...], r.pool[(i + 1) * tokens : (i + 2) * tokens, column]).astype(bf16)

    def down_block(b, expert, out):
        column = pl.ds(pl.multiple_of(expert * F + b * F_BLOCK, F_BLOCK), F_BLOCK)
        out[...] = dot(r.pool[0:tokens, column], r.grads[...], TN).astype(bf16)

    def meet(b, i):
        trades[b][i].wait_recv()
        add_into(owns[i].at[b], owns[i].at[b], others[i].at[b])

    pieces = []
    for own, near, far, out in (
        (r.own_gate.at[0], r.near_gate, r.far_gate, r.gate_total),
        (r.own_up.at[0], r.near_up, r.far_up, r.up_total),
    ):
        pieces += line_pieces(place, own, near, far, out, PARTS)
    line = Line(place, pieces, (r.near_sem, r.far_sem, r.back_sem, r.pass_sem, r.store_sem))

    for copy in piece_loads[MB:]:
        copy.wait()
    for b in range(2):
        if b == 1:
            for i in range(2):
                trades[0][i].wait_send()
        weight_block(b, 1 - core, sends)
        for i in range(2):
            trades[b][i].start()
        weight_block(b, core, [own.at[b] for own in owns[:2]])
        if b == 0:
            for i in range(2):
                meet(0, i)
                line.ready(*range(i * PARTS, (i + 1) * PARTS))
            for copy in piece_loads[:MB] + grad_loads:
                copy.wait()
        else:
            trades[0][2].wait_send()
        down_block(b, 1 - core, sends[2])
        trades[b][2].start()
        down_block(b, core, owns[2].at[b])
        if b == 0:
            meet(0, 2)

    weight_loads = []
    for i in range(2):
        source = r.output_src.at[:, i * side : (i + 1) * side]
        target = r.pool.at[i * MODEL_WIDTH : (i + 1) * MODEL_WIDTH, 0:side]
        weight_loads.append(local(source, target, r.weight_sem.at[i]))
        weight_loads[-1].start()
    for copy in result_copies:
        copy.start()
    for i in range(3):
        meet(1, i)
    rests = [
        local(r.own_gate.at[1], r.gate_rest, r.rest_sem.at[0]),
        local(r.own_up.at[1], r.up_rest, r.rest_sem.at[1]),
        local(r.own_down, r.down_rest, r.rest_sem.at[2]),
    ]
    for copy in rests:
        copy.start()

    r.gain_grad[...] = jnp.zeros_like(r.gain_grad)

    def prepare(m):
        own = slice(m * rows, (m + 1) * rows)
        own_loads[m].wait()
        moe_in_grad = r.row_grad_own[m].astype(f32)
        for k in range(1, SHARDS):
            row_copies[m * (SHARDS - 1) + k - 1].wait_recv()
            moe_in_grad = moe_in_grad + r.row_grad_in[m, k - 1].astype(f32)
        middle = r.middle[own]
        scale = lax.rsqrt(jnp.mean(middle * middle, axis=-1, keepdims=True) + eps)
        unit = middle * scale
        r.gain_grad[m : m + 1] = jnp.sum(moe_in_grad * unit, axis=0, keepdims=True)
        weighted = moe_in_grad * r.gain[...]
        inner = jnp.mean(weighted * unit, axis=-1, keepdims=True)
        middle_grad = r.cotangent[own].astype(f32) + (weighted - unit * inner) * scale
        r.middle_grad[own] = middle_grad
        r.middle_low[own] = middle_grad.astype(bf16)
        if m == 0:
            for copy in weight_loads:
                copy.wait()
        total = dot(r.middle_low[own, 0:side], r.pool[0:MODEL_WIDTH, 0:side], NT)
        total = total + dot(r.middle_low[own, side:], r.pool[MODEL_WIDTH : 2 * MODEL_WIDTH, 0:side], NT)
        r.attn_grad[m] = total.astype(bf16)

    def key_load(step, slot, i):
        m, p = step // PAIRS, step % PAIRS
        lane = pl.multiple_of(p * LANES, LANES) + i * KEY_WIDTH
        return local(r.pairs.at[m, :, pl.ds(lane, LANES)], r.key_value.at[slot, i], r.key_sem.at[slot, i])

    pair_grads = (r.rows.at[:, 0 : 2 * KEY_WIDTH], r.grads.at[:, 0 : 2 * KEY_WIDTH])

    def chunk(of_chip, of_core):
        return pair_grads[0].at[pl.ds(pl.multiple_of((2 * of_chip + of_core) * rows, rows), rows)]

    pair_sum = PairSum(
        place,
        lambda j: chunk(j, core),
        lambda j: chunk(j, 1 - core),
        r.pair_other,
        r.land_left,
        r.core_sem,
        r.left_sem,
    )

    def pair_step(step, carry):
        m, p = step // PAIRS, step % PAIRS
        slot = step % 2
        for i in range(2):
            key_load(step, slot, i).wait()

        @pl.when(step + 1 < MB * PAIRS)
        def _():
            for i in range(2):
                key_load(step + 1, 1 - slot, i).start()

        at = pl.multiple_of(m * rows, rows)
        column = pl.multiple_of(p * PAIR_QUERY, PAIR_QUERY)
        lane = pl.multiple_of(p * LANES, LANES)
        columns = [pl.ds(column + i * LANES, LANES) for i in range(GROUP)]
        scale = 1.0 / HEAD_SIZE
        tiles = [r.query[pl.ds(at, rows), c].astype(f32) * scale for c in columns]
        grads = [r.attn_grad[m, :, c].astype(f32) for c in columns]
        bias = jnp.concatenate([r.bias[m]] * GROUP, axis=1)
        query_grads, key_grad, value_grad = attention_pair_gradient(
            tiles, grads, r.key_value[slot, 0], r.key_value[slot, 1], bias
        )
        for c, tile in zip(columns, query_grads):
            tile = rotate(tile * scale, r.cosine[...], -r.sine[...])
            r.query_low[pl.ds(at, rows), c] = tile.astype(bf16)
        key_low, value_low = key_grad.astype(bf16), value_grad.astype(bf16)
        for micro in range(MB):

            @pl.when(m == micro)
            def _():
                pair_grads[micro][:, pl.ds(lane, LANES)] = key_low
                pair_grads[micro][:, pl.ds(lane + KEY_WIDTH, LANES)] = value_low

        for at_step, actions in SERVICE:

            @pl.when(step == at_step)
            def _():
                for action in actions:
                    action()

        return carry

    serve = line.serve
    SERVICE = (
        (0, (lambda: serve([3], [0]),)),
        (1, (lambda: serve([], [1]),)),
        (2, (lambda: serve([4], [2, 3]),)),
        (3, (pair_sum.trade, lambda: prepare(1), lambda: serve([5, 6], [4], [0, 1]), pair_sum.meet)),
        (4, (lambda: serve([7], [], [2]),)),
        (5, (lambda: pair_sum.step(2), lambda: serve([], [5, 6], [3]))),
        (6, (lambda: serve([], [7], [4]),)),
        (7, (lambda: pair_sum.step(3), lambda: serve([], [], [5]))),
    )
    for i in range(2):
        key_load(0, 0, i).start()
    serve([0])
    prepare(0)
    serve([1, 2])
    lax.fori_loop(0, MB * PAIRS, pair_step, 0)
    second = local(pair_grads[1], r.pair_grad, r.rest_sem.at[3])
    second.start()
    own_loads[MB].wait()
    total = r.middle[0:rows] + r.result_own[...].astype(f32)
    for k in range(1, SHARDS):
        result_copies[k - 1].wait_recv()
        total = total + r.result_in[k - 1].astype(f32)
    r.block_output[...] = total.astype(bf16)
    serve([], [], [6])
    pair_sum.finish(r.pair_low, r.cosine, r.sine)
    serve([], [], [7])
    second.wait()

    for copy in trades[1]:
        copy.wait_send()
    for copy in rests:
        copy.wait()
    for copy in row_copies:
        copy.wait_send()
    for copy in result_copies:
        copy.wait_send()
    pair_sum.drain()
    line.drain()


def backward(query, starts, cosine, sine, middle, cotangent, gain, pairs, row_blocks, grad_blocks, pieces, results, row_grads, output_weight):
    rows = cosine.shape[0]
    length = pairs.shape[1]
    held_rows = 2 * MODEL_WIDTH
    tokens = MB * SHARDS * rows
    dma = pltpu.SemaphoreType.DMA
    anywhere = pl.BlockSpec(memory_space=pl.ANY)
    vmem = pl.BlockSpec(memory_space=pltpu.VMEM)
    shape = jax.ShapeDtypeStruct
    tall, flat = (MODEL_WIDTH, F_BLOCK), (F_BLOCK, MODEL_WIDTH)
    two = lambda s: (2,) + s
    low = lambda s: pltpu.VMEM(s, bf16)
    number = 2 * PARTS
    return pl.pallas_call(
        backward_kernel,
        in_specs=[vmem, pl.BlockSpec(memory_space=pltpu.SMEM)] + [vmem] * 5 + [anywhere] * 9,
        out_specs=[vmem] * 6 + [anywhere] * 6,
        out_shape=[
            shape(query.shape, bf16),
            shape((rows, 2 * KEY_WIDTH), bf16),
            shape((MB * rows, MODEL_WIDTH), bf16),
            shape((MB * rows, MODEL_WIDTH), f32),
            shape((8, MODEL_WIDTH), f32),
            shape((rows, MODEL_WIDTH), bf16),
            shape((held_rows, F_BLOCK), bf16),
            shape((held_rows, F_BLOCK), bf16),
            shape(tall, bf16),
            shape(tall, bf16),
            shape(two(flat), bf16),
            shape((length, 2 * KEY_WIDTH), bf16),
        ],
        scratch_shapes=[
            low((tokens, MODEL_WIDTH)),
            low((MODEL_WIDTH, tokens)),
            low((tokens, MODEL_WIDTH)),
            low((3 * tokens, 2 * F)),
            low(tall),
            low(tall),
            low(flat),
            low(two(tall)),
            low(two(tall)),
            low(two(flat)),
            low(two(tall)),
            low(two(tall)),
            low(two(flat)),
            low(tall),
            low(tall),
            low(tall),
            low(tall),
            low((MB, rows, MODEL_WIDTH)),
            low((MB, SHARDS - 1, rows, MODEL_WIDTH)),
            low((rows, MODEL_WIDTH)),
            low((SHARDS - 1, rows, MODEL_WIDTH)),
            low((MB, rows, MODEL_WIDTH)),
            low((2, 2, length, LANES)),
            pltpu.VMEM((MB, length, rows), f32),
            low((LINE, rows, 2 * KEY_WIDTH)),
            low((LINE - 1, rows, 2 * KEY_WIDTH)),
            dma((4 * MB * SHARDS,)),
            dma((2,)),
            dma((2, 6)),
            dma((4,)),
            dma((2, MB * (SHARDS - 1))),
            dma((2, SHARDS - 1)),
            dma((2, 2)),
            dma((2, LINE)),
            dma((2, LINE - 1)),
        ]
        + line_sems(number),
        compiler_params=pltpu.CompilerParams(
            collective_id=3, has_side_effects=True, vmem_limit_bytes=VMEM_LIMIT
        ),
        name="backward",
    )(query, starts, cosine, sine, middle, cotangent, gain, pairs, row_blocks, grad_blocks, *pieces, results, row_grads, output_weight)


DENSE = ("output", "query", "pair", "gain")
DENSE_PARTS = 4
FINE = 4
GATHER_AFTER = {4: ("output",), 9: ("query",), 13: ("pair", "gain")}
OUTPUT_AFTER = 19


def dense_kernel(
    turned_normed,
    turned_attn,
    query_low,
    pair_low_first,
    middle_low,
    middle_grad,
    tokens,
    gain,
    gain_grad,
    cosine,
    sine,
    middle,
    query_src,
    pair_src,
    pair_grad,
    results_src,
    gate_rest,
    up_rest,
    down_rest,
    input_grad,
    block_output,
    results_in,
    output_total,
    query_total,
    pair_total,
    gain_total,
    gate_total,
    up_total,
    down_total,
    pair_low,
    pair_own,
    pair_other,
    land_left,
    query_weight,
    pair_weight,
    gains,
    send_output,
    send_query,
    own_output,
    own_query,
    own_pair,
    own_gain,
    other_output,
    other_query,
    other_pair,
    other_gain,
    across_output,
    across_query,
    across_pair,
    across_gain,
    sum_output,
    sum_query,
    sum_pair,
    sum_gain,
    near_output,
    near_query,
    near_pair,
    near_gain,
    far_output,
    far_query,
    far_pair,
    far_gain,
    own_gate,
    own_up,
    own_down,
    near_gate,
    near_up,
    near_down,
    far_gate,
    far_up,
    far_down,
    load_sem,
    core_sem,
    left_sem,
    result_sem,
    trade_sem,
    across_sem,
    near_sem,
    far_sem,
    back_sem,
    pass_sem,
    store_sem,
):
    r = types.SimpleNamespace(**locals())
    at = lambda kind, name: getattr(r, kind + "_" + name)
    place = Place()
    core, shard = place.core, place.shard
    rows = r.tokens.shape[0] // MB
    held = MODEL_WIDTH // SHARDS
    half = held // 2
    loads = [
        pltpu.make_async_copy(source, target, r.load_sem.at[i])
        for i, (source, target) in enumerate(
            (
                (r.gate_rest, r.own_gate),
                (r.up_rest, r.own_up),
                (r.down_rest, r.own_down),
                (r.query_src, r.query_weight),
                (r.pair_src, r.pair_weight),
                (r.pair_grad.at[:, core], r.pair_own),
            )
        )
    ]
    for load in loads:
        load.start()
    greet_line(place)
    pair_sum = PairSum(
        place,
        lambda j: r.pair_own.at[j],
        lambda j: r.pair_grad.at[j, 1 - core],
        r.pair_other,
        r.land_left,
        r.core_sem,
        r.left_sem,
    )
    pair_sum.trade()

    pieces = []
    for name, parts in (("gate", FINE), ("up", FINE), ("down", 2 * FINE)):
        pieces += line_pieces(place, at("own", name), at("near", name), at("far", name), getattr(r, name + "_total"), parts)
    expert_pieces = len(pieces)
    for name in DENSE:
        parts = 1 if name == "gain" else DENSE_PARTS
        pieces += line_pieces(
            place, at("sum", name), at("near", name), at("far", name), getattr(r, name + "_total"), parts
        )
    line = Line(place, pieces, (r.near_sem, r.far_sem, r.back_sem, r.pass_sem, r.store_sem))
    for i in range(3):
        loads[i].wait()
    line.ready(0)
    loads[5].wait()
    pair_sum.meet()
    line.ready(*range(1, expert_pieces))

    def block(b, of_core):
        return pl.ds(pl.multiple_of(b * held + of_core * half, half), half)

    trades = {}

    def dense(name, turned, right, sent):
        index = DENSE.index(name)
        trades[name] = []
        for b in range(SHARDS):
            sent[b] = dot(turned[block(b, 1 - core)], right[...]).astype(bf16)
            copy = remote(sent.at[b], at("other", name).at[b], r.trade_sem, index * SHARDS + b, place.partner)
            copy.start()
            trades[name].append(copy)
        for b in range(SHARDS):
            at("own", name)[b] = dot(turned[block(b, core)], right[...]).astype(bf16)

    crossings = {}

    def meet(name):
        own, other, across = at("own", name), at("other", name), at("across", name)
        for b in range(SHARDS):
            trades[name][b].wait_recv()
            add_into(own.at[b], own.at[b], other.at[b])
        crossings[name] = []
        for k in range(1, SHARDS):
            index = DENSE.index(name) * (SHARDS - 1) + k - 1
            copy = remote(own.at[place.peer_index(k)], across.at[k - 1], r.across_sem, index, place.peer(k))
            copy.start()
            crossings[name].append(copy)

    def gather(name):
        for copy in crossings[name]:
            copy.wait_recv()
        across = at("across", name)
        add_into(at("sum", name), at("own", name).at[shard], *[across.at[k] for k in range(SHARDS - 1)])

    dense("output", r.turned_attn, r.middle_low, r.send_output)
    dense("query", r.turned_normed, r.query_low, r.send_query)
    meet("output")
    line.serve([0])
    pair_sum.step(2)
    meet("query")
    pair_sum.step(3)
    for copy in trades["output"]:
        copy.wait_send()
    r.pair_low[0:rows] = r.pair_low_first[...]
    pair_sum.finish(r.pair_low.at[rows : 2 * rows], r.cosine, r.sine)
    dense("pair", r.turned_normed, r.pair_low, r.send_output.at[:, :, 0 : 2 * KEY_WIDTH])
    line.serve([1], [0])
    for load in loads[3:5]:
        load.wait()

    gain_one_grad = jnp.zeros((1, MODEL_WIDTH), f32)
    for m in range(MB):
        own = slice(m * rows, (m + 1) * rows)
        values = r.tokens[own].astype(f32)
        scale = lax.rsqrt(jnp.mean(values * values, axis=-1, keepdims=True) + eps)
        unit = values * scale
        normed_grad = dot(r.query_low[own], r.query_weight[...], NT) + dot(r.pair_low[own], r.pair_weight[...], NT)
        gain_one_grad = gain_one_grad + jnp.sum(normed_grad * unit, axis=0, keepdims=True)
        weighted = normed_grad * r.gain[...]
        inner = jnp.mean(weighted * unit, axis=-1, keepdims=True)
        r.input_grad[own] = r.middle_grad[own] + (weighted - unit * inner) * scale
        if m == 0:
            meet("pair")
            line.serve([2], [1])
    line.serve([3], [2])
    gain_two_grad = jnp.sum(r.gain_grad[...], axis=0, keepdims=True)
    stacked = jnp.concatenate(
        [gain_one_grad, gain_two_grad, jnp.zeros((LANES - 2, MODEL_WIDTH), f32)], axis=0
    )
    r.gains[...] = stacked.T.astype(bf16)
    trades["gain"] = []
    for b in range(SHARDS):
        source = r.gains.at[block(b, 1 - core)]
        index = DENSE.index("gain") * SHARDS + b
        trades["gain"].append(remote(source, r.other_gain.at[b], r.trade_sem, index, place.partner))
        trades["gain"][b].start()
        r.own_gain[b] = r.gains[block(b, core)]
    meet("gain")

    result_copies = []
    for k in range(1, SHARDS):
        source = r.results_src.at[1, place.peer_index(k)]
        result_copies.append(remote(source, r.results_in.at[k - 1], r.result_sem, k - 1, place.peer(k)))
        result_copies[-1].start()
    for copy in trades["pair"]:
        copy.wait_send()
    result_parts = [r.send_output.at[k, 0:rows] for k in range(SHARDS)]
    result_loads = [
        pltpu.make_async_copy(source, target, r.load_sem.at[6 + k])
        for k, (source, target) in enumerate(
            zip([r.results_src.at[1, shard]] + [r.results_in.at[k] for k in range(SHARDS - 1)], result_parts)
        )
    ]
    result_loads[0].start()

    def output_rows():
        for copy, load in zip(result_copies, result_loads[1:]):
            copy.wait_recv()
            load.start()
        total = r.middle[...]
        for load, part in zip(result_loads, result_parts):
            load.wait()
            total = total + part[...].astype(f32)
        r.block_output[...] = total.astype(bf16)

    number = len(pieces)
    first = expert_pieces
    spans = {}
    for name in DENSE:
        parts = 1 if name == "gain" else DENSE_PARTS
        spans[name] = range(first, first + parts)
        first += parts
    lag = 4
    for i in range(number + lag):
        line.serve(
            [i] if 4 <= i < number else [],
            [i - 1] if 4 <= i <= number else [],
            [i - lag] if i >= lag else [],
        )
        for name in GATHER_AFTER.get(i, ()):
            gather(name)
            line.ready(*spans[name])
        if i == OUTPUT_AFTER:
            output_rows()

    for name in DENSE:
        for copy in crossings[name]:
            copy.wait_send()
        if name in ("query", "gain"):
            for copy in trades[name]:
                copy.wait_send()
    for copy in result_copies:
        copy.wait_send()
    pair_sum.drain()
    line.drain()


def dense_weights(vectors, query_weight, pair_weight, pair_grad, results, rests):
    dma = pltpu.SemaphoreType.DMA
    anywhere = pl.BlockSpec(memory_space=pl.ANY)
    vmem = pl.BlockSpec(memory_space=pltpu.VMEM)
    shape = jax.ShapeDtypeStruct
    rows = pair_grad.shape[2]
    low = lambda *s: pltpu.VMEM(s, bf16)
    held = MODEL_WIDTH // SHARDS
    half = held // 2
    widths = (MODEL_WIDTH, MODEL_WIDTH, 2 * KEY_WIDTH, LANES)
    tall = (MODEL_WIDTH, F_BLOCK)
    number = 4 * FINE + 3 * DENSE_PARTS + 1
    return pl.pallas_call(
        dense_kernel,
        in_specs=[vmem] * len(vectors) + [anywhere] * 7,
        out_specs=[vmem] * 2 + [anywhere] * 8,
        out_shape=[
            shape((MB * rows, MODEL_WIDTH), f32),
            shape((rows, MODEL_WIDTH), bf16),
            shape((SHARDS - 1, rows, MODEL_WIDTH), bf16),
        ]
        + [shape((held, w), bf16) for w in widths]
        + [
            shape((2 * MODEL_WIDTH, F_BLOCK), bf16),
            shape((2 * MODEL_WIDTH, F_BLOCK), bf16),
            shape((2 * F, MODEL_WIDTH), bf16),
        ],
        scratch_shapes=[
            low(MB * rows, 2 * KEY_WIDTH),
            low(LINE, rows, 2 * KEY_WIDTH),
            low(LINE, rows, 2 * KEY_WIDTH),
            low(LINE - 1, rows, 2 * KEY_WIDTH),
            low(*query_weight.shape),
            low(*pair_weight.shape),
            low(MODEL_WIDTH, LANES),
            low(SHARDS, half, MODEL_WIDTH),
            low(SHARDS, half, MODEL_WIDTH),
        ]
        + [low(SHARDS, half, w) for w in widths] * 2
        + [low(SHARDS - 1, half, w) for w in widths]
        + [low(half, w) for w in widths] * 3
        + [low(*tall), low(*tall), low(F, MODEL_WIDTH)] * 3
        + [dma((6 + SHARDS,)), dma((2, LINE)), dma((2, LINE - 1)), dma((2, SHARDS - 1)), dma((2, 4 * SHARDS)), dma((2, 4 * (SHARDS - 1)))]
        + line_sems(number),
        compiler_params=pltpu.CompilerParams(
            collective_id=4, has_side_effects=True, vmem_limit_bytes=VMEM_LIMIT
        ),
        name="dense_weights",
    )(*vectors, query_weight, pair_weight, pair_grad, results, *rests)


def widen_kernel(gate_first, gate_second, up_first, up_second, *refs):
    count = len(refs) // 2
    expand_out = refs[count]
    for i, ref in enumerate((gate_first, gate_second, up_first, up_second)):
        expand_out[:, i * F_BLOCK : (i + 1) * F_BLOCK] = ref[...].astype(f32)
    for source, target in zip(refs[:count], refs[count + 1 :]):
        target[...] = source[...].astype(f32)


def widen(expand_parts, arrays):
    steps = 8
    block = lambda a, c: pl.BlockSpec((a.shape[0] // steps, c), lambda i: (i, 0))
    rows = expand_parts[0].shape[0]
    outs = [jax.ShapeDtypeStruct((rows, 2 * F), f32)] + [jax.ShapeDtypeStruct(a.shape, f32) for a in arrays]
    return pl.pallas_call(
        widen_kernel,
        grid=(steps,),
        in_specs=[block(a, a.shape[1]) for a in (*expand_parts, *arrays)],
        out_specs=[block(a, a.shape[1]) for a in outs],
        out_shape=outs,
        compiler_params=pltpu.CompilerParams(vmem_limit_bytes=VMEM_LIMIT),
        name="widen",
    )(*expand_parts, *arrays)


def shards(
    tokens,
    doc_starts,
    routes,
    gates,
    attn_gain,
    w_q,
    key_value_weight,
    w_o,
    moe_gain,
    expert_in,
    expert_out,
    cotangent,
):
    links = Links()
    rows = tokens.shape[2]
    length = rows * links.contexts
    held = expert_in.shape[0]
    chained = links.chips == LINE and links.shards == SHARDS and held == 2
    width = w_q.shape[0]
    flat_tokens = tokens.reshape(MB * rows, MODEL_WIDTH)
    if chained:
        flat_cotangent = cotangent.reshape(MB * rows, MODEL_WIDTH)
        starts = doc_starts[:, 0]
        (
            turned_normed,
            query,
            turned_attn,
            middle,
            gains,
            cosine,
            sine,
            pair_weight,
            query_weight,
            output_weight,
            pairs,
            row_blocks,
            grad_blocks,
            result_blocks,
            row_grad_blocks,
            active,
            gate,
            up,
        ) = forward(
            flat_tokens,
            routes[:, 0].transpose(0, 2, 1),
            gates[:, 0].transpose(0, 2, 1),
            jnp.stack([attn_gain, moe_gain]),
            flat_cotangent,
            starts,
            rotation_constants(length),
            (key_value_weight, w_q, w_o),
            expert_in,
            expert_out,
        )
        result_blocks = result_blocks.reshape(row_blocks.shape)
        row_grad_blocks = row_grad_blocks.reshape(row_blocks.shape)
        gains = gains.reshape(SHARDS, GAIN_ROWS, width).astype(f32)
        gain_one, gain_two = gains[:, 0].reshape(1, MODEL_WIDTH), gains[:, 1].reshape(1, MODEL_WIDTH)
        (
            query_low,
            pair_low,
            middle_low,
            middle_grad,
            gain_two_grad,
            output_first,
            gate_first,
            up_first,
            gate_rest,
            up_rest,
            down_rest,
            pair_grad,
        ) = backward(
            query,
            starts,
            cosine,
            sine,
            middle,
            flat_cotangent,
            gain_two,
            pairs,
            row_blocks,
            grad_blocks,
            (active, gate, up),
            result_blocks,
            row_grad_blocks,
            output_weight,
        )
        (
            input_grad,
            output_second,
            _,
            output_total,
            query_total,
            pair_total,
            gain_total,
            gate_second,
            up_second,
            shrink_total,
        ) = dense_weights(
            (
                turned_normed,
                turned_attn,
                query_low,
                pair_low,
                middle_low,
                middle_grad,
                flat_tokens,
                gain_one,
                gain_two_grad,
                cosine,
                sine,
                middle[rows:],
            ),
            query_weight,
            pair_weight,
            pair_grad.reshape(LINE, 2, rows, 2 * KEY_WIDTH),
            result_blocks,
            (gate_rest, up_rest, down_rest.reshape(F, MODEL_WIDTH)),
        )
        expand_total, shrink_total, output_total, query_total, pair_total = widen(
            (gate_first, gate_second, up_first, up_second),
            (shrink_total, output_total, query_total, pair_total),
        )
        return (
            jnp.stack([output_first, output_second])[:, None],
            input_grad.reshape(MB, 1, rows, MODEL_WIDTH),
            gain_total[:, 0].astype(f32),
            query_total,
            pair_total,
            output_total,
            gain_total[:, 1].astype(f32),
            expand_total.reshape(held, MODEL_WIDTH, 2 * F),
            shrink_total.reshape(held, F, MODEL_WIDTH),
        )

    positions = links.context * rows + jnp.arange(rows, dtype=jnp.int32)
    cosine, sine = rotation_tables(positions)
    key_places = jnp.arange(length, dtype=jnp.int32)
    flat_values = flat_tokens.astype(f32)
    scale_one = lax.rsqrt(jnp.mean(flat_values * flat_values, axis=-1, keepdims=True) + eps)
    unit_one = flat_values * scale_one
    expert_ids = jnp.arange(E, dtype=jnp.int32)
    chosen = (routes.reshape(MB, rows, TOP)[..., None] == expert_ids).astype(f32)
    combine = jnp.sum(gates.reshape(MB, rows, TOP)[..., None] * chosen, axis=2)
    gather = lambda w: lax.all_gather(w, "fsdp", axis=0, tiled=True)
    pair_weight, query_weight, output_weight = gather(key_value_weight), gather(w_q), gather(w_o)
    gain_one, gain_two = gather(attn_gain).astype(f32), gather(moe_gain).astype(f32)
    normed = (unit_one * gain_one).astype(bf16)
    both = lambda table: jnp.concatenate([table] * MB)
    own_pairs = rotate_columns(dot(normed, pair_weight), both(cosine), both(sine), KEY_WIDTH)
    query = rotate_columns(dot(normed, query_weight), both(cosine), both(sine), MODEL_WIDTH)
    own_pairs = own_pairs.reshape(MB, rows, 2 * KEY_WIDTH)
    pairs = lax.all_gather(own_pairs, "ctx", axis=1, tiled=True)

    combine = jnp.concatenate([combine] + [links.across(combine, k) for k in range(1, links.shards)], axis=1)
    combine = lax.dynamic_slice_in_dim(combine, links.shard * held, held, 2)
    combine = combine.transpose(0, 2, 1)[..., None]

    biases, biases_turned = [], []
    for m in range(MB):
        starts = doc_starts[m, 0]
        begin = jnp.max(jnp.where(starts[None, :] <= positions[:, None], starts[None, :], 0), axis=1)
        seen = (key_places[None, :] <= positions[:, None]) & (key_places[None, :] >= begin[:, None])
        biases.append(jnp.where(seen, 0.0, -1e30).astype(f32))
        places, begins = jnp.tile(positions, GROUP), jnp.tile(begin, GROUP)
        seen = (key_places[:, None] <= places[None, :]) & (key_places[:, None] >= begins[None, :])
        biases_turned.append(jnp.where(seen, 0.0, -1e30).astype(f32))

    middles, attns, results, row_grads = [], [], [], []
    rows_kept, grads_kept, pieces_kept = [], [], []
    for m in range(MB):
        own = slice(m * rows, (m + 1) * rows)
        attn = attention_forward(m, query, pairs, biases[m])
        middle = flat_tokens[own].astype(f32) + dot(attn, output_weight)
        scale_two = lax.rsqrt(jnp.mean(middle * middle, axis=-1, keepdims=True) + eps)
        moe_in = (middle * scale_two * gain_two).astype(bf16)
        out_grad = cotangent[m, 0]
        row_parts = [moe_in] + [links.across(moe_in, k) for k in range(1, links.shards)]
        grad_parts = [out_grad] + [links.across(out_grad, k) for k in range(1, links.shards)]
        result, row_grad, pieces = experts(row_parts, grad_parts, combine[m], expert_in, expert_out)
        for parts, sums in ((result, results), (row_grad, row_grads)):
            total = parts[0].astype(f32)
            for k in range(1, links.shards):
                total = total + links.across(parts[k], k).astype(f32)
            sums.append(total)
        middles.append(middle)
        attns.append(attn)
        rows_kept += row_parts
        grads_kept += grad_parts
        pieces_kept.append(pieces)
    merge = lambda items: jnp.concatenate(items, axis=0)
    expert_grads = expert_weights(
        merge(rows_kept), merge(grads_kept), *[merge([p[i] for p in pieces_kept]) for i in range(3)], held
    )
    expert_grads = [g.reshape(-1, g.shape[-1]) for g in expert_grads]
    outputs = [(middles[m] + results[m]).astype(bf16) for m in range(MB)]

    input_grads, query_lows, pair_lows, middle_lows = [], [], [], []
    gain_one_grad, gain_two_grad = 0.0, 0.0
    for m in range(MB):
        own = slice(m * rows, (m + 1) * rows)
        scale_two = lax.rsqrt(jnp.mean(middles[m] * middles[m], axis=-1, keepdims=True) + eps)
        unit_two = middles[m] * scale_two
        moe_in_grad = row_grads[m]
        gain_two_grad = gain_two_grad + jnp.sum(moe_in_grad * unit_two, axis=0)
        weighted = moe_in_grad * gain_two
        inner = jnp.mean(weighted * unit_two, axis=-1, keepdims=True)
        middle_grad = cotangent[m, 0].astype(f32) + (weighted - unit_two * inner) * scale_two
        middle_low = middle_grad.astype(bf16)
        attn_grad = dot(middle_low, output_weight, NT).astype(bf16)
        query_low, pair_grad = attention_backward(
            m, query, cosine, sine, pairs, biases_turned[m], attn_grad
        )
        parts = [lax.psum_scatter(pair_grad, "ctx", scatter_dimension=0, tiled=True)]
        pair_low = pair_gradient(parts, cosine, sine)
        normed_grad = dot(query_low, query_weight, NT) + dot(pair_low, pair_weight, NT)
        gain_one_grad = gain_one_grad + jnp.sum(normed_grad * unit_one[own], axis=0)
        weighted = normed_grad * gain_one
        inner = jnp.mean(weighted * unit_one[own], axis=-1, keepdims=True)
        residual_grad = (weighted - unit_one[own] * inner) * scale_one[own]
        input_grads.append(middle_grad + residual_grad)
        query_lows.append(query_low)
        pair_lows.append(pair_low)
        middle_lows.append(middle_low)

    join = lambda items: jnp.concatenate(items, axis=0)

    output_grad = dot(join(attns), join(middle_lows), TN).astype(bf16)
    query_grad = dot(normed, join(query_lows), TN).astype(bf16)
    pair_weight_grad = dot(normed, join(pair_lows), TN).astype(bf16)
    gain_grads = jnp.stack([gain_one_grad, gain_two_grad], axis=1)
    gain_grads = jnp.pad(gain_grads, ((0, 0), (0, LANES - 2))).astype(bf16)
    dense_grads = [output_grad, query_grad, jnp.concatenate([pair_weight_grad, gain_grads], axis=1)]
    totals = [lax.psum(g, "ctx") for g in expert_grads]
    for g in dense_grads:
        part = lax.psum_scatter(g, "fsdp", scatter_dimension=0, tiled=True)
        totals.append(lax.psum(part, "ctx"))
    gate_total, up_total, down_total, output_total, query_total, pair_total = [t.astype(f32) for t in totals]
    expand_total = jnp.concatenate([gate_total, up_total], axis=1)

    return (
        jnp.stack(outputs)[:, None],
        jnp.stack(input_grads)[:, None],
        pair_total[:, 2 * KEY_WIDTH],
        query_total,
        pair_total[:, : 2 * KEY_WIDTH],
        output_total,
        pair_total[:, 2 * KEY_WIDTH + 1],
        expand_total.reshape(held, MODEL_WIDTH, 2 * F),
        down_total.reshape(held, F, MODEL_WIDTH),
    )


def solution(mesh):
    return jax.shard_map(
        shards,
        mesh=mesh,
        in_specs=(
            P(None, "fsdp", "ctx", None),
            P(None, "fsdp", None),
            P(None, "fsdp", "ctx", None),
            P(None, "fsdp", "ctx", None),
            P("fsdp"),
            P("fsdp", None),
            P("fsdp", None),
            P("fsdp", None),
            P("fsdp"),
            P("fsdp", None, None),
            P("fsdp", None, None),
            P(None, "fsdp", "ctx", None),
        ),
        out_specs=(
            P(None, "fsdp", "ctx", None),
            P(None, "fsdp", "ctx", None),
            P("fsdp"),
            P("fsdp", None),
            P("fsdp", None),
            P("fsdp", None),
            P("fsdp"),
            P("fsdp", None, None),
            P("fsdp", None, None),
        ),
        check_vma=False,
    )
```

time: 908 us -> 380 us (0.42)
  waiting for transfers between devices: 313 us -> 0 us
  starting transfers between devices: 261 us -> 0 us
  Pallas kernels: 113 us -> 364 us
  local copies, waits for them, and re-layouts: 83.8 us -> 4.87 us
  other arithmetic: 68.8 us -> 4.29 us
  matrix products: 35 us -> 0 us
  blocking collectives: 19.1 us -> 0 us
    ppermute x172 -> x0, waiting for transfers between devices: 313 us -> none  [the longest x72 151 us: step(): return lax.ppermute(array, 'ctx', pairs)]
    ppermute x172 -> x0, starting transfers between devices: 261 us -> none  [the longest x72 148 us: step(): return lax.ppermute(array, 'ctx', pairs)]
    pallas_call x10 -> x4, Pallas kernels: 113 us -> 364 us  [the longest x1 140 us: dense_weights(): pl.pallas_call(dense_kernel, in_specs=[vmem] * len(vectors) + [anywhere]...]
    unnamed x259 -> x7, local copies, waits for them, and re-layouts: 38.2 us -> 1.16 us
    dot_general x13 -> x0, matrix products: 35 us -> none  [dot(): return lax.dot_general(left, right, dims, preferred_element_type=f32)]
    convert_element_type x32 -> x1, other arithmetic: 25.5 us -> 1.77 us  [shards(): gain_total[:, 1].astype(f32)]
    all_gather x1 -> x0, blocking collectives: 19.1 us -> none  [shards(): lax.all_gather(jnp.stack([attn_gain, moe_gain]), 'fsdp', axis=1, tiled=True)]
    slice x16 -> x2, local copies, waits for them, and re-layouts: 18 us -> 2.35 us  [the longest x1 1.42 us: shards(): gains[:, 0].reshape(1, MODEL_WIDTH)]
  transfers between devices with their start and end apart: 172 -> 0, of which waited for: 63 -> 0; matrix products, arithmetic and copies ran while one was open for 19% -> 0% of each run, Pallas kernels for 9% -> 0%
where the time goes in v5:
time: 380 us; the launch traced here: 374 us
  Pallas kernels  364 us (96%)
  local copies, waits for them, and re-layouts  4.87 us (1%)
  other arithmetic  4.29 us (1%)
    pallas_call x1, Pallas kernels, dense_weights(): pl.pallas_call(dense_kernel, in_specs=[vmem] * len(vectors) + [anywhere]...  140 us
    pallas_call x1, Pallas kernels, forward(): pl.pallas_call(forward_kernel, in_specs=[vmem] * 5 + [pl.BlockSpec(memory...  129 us
    pallas_call x1, Pallas kernels, backward(): pl.pallas_call(backward_kernel, in_specs=[vmem, pl.BlockSpec(memory_space...  81.6 us
    pallas_call x1, Pallas kernels, widen(): pl.pallas_call(widen_kernel, grid=(steps,), in_specs=[block(a, a.shape[1]...  14.2 us

profile of v5, /device:TPU:0, one launch (start us, length us, event | category | flops | bytes accessed | tf_op | source)
XLA Modules:
  0.0 374.4 jit_solution(13044595092039590547)
XLA Ops:
  0.6 0.7 stack.18
  1.3 0.7 stack.19
  2.0 0.6 pad_maximum_fusion.gain_pair
  2.6 128.5 %forward.1 = (bf16[1536,256]{1,0:T(8,128)(2,1)}, bf16[256,1536]{1,0:T(8,128)(2,1)}, bf16[1536,256]{1,0:T(8,128)(2,1)}, f32[256,1536]{1,0:T(8,128)}, bf16[64,384]...) custom-call(bf16[256,1536]{1,0:T(8,128)(2,1)} %bitcast.30, ...), custom_call_target="tpu_custom_call" | custom-call | tf_op jit(solution)/shard_map/forward/pallas_call | solution.py:937
  131.1 1.4 fusion
  132.5 0.0 copy-start
  132.5 81.6 %backward.1 = (bf16[256,1536]{1,0:T(8,128)(2,1)}, bf16[128,1024]{1,0:T(8,128)(2,1)}, bf16[256,1536]{1,0:T(8,128)(2,1)}, f32[256,1536]{1,0:T(8,128)}, f32[8,1536]...) custom-call(bf16[256,1536]{1,0:T(8,128)(2,1)} %get-tuple-element.53., ...), custom_call_target="tpu_custom_call" | custom-call | tf_op jit(solution)/shard_map/backward/pallas_call | solution.py:1521
  214.1 0.0 copy-done
  214.1 0.9 slice.17.middle
  215.1 0.0 copy-start.2
  215.1 139.9 %dense_weights.1 = (f32[256,1536]{1,0:T(8,128)}, bf16[128,1536]{1,0:T(8,128)(2,1)}, bf16[3,128,1536]{2,1,0:T(8,128)(2,1)}, bf16[384,1536]{1,0:T(8,128)(2,1)}, bf...) custom-call(bf16[1536,256]{1,0:T(8,128)(2,1)} %get-tuple-element.68., ...), custom_call_target="tpu_custom_call" | custom-call | tf_op jit(solution)/shard_map/dense_weights/pallas_call | solution.py:1877
  355.0 0.0 copy-done.2
  355.0 1.9 maximum_bitcast_fusion
  357.0 1.8 convert_reduce_fusion
  358.7 0.0 copy-start.1
  358.8 14.2 %widen.1 = (f32[3072,1024]{1,0:T(8,128)}, f32[1024,1536]{1,0:T(8,128)}, f32[384,1536]{1,0:T(8,128)}, f32[384,1536]{1,0:T(8,128)}, f32[384,1024]{1,0:T(8,128)}) custom-call(bf16[3072,256]{1,0:T(8,128)(2,1)} %get-tuple-element.84.gate_first, bf16[3072,256]{1,0:T(8,128)(2,1)} %get-tuple-element.85.gate_second, bf16[3072,256]{1,0:T(8,128)(2,1)} %get-tuple-element.86.up_first, ...), custom_call_target="tpu_custom_call" | custom-call | tf_op jit(solution)/shard_map/widen/pallas_call | solution.py:1930
  373.0 0.0 copy-done.1
  373.0 1.1 copy.33
Async XLA Ops:
  132.5 81.6 %copy-start = (f32[256,1536]{1,0:T(8,128)S(1)}, f32[256,1536]{1,0:T(8,128)}, u32[]{:S(2)}) copy-start(f32[256,1536]{1,0:T(8,128)} %get-tuple-element.56.middle) | copy-start | bytes 4718596
  215.1 139.9 %copy-start.2 = (bf16[128,1536]{1,0:T(8,128)(2,1)S(1)}, bf16[128,1536]{1,0:T(8,128)(2,1)}, u32[]{:S(2)}) copy-start(bf16[128,1536]{1,0:T(8,128)(2,1)} %get-tuple-element.67) | copy-start | bytes 1179652
  358.7 14.2 %copy-start.1 = (f32[256,1536]{1,0:T(8,128)S(1)}, f32[256,1536]{1,0:T(8,128)}, u32[]{:S(2)}) copy-start(f32[256,1536]{1,0:T(8,128)} %get-tuple-element.82) | copy-start | bytes 4718596

commit v6 on v5

--- a/solution.py
+++ b/solution.py
@@ -497,24 +497,30 @@
     output_src,
     expand_src,
     shrink_src,
-    turned_normed,
-    query,
-    turned_attn,
-    middle,
-    gains,
+    turned_normed_out,
+    query_rows_out,
+    turned_attn_out,
+    middle_out,
+    gain_rows_out,
     cosine,
     sine,
     pair_out,
     query_out,
     output_out,
     pairs,
-    rows_out,
+    turned_out,
     grads_out,
     results_out,
     row_grads_out,
     active_out,
     gate_out,
     up_out,
+    turned_normed,
+    query,
+    turned_attn,
+    middle,
+    gains,
+    turned_rows,
     pair_weight,
     query_weight,
     output_weight,
@@ -549,6 +555,7 @@
     square_relay_sem,
     key_sem,
     emit_sem,
+    last_sem,
 ):
     r = types.SimpleNamespace(**locals())
     place = Place()
@@ -623,7 +630,7 @@
     for m in range(MB):
         combine = jnp.zeros((E, rows), f32)
         for k in range(TOP):
-            combine += jnp.where(expert_row == r.routes[m, k : k + 1], r.gates[m, k : k + 1], 0.0)
+            combine += jnp.where(expert_row == r.routes[m, 0, k : k + 1], r.gates[m, 0, k : k + 1], 0.0)
         r.combine_own[:, m * rows : (m + 1) * rows] = combine
     r.combine_in[shard] = r.combine_own[...]
     small_copies = []
@@ -652,11 +659,16 @@
         Square(place, r.rows_all.at[m], r.square_direct_sem, r.square_relay_sem, 2 * (MB + m)) for m in range(MB)
     ]
 
+    def spread_gains():
+        r.gain_rows_out[...] = jnp.zeros_like(r.gain_rows_out)
+        for b in range(SHARDS):
+            pair = r.gains[b * GAIN_ROWS : b * GAIN_ROWS + 2]
+            r.gain_rows_out[0:2, b * held : (b + 1) * held] = pair.astype(f32)
+
     def gain_times(values, row, write):
         for b in range(SHARDS):
             columns = slice(b * held, (b + 1) * held)
-            at = b * GAIN_ROWS + row
-            write(columns, (values[:, columns] * r.gains[at : at + 1].astype(f32)).astype(bf16))
+            write(columns, (values[:, columns] * r.gain_rows_out[row : row + 1, columns]).astype(bf16))
 
     values = r.tokens[...].astype(f32)
     unit = values * lax.rsqrt(jnp.mean(values * values, axis=-1, keepdims=True) + eps)
@@ -666,6 +678,7 @@
     def write_normed(columns, value):
         r.normed[:, columns] = value
 
+    spread_gains()
     gain_times(unit, 0, write_normed)
     r.turned_normed[...] = r.normed[...].T
     for b in range(SHARDS):
@@ -819,9 +832,14 @@
     active, gate, up = [r.pair_weight.at[i * wide : (i + 1) * wide] for i in range(3)]
     results, row_grads = [r.query_weight.at[i * wide : (i + 1) * wide] for i in range(2)]
 
+    turned = r.turned_rows
+
+    def turn(m):
+        turned[...] = r.rows_all[m].reshape(wide, MODEL_WIDTH).T
+
     def emits(m):
         pairs = (
-            (r.rows_all.at[m], r.rows_out.at[m]),
+            (turned, r.turned_out.at[:, m * wide : (m + 1) * wide]),
             (r.grads_all.at[m], r.grads_out.at[m]),
             (results, r.results_out.at[m]),
             (row_grads, r.row_grads_out.at[m]),
@@ -887,6 +905,19 @@
     finish_attention(1)
     row_squares[1].start()
     grad_squares[1].start()
+    early = [
+        local(source, target, r.last_sem.at[i])
+        for i, (source, target) in enumerate(
+            (
+                (r.turned_normed, r.turned_normed_out),
+                (r.query, r.query_rows_out),
+                (r.turned_attn, r.turned_attn_out),
+                (r.middle, r.middle_out),
+            )
+        )
+    ]
+    for emit in early:
+        emit.start()
     for load in expert_loads:
         load.wait()
     sent_weight(0)
@@ -894,16 +925,20 @@
     grad_squares[0].finish()
     row_squares[0].finish()
     expert_steps(0, {1: row_squares[1].pass_on})
+    turn(0)
     for emit in emits(0):
         emit.start()
     grad_squares[1].pass_on()
     row_squares[1].finish()
     for emit in emits(0):
         emit.wait()
+    turn(1)
     grad_squares[1].finish()
     expert_steps(1, {})
     for emit in emits(1):
         emit.start()
+    for emit in early:
+        emit.wait()
 
     for copy in small_copies:
         copy.wait_send()
@@ -937,26 +972,34 @@
     return pl.pallas_call(
         forward_kernel,
         in_specs=[vmem] * 5 + [pl.BlockSpec(memory_space=pltpu.SMEM)] + [anywhere] * 6,
-        out_specs=[vmem] * 7 + [anywhere] * 11,
+        out_specs=[anywhere] * 4 + [vmem] * 3 + [anywhere] * 11,
         out_shape=[
             shape(tokens.shape[::-1], bf16),
             shape(tokens.shape, bf16),
             shape(tokens.shape[::-1], bf16),
             shape(tokens.shape, f32),
-            shape((SHARDS * GAIN_ROWS, held), bf16),
+            shape((8, MODEL_WIDTH), f32),
             shape((rows, LANES), f32),
             shape((rows, LANES), f32),
         ]
         + [shape(f, bf16) for f in full]
         + [
             shape((MB, length, 2 * KEY_WIDTH), bf16),
-            shape(blocks, bf16),
+            shape((MODEL_WIDTH, MB * wide), bf16),
             shape(blocks, bf16),
             shape((MB, wide, MODEL_WIDTH), bf16),
             shape((MB, wide, MODEL_WIDTH), bf16),
         ]
         + [shape((MB, wide, 2 * F), bf16)] * 3,
-        scratch_shapes=[low(*f) for f in full]
+        scratch_shapes=[
+            low(*tokens.shape[::-1]),
+            low(*tokens.shape),
+            low(*tokens.shape[::-1]),
+            pltpu.VMEM(tokens.shape, f32),
+            low(SHARDS * GAIN_ROWS, held),
+            low(MODEL_WIDTH, wide),
+        ]
+        + [low(*f) for f in full]
         + [
             low(*expert_in.shape),
             low(*expert_out.shape),
@@ -989,6 +1032,7 @@
             dma((2, 4 * MB)),
             dma((2, 2)),
             dma((7 * MB,)),
+            dma((4,)),
         ],
         compiler_params=pltpu.CompilerParams(
             collective_id=1, has_side_effects=True, vmem_limit_bytes=VMEM_LIMIT
@@ -1183,15 +1227,15 @@
 
 
 def backward_kernel(
-    query,
+    query_src,
     starts,
     cosine,
     sine,
-    middle,
-    cotangent,
+    middle_src,
+    cotangent_src,
     gain,
     pairs,
-    rows_src,
+    turned_src,
     grads_src,
     active_src,
     gate_src,
@@ -1199,10 +1243,10 @@
     results_src,
     row_grads_src,
     output_src,
-    query_low,
+    query_low_out,
     pair_low,
-    middle_low,
-    middle_grad,
+    middle_low_out,
+    middle_grad_out,
     gain_grad,
     block_output,
     gate_total,
@@ -1211,6 +1255,12 @@
     up_rest,
     down_rest,
     pair_grad,
+    query,
+    middle,
+    cotangent,
+    query_low,
+    middle_low,
+    middle_grad,
     rows,
     turned,
     grads,
@@ -1251,6 +1301,7 @@
     back_sem,
     pass_sem,
     store_sem,
+    emit_sem,
 ):
     r = types.SimpleNamespace(**locals())
     place = Place()
@@ -1269,19 +1320,22 @@
         return loads[-1]
 
     flat = lambda ref, m: [(ref.at[m, k], m * wide + k * rows) for k in range(SHARDS)]
-    row_loads, grad_loads, piece_loads = [], [], []
-    for m in range(MB):
-        for source, at in flat(r.rows_src, m):
-            row_loads.append(load(source, r.rows.at[at : at + rows]))
-        for source, at in flat(r.grads_src, m):
-            grad_loads.append(load(source, r.grads.at[at : at + rows]))
-    for i, ref in enumerate((r.active_src, r.gate_src, r.up_src)):
+    grad_loads, piece_loads = [], []
+    turned_load = load(r.turned_src, r.turned)
+    for i, ref in ((1, r.gate_src), (2, r.up_src), (0, r.active_src)):
         for m in range(MB):
             at = i * tokens + m * wide
             piece_loads.append(load(ref.at[m], r.pool.at[at : at + wide]))
+    for m in range(MB):
+        for source, at in flat(r.grads_src, m):
+            grad_loads.append(load(source, r.grads.at[at : at + rows]))
     own_loads = [load(r.row_grads_src.at[m, shard], r.row_grad_own.at[m]) for m in range(MB)]
     own_loads.append(load(r.results_src.at[0, shard], r.result_own))
 
+    vector_loads = [
+        load(source, target)
+        for source, target in ((r.middle_src, r.middle), (r.cotangent_src, r.cotangent), (r.query_src, r.query))
+    ]
     greet_line(place)
 
     row_copies, result_copies = [], []
@@ -1302,9 +1356,7 @@
     for m in range(MB):
         r.bias[m] = visible_bias(r.starts, m, place.context, r.bias.shape[1:], 1)
 
-    for copy in row_loads:
-        copy.wait()
-    r.turned[...] = r.rows[...].T
+    turned_load.wait()
     sends = (r.send_gate, r.send_up, r.send_down)
     owns = (r.own_gate, r.own_up, r.own_down)
     others = (r.other_gate, r.other_up, r.other_down)
@@ -1334,8 +1386,13 @@
         pieces += line_pieces(place, own, near, far, out, PARTS)
     line = Line(place, pieces, (r.near_sem, r.far_sem, r.back_sem, r.pass_sem, r.store_sem))
 
-    for copy in piece_loads[MB:]:
+    for copy in piece_loads[: 2 * MB]:
         copy.wait()
+
+    def else_serve(b):
+        if b == 1:
+            line.serve([0])
+
     for b in range(2):
         if b == 1:
             for i in range(2):
@@ -1348,10 +1405,11 @@
             for i in range(2):
                 meet(0, i)
                 line.ready(*range(i * PARTS, (i + 1) * PARTS))
-            for copy in piece_loads[:MB] + grad_loads:
+            for copy in piece_loads[2 * MB :] + grad_loads:
                 copy.wait()
         else:
             trades[0][2].wait_send()
+        else_serve(b)
         down_block(b, 1 - core, sends[2])
         trades[b][2].start()
         down_block(b, core, owns[2].at[b])
@@ -1389,7 +1447,7 @@
         scale = lax.rsqrt(jnp.mean(middle * middle, axis=-1, keepdims=True) + eps)
         unit = middle * scale
         r.gain_grad[m : m + 1] = jnp.sum(moe_in_grad * unit, axis=0, keepdims=True)
-        weighted = moe_in_grad * r.gain[...]
+        weighted = moe_in_grad * r.gain[1:2]
         inner = jnp.mean(weighted * unit, axis=-1, keepdims=True)
         middle_grad = r.cotangent[own].astype(f32) + (weighted - unit * inner) * scale
         r.middle_grad[own] = middle_grad
@@ -1406,7 +1464,7 @@
         lane = pl.multiple_of(p * LANES, LANES) + i * KEY_WIDTH
         return local(r.pairs.at[m, :, pl.ds(lane, LANES)], r.key_value.at[slot, i], r.key_sem.at[slot, i])
 
-    pair_grads = (r.rows.at[:, 0 : 2 * KEY_WIDTH], r.grads.at[:, 0 : 2 * KEY_WIDTH])
+    pair_grads = (r.rows, r.grads.at[:, 0 : 2 * KEY_WIDTH])
 
     def chunk(of_chip, of_core):
         return pair_grads[0].at[pl.ds(pl.multiple_of((2 * of_chip + of_core) * rows, rows), rows)]
@@ -1465,23 +1523,37 @@
 
     serve = line.serve
     SERVICE = (
-        (0, (lambda: serve([3], [0]),)),
-        (1, (lambda: serve([], [1]),)),
-        (2, (lambda: serve([4], [2, 3]),)),
-        (3, (pair_sum.trade, lambda: prepare(1), lambda: serve([5, 6], [4], [0, 1]), pair_sum.meet)),
-        (4, (lambda: serve([7], [], [2]),)),
-        (5, (lambda: pair_sum.step(2), lambda: serve([], [5, 6], [3]))),
-        (6, (lambda: serve([], [7], [4]),)),
-        (7, (lambda: pair_sum.step(3), lambda: serve([], [], [5]))),
+        (1, (lambda: serve([3], [1]),)),
+        (2, (lambda: serve([4], [2], [0]),)),
+        (3, (pair_sum.trade, lambda: prepare(1), lambda: serve([5], [3], [1]), pair_sum.meet)),
+        (4, (lambda: serve([6], [4], [2]),)),
+        (5, (lambda: serve([7], [5], [3]),)),
+        (6, (lambda: serve([], [6], [4]), lambda: pair_sum.step(2))),
+        (7, (lambda: serve([], [7], [5]),)),
     )
     for i in range(2):
         key_load(0, 0, i).start()
-    serve([0])
+    for copy in vector_loads:
+        copy.wait()
+    serve([1])
     prepare(0)
-    serve([1, 2])
+    serve([2], [0])
     lax.fori_loop(0, MB * PAIRS, pair_step, 0)
     second = local(pair_grads[1], r.pair_grad, r.rest_sem.at[3])
     second.start()
+    emits = [
+        local(source, target, r.emit_sem.at[i])
+        for i, (source, target) in enumerate(
+            (
+                (r.query_low, r.query_low_out),
+                (r.middle_low, r.middle_low_out),
+                (r.middle_grad, r.middle_grad_out),
+            )
+        )
+    ]
+    for copy in emits:
+        copy.start()
+    pair_sum.step(3)
     own_loads[MB].wait()
     total = r.middle[0:rows] + r.result_own[...].astype(f32)
     for k in range(1, SHARDS):
@@ -1491,7 +1563,8 @@
     serve([], [], [6])
     pair_sum.finish(r.pair_low, r.cosine, r.sine)
     serve([], [], [7])
-    second.wait()
+    for copy in [second] + emits:
+        copy.wait()
 
     for copy in trades[1]:
         copy.wait_send()
@@ -1505,7 +1578,7 @@
     line.drain()
 
 
-def backward(query, starts, cosine, sine, middle, cotangent, gain, pairs, row_blocks, grad_blocks, pieces, results, row_grads, output_weight):
+def backward(query, starts, cosine, sine, middle, cotangent, gain, pairs, turned_rows, grad_blocks, pieces, results, row_grads, output_weight):
     rows = cosine.shape[0]
     length = pairs.shape[1]
     held_rows = 2 * MODEL_WIDTH
@@ -1520,8 +1593,9 @@
     number = 2 * PARTS
     return pl.pallas_call(
         backward_kernel,
-        in_specs=[vmem, pl.BlockSpec(memory_space=pltpu.SMEM)] + [vmem] * 5 + [anywhere] * 9,
-        out_specs=[vmem] * 6 + [anywhere] * 6,
+        in_specs=[anywhere, pl.BlockSpec(memory_space=pltpu.SMEM), vmem, vmem, anywhere, anywhere, vmem]
+        + [anywhere] * 9,
+        out_specs=[anywhere, vmem, anywhere, anywhere, vmem, vmem] + [anywhere] * 6,
         out_shape=[
             shape(query.shape, bf16),
             shape((rows, 2 * KEY_WIDTH), bf16),
@@ -1537,7 +1611,13 @@
             shape((length, 2 * KEY_WIDTH), bf16),
         ],
         scratch_shapes=[
-            low((tokens, MODEL_WIDTH)),
+            low((MB * rows, MODEL_WIDTH)),
+            pltpu.VMEM((MB * rows, MODEL_WIDTH), f32),
+            low((MB * rows, MODEL_WIDTH)),
+            low((MB * rows, MODEL_WIDTH)),
+            low((MB * rows, MODEL_WIDTH)),
+            pltpu.VMEM((MB * rows, MODEL_WIDTH), f32),
+            low((length, 2 * KEY_WIDTH)),
             low((MODEL_WIDTH, tokens)),
             low((tokens, MODEL_WIDTH)),
             low((3 * tokens, 2 * F)),
@@ -1573,12 +1653,13 @@
             dma((2, LINE)),
             dma((2, LINE - 1)),
         ]
-        + line_sems(number),
+        + line_sems(number)
+        + [dma((3,))],
         compiler_params=pltpu.CompilerParams(
             collective_id=3, has_side_effects=True, vmem_limit_bytes=VMEM_LIMIT
         ),
         name="backward",
-    )(query, starts, cosine, sine, middle, cotangent, gain, pairs, row_blocks, grad_blocks, *pieces, results, row_grads, output_weight)
+    )(query, starts, cosine, sine, middle, cotangent, gain, pairs, turned_rows, grad_blocks, *pieces, results, row_grads, output_weight)
 
 
 DENSE = ("output", "query", "pair", "gain")
@@ -1589,18 +1670,18 @@
 
 
 def dense_kernel(
-    turned_normed,
-    turned_attn,
-    query_low,
+    turned_normed_src,
+    turned_attn_src,
+    query_low_src,
     pair_low_first,
-    middle_low,
-    middle_grad,
-    tokens,
+    middle_low_src,
     gain,
     gain_grad,
     cosine,
     sine,
-    middle,
+    middle_grad_src,
+    tokens_src,
+    middle_src,
     query_src,
     pair_src,
     pair_grad,
@@ -1608,7 +1689,7 @@
     gate_rest,
     up_rest,
     down_rest,
-    input_grad,
+    input_grad_out,
     block_output,
     results_in,
     output_total,
@@ -1618,6 +1699,14 @@
     gate_total,
     up_total,
     down_total,
+    turned_normed,
+    turned_attn,
+    query_low,
+    middle_low,
+    input_grad,
+    middle_grad,
+    tokens,
+    middle,
     pair_low,
     pair_own,
     pair_other,
@@ -1671,12 +1760,13 @@
     back_sem,
     pass_sem,
     store_sem,
+    emit_sem,
 ):
     r = types.SimpleNamespace(**locals())
     at = lambda kind, name: getattr(r, kind + "_" + name)
     place = Place()
     core, shard = place.core, place.shard
-    rows = r.tokens.shape[0] // MB
+    rows = r.middle.shape[0]
     held = MODEL_WIDTH // SHARDS
     half = held // 2
     loads = [
@@ -1689,6 +1779,13 @@
                 (r.query_src, r.query_weight),
                 (r.pair_src, r.pair_weight),
                 (r.pair_grad.at[:, core], r.pair_own),
+                (r.middle_grad_src, r.middle_grad),
+                (r.tokens_src, r.tokens),
+                (r.middle_src.at[rows : 2 * rows], r.middle),
+                (r.turned_attn_src, r.turned_attn),
+                (r.middle_low_src, r.middle_low),
+                (r.turned_normed_src, r.turned_normed),
+                (r.query_low_src, r.query_low),
             )
         )
     ]
@@ -1716,11 +1813,12 @@
             place, at("sum", name), at("near", name), at("far", name), getattr(r, name + "_total"), parts
         )
     line = Line(place, pieces, (r.near_sem, r.far_sem, r.back_sem, r.pass_sem, r.store_sem))
-    for i in range(3):
-        loads[i].wait()
+    loads[0].wait()
     line.ready(0)
     loads[5].wait()
     pair_sum.meet()
+    for i in (1, 2):
+        loads[i].wait()
     line.ready(*range(1, expert_pieces))
 
     def block(b, of_core):
@@ -1759,6 +1857,8 @@
         across = at("across", name)
         add_into(at("sum", name), at("own", name).at[shard], *[across.at[k] for k in range(SHARDS - 1)])
 
+    for load in loads[9:]:
+        load.wait()
     dense("output", r.turned_attn, r.middle_low, r.send_output)
     dense("query", r.turned_normed, r.query_low, r.send_query)
     meet("output")
@@ -1772,7 +1872,7 @@
     pair_sum.finish(r.pair_low.at[rows : 2 * rows], r.cosine, r.sine)
     dense("pair", r.turned_normed, r.pair_low, r.send_output.at[:, :, 0 : 2 * KEY_WIDTH])
     line.serve([1], [0])
-    for load in loads[3:5]:
+    for load in loads[3:5] + loads[6:9]:
         load.wait()
 
     gain_one_grad = jnp.zeros((1, MODEL_WIDTH), f32)
@@ -1783,13 +1883,15 @@
         unit = values * scale
         normed_grad = dot(r.query_low[own], r.query_weight[...], NT) + dot(r.pair_low[own], r.pair_weight[...], NT)
         gain_one_grad = gain_one_grad + jnp.sum(normed_grad * unit, axis=0, keepdims=True)
-        weighted = normed_grad * r.gain[...]
+        weighted = normed_grad * r.gain[0:1]
         inner = jnp.mean(weighted * unit, axis=-1, keepdims=True)
         r.input_grad[own] = r.middle_grad[own] + (weighted - unit * inner) * scale
         if m == 0:
             meet("pair")
             line.serve([2], [1])
     line.serve([3], [2])
+    grad_emit = pltpu.make_async_copy(r.input_grad, r.input_grad_out, r.emit_sem.at[0])
+    grad_emit.start()
     gain_two_grad = jnp.sum(r.gain_grad[...], axis=0, keepdims=True)
     stacked = jnp.concatenate(
         [gain_one_grad, gain_two_grad, jnp.zeros((LANES - 2, MODEL_WIDTH), f32)], axis=0
@@ -1813,7 +1915,7 @@
         copy.wait_send()
     result_parts = [r.send_output.at[k, 0:rows] for k in range(SHARDS)]
     result_loads = [
-        pltpu.make_async_copy(source, target, r.load_sem.at[6 + k])
+        pltpu.make_async_copy(source, target, r.load_sem.at[13 + k])
         for k, (source, target) in enumerate(
             zip([r.results_src.at[1, shard]] + [r.results_in.at[k] for k in range(SHARDS - 1)], result_parts)
         )
@@ -1859,10 +1961,11 @@
     for copy in result_copies:
         copy.wait_send()
     pair_sum.drain()
+    grad_emit.wait()
     line.drain()
 
 
-def dense_weights(vectors, query_weight, pair_weight, pair_grad, results, rests):
+def dense_weights(vectors, streamed, query_weight, pair_weight, pair_grad, results, rests):
     dma = pltpu.SemaphoreType.DMA
     anywhere = pl.BlockSpec(memory_space=pl.ANY)
     vmem = pl.BlockSpec(memory_space=pltpu.VMEM)
@@ -1876,8 +1979,8 @@
     number = 4 * FINE + 3 * DENSE_PARTS + 1
     return pl.pallas_call(
         dense_kernel,
-        in_specs=[vmem] * len(vectors) + [anywhere] * 7,
-        out_specs=[vmem] * 2 + [anywhere] * 8,
+        in_specs=[anywhere] * 3 + [vmem, anywhere] + [vmem] * 4 + [anywhere] * (7 + len(streamed)),
+        out_specs=[anywhere, vmem] + [anywhere] * 8,
         out_shape=[
             shape((MB * rows, MODEL_WIDTH), f32),
             shape((rows, MODEL_WIDTH), bf16),
@@ -1890,6 +1993,14 @@
             shape((2 * F, MODEL_WIDTH), bf16),
         ],
         scratch_shapes=[
+            low(MODEL_WIDTH, MB * rows),
+            low(MODEL_WIDTH, MB * rows),
+            low(MB * rows, MODEL_WIDTH),
+            low(MB * rows, MODEL_WIDTH),
+            pltpu.VMEM((MB * rows, MODEL_WIDTH), f32),
+            pltpu.VMEM((MB * rows, MODEL_WIDTH), f32),
+            low(MB * rows, MODEL_WIDTH),
+            pltpu.VMEM((rows, MODEL_WIDTH), f32),
             low(MB * rows, 2 * KEY_WIDTH),
             low(LINE, rows, 2 * KEY_WIDTH),
             low(LINE, rows, 2 * KEY_WIDTH),
@@ -1904,38 +2015,74 @@
         + [low(SHARDS - 1, half, w) for w in widths]
         + [low(half, w) for w in widths] * 3
         + [low(*tall), low(*tall), low(F, MODEL_WIDTH)] * 3
-        + [dma((6 + SHARDS,)), dma((2, LINE)), dma((2, LINE - 1)), dma((2, SHARDS - 1)), dma((2, 4 * SHARDS)), dma((2, 4 * (SHARDS - 1)))]
-        + line_sems(number),
+        + [dma((13 + SHARDS,)), dma((2, LINE)), dma((2, LINE - 1)), dma((2, SHARDS - 1)), dma((2, 4 * SHARDS)), dma((2, 4 * (SHARDS - 1)))]
+        + line_sems(number)
+        + [dma((1,))],
         compiler_params=pltpu.CompilerParams(
             collective_id=4, has_side_effects=True, vmem_limit_bytes=VMEM_LIMIT
         ),
         name="dense_weights",
-    )(*vectors, query_weight, pair_weight, pair_grad, results, *rests)
-
-
-def widen_kernel(gate_first, gate_second, up_first, up_second, *refs):
-    count = len(refs) // 2
-    expand_out = refs[count]
-    for i, ref in enumerate((gate_first, gate_second, up_first, up_second)):
+    )(*vectors, *streamed, query_weight, pair_weight, pair_grad, results, *rests)
+
+
+def widen_kernel(*refs):
+    r = refs
+    step = pl.program_id(0)
+    parts, (shrink, dense, rows_in, gains, grad) = r[:4], (r[4], r[5:8], r[8:10], r[10], r[11])
+    expand_out, shrink_out, dense_out, rows_out, gain_outs, grad_out = r[12], r[13], r[14:17], r[17], r[18:20], r[20]
+    for i, ref in enumerate(parts):
         expand_out[:, i * F_BLOCK : (i + 1) * F_BLOCK] = ref[...].astype(f32)
-    for source, target in zip(refs[:count], refs[count + 1 :]):
+    shrink_out[...] = shrink[...].astype(f32)
+    grad_out[...] = grad[...]
+
+    for source, target in zip(dense, dense_out):
         target[...] = source[...].astype(f32)
 
-
-def widen(expand_parts, arrays):
-    steps = 8
-    block = lambda a, c: pl.BlockSpec((a.shape[0] // steps, c), lambda i: (i, 0))
-    rows = expand_parts[0].shape[0]
-    outs = [jax.ShapeDtypeStruct((rows, 2 * F), f32)] + [jax.ShapeDtypeStruct(a.shape, f32) for a in arrays]
+    for i in range(MB):
+
+        @pl.when(step // (WIDEN_STEPS // MB) == i)
+        def _():
+            rows_out[...] = rows_in[i][...]
+
+    @pl.when(step == 0)
+    def _():
+        turned = gains[...].astype(f32).T
+        for i in range(2):
+            gain_outs[i][...] = turned[i]
+
+
+WIDEN_STEPS = 8
+
+
+def widen(expand_parts, shrink, dense, rows, gains, grad):
+    n = WIDEN_STEPS
+    every = lambda a: pl.BlockSpec((a.shape[0] // n, a.shape[1]), lambda i: (i, 0))
+    one = lambda a: pl.BlockSpec(a.shape, lambda i: (0, 0))
+    size = MB * rows[0].shape[0] // n
+    half = lambda m: pl.BlockSpec(
+        (size, MODEL_WIDTH), lambda i: (jnp.clip(i - m * (n // MB), 0, n // MB - 1), 0)
+    )
+    shape = jax.ShapeDtypeStruct
+    expand = shape((expand_parts[0].shape[0], 2 * F), f32)
+    joined = shape((MB * rows[0].shape[0], MODEL_WIDTH), bf16)
+    gain = shape((gains.shape[0],), f32)
+    flat = pl.BlockSpec(gain.shape, lambda i: (0,))
+    dense_out = [shape(a.shape, f32) for a in dense]
     return pl.pallas_call(
         widen_kernel,
-        grid=(steps,),
-        in_specs=[block(a, a.shape[1]) for a in (*expand_parts, *arrays)],
-        out_specs=[block(a, a.shape[1]) for a in outs],
-        out_shape=outs,
+        grid=(n,),
+        in_specs=[every(a) for a in expand_parts]
+        + [every(shrink)]
+        + [every(a) for a in dense]
+        + [half(m) for m in range(MB)]
+        + [one(gains), every(grad)],
+        out_specs=[every(expand), every(shrink)]
+        + [every(a) for a in dense]
+        + [every(joined), flat, flat, every(grad)],
+        out_shape=[expand, shape(shrink.shape, f32), *dense_out, joined, gain, gain, shape(grad.shape, f32)],
         compiler_params=pltpu.CompilerParams(vmem_limit_bytes=VMEM_LIMIT),
         name="widen",
-    )(*expand_parts, *arrays)
+    )(*expand_parts, shrink, *dense, *rows, gains, grad)
 
 
 def shards(
@@ -1974,7 +2121,7 @@
             query_weight,
             output_weight,
             pairs,
-            row_blocks,
+            turned_rows,
             grad_blocks,
             result_blocks,
             row_grad_blocks,
@@ -1983,8 +2130,8 @@
             up,
         ) = forward(
             flat_tokens,
-            routes[:, 0].transpose(0, 2, 1),
-            gates[:, 0].transpose(0, 2, 1),
+            routes.transpose(0, 1, 3, 2),
+            gates.transpose(0, 1, 3, 2),
             jnp.stack([attn_gain, moe_gain]),
             flat_cotangent,
             starts,
@@ -1993,10 +2140,8 @@
             expert_in,
             expert_out,
         )
-        result_blocks = result_blocks.reshape(row_blocks.shape)
-        row_grad_blocks = row_grad_blocks.reshape(row_blocks.shape)
-        gains = gains.reshape(SHARDS, GAIN_ROWS, width).astype(f32)
-        gain_one, gain_two = gains[:, 0].reshape(1, MODEL_WIDTH), gains[:, 1].reshape(1, MODEL_WIDTH)
+        result_blocks = result_blocks.reshape(grad_blocks.shape)
+        row_grad_blocks = row_grad_blocks.reshape(grad_blocks.shape)
         (
             query_low,
             pair_low,
@@ -2017,9 +2162,9 @@
             sine,
             middle,
             flat_cotangent,
-            gain_two,
+            gains,
             pairs,
-            row_blocks,
+            turned_rows,
             grad_blocks,
             (active, gate, up),
             result_blocks,
@@ -2044,32 +2189,44 @@
                 query_low,
                 pair_low,
                 middle_low,
-                middle_grad,
-                flat_tokens,
-                gain_one,
+                gains,
                 gain_two_grad,
                 cosine,
                 sine,
-                middle[rows:],
             ),
+            (middle_grad, flat_tokens, middle),
             query_weight,
             pair_weight,
             pair_grad.reshape(LINE, 2, rows, 2 * KEY_WIDTH),
             result_blocks,
             (gate_rest, up_rest, down_rest.reshape(F, MODEL_WIDTH)),
         )
-        expand_total, shrink_total, output_total, query_total, pair_total = widen(
+        (
+            expand_total,
+            shrink_total,
+            output_total,
+            query_total,
+            pair_total,
+            block_output,
+            gain_one_total,
+            gain_two_total,
+            input_grad,
+        ) = widen(
             (gate_first, gate_second, up_first, up_second),
-            (shrink_total, output_total, query_total, pair_total),
+            shrink_total,
+            (output_total, query_total, pair_total),
+            (output_first, output_second),
+            gain_total,
+            input_grad,
         )
         return (
-            jnp.stack([output_first, output_second])[:, None],
+            block_output.reshape(MB, 1, rows, MODEL_WIDTH),
             input_grad.reshape(MB, 1, rows, MODEL_WIDTH),
-            gain_total[:, 0].astype(f32),
+            gain_one_total,
             query_total,
             pair_total,
             output_total,
-            gain_total[:, 1].astype(f32),
+            gain_two_total,
             expand_total.reshape(held, MODEL_WIDTH, 2 * F),
             shrink_total.reshape(held, F, MODEL_WIDTH),
         )

time: 380 us -> 366 us (0.963)
  Pallas kernels: 364 us -> 357 us
    pallas_call x3, Pallas kernels: 236 us -> 230 us  [the longest x1 139 us: dense_weights(): pl.pallas_call(dense_kernel, in_specs=[anywhere] * 3 + [vmem, anywhere] +...]
where the time goes in v6:
time: 366 us; the launch traced here: 360 us
  Pallas kernels  357 us (98%)
    pallas_call x1, Pallas kernels, dense_weights(): pl.pallas_call(dense_kernel, in_specs=[anywhere] * 3 + [vmem, anywhere] +...  139 us
    pallas_call x1, Pallas kernels, forward(): pl.pallas_call(forward_kernel, in_specs=[vmem] * 5 + [pl.BlockSpec(memory...  127 us
    pallas_call x1, Pallas kernels, backward(): pl.pallas_call(backward_kernel, in_specs=[anywhere, pl.BlockSpec(memory_s...  74.8 us
    pallas_call x1, Pallas kernels, widen(): pl.pallas_call(widen_kernel, grid=(n,), in_specs=[every(a) for a in expan...  16.2 us

profile of v6, /device:TPU:0, one launch (start us, length us, event | category | flops | bytes accessed | tf_op | source)
XLA Modules:
  0.0 359.6 jit_solution(18300416224309408710)
XLA Ops:
  0.6 0.7 stack.9
  1.3 0.7 stack.10
  2.0 0.6 pad_maximum_fusion.gain_pair
  2.6 127.2 %forward.1 = (bf16[1536,256]{1,0:T(8,128)(2,1)}, bf16[256,1536]{1,0:T(8,128)(2,1)}, bf16[1536,256]{1,0:T(8,128)(2,1)}, f32[256,1536]{1,0:T(8,128)}, f32[8,1536]{...) custom-call(bf16[256,1536]{1,0:T(8,128)(2,1)} %bitcast.19, ...), custom_call_target="tpu_custom_call" | custom-call | tf_op jit(solution)/shard_map/forward/pallas_call | solution.py:972
  129.8 74.8 %backward.1 = (bf16[256,1536]{1,0:T(8,128)(2,1)}, bf16[128,1024]{1,0:T(8,128)(2,1)}, bf16[256,1536]{1,0:T(8,128)(2,1)}, f32[256,1536]{1,0:T(8,128)}, f32[8,1536]...) custom-call(bf16[256,1536]{1,0:T(8,128)(2,1)} %get-tuple-element.57., ...), custom_call_target="tpu_custom_call" | custom-call | tf_op jit(solution)/shard_map/backward/pallas_call | solution.py:1594
  204.6 138.5 %dense_weights.1 = (f32[256,1536]{1,0:T(8,128)}, bf16[128,1536]{1,0:T(8,128)(2,1)}, bf16[3,128,1536]{2,1,0:T(8,128)(2,1)}, bf16[384,1536]{1,0:T(8,128)(2,1)}, bf...) custom-call(bf16[1536,256]{1,0:T(8,128)(2,1)} %get-tuple-element.72., ...), custom_call_target="tpu_custom_call" | custom-call | tf_op jit(solution)/shard_map/dense_weights/pallas_call | solution.py:1980
  343.1 16.2 %widen.1 = (f32[3072,1024]{1,0:T(8,128)}, f32[1024,1536]{1,0:T(8,128)}, f32[384,1536]{1,0:T(8,128)}, f32[384,1536]{1,0:T(8,128)}, f32[384,1024]{1,0:T(8,128)}, /...) custom-call(bf16[3072,256]{1,0:T(8,128)(2,1)} %get-tuple-element.71.refs_0_, ...), custom_call_target="tpu_custom_call" | custom-call | tf_op jit(solution)/shard_map/widen/pallas_call | solution.py:2071

commit v7 on v6

--- a/solution.py
+++ b/solution.py
@@ -843,10 +843,13 @@
             (r.grads_all.at[m], r.grads_out.at[m]),
             (results, r.results_out.at[m]),
             (row_grads, r.row_grads_out.at[m]),
-            (active, r.active_out.at[m]),
-            (gate, r.gate_out.at[m]),
-            (up, r.up_out.at[m]),
         )
+        for e in range(2):
+            columns = slice(e * F, (e + 1) * F)
+            pairs += tuple(
+                (source.at[:, columns], target.at[m, :, columns])
+                for source, target in ((active, r.active_out), (gate, r.gate_out), (up, r.up_out))
+            )
         return [local(a, b, r.emit_sem.at[m * len(pairs) + i]) for i, (a, b) in enumerate(pairs)]
 
     def expert_steps(m, between):
@@ -928,32 +931,40 @@
     turn(0)
     for emit in emits(0):
         emit.start()
+    for emit in early:
+        emit.wait()
+
+    for copy in small_copies:
+        copy.wait_send()
+    sent_weight(2)
+    for m in range(MB):
+        for t in range(1, LINE):
+            for direction in (1, -1):
+
+                @pl.when(sends(t, direction))
+                def _():
+                    move(m, t, direction).wait_send()
+
+    for square in grad_squares[:1] + row_squares[:1]:
+        square.drain()
     grad_squares[1].pass_on()
     row_squares[1].finish()
     for emit in emits(0):
         emit.wait()
     turn(1)
     grad_squares[1].finish()
-    expert_steps(1, {})
-    for emit in emits(1):
+    last = emits(1)
+
+    def emit_first():
+        for emit in last[:2] + last[4:7]:
+            emit.start()
+
+    expert_steps(1, {1: emit_first})
+    for emit in last[2:4] + last[7:]:
         emit.start()
-    for emit in early:
-        emit.wait()
-
-    for copy in small_copies:
-        copy.wait_send()
-    sent_weight(2)
-    for m in range(MB):
-        for t in range(1, LINE):
-            for direction in (1, -1):
-
-                @pl.when(sends(t, direction))
-                def _():
-                    move(m, t, direction).wait_send()
-
-    for square in grad_squares + row_squares:
+    for square in grad_squares[1:] + row_squares[1:]:
         square.drain()
-    for emit in emits(1):
+    for emit in last:
         emit.wait()
 
 
@@ -1031,7 +1042,7 @@
             dma((2, 4 * MB)),
             dma((2, 4 * MB)),
             dma((2, 2)),
-            dma((7 * MB,)),
+            dma((10 * MB,)),
             dma((4,)),
         ],
         compiler_params=pltpu.CompilerParams(
@@ -1122,10 +1133,12 @@
                 self.outward[i].wait_recv()
                 self.pass_outer[i].start()
 
-    def drain(self):
+    def drain(self, items=None):
+        items = range(len(self.pieces)) if items is None else items
+
         @pl.when(self.inner)
         def _():
-            for i in range(len(self.pieces)):
+            for i in items:
                 self.facing[i].wait_send()
                 self.outward[i].wait_send()
                 self.pass_inner[i].wait_send()
@@ -1133,12 +1146,12 @@
 
         @pl.when(jnp.logical_not(self.inner))
         def _():
-            for i in range(len(self.pieces)):
+            for i in items:
                 self.inward[i].wait_send()
                 self.pass_outer[i].wait_send()
 
-        for copy in self.pass_outer:
-            copy.wait_recv()
+        for i in items:
+            self.pass_outer[i].wait_recv()
 
 
 def line_sems(number):
@@ -1174,10 +1187,15 @@
         for copy in self.trades:
             copy.start()
 
-    def move(self, t):
+    def half(self, ref, h):
+        size = ref.shape[0] // 2
+        return ref.at[h * size : (h + 1) * size]
+
+    def move(self, t, h):
         owner = jnp.clip(self.place.chip - (LINE - t), 0, LAST)
         device = self.place.chip_device(jnp.clip(self.place.chip - 1, 0, LAST))
-        return remote(self.own(owner), self.lands.at[t - 1], self.left_sem, t - 1, device)
+        source, target = self.half(self.own(owner), h), self.half(self.lands.at[t - 1], h)
+        return remote(source, target, self.left_sem, 2 * (t - 1) + h, device)
 
     def meet(self):
         for j in range(LINE):
@@ -1187,23 +1205,26 @@
         @pl.when(self.past == 0)
         def _():
             for t in range(1, LINE):
-                self.move(t).start()
-
-    def take(self, t):
-        self.move(t).wait_recv()
-        owner = jnp.clip(self.place.chip - (LAST - t), 0, LAST)
-        add_into(self.own(owner), self.own(owner), self.lands.at[t - 1])
+                for h in range(2):
+                    self.move(t, h).start()
+
+    def take(self, t, h):
+        self.move(t, h).wait_recv()
+        mine = self.half(self.own(jnp.clip(self.place.chip - (LAST - t), 0, LAST)), h)
+        add_into(mine, mine, self.half(self.lands.at[t - 1], h))
 
     def step(self, t):
         @pl.when((self.past >= 1) & (self.past <= min(t - 1, LINE - 2)))
         def _():
-            self.take(t - 1)
-            self.move(t).start()
+            for h in range(2):
+                self.take(t - 1, h)
+                self.move(t, h).start()
 
     def finish(self, out, cosine, sine):
         @pl.when(self.past >= 1)
         def _():
-            self.take(LAST)
+            for h in range(2):
+                self.take(LAST, h)
 
         mine = self.own(self.place.chip)
         for i in range(2 * KEY_WIDTH // LANES):
@@ -1220,7 +1241,8 @@
 
             @pl.when((self.past <= t - 1) & (self.past <= LINE - 2))
             def _():
-                self.move(t).wait_send()
+                for h in range(2):
+                    self.move(t, h).wait_send()
 
 
 PARTS = 4
@@ -1560,12 +1582,6 @@
         result_copies[k - 1].wait_recv()
         total = total + r.result_in[k - 1].astype(f32)
     r.block_output[...] = total.astype(bf16)
-    serve([], [], [6])
-    pair_sum.finish(r.pair_low, r.cosine, r.sine)
-    serve([], [], [7])
-    for copy in [second] + emits:
-        copy.wait()
-
     for copy in trades[1]:
         copy.wait_send()
     for copy in rests:
@@ -1574,8 +1590,14 @@
         copy.wait_send()
     for copy in result_copies:
         copy.wait_send()
+    line.drain(range(4))
+    serve([], [], [6, 7])
+    pair_sum.finish(r.pair_low, r.cosine, r.sine)
+    for copy in [second] + emits:
+        copy.wait()
+
     pair_sum.drain()
-    line.drain()
+    line.drain(range(4, 2 * PARTS))
 
 
 def backward(query, starts, cosine, sine, middle, cotangent, gain, pairs, turned_rows, grad_blocks, pieces, results, row_grads, output_weight):
@@ -1651,7 +1673,7 @@
             dma((2, SHARDS - 1)),
             dma((2, 2)),
             dma((2, LINE)),
-            dma((2, LINE - 1)),
+            dma((2, 2 * (LINE - 1))),
         ]
         + line_sems(number)
         + [dma((3,))],
@@ -1667,6 +1689,7 @@
 FINE = 4
 GATHER_AFTER = {4: ("output",), 9: ("query",), 13: ("pair", "gain")}
 OUTPUT_AFTER = 19
+DRAIN_LAG = 8
 
 
 def dense_kernel(
@@ -1949,20 +1972,22 @@
         for name in GATHER_AFTER.get(i, ()):
             gather(name)
             line.ready(*spans[name])
+        if DRAIN_LAG <= i < number:
+            line.drain([i - DRAIN_LAG])
         if i == OUTPUT_AFTER:
             output_rows()
-
-    for name in DENSE:
-        for copy in crossings[name]:
-            copy.wait_send()
-        if name in ("query", "gain"):
-            for copy in trades[name]:
+            for name in DENSE:
+                for copy in crossings[name]:
+                    copy.wait_send()
+                if name in ("query", "gain"):
+                    for copy in trades[name]:
+                        copy.wait_send()
+            for copy in result_copies:
                 copy.wait_send()
-    for copy in result_copies:
-        copy.wait_send()
-    pair_sum.drain()
+            pair_sum.drain()
+
     grad_emit.wait()
-    line.drain()
+    line.drain(range(number - DRAIN_LAG, number))
 
 
 def dense_weights(vectors, streamed, query_weight, pair_weight, pair_grad, results, rests):
@@ -2015,7 +2040,7 @@
         + [low(SHARDS - 1, half, w) for w in widths]
         + [low(half, w) for w in widths] * 3
         + [low(*tall), low(*tall), low(F, MODEL_WIDTH)] * 3
-        + [dma((13 + SHARDS,)), dma((2, LINE)), dma((2, LINE - 1)), dma((2, SHARDS - 1)), dma((2, 4 * SHARDS)), dma((2, 4 * (SHARDS - 1)))]
+        + [dma((13 + SHARDS,)), dma((2, LINE)), dma((2, 2 * (LINE - 1))), dma((2, SHARDS - 1)), dma((2, 4 * SHARDS)), dma((2, 4 * (SHARDS - 1)))]
         + line_sems(number)
         + [dma((1,))],
         compiler_params=pltpu.CompilerParams(
@@ -2051,7 +2076,7 @@
             gain_outs[i][...] = turned[i]
 
 
-WIDEN_STEPS = 8
+WIDEN_STEPS = 4
 
 
 def widen(expand_parts, shrink, dense, rows, gains, grad):

time: 366 us -> 364 us (level)
  no operation moved by 1% of the time
where the time goes in v7:
time: 364 us; the launch traced here: 358 us
  Pallas kernels  355 us (98%)
    pallas_call x1, Pallas kernels, dense_weights(): pl.pallas_call(dense_kernel, in_specs=[anywhere] * 3 + [vmem, anywhere] +...  140 us
    pallas_call x1, Pallas kernels, forward(): pl.pallas_call(forward_kernel, in_specs=[vmem] * 5 + [pl.BlockSpec(memory...  127 us
    pallas_call x1, Pallas kernels, backward(): pl.pallas_call(backward_kernel, in_specs=[anywhere, pl.BlockSpec(memory_s...  73.2 us
    pallas_call x1, Pallas kernels, widen(): pl.pallas_call(widen_kernel, grid=(n,), in_specs=[every(a) for a in expan...  14.7 us

profile of v7, /device:TPU:0, one launch (start us, length us, event | category | flops | bytes accessed | tf_op | source)
XLA Modules:
  0.0 358.0 jit_solution(2976769589529743105)
XLA Ops:
  0.6 0.7 stack.9
  1.3 0.7 stack.10
  2.0 0.6 pad_maximum_fusion.gain_pair
  2.6 126.9 %forward.1 = (bf16[1536,256]{1,0:T(8,128)(2,1)}, bf16[256,1536]{1,0:T(8,128)(2,1)}, bf16[1536,256]{1,0:T(8,128)(2,1)}, f32[256,1536]{1,0:T(8,128)}, f32[8,1536]{...) custom-call(bf16[256,1536]{1,0:T(8,128)(2,1)} %bitcast.19, ...), custom_call_target="tpu_custom_call" | custom-call | tf_op jit(solution)/shard_map/forward/pallas_call | solution.py:983
  129.5 73.2 %backward.1 = (bf16[256,1536]{1,0:T(8,128)(2,1)}, bf16[128,1024]{1,0:T(8,128)(2,1)}, bf16[256,1536]{1,0:T(8,128)(2,1)}, f32[256,1536]{1,0:T(8,128)}, f32[8,1536]...) custom-call(bf16[256,1536]{1,0:T(8,128)(2,1)} %get-tuple-element.57., ...), custom_call_target="tpu_custom_call" | custom-call | tf_op jit(solution)/shard_map/backward/pallas_call | solution.py:1616
  202.7 140.2 %dense_weights.1 = (f32[256,1536]{1,0:T(8,128)}, bf16[128,1536]{1,0:T(8,128)(2,1)}, bf16[3,128,1536]{2,1,0:T(8,128)(2,1)}, bf16[384,1536]{1,0:T(8,128)(2,1)}, bf...) custom-call(bf16[1536,256]{1,0:T(8,128)(2,1)} %get-tuple-element.72., ...), custom_call_target="tpu_custom_call" | custom-call | tf_op jit(solution)/shard_map/dense_weights/pallas_call | solution.py:2005
  342.9 14.7 %widen.1 = (f32[3072,1024]{1,0:T(8,128)}, f32[1024,1536]{1,0:T(8,128)}, f32[384,1536]{1,0:T(8,128)}, f32[384,1536]{1,0:T(8,128)}, f32[384,1024]{1,0:T(8,128)}, /...) custom-call(bf16[3072,256]{1,0:T(8,128)(2,1)} %get-tuple-element.71.refs_0_, ...), custom_call_target="tpu_custom_call" | custom-call | tf_op jit(solution)/shard_map/widen/pallas_call | solution.py:2096

commit v8 on v7

--- a/solution.py
+++ b/solution.py
@@ -1382,61 +1382,71 @@
     sends = (r.send_gate, r.send_up, r.send_down)
     owns = (r.own_gate, r.own_up, r.own_down)
     others = (r.other_gate, r.other_up, r.other_down)
-    trades = [
-        [remote(sends[i], others[i].at[b], r.trade_sem, b * 3 + i, place.partner) for i in range(3)]
-        for b in range(2)
-    ]
-
-    def weight_block(b, expert, outs):
+    upper = MODEL_WIDTH // 2
+    parts = [(0, 0), (0, upper), (1, None)]
+
+    def some(ref, start):
+        return ref if start is None else ref.at[start : start + upper]
+
+    trades = {}
+    for b, start in parts:
+        for i in range(2):
+            index = len(trades)
+            trades[b, start, i] = remote(
+                some(sends[i], start), some(others[i].at[b], start), r.trade_sem, index, place.partner
+            )
+    for b in range(2):
+        trades[b, None, 2] = remote(sends[2], others[2].at[b], r.trade_sem, len(trades), place.partner)
+
+    def weight_block(b, start, expert, outs):
         column = pl.ds(pl.multiple_of(expert * F + b * F_BLOCK, F_BLOCK), F_BLOCK)
         for i in range(2):
-            outs[i][...] = dot(r.turned[...], r.pool[(i + 1) * tokens : (i + 2) * tokens, column]).astype(bf16)
+            part = r.pool[(i + 1) * tokens : (i + 2) * tokens, column]
+            some(outs[i], start)[...] = dot(some(r.turned, start)[...], part).astype(bf16)
 
     def down_block(b, expert, out):
         column = pl.ds(pl.multiple_of(expert * F + b * F_BLOCK, F_BLOCK), F_BLOCK)
         out[...] = dot(r.pool[0:tokens, column], r.grads[...], TN).astype(bf16)
 
-    def meet(b, i):
-        trades[b][i].wait_recv()
-        add_into(owns[i].at[b], owns[i].at[b], others[i].at[b])
-
-    pieces = []
-    for own, near, far, out in (
-        (r.own_gate.at[0], r.near_gate, r.far_gate, r.gate_total),
-        (r.own_up.at[0], r.near_up, r.far_up, r.up_total),
-    ):
-        pieces += line_pieces(place, own, near, far, out, PARTS)
+    def meet(b, start, i):
+        trades[b, start, i].wait_recv()
+        mine = some(owns[i].at[b], start)
+        add_into(mine, mine, some(others[i].at[b], start))
+
+    gate_pieces = line_pieces(place, r.own_gate.at[0], r.near_gate, r.far_gate, r.gate_total, PARTS)
+    up_pieces = line_pieces(place, r.own_up.at[0], r.near_up, r.far_up, r.up_total, PARTS)
+    middle_part = PARTS // 2
+    pieces = gate_pieces[:middle_part] + up_pieces[:middle_part] + gate_pieces[middle_part:] + up_pieces[middle_part:]
     line = Line(place, pieces, (r.near_sem, r.far_sem, r.back_sem, r.pass_sem, r.store_sem))
 
     for copy in piece_loads[: 2 * MB]:
         copy.wait()
-
-    def else_serve(b):
+    for n, (b, start) in enumerate(parts):
         if b == 1:
-            line.serve([0])
-
-    for b in range(2):
-        if b == 1:
-            for i in range(2):
-                trades[0][i].wait_send()
-        weight_block(b, 1 - core, sends)
+            for first in (0, upper):
+                for i in range(2):
+                    trades[0, first, i].wait_send()
+        weight_block(b, start, 1 - core, sends)
         for i in range(2):
-            trades[b][i].start()
-        weight_block(b, core, [own.at[b] for own in owns[:2]])
+            trades[b, start, i].start()
+        weight_block(b, start, core, [own.at[b] for own in owns[:2]])
         if b == 0:
             for i in range(2):
-                meet(0, i)
-                line.ready(*range(i * PARTS, (i + 1) * PARTS))
+                meet(b, start, i)
+                line.ready(*range((2 * n + i) * middle_part, (2 * n + i + 1) * middle_part))
+        if start == 0:
+            continue
+        if b == 0:
             for copy in piece_loads[2 * MB :] + grad_loads:
                 copy.wait()
         else:
-            trades[0][2].wait_send()
-        else_serve(b)
+            trades[0, None, 2].wait_send()
+            line.serve([0])
         down_block(b, 1 - core, sends[2])
-        trades[b][2].start()
+        trades[b, None, 2].start()
         down_block(b, core, owns[2].at[b])
         if b == 0:
-            meet(0, 2)
+            meet(0, None, 2)
 
     weight_loads = []
     for i in range(2):
@@ -1447,7 +1457,7 @@
     for copy in result_copies:
         copy.start()
     for i in range(3):
-        meet(1, i)
+        meet(1, None, i)
     rests = [
         local(r.own_gate.at[1], r.gate_rest, r.rest_sem.at[0]),
         local(r.own_up.at[1], r.up_rest, r.rest_sem.at[1]),
@@ -1545,13 +1555,14 @@
 
     serve = line.serve
     SERVICE = (
-        (1, (lambda: serve([3], [1]),)),
-        (2, (lambda: serve([4], [2], [0]),)),
-        (3, (pair_sum.trade, lambda: prepare(1), lambda: serve([5], [3], [1]), pair_sum.meet)),
-        (4, (lambda: serve([6], [4], [2]),)),
-        (5, (lambda: serve([7], [5], [3]),)),
-        (6, (lambda: serve([], [6], [4]), lambda: pair_sum.step(2))),
-        (7, (lambda: serve([], [7], [5]),)),
+        (0, (lambda: serve([3], [1]),)),
+        (1, (lambda: serve([4], [2]),)),
+        (2, (lambda: serve([5], [3], [0]),)),
+        (3, (pair_sum.trade, lambda: prepare(1), lambda: serve([6], [4], [1]), pair_sum.meet)),
+        (4, (lambda: serve([7], [5], [2]),)),
+        (5, (lambda: serve([], [6], [3]),)),
+        (6, (lambda: pair_sum.step(2), lambda: serve([], [7], [4]))),
+        (7, (lambda: serve([], [], [5]),)),
     )
     for i in range(2):
         key_load(0, 0, i).start()
@@ -1582,8 +1593,8 @@
         result_copies[k - 1].wait_recv()
         total = total + r.result_in[k - 1].astype(f32)
     r.block_output[...] = total.astype(bf16)
-    for copy in trades[1]:
-        copy.wait_send()
+    for i in range(3):
+        trades[1, None, i].wait_send()
     for copy in rests:
         copy.wait()
     for copy in row_copies:
@@ -1667,7 +1678,7 @@
             low((LINE - 1, rows, 2 * KEY_WIDTH)),
             dma((4 * MB * SHARDS,)),
             dma((2,)),
-            dma((2, 6)),
+            dma((2, 8)),
             dma((4,)),
             dma((2, MB * (SHARDS - 1))),
             dma((2, SHARDS - 1)),
@@ -2157,7 +2168,7 @@
             flat_tokens,
             routes.transpose(0, 1, 3, 2),
             gates.transpose(0, 1, 3, 2),
-            jnp.stack([attn_gain, moe_gain]),
+            jnp.concatenate([attn_gain, moe_gain]).reshape(2, width),
             flat_cotangent,
             starts,
             rotation_constants(length),

time: 364 us -> 362 us (level)
  no operation moved by 1% of the time
where the time goes in v8:
time: 362 us; the launch traced here: 357 us
  Pallas kernels  354 us (98%)
    pallas_call x1, Pallas kernels, dense_weights(): pl.pallas_call(dense_kernel, in_specs=[anywhere] * 3 + [vmem, anywhere] +...  142 us
    pallas_call x1, Pallas kernels, forward(): pl.pallas_call(forward_kernel, in_specs=[vmem] * 5 + [pl.BlockSpec(memory...  127 us
    pallas_call x1, Pallas kernels, backward(): pl.pallas_call(backward_kernel, in_specs=[anywhere, pl.BlockSpec(memory_s...  70.5 us
    pallas_call x1, Pallas kernels, widen(): pl.pallas_call(widen_kernel, grid=(n,), in_specs=[every(a) for a in expan...  14.7 us

profile of v8, /device:TPU:0, one launch (start us, length us, event | category | flops | bytes accessed | tf_op | source)
XLA Modules:
  0.0 356.6 jit_solution(14721188938881443673)
XLA Ops:
  0.6 0.7 pad_maximum_fusion
  1.3 0.6 reshape.52.gain_pair
  1.9 126.9 %forward.1 = (bf16[1536,256]{1,0:T(8,128)(2,1)}, bf16[256,1536]{1,0:T(8,128)(2,1)}, bf16[1536,256]{1,0:T(8,128)(2,1)}, f32[256,1536]{1,0:T(8,128)}, f32[8,1536]{...) custom-call(bf16[256,1536]{1,0:T(8,128)(2,1)} %bitcast.19, ...), custom_call_target="tpu_custom_call" | custom-call | tf_op jit(solution)/shard_map/forward/pallas_call | solution.py:983
  128.8 70.5 %backward.1 = (bf16[256,1536]{1,0:T(8,128)(2,1)}, bf16[128,1024]{1,0:T(8,128)(2,1)}, bf16[256,1536]{1,0:T(8,128)(2,1)}, f32[256,1536]{1,0:T(8,128)}, f32[8,1536]...) custom-call(bf16[256,1536]{1,0:T(8,128)(2,1)} %get-tuple-element.57., ...), custom_call_target="tpu_custom_call" | custom-call | tf_op jit(solution)/shard_map/backward/pallas_call | solution.py:1627
  199.3 142.1 %dense_weights.1 = (f32[256,1536]{1,0:T(8,128)}, bf16[128,1536]{1,0:T(8,128)(2,1)}, bf16[3,128,1536]{2,1,0:T(8,128)(2,1)}, bf16[384,1536]{1,0:T(8,128)(2,1)}, bf...) custom-call(bf16[1536,256]{1,0:T(8,128)(2,1)} %get-tuple-element.72., ...), custom_call_target="tpu_custom_call" | custom-call | tf_op jit(solution)/shard_map/dense_weights/pallas_call | solution.py:2016
  341.4 14.7 %widen.1 = (f32[3072,1024]{1,0:T(8,128)}, f32[1024,1536]{1,0:T(8,128)}, f32[384,1536]{1,0:T(8,128)}, f32[384,1536]{1,0:T(8,128)}, f32[384,1024]{1,0:T(8,128)}, /...) custom-call(bf16[3072,256]{1,0:T(8,128)(2,1)} %get-tuple-element.71.refs_0_, ...), custom_call_target="tpu_custom_call" | custom-call | tf_op jit(solution)/shard_map/widen/pallas_call | solution.py:2107

commit v9 on v8

--- a/solution.py
+++ b/solution.py
@@ -485,7 +485,7 @@
 
 
 def forward_kernel(
-    tokens,
+    tokens_src,
     routes,
     gates,
     gain_pair,
@@ -519,6 +519,7 @@
     query,
     turned_attn,
     middle,
+    tokens,
     gains,
     turned_rows,
     pair_weight,
@@ -556,6 +557,7 @@
     key_sem,
     emit_sem,
     last_sem,
+    input_sem,
 ):
     r = types.SimpleNamespace(**locals())
     place = Place()
@@ -644,7 +646,12 @@
     table_loads = [
         local(r.tables.at[i, at], table, r.table_sem.at[i]) for i, table in enumerate((r.cosine, r.sine))
     ]
-    for load in table_loads + loads:
+    token_load = local(r.tokens_src, r.tokens, r.input_sem.at[MB])
+    grad_loads = [
+        local(r.cotangent.at[m * rows : (m + 1) * rows], r.grads_all.at[m, shard], r.input_sem.at[m])
+        for m in range(MB)
+    ]
+    for load in [token_load] + table_loads + loads + grad_loads:
         load.start()
     expert_loads = [
         local(r.expand_src, r.expand, r.expert_sem.at[0]),
@@ -652,8 +659,6 @@
     ]
     for load in expert_loads:
         load.start()
-    for m in range(MB):
-        r.grads_all[m, shard] = r.cotangent[m * rows : (m + 1) * rows]
     grad_squares = [Square(place, r.grads_all.at[m], r.square_direct_sem, r.square_relay_sem, 2 * m) for m in range(MB)]
     row_squares = [
         Square(place, r.rows_all.at[m], r.square_direct_sem, r.square_relay_sem, 2 * (MB + m)) for m in range(MB)
@@ -670,6 +675,7 @@
             columns = slice(b * held, (b + 1) * held)
             write(columns, (values[:, columns] * r.gain_rows_out[row : row + 1, columns]).astype(bf16))
 
+    token_load.wait()
     values = r.tokens[...].astype(f32)
     unit = values * lax.rsqrt(jnp.mean(values * values, axis=-1, keepdims=True) + eps)
     for copy in small_copies:
@@ -686,7 +692,7 @@
         r.combine[b] = spread.T
     for m in range(MB):
         r.bias[m] = visible_bias(r.starts, m, place.context, (rows, length), 0)
-    for load in table_loads:
+    for load in table_loads + grad_loads:
         load.wait()
 
     relay_weight(0)
@@ -982,7 +988,7 @@
     blocks = (MB, SHARDS, rows, MODEL_WIDTH)
     return pl.pallas_call(
         forward_kernel,
-        in_specs=[vmem] * 5 + [pl.BlockSpec(memory_space=pltpu.SMEM)] + [anywhere] * 6,
+        in_specs=[anywhere] + [vmem] * 3 + [anywhere, pl.BlockSpec(memory_space=pltpu.SMEM)] + [anywhere] * 6,
         out_specs=[anywhere] * 4 + [vmem] * 3 + [anywhere] * 11,
         out_shape=[
             shape(tokens.shape[::-1], bf16),
@@ -1007,6 +1013,7 @@
             low(*tokens.shape),
             low(*tokens.shape[::-1]),
             pltpu.VMEM(tokens.shape, f32),
+            low(*tokens.shape),
             low(SHARDS * GAIN_ROWS, held),
             low(MODEL_WIDTH, wide),
         ]
@@ -1044,6 +1051,7 @@
             dma((2, 2)),
             dma((10 * MB,)),
             dma((4,)),
+            dma((MB + 1,)),
         ],
         compiler_params=pltpu.CompilerParams(
             collective_id=1, has_side_effects=True, vmem_limit_bytes=VMEM_LIMIT
@@ -1696,9 +1704,10 @@
 
 
 DENSE = ("output", "query", "pair", "gain")
+LINE_ORDER = ("output", "query", "gain", "pair")
 DENSE_PARTS = 4
 FINE = 4
-GATHER_AFTER = {4: ("output",), 9: ("query",), 13: ("pair", "gain")}
+GATHER_AFTER = {4: ("output",), 9: ("query",), 13: ("gain", "pair")}
 OUTPUT_AFTER = 19
 DRAIN_LAG = 8
 
@@ -1841,7 +1850,7 @@
     for name, parts in (("gate", FINE), ("up", FINE), ("down", 2 * FINE)):
         pieces += line_pieces(place, at("own", name), at("near", name), at("far", name), getattr(r, name + "_total"), parts)
     expert_pieces = len(pieces)
-    for name in DENSE:
+    for name in LINE_ORDER:
         parts = 1 if name == "gain" else DENSE_PARTS
         pieces += line_pieces(
             place, at("sum", name), at("near", name), at("far", name), getattr(r, name + "_total"), parts
@@ -1969,7 +1978,7 @@
     number = len(pieces)
     first = expert_pieces
     spans = {}
-    for name in DENSE:
+    for name in LINE_ORDER:
         parts = 1 if name == "gain" else DENSE_PARTS
         spans[name] = range(first, first + parts)
         first += parts

time: 362 us -> 362 us (level)
  no operation moved by 1% of the time
where the time goes in v9:
time: 362 us; the launch traced here: 356 us
  Pallas kernels  354 us (98%)
    pallas_call x1, Pallas kernels, dense_weights(): pl.pallas_call(dense_kernel, in_specs=[anywhere] * 3 + [vmem, anywhere] +...  142 us
    pallas_call x1, Pallas kernels, forward(): pl.pallas_call(forward_kernel, in_specs=[anywhere] + [vmem] * 3 + [anywhe...  126 us
    pallas_call x1, Pallas kernels, backward(): pl.pallas_call(backward_kernel, in_specs=[anywhere, pl.BlockSpec(memory_s...  70.5 us
    pallas_call x1, Pallas kernels, widen(): pl.pallas_call(widen_kernel, grid=(n,), in_specs=[every(a) for a in expan...  14.7 us

profile of v9, /device:TPU:0, one launch (start us, length us, event | category | flops | bytes accessed | tf_op | source)
XLA Modules:
  0.0 356.1 jit_solution(16699505065743349307)
XLA Ops:
  0.6 0.7 pad_maximum_fusion
  1.3 0.6 reshape.52.gain_pair
  1.9 126.3 %forward.1 = (bf16[1536,256]{1,0:T(8,128)(2,1)}, bf16[256,1536]{1,0:T(8,128)(2,1)}, bf16[1536,256]{1,0:T(8,128)(2,1)}, f32[256,1536]{1,0:T(8,128)}, f32[8,1536]{...) custom-call(bf16[256,1536]{1,0:T(8,128)(2,1)} %bitcast.19, ...), custom_call_target="tpu_custom_call" | custom-call | tf_op jit(solution)/shard_map/forward/pallas_call | solution.py:989
  128.3 70.5 %backward.1 = (bf16[256,1536]{1,0:T(8,128)(2,1)}, bf16[128,1024]{1,0:T(8,128)(2,1)}, bf16[256,1536]{1,0:T(8,128)(2,1)}, f32[256,1536]{1,0:T(8,128)}, f32[8,1536]...) custom-call(bf16[256,1536]{1,0:T(8,128)(2,1)} %get-tuple-element.57., ...), custom_call_target="tpu_custom_call" | custom-call | tf_op jit(solution)/shard_map/backward/pallas_call | solution.py:1635
  198.8 142.2 %dense_weights.1 = (f32[256,1536]{1,0:T(8,128)}, bf16[128,1536]{1,0:T(8,128)(2,1)}, bf16[3,128,1536]{2,1,0:T(8,128)(2,1)}, bf16[384,1536]{1,0:T(8,128)(2,1)}, bf...) custom-call(bf16[1536,256]{1,0:T(8,128)(2,1)} %get-tuple-element.72., ...), custom_call_target="tpu_custom_call" | custom-call | tf_op jit(solution)/shard_map/dense_weights/pallas_call | solution.py:2025
  341.0 14.7 %widen.1 = (f32[3072,1024]{1,0:T(8,128)}, f32[1024,1536]{1,0:T(8,128)}, f32[384,1536]{1,0:T(8,128)}, f32[384,1536]{1,0:T(8,128)}, f32[384,1024]{1,0:T(8,128)}, /...) custom-call(bf16[3072,256]{1,0:T(8,128)(2,1)} %get-tuple-element.71.refs_0_, ...), custom_call_target="tpu_custom_call" | custom-call | tf_op jit(solution)/shard_map/widen/pallas_call | solution.py:2116
